TPU v7x, 32 devices: a whole 2x2x4 slice. The times are simulated.
32 devices in a mesh: scene: 2 (over y), queue: 4 (over z), tok: 2 (over x), cfg: 2 (over core).
Axes of the slice: x: 2, y: 2, z: 4, core: 2. Of those that a mesh axis runs over, the one named last changes fastest.
Arguments:
- latents: float32 [32, 16, 96], P(('scene', 'queue'), None, 'tok'), parts along dimension 0, may hold values from -6 to 6
- fresh_noise: float32 [32, 96], P(('scene', 'cfg'), 'tok'), parts along dimension 0, may hold values from -6 to 6
- levels: int32 [32], P(('scene', 'queue')), parts along dimension 0, may hold values from 0 to 15, as said below
- window_mask: int32 [32, 9], P(('scene', 'queue')), parts along dimension 0, may hold values from 0 to 1, as said below
- cond_embed: float32 [4, 1152], P(('scene', 'cfg')), parts along dimension 0, may hold values from -6 to 6
- level_mod: float32 [16, 3, 1152], replicated, may hold values from -3 to 3
- embed_weight: bfloat16 [16, 1152], replicated, may hold values from -1.5 to 1.5
- qkv_weight: bfloat16 [1152, 3, 1152], P(('queue', 'cfg'), None, 'tok'), may hold values from -0.1875 to 0.1875
- query_gain: float32 [72], replicated, may hold values from 0.25 to 1.75
- key_gain: float32 [72], replicated, may hold values from 0.25 to 1.75
- out_weight: bfloat16 [1152, 1152], P('tok', ('queue', 'cfg')), may hold values from -0.1875 to 0.1875
- final_gain: float32 [1152], replicated, may hold values from 0.5 to 1.5
- final_weight: bfloat16 [1152, 16], replicated, may hold values from -0.1875 to 0.1875
- guide_table: float32 [8], replicated, may hold values from 2 to 8
- guide_index: int32 [1], replicated, may hold values from 0 to 7
Outputs:
- velocity: float32 [32, 16, 96], P(('scene', 'queue'), 'cfg', 'tok'), parts along dimension 0
- new_queue: float32 [32, 16, 96], P(('scene', 'queue'), 'cfg', 'tok'), parts along dimension 0
There are 2 independent parts, one for each index of `scene`. A program takes and returns all parts, laid end to end along the dimension named above; an argument that names none is the same for every part. Nothing has to cross between parts.
Inputs may be any that keep to these rules, and one draw needn't show every extreme that they name: levels[f] differs from 16 * f // 16 by at most one; the first frame has level 0 and the last 15. window_mask[f, o] = 1 lets frame f attend frame f + o - 4; window_mask[f, 4] = 1; entries whose frame lies outside 0 to 15 are 0.
All inputs are finite; a program needn't handle non-finite values.
Results may differ from a plain program's by a relative error of at most 0.0065.
Values may be sent and summed in bfloat16 or wider, within the bound.
No kernel may reach another device: no remote copies, remote signals or barrier semaphores. Data moves between devices by JAX's collectives and lax.ppermute only.
A program may use at most 64 MiB of HBM per device.

v0:
```python
import jax
import jax.numpy as jnp
from jax import lax
from jax.sharding import PartitionSpec as P

EPS_NORM = 1e-06
TIME_SHIFT = 3.0


def with_halo(cells, sides, width):
    for axis, dim in sides:
        count = lax.axis_size(axis)
        ends = count - 1
        head = lax.slice_in_dim(cells, 0, width, axis=dim)
        tail = lax.slice_in_dim(cells, cells.shape[dim] - width, cells.shape[dim], axis=dim)
        cells = jnp.concatenate(
            [
                lax.ppermute(tail, axis, [(i, (i + 1) % count) for i in range(ends)]),
                cells,
                lax.ppermute(head, axis, [((i + 1) % count, i) for i in range(ends)]),
            ],
            axis=dim,
        )
    return cells


def from_partner(value, axis, bit):
    return lax.ppermute(value, axis, [(i, i ^ 1 << bit) for i in range(lax.axis_size(axis))])


def shifted(value, axis, steps):
    count = lax.axis_size(axis)
    initial, last = (max(0, -steps), min(count, count - steps))
    return lax.ppermute(value, axis, [(source, source + steps) for source in range(initial, last)])


def layer_norm(values):
    center = jnp.mean(values, axis=-1, keepdims=True)
    deviate = values - center
    spread = jnp.mean(deviate * deviate, axis=-1, keepdims=True)
    return deviate * lax.rsqrt(spread + EPS_NORM)


def rms_norm(values, scaling):
    return (
        values * lax.rsqrt(jnp.mean(values * values, axis=-1, keepdims=True) + EPS_NORM) * scaling
    )


def noise_sigma(fraction):
    return TIME_SHIFT * fraction / (1.0 + (TIME_SHIFT - 1.0) * fraction)


def temporal_attention(
    queries, key_rows, value_rows, window_mask, first_frame, total_frames, window
):
    frames = queries.shape[0]
    numerator = jnp.zeros(queries.shape, jnp.float32)
    denominator = jnp.zeros(queries.shape[:-1], jnp.float32)
    for offset in range(2 * window + 1):
        near_keys = key_rows[offset : offset + frames].astype(jnp.float32)
        near_values = value_rows[offset : offset + frames].astype(jnp.float32)
        scores = jnp.sum(queries * near_keys, axis=-1) * queries.shape[-1] ** (-0.5)
        target = first_frame + jnp.arange(frames, dtype=jnp.int32) + (offset - window)
        allowed = (window_mask[:, offset] == 1) & (target >= 0) & (target < total_frames)
        weights = jnp.exp(scores) * allowed.astype(jnp.float32)[:, None, None]
        numerator = numerator + weights[..., None] * near_values
        denominator = denominator + weights
    return numerator / denominator[..., None]


def on_device(
    latents,
    fresh_noise,
    levels,
    window_mask,
    cond_embed,
    level_mod,
    embed_weight,
    qkv_weight,
    query_gain,
    key_gain,
    out_weight,
    final_gain,
    final_weight,
    guide_table,
    guide_index,
):
    frames = latents.shape[0]
    tok_count = latents.shape[2]
    model_width = embed_weight.shape[1]
    head_dim = query_gain.shape[0]
    levels_all = level_mod.shape[0]
    queue_count = lax.axis_size("queue")
    all_tokens = lax.all_gather(latents, "tok", axis=2, tiled=True)
    seq_tokens = all_tokens.shape[2]
    row_count = frames * seq_tokens
    embedded = (
        jnp.einsum(
            "fcs,cd->fsd",
            all_tokens.astype(jnp.bfloat16),
            embed_weight,
            preferred_element_type=jnp.float32,
        )
        + cond_embed[0]
    )
    one_hot = (levels[:, None] == jnp.arange(levels_all, dtype=jnp.int32)[None, :]).astype(
        jnp.float32
    )
    modulate = jnp.dot(
        one_hot, level_mod.reshape(levels_all, 3 * model_width), precision=lax.Precision.HIGHEST
    ).reshape(frames, 3, model_width)
    normed = (layer_norm(embedded) * (1.0 + modulate[:, None, 1]) + modulate[:, None, 0]).astype(
        jnp.bfloat16
    )
    norm_rows = normed.reshape(row_count, model_width)
    local_cols = qkv_weight.shape[2]
    shard_piece = lax.all_gather(qkv_weight, ("queue", "cfg"), axis=0, tiled=True)
    flat_piece = shard_piece.reshape(shard_piece.shape[0], 3 * local_cols)
    projected = jnp.dot(norm_rows, flat_piece, preferred_element_type=jnp.float32)
    projected = projected.reshape(frames, seq_tokens, 3, local_cols // head_dim, head_dim)
    queries = rms_norm(projected[:, :, 0], query_gain)
    keys_values = jnp.stack(
        [
            rms_norm(projected[:, :, 1], key_gain).astype(jnp.bfloat16),
            projected[:, :, 2].astype(jnp.bfloat16),
        ]
    )
    widened = with_halo(keys_values, (("queue", 1),), frames)
    first_frame = lax.axis_index("queue") * frames
    attended = temporal_attention(
        queries, widened[0], widened[1], window_mask, first_frame, frames * queue_count, frames
    )
    attended = attended.astype(jnp.bfloat16).reshape(frames, seq_tokens, local_cols)
    flat_heads = attended.reshape(row_count, local_cols)
    partial_value = jnp.dot(
        flat_heads,
        lax.all_gather(out_weight, ("queue", "cfg"), axis=1, tiled=True),
        preferred_element_type=jnp.float32,
    )
    mixed_out = lax.psum_scatter(
        partial_value.reshape(frames, seq_tokens, model_width).astype(jnp.bfloat16),
        "tok",
        scatter_dimension=1,
        tiled=True,
    ).astype(jnp.float32)
    own_start = lax.axis_index("tok") * tok_count
    own_embed = lax.dynamic_slice_in_dim(embedded, own_start, tok_count, 1)
    summed = own_embed + modulate[:, None, 2] * mixed_out
    final_rows = (layer_norm(summed) * final_gain).astype(jnp.bfloat16)
    velocity = jnp.einsum(
        "ftd,dc->fct", final_rows, final_weight, preferred_element_type=jnp.float32
    )
    half_values = velocity.shape[1] // 2
    branch_index = lax.axis_index("cfg")
    own_first = branch_index * half_values
    other_first = (1 - branch_index) * half_values
    outgoing = lax.dynamic_slice_in_dim(velocity, other_first, half_values, 1)
    partner = from_partner(outgoing, "cfg", 0)
    mine = lax.dynamic_slice_in_dim(velocity, own_first, half_values, 1)
    is_cond = branch_index == 0
    cond_vel = jnp.where(is_cond, mine, partner)
    uncond_vel = jnp.where(is_cond, partner, mine)
    entries = guide_table.shape[0]
    guidance = jnp.sum(
        guide_table * (jnp.arange(entries, dtype=jnp.int32) == guide_index[0]).astype(jnp.float32)
    )
    guided = uncond_vel + guidance * (cond_vel - uncond_vel)
    current = noise_sigma((levels + 1).astype(jnp.float32) / levels_all)
    upcoming = noise_sigma(levels.astype(jnp.float32) / levels_all)
    own_latents = lax.dynamic_slice_in_dim(latents, own_first, half_values, 1)
    updated = own_latents + (upcoming - current)[:, None, None] * guided
    incoming = shifted(updated[:1], "queue", -1)
    is_last = lax.axis_index("queue") == queue_count - 1
    incoming = jnp.where(is_last, fresh_noise[None], incoming)
    new_queue = jnp.concatenate([updated[1:], incoming], axis=0)
    return (guided, new_queue)


def solution(mesh):
    placed = (
        P(("scene", "queue"), None, "tok"),
        P(("scene", "cfg"), "tok"),
        P(("scene", "queue")),
        P(("scene", "queue"), None),
        P(("scene", "cfg"), None),
        P(),
        P(),
        P(("queue", "cfg"), None, "tok"),
        P(),
        P(),
        P("tok", ("queue", "cfg")),
        P(),
        P(),
        P(),
        P(),
    )
    return jax.shard_map(
        on_device,
        mesh=mesh,
        in_specs=placed,
        out_specs=(P(("scene", "queue"), "cfg", "tok"), P(("scene", "queue"), "cfg", "tok")),
        check_vma=False,
    )
```

profile of v0, /device:TPU:0, one launch (start us, length us, event | category | flops | bytes accessed | tf_op | source)
XLA Modules:
  0.0 155.2 jit_solution(13218939681544908411)
XLA Ops:
  7.2 0.7 all-gather.3.cloned.1.call-update
  8.0 0.7 all-gather.5.cloned.1.call-update
  8.7 0.9 copy.34
  9.6 5.7 %all_gather.9 = bf16[4,16,96]{1,0,2:T(4,128)(2,1)S(1)} all-gather(bf16[4,16,48]{1,0,2:T(4,128)(2,1)S(1)} %copy.34), channel_id=1, replica_groups=mesh['scene'=2,'queue'=4,'tok'=2,'cfg'=2] {'tok'}, dimensions={2}, use_global_device_ids=true | all-gather | bytes 18432 | tf_op jit(solution)/shard_map/all_gather | solution.py:95
  15.3 0.7 reduce
  16.0 1.3 fusion.60
  17.4 0.3 multiply_reduce_fusion
  18.3 0.3 fusion.46
  18.6 42.8 %all-gather.3.cloned.1.call-done = bf16[1152,3,576]{2,0,1:T(8,128)(2,1)} async-done(((bf16[144,3,576]{2,0,1:T(8,128)(2,1)}), bf16[1152,3,576]{2,0,1:T(8,128)(2,1)}) %all-gather.3.cloned.1.call-update) | async-done | bytes 3981328 | tf_op jit(solution)/shard_map/all_gather | solution.py:118
  61.5 6.6 %copy.38 = bf16[1152,3,576]{0,2,1:T(8,128)(2,1)} copy(bf16[1152,3,576]{2,0,1:T(8,128)(2,1)} %all-gather.3.cloned.1.call-done) | data formatting | bytes 7962624 | tf_op jit(solution)/shard_map/all_gather | solution.py:118
  68.0 4.6 %fusion.25 = f32[4,96,3,8,72]{1,4,3,2,0:T(8,128)S(1)} fusion(bf16[3,8,72,1152,1]{3,2,1,0,4:T(8,128)(2,1)} %bitcast.197, f32[4,96,1152]{2,1,0:T(8,128)S(1)} %get-tuple-element.56, f32[4,1152]{1,0:T(4,128)S(1)} %get-tuple-element.53, f32[4,1152]{1,0:T(4,128)S(1)} %get-tuple-element.54, f32[4,96]{1,0:T(4,128)S(1)} %add_rsqrt_fusion.3, ...), kind=kOutput, calls=%fused_computation.57 | convolution fusion | flops 1531035648 | bytes 8444928 | tf_op jit(solution)/shard_map/dot_general | solution.py:120
  72.7 0.3 multiply_reduce_fusion.2
  73.1 0.5 copy-done.7
  74.1 1.7 %collective-permute-start = (bf16[2,4,96,8,72]{2,4,3,1,0:T(8,128)(2,1)S(1)}, bf16[2,4,96,8,72]{2,4,3,1,0:T(8,128)(2,1)S(1)}, u32[]{:S(2)}, u32[]{:S(2)}) collective-permute-start(bf16[2,4,96,8,72]{2,4,3,1,0:T(8,128)(2,1)S(1)} %pad_maximum_fusion.1), channel_id=1, source_target_pairs={{0,4},{4,8},{8,12},{1,5},{5,9},{9,13},{2,6},{6,10},{10,14},{3,7},{... | collective-permute-start | bytes 2654216 | tf_op jit(solution)/shard_map/ppermute | solution.py:18
  75.9 1.3 collective-permute-start.1
  77.3 30.0 %collective-permute-done = bf16[2,4,96,8,72]{2,4,3,1,0:T(8,128)(2,1)S(1)} collective-permute-done((bf16[2,4,96,8,72]{2,4,3,1,0:T(8,128)(2,1)S(1)}, bf16[2,4,96,8,72]{2,4,3,1,0:T(8,128)(2,1)S(1)}, u32[]{:S(2)}, u32[]{:S(2)}) %collective-permute-start) | collective-permute-done | bytes 884768 | tf_op jit(solution)/shard_map/ppermute | solution.py:18
  107.3 2.8 %collective-permute-done.1 = bf16[2,4,96,8,72]{2,4,3,1,0:T(8,128)(2,1)S(1)} collective-permute-done((bf16[2,4,96,8,72]{2,4,3,1,0:T(8,128)(2,1)S(1)}, bf16[2,4,96,8,72]{2,4,3,1,0:T(8,128)(2,1)S(1)}, u32[]{:S(2)}, u32[]{:S(2)}) %collective-permute-start.1) | collective-permute-done | bytes 884768 | tf_op jit(solution)/shard_map/ppermute | solution.py:20
  110.1 1.1 maximum_maximum_fusion
  111.3 2.5 %fusion.23 = (f32[4,96,8]{1,2,0:T(8,128)S(1)}, f32[4,96,8]{1,2,0:T(8,128)S(1)}, f32[4,96,8]{1,2,0:T(8,128)S(1)}, f32[4,96,8]{1,2,0:T(8,128)S(1)}, f32[4,96,8]{1,...) fusion(bf16[2,4,96,8,72]{2,4,3,1,0:T(8,128)(2,1)S(1)} %collecti, ...), kind=kLoop, calls=%fused_computation.52 | loop fusion | flops 7050240 | bytes 5444160 | tf_op jit(solution)/shard_map/reduce_sum | solution.py:63
  113.9 0.8 fusion.58
  115.1 1.2 fusion.8
  116.3 3.3 %convolution_convert_fusion = bf16[4,96,1152]{2,1,0:T(8,128)(2,1)} fusion(bf16[4,96,576]{1,2,0:T(8,128)(2,1)S(1)} %fusion.8, bf16[576,1152]{0,1:T(8,128)(2,1)} %all-gather.5.cloned.1.call-done), kind=kOutput, calls=%fused_computation.1 | convolution fusion | flops 510050304 | bytes 2654208 | tf_op jit(solution)/shard_map/dot_general | solution.py:136
  120.4 17.5 %reduce-scatter.2.cloned.1.call-done = bf16[4,48,1152]{2,1,0:T(8,128)(2,1)} async-done(((bf16[4,96,1152]{2,1,0:T(8,128)(2,1)}), bf16[4,48,1152]{2,1,0:T(8,128)(2,1)}) %reduce-scatter.2.cloned.1.call-update) | async-done | bytes 442384 | tf_op jit(solution)/shard_map/reduce_scatter | solution.py:141
  137.9 1.3 fusion.35
  139.2 0.3 multiply_reduce_fusion.3
  139.6 0.4 fusion.31
  140.2 0.7 fusion.56
  140.8 0.4 collective-permute-done.2
  141.2 1.3 multiply_add_fusion.2
  142.5 1.3 collective-permute-start.3
  143.8 4.2 %collective-permute-done.3 = f32[1,8,48]{2,1,0:T(8,128)S(1)} collective-permute-done((f32[1,8,48]{2,1,0:T(8,128)S(1)}, f32[1,8,48]{2,1,0:T(8,128)S(1)}, u32[]{:S(2)}, u32[]{:S(2)}) %collective-permute-start.3) | collective-permute-done | bytes 1568 | tf_op jit(solution)/shard_map/ppermute | solution.py:34
  148.0 0.6 pad_maximum_fusion.2
  (59 shorter events, 2.2 us)
Async XLA Ops:
  7.2 10.5 %copy-start = (f32[16,3,1152]{2,0,1:T(8,128)S(1)}, f32[16,3,1152]{2,0,1:T(8,128)}, u32[]{:S(2)}) copy-start(f32[16,3,1152]{2,0,1:T(8,128)} %param.20) | copy-start | bytes 663556
  7.2 54.3 %all-gather.3.cloned.1.call-start = ((), (), s32[]{:S(2)}) async-start(), calls=%async_computation.1 | async-start | bytes 4976640 | tf_op jit(solution)/shard_map/all_gather | solution.py:118
  7.9 108.4 %all-gather.5.cloned.1.call-start = ((), (), s32[]{:S(2)}) async-start(), calls=%async_computation.2 | async-start | bytes 1658880 | tf_op jit(solution)/shard_map/all_gather | solution.py:138
  8.7 129.2 %reduce-scatter.2.cloned.1.call-start = ((), (), s32[]{:S(2)}) async-start(), calls=%async_computation.3 | async-start | bytes 1327104 | tf_op jit(solution)/shard_map/reduce_scatter | solution.py:141
  17.3 0.7 copy-start.8
  17.3 0.9 copy-start.4
  73.0 0.7 copy-start.7
  74.1 33.2 %collective-permute-start = (bf16[2,4,96,8,72]{2,4,3,1,0:T(8,128)(2,1)S(1)}, bf16[2,4,96,8,72]{2,4,3,1,0:T(8,128)(2,1)S(1)}, u32[]{:S(2)}, u32[]{:S(2)}) collective-permute-start(bf16[2,4,96,8,72]{2,4,3,1,0:T(8,128)(2,1)S(1)} %pad_maximum_fusion.1), channel_id=1, source_target_pairs={{0,4},{4,8},{8,12},{1,5},{5,9},{9,13},{2,6},{6,10},{10,14},{3,7},{... | collective-permute-start | bytes 2654216 | tf_op jit(solution)/shard_map/ppermute | solution.py:18
  75.9 34.3 %collective-permute-start.1 = (bf16[2,4,96,8,72]{2,4,3,1,0:T(8,128)(2,1)S(1)}, bf16[2,4,96,8,72]{2,4,3,1,0:T(8,128)(2,1)S(1)}, u32[]{:S(2)}, u32[]{:S(2)}) collective-permute-start(bf16[2,4,96,8,72]{2,4,3,1,0:T(8,128)(2,1)S(1)} %pad_maximum_fusion.1), channel_id=1, source_target_pairs={{4,0},{8,4},{12,8},{5,1},{9,5},{13,9},{6,2},{10,6},{14,10},{7,3},{... | collective-permute-start | bytes 2654216 | tf_op jit(solution)/shard_map/ppermute | solution.py:20
  107.3 3.9 %copy-start.1 = (bf16[2,4,96,8,72]{2,4,3,1,0:T(8,128)(2,1)}, bf16[2,4,96,8,72]{2,4,3,1,0:T(8,128)(2,1)S(1)}, u32[]{:S(2)}) copy-start(bf16[2,4,96,8,72]{2,4,3,1,0:T(8,128)(2,1)S(1)} %collective-permute-done) | copy-start | bytes 2654212
  110.1 1.1 copy-start.2
  110.1 1.1 copy-start.9
  113.9 1.1 slice-start
  113.9 1.2 slice-start.1
  137.9 1.3 copy-start.3
  137.9 1.6 %copy-start.10 = (bf16[1152,16]{0,1:T(8,128)(2,1)S(1)}, bf16[1152,16]{0,1:T(8,128)(2,1)}, u32[]{:S(2)}) copy-start(bf16[1152,16]{0,1:T(8,128)(2,1)} %param.27) | copy-start | bytes 110596
  137.9 1.6 %copy-start.11 = (f32[1152]{0:T(1024)S(1)}, f32[1152]{0:T(1024)}, u32[]{:S(2)}) copy-start(f32[1152]{0:T(1024)} %param.26) | copy-start | bytes 13828
  139.5 0.7 copy-start.12
  139.5 1.7 %copy-start.5 = (f32[4,16,48]{2,1,0:T(8,128)S(1)}, f32[4,16,48]{2,1,0:T(8,128)}, u32[]{:S(2)}) copy-start(f32[4,16,48]{2,1,0:T(8,128)} %param.15) | copy-start | bytes 36868
  139.5 8.5 %copy-start.6 = (f32[8,48]{1,0:T(8,128)S(1)}, f32[8,48]{1,0:T(8,128)}, u32[]{:S(2)}) copy-start(f32[8,48]{1,0:T(8,128)} %param.16) | copy-start | bytes 4612
  140.0 1.2 collective-permute-start.2
  142.5 5.5 %collective-permute-start.3 = (f32[1,8,48]{2,1,0:T(8,128)S(1)}, f32[1,8,48]{2,1,0:T(8,128)S(1)}, u32[]{:S(2)}, u32[]{:S(2)}) collective-permute-start(f32[1,8,48]{2,1,0:T(8,128)S(1)} %slice.213), channel_id=1, source_target_pairs={{4,0},{8,4},{12,8},{5,1},{9,5},{13,9},{6,2},{10,6},{14,10},{7,3},{... | collective-permute-start | bytes 4616 | tf_op jit(solution)/shard_map/ppermute | solution.py:34
Sparse Core Ops, SparseCore 0:
  9.6 51.8 all-gather.2
  63.1 25.5 all-gather.4
  119.8 18.0 reduce-scatter.1
where the time goes:
time: 156 us; the launch traced here: 155 us
  waiting for transfers between devices  99.1 us (64%)
  between operations  14.7 us (9%)
  other arithmetic  11.3 us (7%)
  matrix products  9.94 us (6%)
  local copies, waits for them, and re-layouts  9.93 us (6%)
  blocking collectives  5.66 us (4%)
  starting transfers between devices  4.42 us (3%)
    all_gather x1, waiting for transfers between devices, on_device(): lax.all_gather(qkv_weight, ('queue', 'cfg'), axis=0, tiled=True)  42.8 us
    ppermute x1, waiting for transfers between devices, with_halo(): lax.ppermute(tail, axis, [(i, (i + 1) % count) for i in range(ends)])  30 us
    reduce_scatter x1, waiting for transfers between devices, on_device(): lax.psum_scatter(partial_value.reshape(frames, seq_tokens, model_width).a...  17.5 us
    all_gather x1, local copies, waits for them, and re-layouts, on_device(): lax.all_gather(qkv_weight, ('queue', 'cfg'), axis=0, tiled=True)  6.58 us
    all_gather x1, blocking collectives, on_device(): all_tokens = lax.all_gather(latents, 'tok', axis=2, tiled=True)  5.66 us
    dot_general x1, matrix products, on_device(): jnp.dot(norm_rows, flat_piece, preferred_element_type=jnp.float32)  4.63 us
    ppermute x1, waiting for transfers between devices, shifted(): lax.ppermute(value, axis, [(source, source + steps) for source in range(i...  4.18 us
    dot_general x1, matrix products, on_device(): jnp.dot(flat_heads, lax.all_gather(out_weight, ('queue', 'cfg'), axis=1,...  3.33 us
  transfers between devices with their start and end apart: 7, of which 6 were waited for; matrix products, arithmetic and copies ran while one was open for 14% of the time, Pallas kernels for 0%

commit v1 on v0

--- a/solution.py
+++ b/solution.py
@@ -1,10 +1,26 @@
+import functools
+
 import jax
 import jax.numpy as jnp
 from jax import lax
+from jax.experimental import pallas as pl
+from jax.experimental.pallas import tpu as pltpu
 from jax.sharding import PartitionSpec as P
 
 EPS_NORM = 1e-06
 TIME_SHIFT = 3.0
+LANES = 128
+VMEM_BYTES = 40 * 1024 * 1024
+F32 = jnp.float32
+BF16 = jnp.bfloat16
+
+
+def noise_sigma(fraction):
+    return TIME_SHIFT * fraction / (1.0 + (TIME_SHIFT - 1.0) * fraction)
+
+
+def from_partner(value, axis, bit):
+    return lax.ppermute(value, axis, [(i, i ^ 1 << bit) for i in range(lax.axis_size(axis))])
 
 
 def with_halo(cells, sides, width):
@@ -24,10 +40,6 @@
     return cells
 
 
-def from_partner(value, axis, bit):
-    return lax.ppermute(value, axis, [(i, i ^ 1 << bit) for i in range(lax.axis_size(axis))])
-
-
 def shifted(value, axis, steps):
     count = lax.axis_size(axis)
     initial, last = (max(0, -steps), min(count, count - steps))
@@ -45,10 +57,6 @@
     return (
         values * lax.rsqrt(jnp.mean(values * values, axis=-1, keepdims=True) + EPS_NORM) * scaling
     )
-
-
-def noise_sigma(fraction):
-    return TIME_SHIFT * fraction / (1.0 + (TIME_SHIFT - 1.0) * fraction)
 
 
 def temporal_attention(
@@ -69,7 +77,7 @@
     return numerator / denominator[..., None]
 
 
-def on_device(
+def on_device_general(
     latents,
     fresh_noise,
     levels,
@@ -126,10 +134,11 @@
             projected[:, :, 2].astype(jnp.bfloat16),
         ]
     )
-    widened = with_halo(keys_values, (("queue", 1),), frames)
+    window = window_mask.shape[1] // 2
+    widened = with_halo(keys_values, (("queue", 1),), window)
     first_frame = lax.axis_index("queue") * frames
     attended = temporal_attention(
-        queries, widened[0], widened[1], window_mask, first_frame, frames * queue_count, frames
+        queries, widened[0], widened[1], window_mask, first_frame, frames * queue_count, window
     )
     attended = attended.astype(jnp.bfloat16).reshape(frames, seq_tokens, local_cols)
     flat_heads = attended.reshape(row_count, local_cols)
@@ -177,6 +186,367 @@
     return (guided, new_queue)
 
 
+def kernel_call(body, out_shapes, spaces, scratch=(), **cost):
+    kinds = {"v": pltpu.VMEM, "s": pltpu.SMEM}
+    many = isinstance(out_shapes, (list, tuple))
+    return pl.pallas_call(
+        body,
+        out_shape=out_shapes,
+        in_specs=[pl.BlockSpec(memory_space=kinds[k]) for k in spaces],
+        out_specs=[pl.BlockSpec(memory_space=pltpu.VMEM) for _ in out_shapes]
+        if many
+        else pl.BlockSpec(memory_space=pltpu.VMEM),
+        scratch_shapes=list(scratch),
+        compiler_params=pltpu.CompilerParams(vmem_limit_bytes=VMEM_BYTES),
+        cost_estimate=pl.CostEstimate(
+            flops=cost.get("flops", 1000000),
+            bytes_accessed=cost.get("bytes_accessed", 1000000),
+            transcendentals=0,
+        ),
+    )
+
+
+def split_terms(values, terms):
+    parts = []
+    for _ in range(terms):
+        part = values.astype(BF16)
+        parts.append(part)
+        values = values - part.astype(F32)
+    return parts
+
+
+def dot_tn(left, right):
+    return lax.dot_general(
+        left, right, (((0,), (0,)), ((), ())), preferred_element_type=F32
+    )
+
+
+def pack_kernel(head_dim, latents, levels, window_mask, qkv, chunks, packed):
+    for h in range(chunks.shape[0]):
+        first = h * head_dim
+        chunks[h] = jnp.concatenate(
+            [qkv[part, :, first : first + head_dim] for part in range(3)], axis=1
+        )
+    frames, values, tokens = latents.shape
+    span = window_mask.shape[1]
+    pieces = []
+    for f in range(frames):
+        rows = [latents[f]]
+        side = jnp.zeros((packed.shape[0] - values, tokens), F32)
+        row_id = lax.broadcasted_iota(jnp.int32, side.shape, 0)
+        for o in range(span):
+            side = jnp.where(row_id == o, window_mask[f, o].astype(F32), side)
+        side = jnp.where(row_id == span, levels[f].astype(F32), side)
+        rows.append(side)
+        pieces.append(jnp.concatenate(rows, axis=0))
+    packed[...] = jnp.concatenate(pieces, axis=1)
+
+
+def prepare_kernel(
+    frames, values, span, gathered, cond, level_mod, embed, lhs, xin, rstd_out, mask_out
+):
+    width = embed.shape[1]
+    rows = xin.shape[1]
+    queue_tok = gathered.shape[0]
+    branches = cond.shape[0]
+    all_frames = xin.shape[0]
+    toks = queue_tok * frames // all_frames
+    tokens = gathered.shape[2] // frames
+    weights = embed[...].astype(F32)
+    weights = weights - jnp.mean(weights, axis=1, keepdims=True)
+    conds = cond[...]
+    conds = conds - jnp.mean(conds, axis=1, keepdims=True)
+    basis = jnp.concatenate(
+        [weights, conds, jnp.zeros((rows - values - branches, width), F32)], axis=0
+    )
+    gram = lax.dot_general(
+        basis,
+        basis,
+        (((1,), (1,)), ((), ())),
+        preferred_element_type=F32,
+        precision=lax.Precision.HIGHEST,
+    ) * (1.0 / width)
+    row_id = lax.broadcasted_iota(jnp.int32, (rows, LANES), 0)
+    wide_id = lax.broadcasted_iota(jnp.int32, (rows, width), 0)
+    level_id = lax.broadcasted_iota(jnp.int32, (level_mod.shape[1], width), 0).astype(F32)
+    shift_row = values + branches
+    fill = LANES - toks * tokens
+    for f in range(all_frames):
+        q, part = divmod(f, frames)
+        info = [
+            gathered[q * toks + t, :, part * tokens : (part + 1) * tokens] for t in range(toks)
+        ]
+        level = info[0][values + span : values + span + 1, 0:1]
+        chosen = level_id == level
+        shift = jnp.sum(jnp.where(chosen, level_mod[0], 0.0), axis=0, keepdims=True)
+        scale = jnp.sum(jnp.where(chosen, level_mod[1], 0.0), axis=0, keepdims=True)
+        block = basis * (1.0 + scale)
+        block = jnp.where((wide_id == shift_row) | (wide_id == shift_row + 1), shift, block)
+        lhs[f * rows : (f + 1) * rows, :] = block.astype(BF16)
+        info = jnp.concatenate(info + [jnp.ones((info[0].shape[0], fill), F32)], axis=1)
+        mask_out[f] = info[values : values + mask_out.shape[1]]
+        base = jnp.where(row_id < values, info[:rows], 0.0).astype(BF16).astype(F32)
+        for b in range(branches):
+            vec = jnp.where(row_id == values + b, 1.0, base)
+            spread = jnp.sum(
+                vec
+                * jnp.dot(gram, vec, preferred_element_type=F32, precision=lax.Precision.HIGHEST),
+                axis=0,
+                keepdims=True,
+            )
+            spread = jnp.maximum(spread, 0.0) + EPS_NORM
+            rstd = lax.rsqrt(spread)
+            std = spread * rstd
+            high = std.astype(BF16).astype(F32)
+            vec = jnp.where(row_id == shift_row, high, vec)
+            vec = jnp.where(row_id == shift_row + 1, std - high, vec)
+            xin[f, :, b * LANES : (b + 1) * LANES] = vec.astype(BF16)
+            rstd_out[f, :, b * LANES : (b + 1) * LANES] = rstd
+
+
+def attend_kernel(
+    frames, tokens, weight, lhs, xin, rstd_in, mask_in, gain_q, gain_k, out, proj, kfac, vfac, att
+):
+    all_frames, rows, lanes = xin.shape
+    head_dim = gain_q.shape[0]
+    window = (proj.shape[0] - all_frames) // 2
+    span = 2 * window + 1
+    branches = lanes // LANES
+    folded = jnp.dot(lhs[...], weight[...], preferred_element_type=F32)
+    high, low = split_terms(folded, 2)
+    gains = gain_q[...] * gain_k[...] * head_dim ** (-0.5)
+    gains = jnp.broadcast_to(gains, (head_dim, LANES))
+    for side in range(window):
+        for at in (side, all_frames + window + side):
+            proj[at] = jnp.zeros(proj.shape[1:], F32)
+            kfac[at] = jnp.zeros(kfac.shape[1:], F32)
+            vfac[at] = jnp.zeros(vfac.shape[1:], F32)
+    for f in range(all_frames):
+        piece = slice(f * rows, (f + 1) * rows)
+        made = dot_tn(high[piece], xin[f]) + dot_tn(low[piece], xin[f])
+        proj[f + window] = made
+        rstd = rstd_in[f]
+        keys = made[head_dim : 2 * head_dim]
+        square = jnp.mean(keys * keys, axis=0, keepdims=True)
+        kfac[f + window] = rstd * lax.rsqrt(rstd * rstd * square + EPS_NORM)
+        vfac[f + window] = rstd
+
+    def one_frame(f, carry):
+        for b in range(branches):
+            lane = slice(b * LANES, (b + 1) * LANES)
+            query = proj[f + window, 0:head_dim, lane]
+            rstd = vfac[f + window, :, lane]
+            square = jnp.mean(query * query, axis=0, keepdims=True)
+            qfac = rstd * lax.rsqrt(rstd * rstd * square + EPS_NORM)
+            query = query * gains
+            total = jnp.zeros((head_dim, LANES), F32)
+            norm = jnp.zeros((1, LANES), F32)
+            for o in range(span):
+                keys = proj[f + o, head_dim : 2 * head_dim, lane]
+                score = jnp.sum(query * keys, axis=0, keepdims=True)
+                score = score * (qfac * kfac[f + o, :, lane])
+                part = jnp.exp(score) * mask_in[f, o : o + 1, :]
+                norm = norm + part
+                total = total + (part * vfac[f + o, :, lane]) * proj[f + o, 2 * head_dim :, lane]
+            att[f, b] = total / norm
+        return carry
+
+    lax.fori_loop(0, all_frames, one_frame, 0)
+    toks = out.shape[0] * frames // (all_frames * branches)
+    queues = all_frames // frames
+    for t in range(toks):
+        for q in range(queues):
+            for b in range(branches):
+                pieces = [
+                    att[min(q * frames + i, all_frames - 1), b, :, t * tokens : (t + 1) * tokens]
+                    for i in range(frames + 1)
+                ]
+                at = (t * queues + q) * branches + b
+                out[at] = jnp.concatenate(pieces, axis=1).astype(BF16)
+
+
+def rows_kernel(
+    values, span, packed, following, cond, level_mod, embed, final_gain, emb_out, gate_out, gain_out
+):
+    levels_all, width = level_mod.shape
+    info = jnp.concatenate([packed[...], following[...]], axis=1)
+    lanes = info.shape[1]
+    vec = info[:values].astype(BF16)
+    ones = jnp.ones((16, lanes), BF16)
+    zero = jnp.zeros((13, width), BF16)
+    weights = jnp.concatenate([embed[...]] + split_terms(cond[...], 3) + [zero], axis=0)
+    emb_out[...] = dot_tn(weights, jnp.concatenate([vec, ones], axis=0))
+    level = info[values + span : values + span + 1]
+    one_hot = (lax.broadcasted_iota(jnp.int32, (levels_all, lanes), 0).astype(F32) == level).astype(
+        F32
+    ).astype(BF16)
+    gates = jnp.concatenate(split_terms(level_mod[...], 3), axis=0)
+    gate_out[...] = dot_tn(gates, jnp.concatenate([one_hot] * 3, axis=0))
+    gains = jnp.concatenate(split_terms(final_gain[...], 3) + [zero], axis=0)
+    gain_out[...] = dot_tn(gains, ones)
+
+
+def finish_kernel(half, attended, out_w, emb, gate, gain, final_w, branch, mine, send, scratch):
+    group = out_w.shape[2]
+    mixed = jnp.zeros(emb.shape, F32)
+    for g in range(out_w.shape[0]):
+        made = jnp.dot(
+            out_w[g], attended[g * group : (g + 1) * group, :], preferred_element_type=F32
+        )
+        mixed = mixed + made.astype(BF16).astype(F32)
+    summed = emb[...] + gate[...] * mixed
+    center = jnp.mean(summed, axis=0, keepdims=True)
+    deviate = summed - center
+    spread = jnp.mean(deviate * deviate, axis=0, keepdims=True)
+    final = (deviate * lax.rsqrt(spread + EPS_NORM) * gain[...]).astype(BF16)
+    scratch[...] = jnp.dot(final_w[...], final, preferred_element_type=F32)
+    own = pl.multiple_of(branch[0] * half, half)
+    other = pl.multiple_of((1 - branch[0]) * half, half)
+    mine[...] = scratch[pl.ds(own, half), :]
+    send[...] = scratch[pl.ds(other, half), :]
+
+
+def update_kernel(
+    values, span, levels_all, mine, partner, packed, following, noise, table, index, place, vel, new
+):
+    half = mine.shape[0]
+    frames, _, tokens = vel.shape
+    is_cond = place[0] == 0
+    own = pl.multiple_of(place[0] * half, half)
+    here, there = mine[...], partner[...]
+    cond = jnp.where(is_cond, here, there)
+    uncond = jnp.where(is_cond, there, here)
+    guided = uncond + table[index[0]] * (cond - uncond)
+    level = jnp.concatenate(
+        [packed[values + span : values + span + 1], following[values + span : values + span + 1]],
+        axis=1,
+    )
+    current = noise_sigma((level + 1.0) / levels_all)
+    upcoming = noise_sigma(level / levels_all)
+    latents = jnp.concatenate([packed[pl.ds(own, half), :], following[pl.ds(own, half), :]], axis=1)
+    updated = latents + (upcoming - current) * guided
+    is_last = place[1] == 1
+    for f in range(frames):
+        vel[f] = guided[:, f * tokens : (f + 1) * tokens]
+        moved = updated[:, (f + 1) * tokens : (f + 2) * tokens]
+        if f == frames - 1:
+            moved = jnp.where(is_last, noise[...], moved)
+        new[f] = moved
+
+
+def on_device_heads(
+    latents,
+    fresh_noise,
+    levels,
+    window_mask,
+    cond_embed,
+    level_mod,
+    embed_weight,
+    qkv_weight,
+    query_gain,
+    key_gain,
+    out_weight,
+    final_gain,
+    final_weight,
+    guide_table,
+    guide_index,
+):
+    frames, values, tokens = latents.shape
+    width = embed_weight.shape[1]
+    head_dim = query_gain.shape[0]
+    levels_all = level_mod.shape[0]
+    span = window_mask.shape[1]
+    window = span // 2
+    queues, toks, branches = (lax.axis_size(a) for a in ("queue", "tok", "cfg"))
+    group = queues * branches
+    q_at, branch = lax.axis_index("queue"), lax.axis_index("cfg")
+    all_frames = queues * frames
+    rows = -(-max(values + 4, values + span + 1) // 16) * 16
+    local_rows = qkv_weight.shape[0]
+    lanes = branches * LANES
+    row_lanes = (frames + 1) * tokens
+
+    chunks, packed = kernel_call(
+        functools.partial(pack_kernel, head_dim),
+        [
+            jax.ShapeDtypeStruct((group, local_rows, 3 * head_dim), BF16),
+            jax.ShapeDtypeStruct((rows, frames * tokens), F32),
+        ],
+        "vssv",
+    )(latents, levels, window_mask, jnp.transpose(qkv_weight, (1, 0, 2)))
+    gathered = lax.all_gather(packed, ("queue", "tok"), axis=0)
+    cond_other = from_partner(cond_embed, "cfg", 0)
+    weight = lax.all_to_all(chunks, ("queue", "cfg"), 0, 0).reshape(width, 3 * head_dim)
+    out_all = lax.all_gather(out_weight.T, ("tok", "queue", "cfg"), axis=0)
+    out_all = out_all.reshape(toks, width, out_weight.shape[0])
+
+    conds = jnp.where(
+        branch == 0,
+        jnp.concatenate([cond_embed, cond_other], axis=0),
+        jnp.concatenate([cond_other, cond_embed], axis=0),
+    )
+    mods = jnp.transpose(level_mod, (1, 0, 2))
+    lhs, xin, rstd, masks = kernel_call(
+        functools.partial(prepare_kernel, frames, values, span),
+        [
+            jax.ShapeDtypeStruct((all_frames * rows, width), BF16),
+            jax.ShapeDtypeStruct((all_frames, rows, lanes), BF16),
+            jax.ShapeDtypeStruct((all_frames, 1, lanes), F32),
+            jax.ShapeDtypeStruct((all_frames, rows - values, LANES), F32),
+        ],
+        "vvvv",
+    )(gathered, conds, mods, embed_weight)
+    attended = kernel_call(
+        functools.partial(attend_kernel, frames, tokens),
+        jax.ShapeDtypeStruct((toks * group, head_dim, row_lanes), BF16),
+        "vvvvvvv",
+        [
+            pltpu.VMEM((all_frames + 2 * window, 3 * head_dim, lanes), F32),
+            pltpu.VMEM((all_frames + 2 * window, 1, lanes), F32),
+            pltpu.VMEM((all_frames + 2 * window, 1, lanes), F32),
+            pltpu.VMEM((all_frames, branches, head_dim, LANES), F32),
+        ],
+    )(weight, lhs, xin, rstd, masks, query_gain[:, None], key_gain[:, None])
+    received = lax.all_to_all(attended, ("tok", "queue", "cfg"), 0, 0).reshape(width, row_lanes)
+
+    following = lax.dynamic_index_in_dim(
+        gathered,
+        jnp.minimum(q_at + 1, queues - 1) * toks + lax.axis_index("tok"),
+        0,
+        keepdims=False,
+    )[:, :tokens]
+    wide = jax.ShapeDtypeStruct((width, row_lanes), F32)
+    emb, gate, gain = kernel_call(
+        functools.partial(rows_kernel, values, span), [wide, wide, wide], "vvvvvv"
+    )(packed, following, cond_embed, mods[2], embed_weight, final_gain[None])
+    half = values // 2
+    half_shape = jax.ShapeDtypeStruct((half, row_lanes), F32)
+    mine, send = kernel_call(
+        functools.partial(finish_kernel, half),
+        [half_shape, half_shape],
+        "vvvvvvs",
+        [pltpu.VMEM((values, row_lanes), F32)],
+    )(received, out_all, emb, gate, gain, final_weight.T, branch[None])
+    partner = from_partner(send, "cfg", 0)
+    place = jnp.stack([branch, (q_at == queues - 1).astype(jnp.int32)])
+    shape = jax.ShapeDtypeStruct((frames, half, tokens), F32)
+    return kernel_call(
+        functools.partial(update_kernel, values, span, levels_all),
+        [shape, shape],
+        "vvvvvsss",
+    )(mine, partner, packed, following, fresh_noise, guide_table, guide_index, place)
+
+
+def on_device(*args):
+    latents, qkv_weight, query_gain = args[0], args[7], args[8]
+    local_heads = qkv_weight.shape[2] // query_gain.shape[0]
+    one_head_each = local_heads == lax.axis_size("queue") * lax.axis_size("cfg")
+    fits = latents.shape[2] * lax.axis_size("tok") <= LANES
+    if one_head_each and fits:
+        return tuple(on_device_heads(*args))
+    return on_device_general(*args)
+
+
 def solution(mesh):
     placed = (
         P(("scene", "queue"), None, "tok"),

time: 156 us -> 107 us (0.69)
  waiting for transfers between devices: 99.1 us -> 14.3 us
  blocking collectives: 5.66 us -> 45.4 us
  Pallas kernels: 0 us -> 12.8 us
  other arithmetic: 11.3 us -> 0.09 us
  matrix products: 9.94 us -> 0 us
  starting transfers between devices: 4.42 us -> 11.3 us
  local copies, waits for them, and re-layouts: 9.93 us -> 7.52 us
    all_gather x2 -> x1, waiting for transfers between devices: 42.9 us -> 0.01 us  [on_device_heads(): out_all = lax.all_gather(out_weight.T, ('tok', 'queue', 'cfg'), axis=0)]
    all_gather x1, blocking collectives: 5.66 us -> 45.4 us  [on_device_heads(): gathered = lax.all_gather(packed, ('queue', 'tok'), axis=0)]
    ppermute x3 -> x0, waiting for transfers between devices: 37 us -> none  [the longest x1 30 us: with_halo(): lax.ppermute(tail, axis, [(i, (i + 1) % count) for i in range(ends)])]
    reduce_scatter x1 -> x0, waiting for transfers between devices: 17.5 us -> none  [on_device(): lax.psum_scatter(partial_value.reshape(frames, seq_tokens, model_width).a...]
    all_to_all x0 -> x2, waiting for transfers between devices: none -> 13.5 us  [the longest x1 13.5 us: on_device_heads(): lax.all_to_all(attended, ('tok', 'queue', 'cfg'), 0, 0)]
    pallas_call x0 -> x6, Pallas kernels: none -> 12.8 us  [the longest x1 5.67 us: on_device_heads(): kernel_call(functools.partial(attend_kernel, frames, tokens), jax.ShapeDt...]
    all_to_all x0 -> x2, starting transfers between devices: none -> 10 us  [the longest x1 6.33 us: on_device_heads(): lax.all_to_all(chunks, ('queue', 'cfg'), 0, 0).reshape(width, 3 * head_dim)]
    dot_general x5 -> x0, matrix products: 9.94 us -> none  [the longest x1 4.63 us: on_device(): jnp.dot(norm_rows, flat_piece, preferred_element_type=jnp.float32)]
  transfers between devices with their start and end apart: 7 -> 5, of which waited for: 6 -> 2; matrix products, arithmetic and copies ran while one was open for 14% -> 0% of each run, Pallas kernels for 0% -> 9%
where the time goes in v1:
time: 107 us; the launch traced here: 106 us
  blocking collectives  45.4 us (42%)
  between operations  14.8 us (14%)
  waiting for transfers between devices  14.3 us (13%)
  Pallas kernels  12.8 us (12%)
  starting transfers between devices  11.3 us (11%)
  local copies, waits for them, and re-layouts  7.52 us (7%)
    all_gather x1, blocking collectives, on_device_heads(): gathered = lax.all_gather(packed, ('queue', 'tok'), axis=0)  45.4 us
    all_to_all x1, waiting for transfers between devices, on_device_heads(): lax.all_to_all(attended, ('tok', 'queue', 'cfg'), 0, 0)  13.5 us
    unnamed x32, local copies, waits for them, and re-layouts  7.3 us
    all_to_all x1, starting transfers between devices, on_device_heads(): lax.all_to_all(chunks, ('queue', 'cfg'), 0, 0).reshape(width, 3 * head_dim)  6.33 us
    pallas_call x1, Pallas kernels, on_device_heads(): kernel_call(functools.partial(attend_kernel, frames, tokens), jax.ShapeDt...  5.67 us
    all_to_all x1, starting transfers between devices, on_device_heads(): lax.all_to_all(attended, ('tok', 'queue', 'cfg'), 0, 0)  3.71 us
  transfers between devices with their start and end apart: 5, of which 2 were waited for; matrix products, arithmetic and copies ran while one was open for 0% of the time, Pallas kernels for 9%

profile of v1, /device:TPU:0, one launch (start us, length us, event | category | flops | bytes accessed | tf_op | source)
XLA Modules:
  0.0 106.2 jit_solution(2011952258897807779)
XLA Ops:
  7.2 0.0 copy-start.8
  7.2 0.0 copy-start.14
  7.2 0.0 all-gather.4.cloned.1.call-start
  7.3 0.7 all-gather.4.cloned.1.call-update
  7.9 1.0 copy-done.3
  9.0 0.8 copy-done.7
  9.7 0.7 copy-done.10
  10.4 0.7 copy-done.12
  11.1 1.8 %shard_map.158 = (bf16[8,144,216]{2,1,0:T(8,128)(2,1)}, f32[32,192]{1,0:T(8,128)S(1)}) custom-call(f32[4,16,48]{2,1,0:T(8,128)S(1)} %copy-done.7, s32[4]{0:T(128)S(1)} %copy-done.12, s32[4,9]{1,0:T(4,128)S(1)} %copy-done.10, bf16[3,144,576]{2,1,0:T(8,128)(2,1)S(1)} %bitcast.21), custom_call_target="tpu_custom_call" | custom-call | flops 1000000 | bytes 1000000 | tf_op jit(solution)/shard_map/pallas_call | solution.py:469
  12.8 6.3 %all-to-all-start = ((bf16[8,144,216]{2,1,0:T(8,128)(2,1)}), bf16[8,144,216]{2,1,0:T(8,128)(2,1)S(1)}, u32[]{:S(2)}, u32[]{:S(2)}) async-start(bf16[8,144,216]{2,1,0:T(8,128)(2,1)} %get-tuple-element.13), calls=%async_computation | async-start | bytes 1179648 | tf_op jit(solution)/shard_map/all_to_all | solution.py:479
  19.2 0.5 collective-permute-start
  19.7 45.4 %all-gather = f32[256,192]{1,0:T(8,128)S(1)} all-gather(f32[32,192]{1,0:T(8,128)S(1)} %get-tuple-element.14.packed), channel_id=2, replica_groups=mesh['scene'=2,'queue'=4,'tok'=2,'cfg'=2] {'queue','tok'}, dimensions={0}, use_global_device_ids=true | all-gather | bytes 221184 | tf_op jit(solution)/shard_map/all_gather | solution.py:477
  65.1 0.0 copy-done.14
  65.1 0.1 copy.17.gain_q
  65.2 0.1 copy.18.gain_k
  65.3 0.0 collective-permute-done
  65.3 1.8 %shard_map.159 = (bf16[512,1152]{1,0:T(8,128)(2,1)S(1)}, bf16[16,32,256]{2,1,0:T(8,128)(2,1)S(1)}, f32[16,1,256]{2,1,0:T(1,128)S(1)}, f32[16,16,128]{2,1,0:T(8,128)S(1)}) custom-call(f32[8,32,192]{2,1,0:T(8,128)S(1)} %bitcast.19, f32[2,1152]{1,0:T(2,128)S(1)} %maximum_select_fusion.cond, f32[3,16,1152]{2,1,0:T(8,128)S(1)} %bitcast.22, ...), custom_call_target="tpu_custom_call" | custom-call | flops 1000000 | bytes 1000000 | tf_op jit(solution)/shard_map/pallas_call | solution.py:489
  67.1 0.0 all-to-all-done
  67.1 5.7 %shard_map.160 = bf16[16,72,240]{2,1,0:T(8,128)(2,1)} custom-call(bf16[1152,216]{1,0:T(8,128)(2,1)S(1)} %bitcast.18, bf16[512,1152]{1,0:T(8,128)(2,1)S(1)} %get-tuple-element.15.lhs, bf16[16,32,256]{2,1,0:T(8,128)(2,1)S(1)} %get-tuple-element.16.xin, f32[16,1,256]{2,1,0:T(1,128)S(1)} %get-tuple-element.17.rstd_in, ...), custom_call_target="tpu_custom_call" | custom-call | flops 1000000 | bytes 1000000 | tf_op jit(solution)/shard_map/pallas_call | solution.py:499
  72.8 3.7 %all-to-all-start.1 = ((bf16[16,72,240]{2,1,0:T(8,128)(2,1)}), bf16[16,72,240]{2,1,0:T(8,128)(2,1)S(1)}, u32[]{:S(2)}, u32[]{:S(2)}) async-start(bf16[16,72,240]{2,1,0:T(8,128)(2,1)} %shard_map.160), calls=%async_computation.1 | async-start | bytes 1179648 | tf_op jit(solution)/shard_map/all_to_all | solution.py:510
  76.5 0.0 copy-done.13
  76.6 0.7 shard_map.161
  77.3 1.0 copy-done.1
  78.3 13.5 %all-to-all-done.1 = bf16[16,72,240]{2,1,0:T(8,128)(2,1)S(1)} async-done(((bf16[16,72,240]{2,1,0:T(8,128)(2,1)}), bf16[16,72,240]{2,1,0:T(8,128)(2,1)S(1)}, u32[]{:S(2)}, u32[]{:S(2)}) %all-to-all-start.1) | async-done | bytes 552992 | tf_op jit(solution)/shard_map/all_to_all | solution.py:510
  91.8 1.8 %copy-done = bf16[2304,576]{1,0:T(8,128)(2,1)S(1)} copy-done((bf16[2304,576]{1,0:T(8,128)(2,1)S(1)}, bf16[2304,576]{1,0:T(8,128)(2,1)}, u32[]{:S(2)}) %copy-start) | copy-done | bytes 2654232
  93.6 1.3 %copy-done.2 = f32[1152,240]{1,0:T(8,128)S(1)} copy-done((f32[1152,240]{1,0:T(8,128)S(1)}, f32[1152,240]{1,0:T(8,128)}, u32[]{:S(2)}) %copy-start.2) | copy-done | bytes 1105944
  94.9 1.6 %shard_map.162 = (f32[8,240]{1,0:T(8,128)S(1)}, f32[8,240]{1,0:T(8,128)S(1)}) custom-call(bf16[1152,240]{1,0:T(8,128)(2,1)S(1)} %bitcast.17, bf16[2,1152,576]{2,1,0:T(8,128)(2,1)S(1)} %bitcast.16, f32[1152,240]{1,0:T(8,128)S(1)} %get-tuple-element.19.emb, f32[1152,240]{1,0:T(8,128)S(1)} %get-tuple-element.20.gate, f32[1152,240]{1,0:T(8,128)S(1)} %copy-done.2, ...), custom_call_target="tpu_custom_call" | custom-call | flops 1000000 | bytes 1000000 | tf_op jit(solution)/shard_map/pallas_call | solution.py:524
  96.5 0.7 collective-permute-start.1
  97.2 0.1 pad_add_fusion.place
  97.9 0.1 collective-permute-done.1.partner
  98.0 0.0 copy-done.11
  98.0 1.3 %shard_map.163 = (f32[4,8,48]{2,1,0:T(8,128)}, f32[4,8,48]{2,1,0:T(8,128)}) custom-call(f32[8,240]{1,0:T(8,128)S(1)} %get-tuple-element.22.mine, f32[8,240]{1,0:T(8,128)S(1)} %collective-permute-done.1.partner, f32[32,192]{1,0:T(8,128)S(1)} %get-tuple-element.14.packed, f32[32,48]{1,0:T(8,128)S(1)} %slice.8.following, f32[8,48]{1,0:T(8,128)S(1)} %copy-done.9, ...), custom_call_target="tpu_custom_call" | custom-call | flops 1000000 | bytes 1000000 | tf_op jit(solution)/shard_map/pallas_call | solution.py:533
  (26 shorter events, 0.1 us)
Async XLA Ops:
  7.2 12.0 %copy-start.8 = (f32[1,1152]{1,0:T(1,128)S(1)}, f32[1,1152]{1,0:T(1,128)}, u32[]{:S(2)}) copy-start(f32[1,1152]{1,0:T(1,128)} %cond.1) | copy-start | bytes 13828
  7.2 57.9 %copy-start.14 = (f32[72]{0:T(128)S(1)}, f32[72]{0:T(128)}, u32[]{:S(2)}) copy-start(f32[72]{0:T(128)} %param.23) | copy-start | bytes 868
  7.2 58.0 %copy-start.15 = (f32[72]{0:T(128)S(1)}, f32[72]{0:T(128)}, u32[]{:S(2)}) copy-start(f32[72]{0:T(128)} %param.24) | copy-start | bytes 868
  7.2 84.6 %all-gather.4.cloned.1.call-start = ((), (), s32[]{:S(2)}) async-start(), calls=%async_computation.2 | async-start | bytes 3133440 | tf_op jit(solution)/shard_map/all_gather | solution.py:480
  7.2 58.0 %copy-start.5 = (bf16[16,1152]{1,0:T(8,128)(2,1)S(1)}, bf16[16,1152]{1,0:T(8,128)(2,1)}, u32[]{:S(2)}) copy-start(bf16[16,1152]{1,0:T(8,128)(2,1)} %embed.3) | copy-start | bytes 110596
  7.9 1.1 copy-start.3
  9.0 0.8 copy-start.7
  9.7 0.7 copy-start.10
  10.4 0.7 copy-start.12
  11.1 54.2 %copy-start.4 = (f32[16,3,1152]{2,0,1:T(8,128)S(1)}, f32[16,3,1152]{2,0,1:T(8,128)}, u32[]{:S(2)}) copy-start(f32[16,3,1152]{2,0,1:T(8,128)} %param.20) | copy-start | bytes 663556
  12.8 54.2 %all-to-all-start = ((bf16[8,144,216]{2,1,0:T(8,128)(2,1)}), bf16[8,144,216]{2,1,0:T(8,128)(2,1)S(1)}, u32[]{:S(2)}, u32[]{:S(2)}) async-start(bf16[8,144,216]{2,1,0:T(8,128)(2,1)} %get-tuple-element.13), calls=%async_computation | async-start | bytes 1179648 | tf_op jit(solution)/shard_map/all_to_all | solution.py:479
  19.2 46.1 %collective-permute-start = (f32[1,1152]{1,0:T(1,128)S(1)}, f32[1,1152]{1,0:T(1,128)S(1)}, u32[]{:S(2)}, u32[]{:S(2)}) collective-permute-start(f32[1,1152]{1,0:T(1,128)S(1)} %copy-done.8), channel_id=1, source_target_pairs={{0,1},{1,0},{2,3},{3,2},{4,5},{5,4},{6,7},{7,6},{8,9},{9,8},{10,11... | collective-permute-start | bytes 13832 | tf_op jit(solution)/shard_map/ppermute | solution.py:23
  72.8 3.8 %copy-start.13 = (f32[1152]{0:T(1024)S(1)}, f32[1152]{0:T(1024)}, u32[]{:S(2)}) copy-start(f32[1152]{0:T(1024)} %param.26) | copy-start | bytes 13828
  72.8 19.0 %copy-start.6 = (bf16[1152,16]{0,1:T(8,128)(2,1)S(1)}, bf16[1152,16]{0,1:T(8,128)(2,1)}, u32[]{:S(2)}) copy-start(bf16[1152,16]{0,1:T(8,128)(2,1)} %param.27) | copy-start | bytes 110596
  72.8 19.0 %all-to-all-start.1 = ((bf16[16,72,240]{2,1,0:T(8,128)(2,1)}), bf16[16,72,240]{2,1,0:T(8,128)(2,1)S(1)}, u32[]{:S(2)}, u32[]{:S(2)}) async-start(bf16[16,72,240]{2,1,0:T(8,128)(2,1)} %shard_map.160), calls=%async_computation.1 | async-start | bytes 1179648 | tf_op jit(solution)/shard_map/all_to_all | solution.py:510
  77.2 1.0 copy-start.1
  91.8 1.8 %copy-start = (bf16[2304,576]{1,0:T(8,128)(2,1)S(1)}, bf16[2304,576]{1,0:T(8,128)(2,1)}, u32[]{:S(2)}) copy-start(bf16[2304,576]{1,0:T(8,128)(2,1)} %all-gather.4.cloned.1.call-done) | copy-start | bytes 7962628
  93.6 1.3 %copy-start.2 = (f32[1152,240]{1,0:T(8,128)S(1)}, f32[1152,240]{1,0:T(8,128)}, u32[]{:S(2)}) copy-start(f32[1152,240]{1,0:T(8,128)} %copy-done.1) | copy-start | bytes 3317764
  94.9 3.1 %copy-start.9 = (f32[8,48]{1,0:T(8,128)S(1)}, f32[8,48]{1,0:T(8,128)}, u32[]{:S(2)}) copy-start(f32[8,48]{1,0:T(8,128)} %noise.1) | copy-start | bytes 4612
  94.9 3.1 %copy-start.11 = (f32[8]{0:T(128)S(1)}, f32[8]{0:T(128)}, u32[]{:S(2)}) copy-start(f32[8]{0:T(128)} %table.1) | copy-start | bytes 100
  96.5 1.5 %collective-permute-start.1 = (f32[8,240]{1,0:T(8,128)S(1)}, f32[8,240]{1,0:T(8,128)S(1)}, u32[]{:S(2)}, u32[]{:S(2)}) collective-permute-start(f32[8,240]{1,0:T(8,128)S(1)} %get-tuple-element.23), channel_id=1, source_target_pairs={{0,1},{1,0},{2,3},{3,2},{4,5},{5,4},{6,7},{7,6},{8,9},{9,8},{10,11... | collective-permute-start | bytes 23048 | tf_op jit(solution)/shard_map/ppermute | solution.py:23
Sparse Core Ops, SparseCore 0:
  10.3 56.0 all-gather.3

commit v2 on v1

--- a/solution.py
+++ b/solution.py
@@ -11,6 +11,7 @@
 TIME_SHIFT = 3.0
 LANES = 128
 VMEM_BYTES = 40 * 1024 * 1024
+WHOLE_VMEM = 62 * 1024 * 1024
 F32 = jnp.float32
 BF16 = jnp.bfloat16
 
@@ -186,18 +187,16 @@
     return (guided, new_queue)
 
 
-def kernel_call(body, out_shapes, spaces, scratch=(), **cost):
-    kinds = {"v": pltpu.VMEM, "s": pltpu.SMEM}
+def kernel_call(body, out_shapes, spaces, scratch=(), vmem=VMEM_BYTES, **cost):
+    kinds = {"v": pl.BlockSpec(), "s": pl.BlockSpec(memory_space=pltpu.SMEM)}
     many = isinstance(out_shapes, (list, tuple))
     return pl.pallas_call(
         body,
         out_shape=out_shapes,
-        in_specs=[pl.BlockSpec(memory_space=kinds[k]) for k in spaces],
-        out_specs=[pl.BlockSpec(memory_space=pltpu.VMEM) for _ in out_shapes]
-        if many
-        else pl.BlockSpec(memory_space=pltpu.VMEM),
+        in_specs=[kinds[k] for k in spaces],
+        out_specs=[pl.BlockSpec() for _ in out_shapes] if many else pl.BlockSpec(),
         scratch_shapes=list(scratch),
-        compiler_params=pltpu.CompilerParams(vmem_limit_bytes=VMEM_BYTES),
+        compiler_params=pltpu.CompilerParams(vmem_limit_bytes=vmem),
         cost_estimate=pl.CostEstimate(
             flops=cost.get("flops", 1000000),
             bytes_accessed=cost.get("bytes_accessed", 1000000),
@@ -235,8 +234,8 @@
         side = jnp.zeros((packed.shape[0] - values, tokens), F32)
         row_id = lax.broadcasted_iota(jnp.int32, side.shape, 0)
         for o in range(span):
-            side = jnp.where(row_id == o, window_mask[f, o].astype(F32), side)
-        side = jnp.where(row_id == span, levels[f].astype(F32), side)
+            side = jnp.where(row_id == o, window_mask[f : f + 1, o : o + 1].astype(F32), side)
+        side = jnp.where(row_id == span, levels[:, f : f + 1].astype(F32), side)
         rows.append(side)
         pieces.append(jnp.concatenate(rows, axis=0))
     packed[...] = jnp.concatenate(pieces, axis=1)
@@ -386,15 +385,36 @@
     gain_out[...] = dot_tn(gains, ones)
 
 
-def finish_kernel(half, attended, out_w, emb, gate, gain, final_w, branch, mine, send, scratch):
-    group = out_w.shape[2]
-    mixed = jnp.zeros(emb.shape, F32)
-    for g in range(out_w.shape[0]):
-        made = jnp.dot(
-            out_w[g], attended[g * group : (g + 1) * group, :], preferred_element_type=F32
-        )
-        mixed = mixed + made.astype(BF16).astype(F32)
-    summed = emb[...] + gate[...] * mixed
+def finish_kernel(
+    half,
+    toks,
+    attended,
+    out_own,
+    out_other,
+    emb,
+    gate,
+    gain,
+    final_w,
+    branch,
+    mine,
+    send,
+    scratch,
+    mixed,
+):
+    queues, columns, group = out_own.shape[0] // toks, out_own.shape[1], out_own.shape[2]
+    for core, held in ((branch[0], out_own), (1 - branch[0], out_other)):
+        for q in range(queues):
+            total = jnp.zeros((columns, attended.shape[1]), F32)
+            for t in range(toks):
+                made = jnp.dot(
+                    held[t * queues + q],
+                    attended[t * group : (t + 1) * group, :],
+                    preferred_element_type=F32,
+                )
+                total = total + made.astype(BF16).astype(F32)
+            first = pl.multiple_of((2 * q + core) * columns, 8)
+            mixed[pl.ds(first, columns), :] = total
+    summed = emb[...] + gate[...] * mixed[...]
     center = jnp.mean(summed, axis=0, keepdims=True)
     deviate = summed - center
     spread = jnp.mean(deviate * deviate, axis=0, keepdims=True)
@@ -472,13 +492,16 @@
             jax.ShapeDtypeStruct((group, local_rows, 3 * head_dim), BF16),
             jax.ShapeDtypeStruct((rows, frames * tokens), F32),
         ],
-        "vssv",
-    )(latents, levels, window_mask, jnp.transpose(qkv_weight, (1, 0, 2)))
+        "vvvv",
+        vmem=WHOLE_VMEM,
+    )(latents, levels[None], window_mask, jnp.transpose(qkv_weight, (1, 0, 2)))
     gathered = lax.all_gather(packed, ("queue", "tok"), axis=0)
     cond_other = from_partner(cond_embed, "cfg", 0)
     weight = lax.all_to_all(chunks, ("queue", "cfg"), 0, 0).reshape(width, 3 * head_dim)
-    out_all = lax.all_gather(out_weight.T, ("tok", "queue", "cfg"), axis=0)
-    out_all = out_all.reshape(toks, width, out_weight.shape[0])
+    out_own, gathered = lax.optimization_barrier((out_weight.T, gathered))
+    out_own = jnp.broadcast_to(out_own[None], (toks * queues,) + out_own.shape)
+    out_own = lax.all_to_all(out_own, ("tok", "queue"), 0, 0)
+    out_other = from_partner(out_own, "cfg", 0)
 
     conds = jnp.where(
         branch == 0,
@@ -522,11 +545,11 @@
     half = values // 2
     half_shape = jax.ShapeDtypeStruct((half, row_lanes), F32)
     mine, send = kernel_call(
-        functools.partial(finish_kernel, half),
+        functools.partial(finish_kernel, half, toks),
         [half_shape, half_shape],
-        "vvvvvvs",
-        [pltpu.VMEM((values, row_lanes), F32)],
-    )(received, out_all, emb, gate, gain, final_weight.T, branch[None])
+        "vvvvvvvs",
+        [pltpu.VMEM((values, row_lanes), F32), pltpu.VMEM((width, row_lanes), F32)],
+    )(received, out_own, out_other, emb, gate, gain, final_weight.T, branch[None])
     partner = from_partner(send, "cfg", 0)
     place = jnp.stack([branch, (q_at == queues - 1).astype(jnp.int32)])
     shape = jax.ShapeDtypeStruct((frames, half, tokens), F32)

time: 107 us -> 134 us (1.25)
  blocking collectives: 45.4 us -> 69.4 us
  local copies, waits for them, and re-layouts: 7.52 us -> 26.9 us
  between operations: 14.8 us -> 1.38 us
  starting transfers between devices: 11.3 us -> 8.57 us
  waiting for transfers between devices: 14.3 us -> 12.3 us
    all_to_all x0 -> x1, blocking collectives: none -> 34.7 us  [on_device_heads(): out_own = lax.all_to_all(out_own, ('tok', 'queue'), 0, 0)]
    unnamed x32 -> x52, local copies, waits for them, and re-layouts: 7.3 us -> 20.2 us
    all_gather x1, blocking collectives: 45.4 us -> 34.7 us  [on_device_heads(): gathered = lax.all_gather(packed, ('queue', 'tok'), axis=0)]
    all_to_all x1, waiting for transfers between devices: 13.5 us -> 5.68 us  [on_device_heads(): lax.all_to_all(attended, ('tok', 'queue', 'cfg'), 0, 0)]
    all_to_all x1, waiting for transfers between devices: 0.01 us -> 6.5 us  [on_device_heads(): lax.all_to_all(chunks, ('queue', 'cfg'), 0, 0).reshape(width, 3 * head_dim)]
    all_to_all x1, starting transfers between devices: 6.33 us -> 3.67 us  [on_device_heads(): lax.all_to_all(chunks, ('queue', 'cfg'), 0, 0).reshape(width, 3 * head_dim)]
  transfers between devices with their start and end apart: 5 -> 5, of which waited for: 2 -> 3; matrix products, arithmetic and copies ran while one was open for 0% -> 4% of each run, Pallas kernels for 9% -> 6%
where the time goes in v2:
time: 134 us; the launch traced here: 132 us
  blocking collectives  69.4 us (52%)
  local copies, waits for them, and re-layouts  26.9 us (20%)
  Pallas kernels  13.6 us (10%)
  waiting for transfers between devices  12.3 us (9%)
  starting transfers between devices  8.57 us (6%)
  between operations  1.38 us (1%)
    all_gather x1, blocking collectives, on_device_heads(): gathered = lax.all_gather(packed, ('queue', 'tok'), axis=0)  34.7 us
    all_to_all x1, blocking collectives, on_device_heads(): out_own = lax.all_to_all(out_own, ('tok', 'queue'), 0, 0)  34.7 us
    unnamed x52, local copies, waits for them, and re-layouts  20.2 us
    all_to_all x1, waiting for transfers between devices, on_device_heads(): lax.all_to_all(chunks, ('queue', 'cfg'), 0, 0).reshape(width, 3 * head_dim)  6.5 us
    all_to_all x1, waiting for transfers between devices, on_device_heads(): lax.all_to_all(attended, ('tok', 'queue', 'cfg'), 0, 0)  5.68 us
    pallas_call x1, Pallas kernels, on_device_heads(): kernel_call(functools.partial(attend_kernel, frames, tokens), jax.ShapeDt...  5.64 us
    all_to_all x1, starting transfers between devices, on_device_heads(): lax.all_to_all(chunks, ('queue', 'cfg'), 0, 0).reshape(width, 3 * head_dim)  3.67 us
    all_to_all x1, starting transfers between devices, on_device_heads(): lax.all_to_all(attended, ('tok', 'queue', 'cfg'), 0, 0)  3.58 us
  transfers between devices with their start and end apart: 5, of which 3 were waited for; matrix products, arithmetic and copies ran while one was open for 4% of the time, Pallas kernels for 6%

profile of v2, /device:TPU:0, one launch (start us, length us, event | category | flops | bytes accessed | tf_op | source)
XLA Modules:
  0.0 132.3 jit_solution(17094803955270762564)
XLA Ops:
  0.6 2.4 %shard_map.158 = (bf16[8,144,216]{2,1,0:T(8,128)(2,1)}, f32[32,192]{1,0:T(8,128)}) custom-call(f32[4,16,48]{2,1,0:T(8,128)} %latents.1, s32[1,4]{1,0:T(1,128)} %bitcast.27, s32[4,9]{1,0:T(4,128)} %window_mask.1, bf16[3,144,576]{2,1,0:T(8,128)(2,1)} %bitcast.23), custom_call_target="tpu_custom_call" | custom-call | flops 1000000 | bytes 1000000 | tf_op jit(solution)/shard_map/pallas_call | solution.py:489
  3.0 34.7 %all-gather = f32[256,192]{1,0:T(8,128)} all-gather(f32[32,192]{1,0:T(8,128)} %get-tuple-element.16.packed), channel_id=2, replica_groups=mesh['scene'=2,'queue'=4,'tok'=2,'cfg'=2] {'queue','tok'}, dimensions={0}, use_global_device_ids=true | all-gather | bytes 221184 | tf_op jit(solution)/shard_map/all_gather | solution.py:498
  37.7 1.0 broadcast_in_dim.24
  38.8 34.7 %all_to_all.15.out_own = bf16[8,144,576]{2,1,0:T(8,128)(2,1)S(1)} all-to-all(bf16[8,144,576]{2,1,0:T(8,128)(2,1)S(1)} %broadcast_in_dim.24), channel_id=1, replica_groups=mesh['scene'=2,'queue'=4,'tok'=2,'cfg'=2] {'tok','queue'}, dimensions={0} | all-to-all | bytes 2654208 | tf_op jit(solution)/shard_map/all_to_all | solution.py:503
  73.5 3.7 %all-to-all-start = ((bf16[8,144,216]{2,1,0:T(8,128)(2,1)}), bf16[8,144,216]{2,1,0:T(8,128)(2,1)S(1)}, u32[]{:S(2)}, u32[]{:S(2)}) async-start(bf16[8,144,216]{2,1,0:T(8,128)(2,1)} %get-tuple-element.15), calls=%async_computation | async-start | bytes 1179648 | tf_op jit(solution)/shard_map/all_to_all | solution.py:500
  77.7 1.4 %copy.17.gain_q = f32[72,1]{1,0:T(8,128)} copy(f32[72,1]{0,1:T(1,128)} %bitcast.25) | data formatting | bytes 576 | tf_op jit(solution)/shard_map/broadcast_in_dim | solution.py:532
  79.1 1.4 %copy.18.gain_k = f32[72,1]{1,0:T(8,128)} copy(f32[72,1]{0,1:T(1,128)} %bitcast.26) | data formatting | bytes 576 | tf_op jit(solution)/shard_map/broadcast_in_dim | solution.py:532
  80.5 0.9 copy-done
  81.5 0.9 copy-done.9
  82.4 0.8 copy-done.14
  83.2 1.8 %shard_map.159 = (bf16[512,1152]{1,0:T(8,128)(2,1)S(1)}, bf16[16,32,256]{2,1,0:T(8,128)(2,1)S(1)}, f32[16,1,256]{2,1,0:T(1,128)S(1)}, f32[16,16,128]{2,1,0:T(8,128)S(1)}) custom-call(f32[8,32,192]{2,1,0:T(8,128)S(1)} %bitcast.19, f32[2,1152]{1,0:T(2,128)S(1)} %maximum_select_fusion.cond, f32[3,16,1152]{2,1,0:T(8,128)S(1)} %bitcast.21, ...), custom_call_target="tpu_custom_call" | custom-call | flops 1000000 | bytes 1000000 | tf_op jit(solution)/shard_map/pallas_call | solution.py:512
  85.0 1.0 copy-done.7
  87.3 6.5 %all-to-all-done = bf16[8,144,216]{2,1,0:T(8,128)(2,1)S(1)} async-done(((bf16[8,144,216]{2,1,0:T(8,128)(2,1)}), bf16[8,144,216]{2,1,0:T(8,128)(2,1)S(1)}, u32[]{:S(2)}, u32[]{:S(2)}) %all-to-all-start) | async-done | bytes 497696 | tf_op jit(solution)/shard_map/all_to_all | solution.py:500
  93.8 1.3 copy-done.8
  95.1 0.9 copy-done.13
  96.1 0.8 copy-done.16
  96.8 0.8 copy-done.17
  97.6 0.9 copy-done.19
  98.5 5.6 %shard_map.160 = bf16[16,72,240]{2,1,0:T(8,128)(2,1)} custom-call(bf16[1152,216]{1,0:T(8,128)(2,1)S(1)} %bitcast.17, bf16[512,1152]{1,0:T(8,128)(2,1)S(1)} %copy-done.8, bf16[16,32,256]{2,1,0:T(8,128)(2,1)S(1)} %copy-done.13, f32[16,1,256]{2,1,0:T(1,128)S(1)} %get-tuple-element.20.rstd_in, f32[16,16,128]{2,1,0:T(8,128)S(1)} %copy-done.19, ...), custom_call_target="tpu_custom_call" | custom-call | flops 1000000 | bytes 1000000 | tf_op jit(solution)/shard_map/pallas_call | solution.py:522
  104.1 3.6 %all-to-all-start.1 = ((bf16[16,72,240]{2,1,0:T(8,128)(2,1)}), bf16[16,72,240]{2,1,0:T(8,128)(2,1)S(1)}, u32[]{:S(2)}, u32[]{:S(2)}) async-start(bf16[16,72,240]{2,1,0:T(8,128)(2,1)} %shard_map.160), calls=%async_computation.1 | async-start | bytes 1179648 | tf_op jit(solution)/shard_map/all_to_all | solution.py:533
  108.5 1.3 broadcast_in_dim.25.final_gain
  109.8 0.9 slice_bitcast_fusion.level_mod
  111.4 0.8 copy-done.15
  114.3 1.0 copy-done.1
  115.3 1.0 copy-done.3
  116.3 1.0 copy-done.5
  117.3 5.7 %all-to-all-done.1 = bf16[16,72,240]{2,1,0:T(8,128)(2,1)S(1)} async-done(((bf16[16,72,240]{2,1,0:T(8,128)(2,1)}), bf16[16,72,240]{2,1,0:T(8,128)(2,1)S(1)}, u32[]{:S(2)}, u32[]{:S(2)}) %all-to-all-start.1) | async-done | bytes 552992 | tf_op jit(solution)/shard_map/all_to_all | solution.py:533
  123.0 1.3 copy-done.2
  124.3 1.3 copy-done.4
  125.6 1.3 copy-done.6
  127.6 1.8 %shard_map.162 = (f32[8,240]{1,0:T(8,128)S(1)}, f32[8,240]{1,0:T(8,128)S(1)}) custom-call(bf16[1152,240]{1,0:T(8,128)(2,1)S(1)} %bitcast.16, bf16[8,144,576]{2,1,0:T(8,128)(2,1)S(1)} %all_to_all.15.out_own, bf16[8,144,576]{2,1,0:T(8,128)(2,1)S(1)} %collective-permute-done.1.out_other, f32[1152,240]{1,0:T(8,128)S(1)} %copy-done.2, f32[1152,240]{1,0:T(8,128)S(1)} %copy-done.4, ...), custom_call_target="tpu_custom_call" | custom-call | flops 1000000 | bytes 1000000 | tf_op jit(solution)/shard_map/pallas_call | solution.py:547
  131.0 1.3 shard_map.163
  (47 shorter events, 7.3 us)
Async XLA Ops:
  73.5 4.1 %copy-start.22 = (f32[1,1152]{1,0:T(1,128)S(1)}, f32[1,1152]{1,0:T(1,128)}, u32[]{:S(2)}) copy-start(f32[1,1152]{1,0:T(1,128)} %cond.1) | copy-start | bytes 13828
  73.5 20.4 %all-to-all-start = ((bf16[8,144,216]{2,1,0:T(8,128)(2,1)}), bf16[8,144,216]{2,1,0:T(8,128)(2,1)S(1)}, u32[]{:S(2)}, u32[]{:S(2)}) async-start(bf16[8,144,216]{2,1,0:T(8,128)(2,1)} %get-tuple-element.15), calls=%async_computation | async-start | bytes 1179648 | tf_op jit(solution)/shard_map/all_to_all | solution.py:500
  77.2 45.9 %collective-permute-start.1 = (bf16[8,144,576]{2,1,0:T(8,128)(2,1)S(1)}, bf16[8,144,576]{2,1,0:T(8,128)(2,1)S(1)}, u32[]{:S(2)}, u32[]{:S(2)}) collective-permute-start(bf16[8,144,576]{2,1,0:T(8,128)(2,1)S(1)} %all_to_all.15.out_own), channel_id=1, source_target_pairs={{0,1},{1,0},{2,3},{3,2},{4,5},{5,4},{6,7},{7,6},{8,9},{9,8},{10,11... | collective-permute-start | bytes 3981320 | tf_op jit(solution)/shard_map/ppermute | solution.py:24
  77.6 2.9 %collective-permute-start = (f32[1,1152]{1,0:T(1,128)S(1)}, f32[1,1152]{1,0:T(1,128)S(1)}, u32[]{:S(2)}, u32[]{:S(2)}) collective-permute-start(f32[1,1152]{1,0:T(1,128)S(1)} %copy-done.22), channel_id=1, source_target_pairs={{0,1},{1,0},{2,3},{3,2},{4,5},{5,4},{6,7},{7,6},{8,9},{9,8},{10,11... | collective-permute-start | bytes 13832 | tf_op jit(solution)/shard_map/ppermute | solution.py:24
  80.5 1.0 copy-start
  81.5 0.9 copy-start.9
  82.4 0.8 copy-start.14
  84.9 1.0 copy-start.7
  86.0 0.7 copy-start.12
  86.7 0.6 copy-start.18
  93.8 1.3 copy-start.8
  95.1 0.9 copy-start.13
  96.1 0.8 copy-start.16
  96.8 0.8 copy-start.17
  97.6 0.9 copy-start.19
  104.1 18.9 %all-to-all-start.1 = ((bf16[16,72,240]{2,1,0:T(8,128)(2,1)}), bf16[16,72,240]{2,1,0:T(8,128)(2,1)S(1)}, u32[]{:S(2)}, u32[]{:S(2)}) async-start(bf16[16,72,240]{2,1,0:T(8,128)(2,1)} %shard_map.160), calls=%async_computation.1 | async-start | bytes 1179648 | tf_op jit(solution)/shard_map/all_to_all | solution.py:533
  110.7 0.8 copy-start.10
  111.4 0.8 copy-start.15
  112.2 0.7 copy-start.21
  112.9 0.7 copy-start.23
  114.3 1.0 copy-start.1
  115.3 1.0 copy-start.3
  116.3 1.0 copy-start.5
  123.0 1.3 copy-start.2
  124.3 1.3 copy-start.4
  125.6 1.3 copy-start.6
  126.8 0.8 copy-start.20
  127.6 3.4 %copy-start.11 = (f32[32,192]{1,0:T(8,128)S(1)}, f32[32,192]{1,0:T(8,128)}, u32[]{:S(2)}) copy-start(f32[32,192]{1,0:T(8,128)} %get-tuple-element.16.packed) | copy-start | bytes 73732
  127.6 3.4 %copy-start.24 = (f32[8,48]{1,0:T(8,128)S(1)}, f32[8,48]{1,0:T(8,128)}, u32[]{:S(2)}) copy-start(f32[8,48]{1,0:T(8,128)} %noise.1) | copy-start | bytes 4612
  127.6 3.4 %copy-start.25 = (f32[8]{0:T(128)S(1)}, f32[8]{0:T(128)}, u32[]{:S(2)}) copy-start(f32[8]{0:T(128)} %table.1) | copy-start | bytes 100
  129.4 1.6 %collective-permute-start.2 = (f32[8,240]{1,0:T(8,128)S(1)}, f32[8,240]{1,0:T(8,128)S(1)}, u32[]{:S(2)}, u32[]{:S(2)}) collective-permute-start(f32[8,240]{1,0:T(8,128)S(1)} %get-tuple-element.27), channel_id=1, source_target_pairs={{0,1},{1,0},{2,3},{3,2},{4,5},{5,4},{6,7},{7,6},{8,9},{9,8},{10,11... | collective-permute-start | bytes 23048 | tf_op jit(solution)/shard_map/ppermute | solution.py:24

commit v3 on v2

--- a/solution.py
+++ b/solution.py
@@ -10,7 +10,7 @@
 EPS_NORM = 1e-06
 TIME_SHIFT = 3.0
 LANES = 128
-VMEM_BYTES = 40 * 1024 * 1024
+VMEM_BYTES = 20 * 1024 * 1024
 WHOLE_VMEM = 62 * 1024 * 1024
 F32 = jnp.float32
 BF16 = jnp.bfloat16
@@ -220,43 +220,61 @@
     )
 
 
-def pack_kernel(head_dim, latents, levels, window_mask, qkv, chunks, packed):
-    for h in range(chunks.shape[0]):
-        first = h * head_dim
-        chunks[h] = jnp.concatenate(
-            [qkv[part, :, first : first + head_dim] for part in range(3)], axis=1
+def place_of(axis):
+    return lax.axis_index(axis)
+
+
+def pack_kernel(head_dim, copies_frames, latents, levels, window_mask, qkv, *outs):
+    scratch = outs[-1]
+    copies, packed, first = outs[-4:-1]
+    chunks = outs[:-4]
+    scene, q, core = (place_of(a) for a in ("scene", "queue", "cfg"))
+    for h in range(scratch.shape[0]):
+        start = h * head_dim
+        scratch[h] = jnp.concatenate(
+            [qkv[part, :, start : start + head_dim] for part in range(3)], axis=1
         )
+    for k, chunk in enumerate(chunks):
+        chunk[...] = scratch[scene * len(chunks) + (q ^ k)]
     frames, values, tokens = latents.shape
     span = window_mask.shape[1]
-    pieces = []
+    shares = []
+    own = []
     for f in range(frames):
-        rows = [latents[f]]
-        side = jnp.zeros((packed.shape[0] - values, tokens), F32)
+        level = levels[:, f : f + 1].astype(F32)
+        side = jnp.zeros((copies.shape[1] - values, tokens), F32)
         row_id = lax.broadcasted_iota(jnp.int32, side.shape, 0)
         for o in range(span):
             side = jnp.where(row_id == o, window_mask[f : f + 1, o : o + 1].astype(F32), side)
-        side = jnp.where(row_id == span, levels[:, f : f + 1].astype(F32), side)
-        rows.append(side)
-        pieces.append(jnp.concatenate(rows, axis=0))
-    packed[...] = jnp.concatenate(pieces, axis=1)
+        side = jnp.where(row_id == span, level, side)
+        shares.append(jnp.concatenate([latents[f], side], axis=0))
+        fill = jnp.broadcast_to(level, (packed.shape[0] - values, tokens))
+        own.append(jnp.concatenate([latents[f], fill], axis=0))
+    lower = jnp.concatenate(shares[:copies_frames], axis=1)
+    upper = jnp.concatenate(shares[copies_frames:], axis=1)
+    share = jnp.where(core == 0, lower, upper).astype(BF16)
+    for at in range(copies.shape[0]):
+        copies[at] = share
+    packed[...] = jnp.concatenate(own, axis=1)
+    first[...] = own[0]
 
 
 def prepare_kernel(
-    frames, values, span, gathered, cond, level_mod, embed, lhs, xin, rstd_out, mask_out
+    frames, values, span, mine, other, cond, level_mod, embed, lhs, xin, rstd_out, mask_out
 ):
     width = embed.shape[1]
-    rows = xin.shape[1]
-    queue_tok = gathered.shape[0]
-    branches = cond.shape[0]
-    all_frames = xin.shape[0]
-    toks = queue_tok * frames // all_frames
-    tokens = gathered.shape[2] // frames
+    scenes, all_frames, rows, _ = xin.shape
+    queues = all_frames // frames
+    toks = mine.shape[0] // (scenes * queues)
+    per_core = frames // 2
+    tokens = mine.shape[2] // per_core
+    core = place_of("cfg")
     weights = embed[...].astype(F32)
     weights = weights - jnp.mean(weights, axis=1, keepdims=True)
     conds = cond[...]
     conds = conds - jnp.mean(conds, axis=1, keepdims=True)
     basis = jnp.concatenate(
-        [weights, conds, jnp.zeros((rows - values - branches, width), F32)], axis=0
+        [weights, conds, jnp.zeros((rows - values - scenes, width), F32)], axis=0
     )
     gram = lax.dot_general(
         basis,
@@ -268,50 +286,66 @@
     row_id = lax.broadcasted_iota(jnp.int32, (rows, LANES), 0)
     wide_id = lax.broadcasted_iota(jnp.int32, (rows, width), 0)
     level_id = lax.broadcasted_iota(jnp.int32, (level_mod.shape[1], width), 0).astype(F32)
-    shift_row = values + branches
+    shift_row = values + scenes
     fill = LANES - toks * tokens
-    for f in range(all_frames):
-        q, part = divmod(f, frames)
-        info = [
-            gathered[q * toks + t, :, part * tokens : (part + 1) * tokens] for t in range(toks)
-        ]
-        level = info[0][values + span : values + span + 1, 0:1]
-        chosen = level_id == level
-        shift = jnp.sum(jnp.where(chosen, level_mod[0], 0.0), axis=0, keepdims=True)
-        scale = jnp.sum(jnp.where(chosen, level_mod[1], 0.0), axis=0, keepdims=True)
-        block = basis * (1.0 + scale)
-        block = jnp.where((wide_id == shift_row) | (wide_id == shift_row + 1), shift, block)
-        lhs[f * rows : (f + 1) * rows, :] = block.astype(BF16)
-        info = jnp.concatenate(info + [jnp.ones((info[0].shape[0], fill), F32)], axis=1)
-        mask_out[f] = info[values : values + mask_out.shape[1]]
-        base = jnp.where(row_id < values, info[:rows], 0.0).astype(BF16).astype(F32)
-        for b in range(branches):
-            vec = jnp.where(row_id == values + b, 1.0, base)
-            spread = jnp.sum(
-                vec
-                * jnp.dot(gram, vec, preferred_element_type=F32, precision=lax.Precision.HIGHEST),
-                axis=0,
-                keepdims=True,
-            )
-            spread = jnp.maximum(spread, 0.0) + EPS_NORM
-            rstd = lax.rsqrt(spread)
-            std = spread * rstd
-            high = std.astype(BF16).astype(F32)
-            vec = jnp.where(row_id == shift_row, high, vec)
-            vec = jnp.where(row_id == shift_row + 1, std - high, vec)
-            xin[f, :, b * LANES : (b + 1) * LANES] = vec.astype(BF16)
-            rstd_out[f, :, b * LANES : (b + 1) * LANES] = rstd
-
-
-def attend_kernel(
-    frames, tokens, weight, lhs, xin, rstd_in, mask_in, gain_q, gain_k, out, proj, kfac, vfac, att
-):
-    all_frames, rows, lanes = xin.shape
+    for y in range(scenes):
+        for q in range(queues):
+            first = (y * queues + q) * toks
+            held = []
+            for t in range(toks):
+                one, two = mine[first + t].astype(F32), other[first + t].astype(F32)
+                held.append((jnp.where(core == 0, one, two), jnp.where(core == 0, two, one)))
+            for part in range(frames):
+                f = q * frames + part
+                at = part % per_core * tokens
+                info = [pair[part // per_core][:, at : at + tokens] for pair in held]
+                level = info[0][values + span : values + span + 1, 0:1]
+                chosen = level_id == level
+                shift = jnp.sum(jnp.where(chosen, level_mod[0], 0.0), axis=0, keepdims=True)
+                scale = jnp.sum(jnp.where(chosen, level_mod[1], 0.0), axis=0, keepdims=True)
+                block = basis * (1.0 + scale)
+                block = jnp.where((wide_id == shift_row) | (wide_id == shift_row + 1), shift, block)
+                to = (y * all_frames + f) * rows
+                lhs[to : to + rows, :] = block.astype(BF16)
+                info = jnp.concatenate(info + [jnp.ones((info[0].shape[0], fill), F32)], axis=1)
+                mask_out[y, f] = info[values : values + mask_out.shape[2]]
+                vec = jnp.where(row_id < values, info[:rows], 0.0)
+                vec = jnp.where(row_id == values + y, 1.0, vec)
+                spread = jnp.sum(
+                    vec
+                    * jnp.dot(
+                        gram, vec, preferred_element_type=F32, precision=lax.Precision.HIGHEST
+                    ),
+                    axis=0,
+                    keepdims=True,
+                )
+                spread = jnp.maximum(spread, 0.0) + EPS_NORM
+                rstd = lax.rsqrt(spread)
+                std = spread * rstd
+                high = std.astype(BF16).astype(F32)
+                vec = jnp.where(row_id == shift_row, high, vec)
+                vec = jnp.where(row_id == shift_row + 1, std - high, vec)
+                xin[y, f] = vec.astype(BF16)
+                rstd_out[f, :, y * LANES : (y + 1) * LANES] = rstd
+
+
+def attend_kernel(frames, tokens, queues, *refs):
+    pieces = refs[: 2 * queues]
+    lhs, xin, rstd_in, mask_in, gain_q, gain_k, out, whole, proj, kfac, vfac, att = refs[
+        2 * queues :
+    ]
+    scenes, all_frames, rows, _ = xin.shape
     head_dim = gain_q.shape[0]
     window = (proj.shape[0] - all_frames) // 2
     span = 2 * window + 1
-    branches = lanes // LANES
-    folded = jnp.dot(lhs[...], weight[...], preferred_element_type=F32)
+    q_at, core = place_of("queue"), place_of("cfg")
+    part_rows = pieces[0].shape[0]
+    for k in range(queues):
+        for side in range(2):
+            owner = core if side == 0 else 1 - core
+            first = pl.multiple_of(((q_at ^ k) * 2 + owner) * part_rows, 16)
+            whole[pl.ds(first, part_rows), :] = pieces[side * queues + k][...]
+    folded = jnp.dot(lhs[...], whole[...], preferred_element_type=F32)
     high, low = split_terms(folded, 2)
     gains = gain_q[...] * gain_k[...] * head_dim ** (-0.5)
     gains = jnp.broadcast_to(gains, (head_dim, LANES))
@@ -320,19 +354,22 @@
             proj[at] = jnp.zeros(proj.shape[1:], F32)
             kfac[at] = jnp.zeros(kfac.shape[1:], F32)
             vfac[at] = jnp.zeros(vfac.shape[1:], F32)
-    for f in range(all_frames):
-        piece = slice(f * rows, (f + 1) * rows)
-        made = dot_tn(high[piece], xin[f]) + dot_tn(low[piece], xin[f])
-        proj[f + window] = made
-        rstd = rstd_in[f]
-        keys = made[head_dim : 2 * head_dim]
-        square = jnp.mean(keys * keys, axis=0, keepdims=True)
-        kfac[f + window] = rstd * lax.rsqrt(rstd * rstd * square + EPS_NORM)
-        vfac[f + window] = rstd
+    for y in range(scenes):
+        lane = slice(y * LANES, (y + 1) * LANES)
+        for f in range(all_frames):
+            first = (y * all_frames + f) * rows
+            piece = slice(first, first + rows)
+            made = dot_tn(high[piece], xin[y, f]) + dot_tn(low[piece], xin[y, f])
+            proj[f + window, :, lane] = made
+            rstd = rstd_in[f, :, lane]
+            keys = made[head_dim : 2 * head_dim]
+            square = jnp.mean(keys * keys, axis=0, keepdims=True)
+            kfac[f + window, :, lane] = rstd * lax.rsqrt(rstd * rstd * square + EPS_NORM)
+            vfac[f + window, :, lane] = rstd
 
     def one_frame(f, carry):
-        for b in range(branches):
-            lane = slice(b * LANES, (b + 1) * LANES)
+        for y in range(scenes):
+            lane = slice(y * LANES, (y + 1) * LANES)
             query = proj[f + window, 0:head_dim, lane]
             rstd = vfac[f + window, :, lane]
             square = jnp.mean(query * query, axis=0, keepdims=True)
@@ -344,30 +381,29 @@
                 keys = proj[f + o, head_dim : 2 * head_dim, lane]
                 score = jnp.sum(query * keys, axis=0, keepdims=True)
                 score = score * (qfac * kfac[f + o, :, lane])
-                part = jnp.exp(score) * mask_in[f, o : o + 1, :]
+                part = jnp.exp(score) * mask_in[y, f, o : o + 1, :]
                 norm = norm + part
                 total = total + (part * vfac[f + o, :, lane]) * proj[f + o, 2 * head_dim :, lane]
-            att[f, b] = total / norm
+            att[f, y] = total / norm
         return carry
 
     lax.fori_loop(0, all_frames, one_frame, 0)
-    toks = out.shape[0] * frames // (all_frames * branches)
-    queues = all_frames // frames
+    toks = out.shape[0] // (scenes * queues)
     for t in range(toks):
-        for q in range(queues):
-            for b in range(branches):
-                pieces = [
-                    att[min(q * frames + i, all_frames - 1), b, :, t * tokens : (t + 1) * tokens]
+        for y in range(scenes):
+            for q in range(queues):
+                parts = [
+                    att[min(q * frames + i, all_frames - 1), y, :, t * tokens : (t + 1) * tokens]
                     for i in range(frames + 1)
                 ]
-                at = (t * queues + q) * branches + b
-                out[at] = jnp.concatenate(pieces, axis=1).astype(BF16)
+                at = (t * scenes + y) * queues + q
+                out[at] = jnp.concatenate(parts, axis=1).astype(BF16)
 
 
 def rows_kernel(
-    values, span, packed, following, cond, level_mod, embed, final_gain, emb_out, gate_out, gain_out
+    values, packed, following, cond, level_mod, embed, final_gain, emb_out, gate_out, gain_out
 ):
-    levels_all, width = level_mod.shape
+    levels_all, width = level_mod.shape[1:]
     info = jnp.concatenate([packed[...], following[...]], axis=1)
     lanes = info.shape[1]
     vec = info[:values].astype(BF16)
@@ -375,83 +411,79 @@
     zero = jnp.zeros((13, width), BF16)
     weights = jnp.concatenate([embed[...]] + split_terms(cond[...], 3) + [zero], axis=0)
     emb_out[...] = dot_tn(weights, jnp.concatenate([vec, ones], axis=0))
-    level = info[values + span : values + span + 1]
+    level = info[values : values + 1]
     one_hot = (lax.broadcasted_iota(jnp.int32, (levels_all, lanes), 0).astype(F32) == level).astype(
         F32
     ).astype(BF16)
-    gates = jnp.concatenate(split_terms(level_mod[...], 3), axis=0)
+    gates = jnp.concatenate(split_terms(level_mod[2], 3), axis=0)
     gate_out[...] = dot_tn(gates, jnp.concatenate([one_hot] * 3, axis=0))
     gains = jnp.concatenate(split_terms(final_gain[...], 3) + [zero], axis=0)
     gain_out[...] = dot_tn(gains, ones)
 
 
-def finish_kernel(
-    half,
-    toks,
-    attended,
-    out_own,
-    out_other,
-    emb,
-    gate,
-    gain,
-    final_w,
-    branch,
-    mine,
-    send,
-    scratch,
-    mixed,
-):
-    queues, columns, group = out_own.shape[0] // toks, out_own.shape[1], out_own.shape[2]
-    for core, held in ((branch[0], out_own), (1 - branch[0], out_other)):
-        for q in range(queues):
-            total = jnp.zeros((columns, attended.shape[1]), F32)
-            for t in range(toks):
-                made = jnp.dot(
-                    held[t * queues + q],
-                    attended[t * group : (t + 1) * group, :],
-                    preferred_element_type=F32,
-                )
-                total = total + made.astype(BF16).astype(F32)
-            first = pl.multiple_of((2 * q + core) * columns, 8)
-            mixed[pl.ds(first, columns), :] = total
+def finish_kernel(half, queues, attended, *refs):
+    parts = refs[:8]
+    emb, gate, gain, final_w, mine, send, scratch, mixed = refs[8:]
+    scene, q_at, tok, core = (place_of(a) for a in ("scene", "queue", "tok", "cfg"))
+    group = parts[0].shape[1]
+    columns = parts[0].shape[0] // queues
+    held = [
+        attended[pl.ds(pl.multiple_of(at * group, 16), group), :] for at in (tok, 1 - tok)
+    ]
+    for n in range(4):
+        owner = core if n // 2 == 0 else 1 - core
+        plane = scene if n % 2 == 0 else 1 - scene
+        total = None
+        for t in range(2):
+            made = jnp.dot(parts[2 * n + t][...], held[t], preferred_element_type=F32)
+            made = made.astype(BF16).astype(F32)
+            total = made if total is None else total + made
+        for k in range(queues):
+            first = (((q_at ^ k) * 2 + owner) * 2 + plane) * columns
+            mixed[pl.ds(pl.multiple_of(first, 8), columns), :] = total[
+                k * columns : (k + 1) * columns
+            ]
     summed = emb[...] + gate[...] * mixed[...]
     center = jnp.mean(summed, axis=0, keepdims=True)
     deviate = summed - center
     spread = jnp.mean(deviate * deviate, axis=0, keepdims=True)
     final = (deviate * lax.rsqrt(spread + EPS_NORM) * gain[...]).astype(BF16)
     scratch[...] = jnp.dot(final_w[...], final, preferred_element_type=F32)
-    own = pl.multiple_of(branch[0] * half, half)
-    other = pl.multiple_of((1 - branch[0]) * half, half)
+    own = pl.multiple_of(core * half, half)
+    other = pl.multiple_of((1 - core) * half, half)
     mine[...] = scratch[pl.ds(own, half), :]
     send[...] = scratch[pl.ds(other, half), :]
 
 
 def update_kernel(
-    values, span, levels_all, mine, partner, packed, following, noise, table, index, place, vel, new
+    values, levels_all, mine, partner, packed, following, noise, table, index, vel, new
 ):
     half = mine.shape[0]
     frames, _, tokens = vel.shape
-    is_cond = place[0] == 0
-    own = pl.multiple_of(place[0] * half, half)
+    core = place_of("cfg")
+    own = pl.multiple_of(core * half, half)
     here, there = mine[...], partner[...]
-    cond = jnp.where(is_cond, here, there)
-    uncond = jnp.where(is_cond, there, here)
+    cond = jnp.where(core == 0, here, there)
+    uncond = jnp.where(core == 0, there, here)
     guided = uncond + table[index[0]] * (cond - uncond)
     level = jnp.concatenate(
-        [packed[values + span : values + span + 1], following[values + span : values + span + 1]],
-        axis=1,
+        [packed[values : values + 1], following[values : values + 1]], axis=1
     )
     current = noise_sigma((level + 1.0) / levels_all)
     upcoming = noise_sigma(level / levels_all)
     latents = jnp.concatenate([packed[pl.ds(own, half), :], following[pl.ds(own, half), :]], axis=1)
     updated = latents + (upcoming - current) * guided
-    is_last = place[1] == 1
+    is_last = place_of("queue") == lax.axis_size("queue") - 1
     for f in range(frames):
         vel[f] = guided[:, f * tokens : (f + 1) * tokens]
         moved = updated[:, (f + 1) * tokens : (f + 2) * tokens]
         if f == frames - 1:
             moved = jnp.where(is_last, noise[...], moved)
         new[f] = moved
+
+
+def swapped(value, axis, mask):
+    return lax.ppermute(value, axis, [(i, i ^ mask) for i in range(lax.axis_size(axis))])
 
 
 def on_device_heads(
@@ -477,95 +509,107 @@
     levels_all = level_mod.shape[0]
     span = window_mask.shape[1]
     window = span // 2
-    queues, toks, branches = (lax.axis_size(a) for a in ("queue", "tok", "cfg"))
-    group = queues * branches
-    q_at, branch = lax.axis_index("queue"), lax.axis_index("cfg")
+    scenes, queues, toks = (lax.axis_size(a) for a in ("scene", "queue", "tok"))
+    chips = scenes * queues * toks
     all_frames = queues * frames
-    rows = -(-max(values + 4, values + span + 1) // 16) * 16
+    rows = -(-max(values + scenes + 2, values + span + 1) // 16) * 16
+    own_rows = -(-(values + 1) // 8) * 8
     local_rows = qkv_weight.shape[0]
-    lanes = branches * LANES
+    local_heads = qkv_weight.shape[2] // head_dim
+    lanes = scenes * LANES
     row_lanes = (frames + 1) * tokens
-
-    chunks, packed = kernel_call(
-        functools.partial(pack_kernel, head_dim),
-        [
-            jax.ShapeDtypeStruct((group, local_rows, 3 * head_dim), BF16),
-            jax.ShapeDtypeStruct((rows, frames * tokens), F32),
+    per_core = frames // 2
+    mods = jnp.transpose(level_mod, (1, 0, 2))
+
+    chunk = jax.ShapeDtypeStruct((local_rows, 3 * head_dim), BF16)
+    *chunks, copies, packed, first = kernel_call(
+        functools.partial(pack_kernel, head_dim, per_core),
+        [chunk] * queues
+        + [
+            jax.ShapeDtypeStruct((chips, rows, per_core * tokens), BF16),
+            jax.ShapeDtypeStruct((own_rows, frames * tokens), F32),
+            jax.ShapeDtypeStruct((own_rows, tokens), F32),
         ],
         "vvvv",
+        [pltpu.VMEM((local_heads, local_rows, 3 * head_dim), BF16)],
         vmem=WHOLE_VMEM,
     )(latents, levels[None], window_mask, jnp.transpose(qkv_weight, (1, 0, 2)))
-    gathered = lax.all_gather(packed, ("queue", "tok"), axis=0)
-    cond_other = from_partner(cond_embed, "cfg", 0)
-    weight = lax.all_to_all(chunks, ("queue", "cfg"), 0, 0).reshape(width, 3 * head_dim)
-    out_own, gathered = lax.optimization_barrier((out_weight.T, gathered))
-    out_own = jnp.broadcast_to(out_own[None], (toks * queues,) + out_own.shape)
-    out_own = lax.all_to_all(out_own, ("tok", "queue"), 0, 0)
-    out_other = from_partner(out_own, "cfg", 0)
+
+    near = [chunks[0]] + [swapped(chunks[k], "queue", k) for k in range(1, queues)]
+    far = [swapped(piece, "cfg", 1) for piece in near]
+    shares = lax.all_to_all(copies, ("scene", "queue", "tok"), 0, 0)
+    other_shares = swapped(shares, "cfg", 1)
+    cond_far = swapped(cond_embed, "scene", 1)
+    following = lax.ppermute(first, "queue", [(i + 1, i) for i in range(queues - 1)])
+
+    columns = out_weight.shape[1] // scenes
+    out_half = lax.dynamic_slice_in_dim(
+        out_weight.T, lax.axis_index("scene") * columns, columns, 0
+    )
+    out_half, shares = lax.optimization_barrier((out_half, shares))
+    part = jnp.concatenate(
+        [out_half] + [swapped(out_half, "queue", k) for k in range(1, queues)], axis=0
+    )
+    part_tok = swapped(part, "tok", 1)
+    parts = [part, part_tok, swapped(part, "scene", 1), swapped(part_tok, "scene", 1)]
+    parts = parts + [swapped(piece, "cfg", 1) for piece in parts]
 
     conds = jnp.where(
-        branch == 0,
-        jnp.concatenate([cond_embed, cond_other], axis=0),
-        jnp.concatenate([cond_other, cond_embed], axis=0),
-    )
-    mods = jnp.transpose(level_mod, (1, 0, 2))
+        lax.axis_index("scene") == 0,
+        jnp.concatenate([cond_embed, cond_far], axis=0),
+        jnp.concatenate([cond_far, cond_embed], axis=0),
+    )
     lhs, xin, rstd, masks = kernel_call(
         functools.partial(prepare_kernel, frames, values, span),
         [
-            jax.ShapeDtypeStruct((all_frames * rows, width), BF16),
-            jax.ShapeDtypeStruct((all_frames, rows, lanes), BF16),
+            jax.ShapeDtypeStruct((scenes * all_frames * rows, width), BF16),
+            jax.ShapeDtypeStruct((scenes, all_frames, rows, LANES), BF16),
             jax.ShapeDtypeStruct((all_frames, 1, lanes), F32),
-            jax.ShapeDtypeStruct((all_frames, rows - values, LANES), F32),
+            jax.ShapeDtypeStruct((scenes, all_frames, rows - values, LANES), F32),
         ],
-        "vvvv",
-    )(gathered, conds, mods, embed_weight)
+        "vvvvv",
+    )(shares, other_shares, conds, mods, embed_weight)
     attended = kernel_call(
-        functools.partial(attend_kernel, frames, tokens),
-        jax.ShapeDtypeStruct((toks * group, head_dim, row_lanes), BF16),
-        "vvvvvvv",
+        functools.partial(attend_kernel, frames, tokens, queues),
+        jax.ShapeDtypeStruct((chips, head_dim, row_lanes), BF16),
+        "v" * (2 * queues + 6),
         [
+            pltpu.VMEM((width, 3 * head_dim), BF16),
             pltpu.VMEM((all_frames + 2 * window, 3 * head_dim, lanes), F32),
             pltpu.VMEM((all_frames + 2 * window, 1, lanes), F32),
             pltpu.VMEM((all_frames + 2 * window, 1, lanes), F32),
-            pltpu.VMEM((all_frames, branches, head_dim, LANES), F32),
+            pltpu.VMEM((all_frames, scenes, head_dim, LANES), F32),
         ],
-    )(weight, lhs, xin, rstd, masks, query_gain[:, None], key_gain[:, None])
-    received = lax.all_to_all(attended, ("tok", "queue", "cfg"), 0, 0).reshape(width, row_lanes)
-
-    following = lax.dynamic_index_in_dim(
-        gathered,
-        jnp.minimum(q_at + 1, queues - 1) * toks + lax.axis_index("tok"),
-        0,
-        keepdims=False,
-    )[:, :tokens]
+    )(*near, *far, lhs, xin, rstd, masks, query_gain[:, None], key_gain[:, None])
+    received = lax.all_to_all(attended, ("tok", "scene", "queue"), 0, 0)
+    received = received.reshape(width, row_lanes)
+
     wide = jax.ShapeDtypeStruct((width, row_lanes), F32)
     emb, gate, gain = kernel_call(
-        functools.partial(rows_kernel, values, span), [wide, wide, wide], "vvvvvv"
-    )(packed, following, cond_embed, mods[2], embed_weight, final_gain[None])
+        functools.partial(rows_kernel, values), [wide, wide, wide], "vvvvvv"
+    )(packed, following, cond_embed, mods, embed_weight, final_gain[None])
     half = values // 2
     half_shape = jax.ShapeDtypeStruct((half, row_lanes), F32)
     mine, send = kernel_call(
-        functools.partial(finish_kernel, half, toks),
+        functools.partial(finish_kernel, half, queues),
         [half_shape, half_shape],
-        "vvvvvvvs",
+        "v" * 13,
         [pltpu.VMEM((values, row_lanes), F32), pltpu.VMEM((width, row_lanes), F32)],
-    )(received, out_own, out_other, emb, gate, gain, final_weight.T, branch[None])
-    partner = from_partner(send, "cfg", 0)
-    place = jnp.stack([branch, (q_at == queues - 1).astype(jnp.int32)])
+    )(received, *parts, emb, gate, gain, final_weight.T)
+    partner = swapped(send, "cfg", 1)
     shape = jax.ShapeDtypeStruct((frames, half, tokens), F32)
     return kernel_call(
-        functools.partial(update_kernel, values, span, levels_all),
-        [shape, shape],
-        "vvvvvsss",
-    )(mine, partner, packed, following, fresh_noise, guide_table, guide_index, place)
+        functools.partial(update_kernel, values, levels_all), [shape, shape], "vvvvvss"
+    )(mine, partner, packed, following, fresh_noise, guide_table, guide_index)
 
 
 def on_device(*args):
     latents, qkv_weight, query_gain = args[0], args[7], args[8]
     local_heads = qkv_weight.shape[2] // query_gain.shape[0]
-    one_head_each = local_heads == lax.axis_size("queue") * lax.axis_size("cfg")
-    fits = latents.shape[2] * lax.axis_size("tok") <= LANES
-    if one_head_each and fits:
+    scenes, queues, toks, cores = (lax.axis_size(a) for a in ("scene", "queue", "tok", "cfg"))
+    pairs = scenes == toks == cores == 2 and queues & (queues - 1) == 0
+    fits = latents.shape[2] * toks <= LANES and latents.shape[0] % cores == 0
+    if pairs and fits and local_heads == scenes * queues:
         return tuple(on_device_heads(*args))
     return on_device_general(*args)
 

time: 134 us -> 95.7 us (0.71)
  blocking collectives: 69.4 us -> 0 us
  starting transfers between devices: 8.57 us -> 33.2 us
  waiting for transfers between devices: 12.3 us -> 29.2 us
  local copies, waits for them, and re-layouts: 26.9 us -> 14.9 us
  Pallas kernels: 13.6 us -> 15.4 us
    all_gather x1 -> x0, blocking collectives: 34.7 us -> none  [on_device_heads(): gathered = lax.all_gather(packed, ('queue', 'tok'), axis=0)]
    all_to_all x1 -> x0, blocking collectives: 34.7 us -> none  [on_device_heads(): out_own = lax.all_to_all(out_own, ('tok', 'queue'), 0, 0)]
    ppermute x3 -> x21, waiting for transfers between devices: 0.15 us -> 29.2 us  [the longest x20 24.9 us: swapped(): lax.ppermute(value, axis, [(i, i ^ mask) for i in range(lax.axis_size(axi...]
    ppermute x3 -> x21, starting transfers between devices: 1.32 us -> 20.1 us  [the longest x20 18.8 us: swapped(): lax.ppermute(value, axis, [(i, i ^ mask) for i in range(lax.axis_size(axi...]
    all_to_all x2, waiting for transfers between devices: 12.2 us -> 0.01 us  [the longest x1 0.01 us: on_device_heads(): received = lax.all_to_all(attended, ('tok', 'scene', 'queue'), 0, 0)]
    unnamed x52 -> x53, local copies, waits for them, and re-layouts: 20.2 us -> 13.4 us
    all_to_all x2, starting transfers between devices: 7.25 us -> 13 us  [the longest x1 8.44 us: on_device_heads(): shares = lax.all_to_all(copies, ('scene', 'queue', 'tok'), 0, 0)]
    squeeze x2 -> x0, local copies, waits for them, and re-layouts: 1.65 us -> none  [the longest x1 0.89 us: on_device_heads(): mods[2]]
  transfers between devices with their start and end apart: 5 -> 23, of which waited for: 3 -> 6; matrix products, arithmetic and copies ran while one was open for 4% -> 2% of each run, Pallas kernels for 6% -> 10%
where the time goes in v3:
time: 95.7 us; the launch traced here: 95 us
  starting transfers between devices  33.2 us (35%)
  waiting for transfers between devices  29.2 us (31%)
  Pallas kernels  15.4 us (16%)
  local copies, waits for them, and re-layouts  14.9 us (16%)
  between operations  1.53 us (2%)
    ppermute x20, waiting for transfers between devices, swapped(): lax.ppermute(value, axis, [(i, i ^ mask) for i in range(lax.axis_size(axi...  24.9 us
    ppermute x20, starting transfers between devices, swapped(): lax.ppermute(value, axis, [(i, i ^ mask) for i in range(lax.axis_size(axi...  18.8 us
    unnamed x53, local copies, waits for them, and re-layouts  13.4 us
    all_to_all x1, starting transfers between devices, on_device_heads(): shares = lax.all_to_all(copies, ('scene', 'queue', 'tok'), 0, 0)  8.44 us
    pallas_call x1, Pallas kernels, on_device_heads(): kernel_call(functools.partial(attend_kernel, frames, tokens, queues), jax...  6.76 us
    all_to_all x1, starting transfers between devices, on_device_heads(): received = lax.all_to_all(attended, ('tok', 'scene', 'queue'), 0, 0)  4.59 us
    ppermute x1, waiting for transfers between devices, on_device_heads(): lax.ppermute(first, 'queue', [(i + 1, i) for i in range(queues - 1)])  4.27 us
    pallas_call x1, Pallas kernels, on_device_heads(): kernel_call(functools.partial(pack_kernel, head_dim, per_core), [chunk] *...  2.37 us
  transfers between devices with their start and end apart: 23, of which 6 were waited for; matrix products, arithmetic and copies ran while one was open for 2% of the time, Pallas kernels for 10%

profile of v3, /device:TPU:0, one launch (start us, length us, event | category | flops | bytes accessed | tf_op | source)
XLA Modules:
  0.0 95.0 jit_solution(8227024104330402905)
XLA Ops:
  0.7 2.4 %shard_map.158 = (bf16[144,216]{1,0:T(8,128)(2,1)}, bf16[144,216]{1,0:T(8,128)(2,1)}, bf16[144,216]{1,0:T(8,128)(2,1)}, bf16[144,216]{1,0:T(8,128)(2,1)}, bf16[1...) custom-call(f32[4,16,48]{2,1,0:T(8,128)} %latents.1, s32[1,4]{1,0:T(1,128)} %bitcast.16, ...), custom_call_target="tpu_custom_call" | custom-call | flops 1000000 | bytes 1000000 | tf_op jit(solution)/shard_map/pallas_call | solution.py:525
  3.0 8.4 %all-to-all-start = ((bf16[16,32,96]{2,1,0:T(8,128)(2,1)}), bf16[16,32,96]{2,1,0:T(8,128)(2,1)S(1)}, u32[]{:S(2)}, u32[]{:S(2)}) async-start(bf16[16,32,96]{2,1,0:T(8,128)(2,1)} %get-tuple-element.24), calls=%async_computation | async-start | bytes 262144 | tf_op jit(solution)/shard_map/all_to_all | solution.py:540
  11.5 1.9 %collective-permute-start.8 = (f32[1,1152]{1,0:T(1,128)}, f32[1,1152]{1,0:T(1,128)S(1)}, u32[]{:S(2)}, u32[]{:S(2)}) collective-permute-start(f32[1,1152]{1,0:T(1,128)} %cond.1), channel_id=1, source_target_pairs={{0,16},{16,0},{1,17},{17,1},{2,18},{18,2},{3,19},{19,3},{4,20},{20... | collective-permute-start | bytes 13832 | tf_op jit(solution)/shard_map/ppermute | solution.py:486
  13.4 1.5 %collective-permute-start = (bf16[144,216]{1,0:T(8,128)(2,1)}, bf16[144,216]{1,0:T(8,128)(2,1)S(1)}, u32[]{:S(2)}, u32[]{:S(2)}) collective-permute-start(bf16[144,216]{1,0:T(8,128)(2,1)} %get-tuple-element.21), channel_id=1, source_target_pairs={{0,4},{4,0},{8,12},{12,8},{1,5},{5,1},{9,13},{13,9},{2,6},{6,2},{1... | collective-permute-start | bytes 186632 | tf_op jit(solution)/shard_map/ppermute | solution.py:486
  14.9 2.4 %collective-permute-start.1 = (bf16[144,216]{1,0:T(8,128)(2,1)}, bf16[144,216]{1,0:T(8,128)(2,1)S(1)}, u32[]{:S(2)}, u32[]{:S(2)}) collective-permute-start(bf16[144,216]{1,0:T(8,128)(2,1)} %get-tuple-element.22), channel_id=1, source_target_pairs={{0,8},{4,12},{8,0},{12,4},{1,9},{5,13},{9,1},{13,5},{2,10},{6,14},... | collective-permute-start | bytes 186632 | tf_op jit(solution)/shard_map/ppermute | solution.py:486
  19.3 0.8 maximum_select_fusion.cond
  20.8 3.3 %collective-permute-start.10 = (bf16[72,576]{1,0:T(8,128)(2,1)S(1)}, bf16[72,576]{1,0:T(8,128)(2,1)S(1)}, u32[]{:S(2)}, u32[]{:S(2)}) collective-permute-start(bf16[72,576]{1,0:T(8,128)(2,1)S(1)} %dynamic-slice_bitcast_fusion), channel_id=1, source_target_pairs={{0,8},{4,12},{8,0},{12,4},{1,9},{5,13},{9,1},{13,5},{2,10},{6,14},... | collective-permute-start | bytes 248840 | tf_op jit(solution)/shard_map/ppermute | solution.py:486
  24.0 1.1 %collective-permute-done.9 = bf16[72,576]{1,0:T(8,128)(2,1)S(1)} collective-permute-done((bf16[72,576]{1,0:T(8,128)(2,1)S(1)}, bf16[72,576]{1,0:T(8,128)(2,1)S(1)}, u32[]{:S(2)}, u32[]{:S(2)}) %collective-permute-start.9) | collective-permute-done | bytes 82976 | tf_op jit(solution)/shard_map/ppermute | solution.py:486
  26.3 1.9 %collective-permute-done.10 = bf16[72,576]{1,0:T(8,128)(2,1)S(1)} collective-permute-done((bf16[72,576]{1,0:T(8,128)(2,1)S(1)}, bf16[72,576]{1,0:T(8,128)(2,1)S(1)}, u32[]{:S(2)}, u32[]{:S(2)}) %collective-permute-start.10) | collective-permute-done | bytes 82976 | tf_op jit(solution)/shard_map/ppermute | solution.py:486
  28.2 2.5 %collective-permute-start.11 = (bf16[72,576]{1,0:T(8,128)(2,1)S(1)}, bf16[72,576]{1,0:T(8,128)(2,1)S(1)}, u32[]{:S(2)}, u32[]{:S(2)}) collective-permute-start(bf16[72,576]{1,0:T(8,128)(2,1)S(1)} %dynamic-slice_bitcast_fusion), channel_id=1, source_target_pairs={{0,12},{4,8},{8,4},{12,0},{1,13},{5,9},{9,5},{13,1},{2,14},{6,10},... | collective-permute-start | bytes 248840 | tf_op jit(solution)/shard_map/ppermute | solution.py:486
  30.7 2.3 %shard_map.159 = (bf16[1024,1152]{1,0:T(8,128)(2,1)S(1)}, bf16[2,16,32,128]{3,2,1,0:T(8,128)(2,1)S(1)}, f32[16,1,256]{2,1,0:T(1,128)S(1)}, f32[2,16,16,128]{3,2,1,0:T(8,128)S(1)}) custom-call(bf16[16,32,96]{2,1,0:T(8,128)(2,1)S(1)} %all-to-all-done.mine, bf16[16,32,96]{2,1,0:T(8,128)(2,1)S(1)} %collective-permute-done.7.other, ...), custom_call_target="tpu_custom_call" | custom-call | flops 1000000 | bytes 1000000 | tf_op jit(solution)/shard_map/pallas_call | solution.py:562
  33.1 6.8 %shard_map.160 = bf16[16,72,240]{2,1,0:T(8,128)(2,1)} custom-call(bf16[144,216]{1,0:T(8,128)(2,1)S(1)} %copy-done.18, bf16[144,216]{1,0:T(8,128)(2,1)S(1)} %collective-permute-done.refs_1_, bf16[144,216]{1,0:T(8,128)(2,1)S(1)} %collective-permute-done.1.refs_2_, bf16[144,216]{1,0:T(8,128)(2,1)S(1)} %collective-permute-done.2.refs_3_, ...), custom_call_target="tpu_custom_call" | custom-call | flops 1000000 | bytes 1000000 | tf_op jit(solution)/shard_map/pallas_call | solution.py:572
  39.9 4.6 %all-to-all-start.1 = ((bf16[16,72,240]{2,1,0:T(8,128)(2,1)}), bf16[16,72,240]{2,1,0:T(8,128)(2,1)S(1)}, u32[]{:S(2)}, u32[]{:S(2)}) async-start(bf16[16,72,240]{2,1,0:T(8,128)(2,1)} %shard_map.160), calls=%async_computation.1 | async-start | bytes 1179648 | tf_op jit(solution)/shard_map/all_to_all | solution.py:584
  44.5 2.0 %collective-permute-start.12 = (bf16[288,576]{1,0:T(8,128)(2,1)S(1)}, bf16[288,576]{1,0:T(8,128)(2,1)S(1)}, u32[]{:S(2)}, u32[]{:S(2)}) collective-permute-start(bf16[288,576]{1,0:T(8,128)(2,1)S(1)} %constant_dynamic-update-slice_fusion.refs_0_), channel_id=1, source_target_pairs={{0,2},{2,0},{1,3},{3,1},{4,6},{6,4},{5,7},{7,5},{8,10},{10,8},{9,1... | collective-permute-start | bytes 995336 | tf_op jit(solution)/shard_map/ppermute | solution.py:486
  46.5 1.5 %collective-permute-start.13 = (bf16[288,576]{1,0:T(8,128)(2,1)S(1)}, bf16[288,576]{1,0:T(8,128)(2,1)S(1)}, u32[]{:S(2)}, u32[]{:S(2)}) collective-permute-start(bf16[288,576]{1,0:T(8,128)(2,1)S(1)} %constant_dynamic-update-slice_fusion.refs_0_), channel_id=1, source_target_pairs={{0,16},{16,0},{1,17},{17,1},{2,18},{18,2},{3,19},{19,3},{4,20},{20... | collective-permute-start | bytes 995336 | tf_op jit(solution)/shard_map/ppermute | solution.py:486
  47.9 13.4 %collective-permute-done.12.refs_1_ = bf16[288,576]{1,0:T(8,128)(2,1)S(1)} collective-permute-done((bf16[288,576]{1,0:T(8,128)(2,1)S(1)}, bf16[288,576]{1,0:T(8,128)(2,1)S(1)}, u32[]{:S(2)}, u32[]{:S(2)}) %collective-permute-start.12) | collective-permute-done | bytes 331808 | tf_op jit(solution)/shard_map/ppermute | solution.py:486
  61.3 1.1 %collective-permute-start.14 = (bf16[288,576]{1,0:T(8,128)(2,1)S(1)}, bf16[288,576]{1,0:T(8,128)(2,1)S(1)}, u32[]{:S(2)}, u32[]{:S(2)}) collective-permute-start(bf16[288,576]{1,0:T(8,128)(2,1)S(1)} %collective-permute-done.12.refs_1_), channel_id=1, source_target_pairs={{0,16},{16,0},{1,17},{17,1},{2,18},{18,2},{3,19},{19,3},{4,20},{20... | collective-permute-start | bytes 995336 | tf_op jit(solution)/shard_map/ppermute | solution.py:486
  62.9 8.0 %collective-permute-done.14.refs_3_ = bf16[288,576]{1,0:T(8,128)(2,1)S(1)} collective-permute-done((bf16[288,576]{1,0:T(8,128)(2,1)S(1)}, bf16[288,576]{1,0:T(8,128)(2,1)S(1)}, u32[]{:S(2)}, u32[]{:S(2)}) %collective-permute-start.14) | collective-permute-done | bytes 331808 | tf_op jit(solution)/shard_map/ppermute | solution.py:486
  70.9 0.8 copy-done.6
  71.7 1.3 %collective-permute-start.19 = (f32[24,48]{1,0:T(8,128)S(1)}, f32[24,48]{1,0:T(8,128)S(1)}, u32[]{:S(2)}, u32[]{:S(2)}) collective-permute-start(f32[24,48]{1,0:T(8,128)S(1)} %copy-done.24), channel_id=1, source_target_pairs={{4,0},{8,4},{12,8},{5,1},{9,5},{13,9},{6,2},{10,6},{14,10},{7,3},{... | collective-permute-start | bytes 13832 | tf_op jit(solution)/shard_map/ppermute | solution.py:543
  73.0 4.3 %collective-permute-done.19.following = f32[24,48]{1,0:T(8,128)S(1)} collective-permute-done((f32[24,48]{1,0:T(8,128)S(1)}, f32[24,48]{1,0:T(8,128)S(1)}, u32[]{:S(2)}, u32[]{:S(2)}) %collective-permute-start.19) | collective-permute-done | bytes 4640 | tf_op jit(solution)/shard_map/ppermute | solution.py:543
  78.0 1.1 %copy-done.1 = f32[1152,240]{1,0:T(8,128)} copy-done((f32[1152,240]{1,0:T(8,128)}, f32[1152,240]{1,0:T(8,128)S(1)}, u32[]{:S(2)}) %copy-start.1) | copy-done | bytes 1105944
  79.0 1.0 %copy-done.3 = f32[1152,240]{1,0:T(8,128)} copy-done((f32[1152,240]{1,0:T(8,128)}, f32[1152,240]{1,0:T(8,128)S(1)}, u32[]{:S(2)}) %copy-start.3) | copy-done | bytes 1105944
  83.1 1.3 %copy-done.2 = f32[1152,240]{1,0:T(8,128)S(1)} copy-done((f32[1152,240]{1,0:T(8,128)S(1)}, f32[1152,240]{1,0:T(8,128)}, u32[]{:S(2)}) %copy-start.2) | copy-done | bytes 1105944
  84.3 1.3 %copy-done.4 = f32[1152,240]{1,0:T(8,128)S(1)} copy-done((f32[1152,240]{1,0:T(8,128)S(1)}, f32[1152,240]{1,0:T(8,128)}, u32[]{:S(2)}) %copy-start.4) | copy-done | bytes 1105944
  85.6 1.0 %copy-done.7 = bf16[288,576]{1,0:T(8,128)(2,1)S(1)} copy-done((bf16[288,576]{1,0:T(8,128)(2,1)S(1)}, bf16[288,576]{1,0:T(8,128)(2,1)}, u32[]{:S(2)}) %copy-start.7) | copy-done | bytes 331800
  86.6 1.0 %copy-done.9 = bf16[288,576]{1,0:T(8,128)(2,1)S(1)} copy-done((bf16[288,576]{1,0:T(8,128)(2,1)S(1)}, bf16[288,576]{1,0:T(8,128)(2,1)}, u32[]{:S(2)}) %copy-start.9) | copy-done | bytes 331800
  87.6 1.0 %copy-done.11 = bf16[288,576]{1,0:T(8,128)(2,1)S(1)} copy-done((bf16[288,576]{1,0:T(8,128)(2,1)S(1)}, bf16[288,576]{1,0:T(8,128)(2,1)}, u32[]{:S(2)}) %copy-start.11) | copy-done | bytes 331800
  88.6 1.0 %copy-done.13 = bf16[288,576]{1,0:T(8,128)(2,1)S(1)} copy-done((bf16[288,576]{1,0:T(8,128)(2,1)S(1)}, bf16[288,576]{1,0:T(8,128)(2,1)}, u32[]{:S(2)}) %copy-start.13) | copy-done | bytes 331800
  89.6 1.0 %copy-done.15 = bf16[288,576]{1,0:T(8,128)(2,1)S(1)} copy-done((bf16[288,576]{1,0:T(8,128)(2,1)S(1)}, bf16[288,576]{1,0:T(8,128)(2,1)}, u32[]{:S(2)}) %copy-start.15) | copy-done | bytes 331800
  90.6 1.9 %shard_map.162 = (f32[8,240]{1,0:T(8,128)S(1)}, f32[8,240]{1,0:T(8,128)S(1)}) custom-call(bf16[1152,240]{1,0:T(8,128)(2,1)S(1)} %bitcast.9, bf16[288,576]{1,0:T(8,128)(2,1)S(1)} %constant_dynamic-update-slice_fusion.refs_0_, bf16[288,576]{1,0:T(8,128)(2,1)S(1)} %collective-permute-done.12.refs_1_, bf16[288,576]{1,0:T(8,128)(2,1)S(1)} %collective-permute-done.13.refs_2_, ...), custom_call_target="tpu_custom_call" | custom-call | flops 1000000 | bytes 1000000 | tf_op jit(solution)/shard_map/pallas_call | solution.py:593
  93.7 1.3 %shard_map.163 = (f32[4,8,48]{2,1,0:T(8,128)}, f32[4,8,48]{2,1,0:T(8,128)}) custom-call(f32[8,240]{1,0:T(8,128)S(1)} %get-tuple-element.36.mine, f32[8,240]{1,0:T(8,128)S(1)} %collective-permute-done.20.partner, f32[24,192]{1,0:T(8,128)S(1)} %copy-done.17, f32[24,48]{1,0:T(8,128)S(1)} %collective-permute-done.19.following, f32[8,48]{1,0:T(8,128)S(1)} %copy-done.21, ...), custom_call_target="tpu_custom_call" | custom-call | flops 1000000 | bytes 1000000 | tf_op jit(solution)/shard_map/pallas_call | solution.py:601
  (79 shorter events, 8.7 us)
Async XLA Ops:
  0.6 17.2 %copy-start = (bf16[576,144]{0,1:T(8,128)(2,1)S(1)}, bf16[576,144]{0,1:T(8,128)(2,1)}, u32[]{:S(2)}) copy-start(bf16[576,144]{0,1:T(8,128)(2,1)} %param.25) | copy-start | bytes 497668
  0.6 30.0 %copy-start.5 = (f32[16,3,1152]{2,0,1:T(8,128)S(1)}, f32[16,3,1152]{2,0,1:T(8,128)}, u32[]{:S(2)}) copy-start(f32[16,3,1152]{2,0,1:T(8,128)} %param.20) | copy-start | bytes 663556
  0.7 30.0 %copy-start.16 = (bf16[16,1152]{1,0:T(8,128)(2,1)S(1)}, bf16[16,1152]{1,0:T(8,128)(2,1)}, u32[]{:S(2)}) copy-start(bf16[16,1152]{1,0:T(8,128)(2,1)} %embed.3) | copy-start | bytes 110596
  3.0 30.0 %copy-start.18 = (bf16[144,216]{1,0:T(8,128)(2,1)S(1)}, bf16[144,216]{1,0:T(8,128)(2,1)}, u32[]{:S(2)}) copy-start(bf16[144,216]{1,0:T(8,128)(2,1)} %get-tuple-element.20.refs_0_) | copy-start | bytes 186628
  3.0 17.1 %all-to-all-start = ((bf16[16,32,96]{2,1,0:T(8,128)(2,1)}), bf16[16,32,96]{2,1,0:T(8,128)(2,1)S(1)}, u32[]{:S(2)}, u32[]{:S(2)}) async-start(bf16[16,32,96]{2,1,0:T(8,128)(2,1)} %get-tuple-element.24), calls=%async_computation | async-start | bytes 262144 | tf_op jit(solution)/shard_map/all_to_all | solution.py:540
  11.5 7.8 %collective-permute-start.8 = (f32[1,1152]{1,0:T(1,128)}, f32[1,1152]{1,0:T(1,128)S(1)}, u32[]{:S(2)}, u32[]{:S(2)}) collective-permute-start(f32[1,1152]{1,0:T(1,128)} %cond.1), channel_id=1, source_target_pairs={{0,16},{16,0},{1,17},{17,1},{2,18},{18,2},{3,19},{19,3},{4,20},{20... | collective-permute-start | bytes 13832 | tf_op jit(solution)/shard_map/ppermute | solution.py:486
  13.4 11.8 %collective-permute-start = (bf16[144,216]{1,0:T(8,128)(2,1)}, bf16[144,216]{1,0:T(8,128)(2,1)S(1)}, u32[]{:S(2)}, u32[]{:S(2)}) collective-permute-start(bf16[144,216]{1,0:T(8,128)(2,1)} %get-tuple-element.21), channel_id=1, source_target_pairs={{0,4},{4,0},{8,12},{12,8},{1,5},{5,1},{9,13},{13,9},{2,6},{6,2},{1... | collective-permute-start | bytes 186632 | tf_op jit(solution)/shard_map/ppermute | solution.py:486
  14.9 10.9 %collective-permute-start.1 = (bf16[144,216]{1,0:T(8,128)(2,1)}, bf16[144,216]{1,0:T(8,128)(2,1)S(1)}, u32[]{:S(2)}, u32[]{:S(2)}) collective-permute-start(bf16[144,216]{1,0:T(8,128)(2,1)} %get-tuple-element.22), channel_id=1, source_target_pairs={{0,8},{4,12},{8,0},{12,4},{1,9},{5,13},{9,1},{13,5},{2,10},{6,14},... | collective-permute-start | bytes 186632 | tf_op jit(solution)/shard_map/ppermute | solution.py:486
  17.2 8.6 %collective-permute-start.2 = (bf16[144,216]{1,0:T(8,128)(2,1)}, bf16[144,216]{1,0:T(8,128)(2,1)S(1)}, u32[]{:S(2)}, u32[]{:S(2)}) collective-permute-start(bf16[144,216]{1,0:T(8,128)(2,1)} %get-tuple-element.23), channel_id=1, source_target_pairs={{0,12},{4,8},{8,4},{12,0},{1,13},{5,9},{9,5},{13,1},{2,14},{6,10},... | collective-permute-start | bytes 186632 | tf_op jit(solution)/shard_map/ppermute | solution.py:486
  20.1 5.0 %collective-permute-start.9 = (bf16[72,576]{1,0:T(8,128)(2,1)S(1)}, bf16[72,576]{1,0:T(8,128)(2,1)S(1)}, u32[]{:S(2)}, u32[]{:S(2)}) collective-permute-start(bf16[72,576]{1,0:T(8,128)(2,1)S(1)} %dynamic-slice_bitcast_fusion), channel_id=1, source_target_pairs={{0,4},{4,0},{8,12},{12,8},{1,5},{5,1},{9,13},{13,9},{2,6},{6,2},{1... | collective-permute-start | bytes 248840 | tf_op jit(solution)/shard_map/ppermute | solution.py:486
  20.8 7.4 %collective-permute-start.10 = (bf16[72,576]{1,0:T(8,128)(2,1)S(1)}, bf16[72,576]{1,0:T(8,128)(2,1)S(1)}, u32[]{:S(2)}, u32[]{:S(2)}) collective-permute-start(bf16[72,576]{1,0:T(8,128)(2,1)S(1)} %dynamic-slice_bitcast_fusion), channel_id=1, source_target_pairs={{0,8},{4,12},{8,0},{12,4},{1,9},{5,13},{9,1},{13,5},{2,10},{6,14},... | collective-permute-start | bytes 248840 | tf_op jit(solution)/shard_map/ppermute | solution.py:486
  25.1 3.0 %collective-permute-start.7 = (bf16[16,32,96]{2,1,0:T(8,128)(2,1)S(1)}, bf16[16,32,96]{2,1,0:T(8,128)(2,1)S(1)}, u32[]{:S(2)}, u32[]{:S(2)}) collective-permute-start(bf16[16,32,96]{2,1,0:T(8,128)(2,1)S(1)} %all-to-all-done.mine), channel_id=1, source_target_pairs={{0,1},{1,0},{2,3},{3,2},{4,5},{5,4},{6,7},{7,6},{8,9},{9,8},{10,11... | collective-permute-start | bytes 294920 | tf_op jit(solution)/shard_map/ppermute | solution.py:486
  25.2 7.8 %collective-permute-start.3 = (bf16[144,216]{1,0:T(8,128)(2,1)}, bf16[144,216]{1,0:T(8,128)(2,1)S(1)}, u32[]{:S(2)}, u32[]{:S(2)}) collective-permute-start(bf16[144,216]{1,0:T(8,128)(2,1)} %get-tuple-element.20.refs_0_), channel_id=1, source_target_pairs={{0,1},{1,0},{2,3},{3,2},{4,5},{5,4},{6,7},{7,6},{8,9},{9,8},{10,11... | collective-permute-start | bytes 186632 | tf_op jit(solution)/shard_map/ppermute | solution.py:486
  25.8 7.3 %collective-permute-start.4 = (bf16[144,216]{1,0:T(8,128)(2,1)S(1)}, bf16[144,216]{1,0:T(8,128)(2,1)S(1)}, u32[]{:S(2)}, u32[]{:S(2)}) collective-permute-start(bf16[144,216]{1,0:T(8,128)(2,1)S(1)} %collective-permute-done.refs_1_), channel_id=1, source_target_pairs={{0,1},{1,0},{2,3},{3,2},{4,5},{5,4},{6,7},{7,6},{8,9},{9,8},{10,11... | collective-permute-start | bytes 186632 | tf_op jit(solution)/shard_map/ppermute | solution.py:486
  25.8 7.2 %collective-permute-start.5 = (bf16[144,216]{1,0:T(8,128)(2,1)S(1)}, bf16[144,216]{1,0:T(8,128)(2,1)S(1)}, u32[]{:S(2)}, u32[]{:S(2)}) collective-permute-start(bf16[144,216]{1,0:T(8,128)(2,1)S(1)} %collective-permute-done.1.refs_2_), channel_id=1, source_target_pairs={{0,1},{1,0},{2,3},{3,2},{4,5},{5,4},{6,7},{7,6},{8,9},{9,8},{10,11... | collective-permute-start | bytes 186632 | tf_op jit(solution)/shard_map/ppermute | solution.py:486
  28.2 4.9 %collective-permute-start.6 = (bf16[144,216]{1,0:T(8,128)(2,1)S(1)}, bf16[144,216]{1,0:T(8,128)(2,1)S(1)}, u32[]{:S(2)}, u32[]{:S(2)}) collective-permute-start(bf16[144,216]{1,0:T(8,128)(2,1)S(1)} %collective-permute-done.2.refs_3_), channel_id=1, source_target_pairs={{0,1},{1,0},{2,3},{3,2},{4,5},{5,4},{6,7},{7,6},{8,9},{9,8},{10,11... | collective-permute-start | bytes 186632 | tf_op jit(solution)/shard_map/ppermute | solution.py:486
  28.2 16.3 %collective-permute-start.11 = (bf16[72,576]{1,0:T(8,128)(2,1)S(1)}, bf16[72,576]{1,0:T(8,128)(2,1)S(1)}, u32[]{:S(2)}, u32[]{:S(2)}) collective-permute-start(bf16[72,576]{1,0:T(8,128)(2,1)S(1)} %dynamic-slice_bitcast_fusion), channel_id=1, source_target_pairs={{0,12},{4,8},{8,4},{12,0},{1,13},{5,9},{9,5},{13,1},{2,14},{6,10},... | collective-permute-start | bytes 248840 | tf_op jit(solution)/shard_map/ppermute | solution.py:486
  39.8 31.8 %copy-start.24 = (f32[24,48]{1,0:T(8,128)S(1)}, f32[24,48]{1,0:T(8,128)}, u32[]{:S(2)}) copy-start(f32[24,48]{1,0:T(8,128)} %get-tuple-element.32) | copy-start | bytes 13828
  39.8 33.1 %copy-start.23 = (f32[1152]{0:T(1024)S(1)}, f32[1152]{0:T(1024)}, u32[]{:S(2)}) copy-start(f32[1152]{0:T(1024)} %param.26) | copy-start | bytes 13828
  39.8 37.4 %copy-start.17 = (f32[24,192]{1,0:T(8,128)S(1)}, f32[24,192]{1,0:T(8,128)}, u32[]{:S(2)}) copy-start(f32[24,192]{1,0:T(8,128)} %get-tuple-element.31.packed) | copy-start | bytes 55300
  39.8 37.4 %copy-start.20 = (f32[1,1152]{1,0:T(1,128)S(1)}, f32[1,1152]{1,0:T(1,128)}, u32[]{:S(2)}) copy-start(f32[1,1152]{1,0:T(1,128)} %cond.1) | copy-start | bytes 13828
  39.8 43.2 %copy-start.19 = (bf16[1152,16]{0,1:T(8,128)(2,1)S(1)}, bf16[1152,16]{0,1:T(8,128)(2,1)}, u32[]{:S(2)}) copy-start(bf16[1152,16]{0,1:T(8,128)(2,1)} %param.27) | copy-start | bytes 110596
  39.9 43.2 %all-to-all-start.1 = ((bf16[16,72,240]{2,1,0:T(8,128)(2,1)}), bf16[16,72,240]{2,1,0:T(8,128)(2,1)S(1)}, u32[]{:S(2)}, u32[]{:S(2)}) async-start(bf16[16,72,240]{2,1,0:T(8,128)(2,1)} %shard_map.160), calls=%async_computation.1 | async-start | bytes 1179648 | tf_op jit(solution)/shard_map/all_to_all | solution.py:584
  44.5 16.8 %collective-permute-start.12 = (bf16[288,576]{1,0:T(8,128)(2,1)S(1)}, bf16[288,576]{1,0:T(8,128)(2,1)S(1)}, u32[]{:S(2)}, u32[]{:S(2)}) collective-permute-start(bf16[288,576]{1,0:T(8,128)(2,1)S(1)} %constant_dynamic-update-slice_fusion.refs_0_), channel_id=1, source_target_pairs={{0,2},{2,0},{1,3},{3,1},{4,6},{6,4},{5,7},{7,5},{8,10},{10,8},{9,1... | collective-permute-start | bytes 995336 | tf_op jit(solution)/shard_map/ppermute | solution.py:486
  46.5 16.4 %collective-permute-start.13 = (bf16[288,576]{1,0:T(8,128)(2,1)S(1)}, bf16[288,576]{1,0:T(8,128)(2,1)S(1)}, u32[]{:S(2)}, u32[]{:S(2)}) collective-permute-start(bf16[288,576]{1,0:T(8,128)(2,1)S(1)} %constant_dynamic-update-slice_fusion.refs_0_), channel_id=1, source_target_pairs={{0,16},{16,0},{1,17},{17,1},{2,18},{18,2},{3,19},{19,3},{4,20},{20... | collective-permute-start | bytes 995336 | tf_op jit(solution)/shard_map/ppermute | solution.py:486
  61.3 9.6 %collective-permute-start.14 = (bf16[288,576]{1,0:T(8,128)(2,1)S(1)}, bf16[288,576]{1,0:T(8,128)(2,1)S(1)}, u32[]{:S(2)}, u32[]{:S(2)}) collective-permute-start(bf16[288,576]{1,0:T(8,128)(2,1)S(1)} %collective-permute-done.12.refs_1_), channel_id=1, source_target_pairs={{0,16},{16,0},{1,17},{17,1},{2,18},{18,2},{3,19},{19,3},{4,20},{20... | collective-permute-start | bytes 995336 | tf_op jit(solution)/shard_map/ppermute | solution.py:486
  62.4 17.7 %collective-permute-start.15 = (bf16[288,576]{1,0:T(8,128)(2,1)S(1)}, bf16[288,576]{1,0:T(8,128)(2,1)S(1)}, u32[]{:S(2)}, u32[]{:S(2)}) collective-permute-start(bf16[288,576]{1,0:T(8,128)(2,1)S(1)} %constant_dynamic-update-slice_fusion.refs_0_), channel_id=1, source_target_pairs={{0,1},{1,0},{2,3},{3,2},{4,5},{5,4},{6,7},{7,6},{8,9},{9,8},{10,11... | collective-permute-start | bytes 995336 | tf_op jit(solution)/shard_map/ppermute | solution.py:486
  62.4 18.4 %collective-permute-start.16 = (bf16[288,576]{1,0:T(8,128)(2,1)S(1)}, bf16[288,576]{1,0:T(8,128)(2,1)S(1)}, u32[]{:S(2)}, u32[]{:S(2)}) collective-permute-start(bf16[288,576]{1,0:T(8,128)(2,1)S(1)} %collective-permute-done.12.refs_1_), channel_id=1, source_target_pairs={{0,1},{1,0},{2,3},{3,2},{4,5},{5,4},{6,7},{7,6},{8,9},{9,8},{10,11... | collective-permute-start | bytes 995336 | tf_op jit(solution)/shard_map/ppermute | solution.py:486
  62.9 18.6 %collective-permute-start.17 = (bf16[288,576]{1,0:T(8,128)(2,1)S(1)}, bf16[288,576]{1,0:T(8,128)(2,1)S(1)}, u32[]{:S(2)}, u32[]{:S(2)}) collective-permute-start(bf16[288,576]{1,0:T(8,128)(2,1)S(1)} %collective-permute-done.13.refs_2_), channel_id=1, source_target_pairs={{0,1},{1,0},{2,3},{3,2},{4,5},{5,4},{6,7},{7,6},{8,9},{9,8},{10,11... | collective-permute-start | bytes 995336 | tf_op jit(solution)/shard_map/ppermute | solution.py:486
  70.9 11.4 %collective-permute-start.18 = (bf16[288,576]{1,0:T(8,128)(2,1)S(1)}, bf16[288,576]{1,0:T(8,128)(2,1)S(1)}, u32[]{:S(2)}, u32[]{:S(2)}) collective-permute-start(bf16[288,576]{1,0:T(8,128)(2,1)S(1)} %collective-permute-done.14.refs_3_), channel_id=1, source_target_pairs={{0,1},{1,0},{2,3},{3,2},{4,5},{5,4},{6,7},{7,6},{8,9},{9,8},{10,11... | collective-permute-start | bytes 995336 | tf_op jit(solution)/shard_map/ppermute | solution.py:486
  71.7 5.6 %collective-permute-start.19 = (f32[24,48]{1,0:T(8,128)S(1)}, f32[24,48]{1,0:T(8,128)S(1)}, u32[]{:S(2)}, u32[]{:S(2)}) collective-permute-start(f32[24,48]{1,0:T(8,128)S(1)} %copy-done.24), channel_id=1, source_target_pairs={{4,0},{8,4},{12,8},{5,1},{9,5},{13,9},{6,2},{10,6},{14,10},{7,3},{... | collective-permute-start | bytes 13832 | tf_op jit(solution)/shard_map/ppermute | solution.py:543
  92.5 1.2 %collective-permute-start.20 = (f32[8,240]{1,0:T(8,128)S(1)}, f32[8,240]{1,0:T(8,128)S(1)}, u32[]{:S(2)}, u32[]{:S(2)}) collective-permute-start(f32[8,240]{1,0:T(8,128)S(1)} %get-tuple-element.37), channel_id=1, source_target_pairs={{0,1},{1,0},{2,3},{3,2},{4,5},{5,4},{6,7},{7,6},{8,9},{9,8},{10,11... | collective-permute-start | bytes 23048 | tf_op jit(solution)/shard_map/ppermute | solution.py:486
  (16 other events, 19.6 us)

commit v4 on v3

--- a/solution.py
+++ b/solution.py
@@ -188,7 +188,11 @@
 
 
 def kernel_call(body, out_shapes, spaces, scratch=(), vmem=VMEM_BYTES, **cost):
-    kinds = {"v": pl.BlockSpec(), "s": pl.BlockSpec(memory_space=pltpu.SMEM)}
+    kinds = {
+        "v": pl.BlockSpec(),
+        "s": pl.BlockSpec(memory_space=pltpu.SMEM),
+        "a": pl.BlockSpec(memory_space=pl.ANY),
+    }
     many = isinstance(out_shapes, (list, tuple))
     return pl.pallas_call(
         body,
@@ -260,7 +264,19 @@
 
 
 def prepare_kernel(
-    frames, values, span, mine, other, cond, level_mod, embed, lhs, xin, rstd_out, mask_out
+    frames,
+    values,
+    span,
+    mine,
+    other,
+    cond,
+    cond_far,
+    level_mod,
+    embed,
+    lhs,
+    xin,
+    rstd_out,
+    mask_out,
 ):
     width = embed.shape[1]
     scenes, all_frames, rows, _ = xin.shape
@@ -271,7 +287,11 @@
     core = place_of("cfg")
     weights = embed[...].astype(F32)
     weights = weights - jnp.mean(weights, axis=1, keepdims=True)
-    conds = cond[...]
+    here, there = cond[...], cond_far[...]
+    is_first = place_of("scene") == 0
+    conds = jnp.concatenate(
+        [jnp.where(is_first, here, there), jnp.where(is_first, there, here)], axis=0
+    )
     conds = conds - jnp.mean(conds, axis=1, keepdims=True)
     basis = jnp.concatenate(
         [weights, conds, jnp.zeros((rows - values - scenes, width), F32)], axis=0
@@ -335,7 +355,7 @@
         2 * queues :
     ]
     scenes, all_frames, rows, _ = xin.shape
-    head_dim = gain_q.shape[0]
+    head_dim = gain_q.shape[1]
     window = (proj.shape[0] - all_frames) // 2
     span = 2 * window + 1
     q_at, core = place_of("queue"), place_of("cfg")
@@ -347,8 +367,9 @@
             whole[pl.ds(first, part_rows), :] = pieces[side * queues + k][...]
     folded = jnp.dot(lhs[...], whole[...], preferred_element_type=F32)
     high, low = split_terms(folded, 2)
-    gains = gain_q[...] * gain_k[...] * head_dim ** (-0.5)
-    gains = jnp.broadcast_to(gains, (head_dim, LANES))
+    gains = split_terms(gain_q[...] * gain_k[...] * head_dim ** (-0.5), 3)
+    gains = jnp.concatenate(gains + [jnp.zeros((13, head_dim), BF16)], axis=0)
+    gains = dot_tn(gains, jnp.ones((16, LANES), BF16))
     for side in range(window):
         for at in (side, all_frames + window + side):
             proj[at] = jnp.zeros(proj.shape[1:], F32)
@@ -400,42 +421,48 @@
                 out[at] = jnp.concatenate(parts, axis=1).astype(BF16)
 
 
-def rows_kernel(
-    values, packed, following, cond, level_mod, embed, final_gain, emb_out, gate_out, gain_out
-):
-    levels_all, width = level_mod.shape[1:]
+def finish_kernel(half, values, queues, *refs):
+    count = 16
+    sources, mine, send, held = refs[:count], refs[count], refs[count + 1], refs[count + 2 : -5]
+    scratch, mixed, emb, gate, sems = refs[-5:]
+    copies = []
+    for i in range(count):
+        source = sources[i].at[2] if i == 3 else sources[i]
+        copies.append(pltpu.make_async_copy(source, held[i], sems.at[i]))
+    for copy in copies:
+        copy.start()
+    for copy in copies[:7]:
+        copy.wait()
+    packed, following, cond, gates, embed, final_gain, final_w, attended = held[:8]
+    parts = held[8:]
+    scene, q_at, tok, core = (place_of(a) for a in ("scene", "queue", "tok", "cfg"))
+
+    levels_all, width = gates.shape
     info = jnp.concatenate([packed[...], following[...]], axis=1)
     lanes = info.shape[1]
     vec = info[:values].astype(BF16)
     ones = jnp.ones((16, lanes), BF16)
     zero = jnp.zeros((13, width), BF16)
     weights = jnp.concatenate([embed[...]] + split_terms(cond[...], 3) + [zero], axis=0)
-    emb_out[...] = dot_tn(weights, jnp.concatenate([vec, ones], axis=0))
+    emb[...] = dot_tn(weights, jnp.concatenate([vec, ones], axis=0))
     level = info[values : values + 1]
     one_hot = (lax.broadcasted_iota(jnp.int32, (levels_all, lanes), 0).astype(F32) == level).astype(
         F32
     ).astype(BF16)
-    gates = jnp.concatenate(split_terms(level_mod[2], 3), axis=0)
-    gate_out[...] = dot_tn(gates, jnp.concatenate([one_hot] * 3, axis=0))
-    gains = jnp.concatenate(split_terms(final_gain[...], 3) + [zero], axis=0)
-    gain_out[...] = dot_tn(gains, ones)
-
-
-def finish_kernel(half, queues, attended, *refs):
-    parts = refs[:8]
-    emb, gate, gain, final_w, mine, send, scratch, mixed = refs[8:]
-    scene, q_at, tok, core = (place_of(a) for a in ("scene", "queue", "tok", "cfg"))
+    gate_terms = jnp.concatenate(split_terms(gates[...], 3), axis=0)
+    gate[...] = dot_tn(gate_terms, jnp.concatenate([one_hot] * 3, axis=0))
+
     group = parts[0].shape[1]
     columns = parts[0].shape[0] // queues
-    held = [
-        attended[pl.ds(pl.multiple_of(at * group, 16), group), :] for at in (tok, 1 - tok)
-    ]
+    copies[7].wait()
+    rows = [attended[pl.ds(pl.multiple_of(at * group, 16), group), :] for at in (tok, 1 - tok)]
     for n in range(4):
         owner = core if n // 2 == 0 else 1 - core
         plane = scene if n % 2 == 0 else 1 - scene
         total = None
         for t in range(2):
-            made = jnp.dot(parts[2 * n + t][...], held[t], preferred_element_type=F32)
+            copies[8 + 2 * n + t].wait()
+            made = jnp.dot(parts[2 * n + t][...], rows[t], preferred_element_type=F32)
             made = made.astype(BF16).astype(F32)
             total = made if total is None else total + made
         for k in range(queues):
@@ -447,7 +474,9 @@
     center = jnp.mean(summed, axis=0, keepdims=True)
     deviate = summed - center
     spread = jnp.mean(deviate * deviate, axis=0, keepdims=True)
-    final = (deviate * lax.rsqrt(spread + EPS_NORM) * gain[...]).astype(BF16)
+    gain_terms = jnp.concatenate(split_terms(final_gain[...], 3) + [zero], axis=0)
+    gain = dot_tn(gain_terms, ones)
+    final = (deviate * lax.rsqrt(spread + EPS_NORM) * gain).astype(BF16)
     scratch[...] = jnp.dot(final_w[...], final, preferred_element_type=F32)
     own = pl.multiple_of(core * half, half)
     other = pl.multiple_of((1 - core) * half, half)
@@ -483,7 +512,8 @@
 
 
 def swapped(value, axis, mask):
-    return lax.ppermute(value, axis, [(i, i ^ mask) for i in range(lax.axis_size(axis))])
+    count = lax.axis_size(axis)
+    return lax.ppermute(value, axis, [(i, i ^ mask) for i in range(count)])
 
 
 def on_device_heads(
@@ -546,19 +576,17 @@
     out_half = lax.dynamic_slice_in_dim(
         out_weight.T, lax.axis_index("scene") * columns, columns, 0
     )
-    out_half, shares = lax.optimization_barrier((out_half, shares))
     part = jnp.concatenate(
         [out_half] + [swapped(out_half, "queue", k) for k in range(1, queues)], axis=0
     )
-    part_tok = swapped(part, "tok", 1)
-    parts = [part, part_tok, swapped(part, "scene", 1), swapped(part_tok, "scene", 1)]
+    parts = [
+        part,
+        swapped(part, "tok", 1),
+        swapped(part, "scene", 1),
+        swapped(part, ("scene", "tok"), 3),
+    ]
     parts = parts + [swapped(piece, "cfg", 1) for piece in parts]
 
-    conds = jnp.where(
-        lax.axis_index("scene") == 0,
-        jnp.concatenate([cond_embed, cond_far], axis=0),
-        jnp.concatenate([cond_far, cond_embed], axis=0),
-    )
     lhs, xin, rstd, masks = kernel_call(
         functools.partial(prepare_kernel, frames, values, span),
         [
@@ -567,8 +595,10 @@
             jax.ShapeDtypeStruct((all_frames, 1, lanes), F32),
             jax.ShapeDtypeStruct((scenes, all_frames, rows - values, LANES), F32),
         ],
-        "vvvvv",
-    )(shares, other_shares, conds, mods, embed_weight)
+        "vvvvvv",
+        bytes_accessed=8_000_000,
+    )(shares, other_shares, cond_embed, cond_far, mods, embed_weight)
+    lhs, part = lax.optimization_barrier((lhs, part))
     attended = kernel_call(
         functools.partial(attend_kernel, frames, tokens, queues),
         jax.ShapeDtypeStruct((chips, head_dim, row_lanes), BF16),
@@ -580,22 +610,39 @@
             pltpu.VMEM((all_frames + 2 * window, 1, lanes), F32),
             pltpu.VMEM((all_frames, scenes, head_dim, LANES), F32),
         ],
-    )(*near, *far, lhs, xin, rstd, masks, query_gain[:, None], key_gain[:, None])
+        bytes_accessed=24_000_000,
+    )(*near, *far, lhs, xin, rstd, masks, query_gain[None], key_gain[None])
     received = lax.all_to_all(attended, ("tok", "scene", "queue"), 0, 0)
     received = received.reshape(width, row_lanes)
 
-    wide = jax.ShapeDtypeStruct((width, row_lanes), F32)
-    emb, gate, gain = kernel_call(
-        functools.partial(rows_kernel, values), [wide, wide, wide], "vvvvvv"
-    )(packed, following, cond_embed, mods, embed_weight, final_gain[None])
     half = values // 2
     half_shape = jax.ShapeDtypeStruct((half, row_lanes), F32)
+    wide = pltpu.VMEM((width, row_lanes), F32)
+    operands = (
+        packed,
+        following,
+        cond_embed,
+        mods,
+        embed_weight,
+        final_gain[None],
+        final_weight.T,
+        received,
+        *parts,
+    )
+    places = [
+        pltpu.VMEM(a.shape[1:] if i == 3 else a.shape, a.dtype) for i, a in enumerate(operands)
+    ]
     mine, send = kernel_call(
-        functools.partial(finish_kernel, half, queues),
+        functools.partial(finish_kernel, half, values, queues),
         [half_shape, half_shape],
-        "v" * 13,
-        [pltpu.VMEM((values, row_lanes), F32), pltpu.VMEM((width, row_lanes), F32)],
-    )(received, *parts, emb, gate, gain, final_weight.T)
+        "a" * len(operands),
+        places
+        + [pltpu.VMEM((values, row_lanes), F32)]
+        + [wide] * 3
+        + [pltpu.SemaphoreType.DMA((len(operands),))],
+        vmem=WHOLE_VMEM,
+        bytes_accessed=8_000_000,
+    )(*operands)
     partner = swapped(send, "cfg", 1)
     shape = jax.ShapeDtypeStruct((frames, half, tokens), F32)
     return kernel_call(

time: 95.7 us -> 96.8 us (1.011)
  waiting for transfers between devices: 29.2 us -> 36.4 us
  local copies, waits for them, and re-layouts: 14.9 us -> 8.99 us
  Pallas kernels: 15.4 us -> 18.8 us
  starting transfers between devices: 33.2 us -> 30.4 us
    ppermute x20, waiting for transfers between devices: 24.9 us -> 32.7 us  [swapped(): return lax.ppermute(value, axis, [(i, i ^ mask) for i in range(count)])]
    unnamed x53 -> x46, local copies, waits for them, and re-layouts: 13.4 us -> 8.38 us
    pallas_call x2 -> x1, Pallas kernels: 2.6 us -> 6.19 us  [on_device_heads(): kernel_call(functools.partial(finish_kernel, half, values, queues), [half...]
    ppermute x20, starting transfers between devices: 18.8 us -> 15.5 us  [swapped(): return lax.ppermute(value, axis, [(i, i ^ mask) for i in range(count)])]
    broadcast_in_dim x2 -> x0, local copies, waits for them, and re-layouts: 1.49 us -> none  [the longest x1 0.75 us: on_device_heads(): query_gain[:, None]]
  transfers between devices with their start and end apart: 23 -> 23, of which waited for: 6 -> 7; matrix products, arithmetic and copies ran while one was open for 2% -> 1% of each run, Pallas kernels for 10% -> 2%
where the time goes in v4:
time: 96.8 us; the launch traced here: 96.1 us
  waiting for transfers between devices  36.4 us (38%)
  starting transfers between devices  30.4 us (31%)
  Pallas kernels  18.8 us (19%)
  local copies, waits for them, and re-layouts  8.99 us (9%)
  between operations  1.51 us (2%)
    ppermute x20, waiting for transfers between devices, swapped(): return lax.ppermute(value, axis, [(i, i ^ mask) for i in range(count)])  32.7 us
    ppermute x20, starting transfers between devices, swapped(): return lax.ppermute(value, axis, [(i, i ^ mask) for i in range(count)])  15.5 us
    unnamed x46, local copies, waits for them, and re-layouts  8.38 us
    all_to_all x1, starting transfers between devices, on_device_heads(): shares = lax.all_to_all(copies, ('scene', 'queue', 'tok'), 0, 0)  8.31 us
    pallas_call x1, Pallas kernels, on_device_heads(): kernel_call(functools.partial(attend_kernel, frames, tokens, queues), jax...  6.66 us
    pallas_call x1, Pallas kernels, on_device_heads(): kernel_call(functools.partial(finish_kernel, half, values, queues), [half...  6.19 us
    all_to_all x1, starting transfers between devices, on_device_heads(): received = lax.all_to_all(attended, ('tok', 'scene', 'queue'), 0, 0)  5.35 us
    ppermute x1, waiting for transfers between devices, on_device_heads(): lax.ppermute(first, 'queue', [(i + 1, i) for i in range(queues - 1)])  3.68 us
  transfers between devices with their start and end apart: 23, of which 7 were waited for; matrix products, arithmetic and copies ran while one was open for 1% of the time, Pallas kernels for 2%

profile of v4, /device:TPU:0, one launch (start us, length us, event | category | flops | bytes accessed | tf_op | source)
XLA Modules:
  0.0 96.1 jit_solution(9471334172192976062)
XLA Ops:
  0.6 2.4 %shard_map.158 = (bf16[144,216]{1,0:T(8,128)(2,1)}, bf16[144,216]{1,0:T(8,128)(2,1)}, bf16[144,216]{1,0:T(8,128)(2,1)}, bf16[144,216]{1,0:T(8,128)(2,1)}, bf16[1...) custom-call(f32[4,16,48]{2,1,0:T(8,128)} %latents.1, s32[1,4]{1,0:T(1,128)} %bitcast.16, ...), custom_call_target="tpu_custom_call" | custom-call | flops 1000000 | bytes 1000000 | tf_op jit(solution)/shard_map/pallas_call | solution.py:555
  3.0 8.3 %all-to-all-start = ((bf16[16,32,96]{2,1,0:T(8,128)(2,1)}), bf16[16,32,96]{2,1,0:T(8,128)(2,1)S(1)}, u32[]{:S(2)}, u32[]{:S(2)}) async-start(bf16[16,32,96]{2,1,0:T(8,128)(2,1)} %get-tuple-element.22), calls=%async_computation | async-start | bytes 262144 | tf_op jit(solution)/shard_map/all_to_all | solution.py:570
  11.3 1.9 %collective-permute-start.1 = (bf16[144,216]{1,0:T(8,128)(2,1)}, bf16[144,216]{1,0:T(8,128)(2,1)S(1)}, u32[]{:S(2)}, u32[]{:S(2)}) collective-permute-start(bf16[144,216]{1,0:T(8,128)(2,1)} %get-tuple-element.19), channel_id=1, source_target_pairs={{0,4},{4,0},{8,12},{12,8},{1,5},{5,1},{9,13},{13,9},{2,6},{6,2},{1... | collective-permute-start | bytes 186632 | tf_op jit(solution)/shard_map/ppermute | solution.py:516
  13.5 2.8 %collective-permute-start.11 = (bf16[72,576]{1,0:T(8,128)(2,1)S(1)}, bf16[72,576]{1,0:T(8,128)(2,1)S(1)}, u32[]{:S(2)}, u32[]{:S(2)}) collective-permute-start(bf16[72,576]{1,0:T(8,128)(2,1)S(1)} %dynamic-slice_bitcast_fusion), channel_id=1, source_target_pairs={{0,8},{4,12},{8,0},{12,4},{1,9},{5,13},{9,1},{13,5},{2,10},{6,14},... | collective-permute-start | bytes 248840 | tf_op jit(solution)/shard_map/ppermute | solution.py:516
  16.3 1.5 %collective-permute-start.12 = (bf16[72,576]{1,0:T(8,128)(2,1)S(1)}, bf16[72,576]{1,0:T(8,128)(2,1)S(1)}, u32[]{:S(2)}, u32[]{:S(2)}) collective-permute-start(bf16[72,576]{1,0:T(8,128)(2,1)S(1)} %dynamic-slice_bitcast_fusion), channel_id=1, source_target_pairs={{0,12},{4,8},{8,4},{12,0},{1,13},{5,9},{9,5},{13,1},{2,14},{6,10},... | collective-permute-start | bytes 248840 | tf_op jit(solution)/shard_map/ppermute | solution.py:516
  17.7 1.5 %collective-permute-start.9 = (f32[1,1152]{1,0:T(1,128)}, f32[1,1152]{1,0:T(1,128)S(1)}, u32[]{:S(2)}, u32[]{:S(2)}) collective-permute-start(f32[1,1152]{1,0:T(1,128)} %refs_2_.1), channel_id=1, source_target_pairs={{0,16},{16,0},{1,17},{17,1},{2,18},{18,2},{3,19},{19,3},{4,20},{20... | collective-permute-start | bytes 13832 | tf_op jit(solution)/shard_map/ppermute | solution.py:516
  19.2 2.4 %collective-permute-done.9.cond_far = f32[1,1152]{1,0:T(1,128)S(1)} collective-permute-done((f32[1,1152]{1,0:T(1,128)}, f32[1,1152]{1,0:T(1,128)S(1)}, u32[]{:S(2)}, u32[]{:S(2)}) %collective-permute-start.9) | collective-permute-done | bytes 4640 | tf_op jit(solution)/shard_map/ppermute | solution.py:516
  21.6 1.5 %collective-permute-start.2 = (bf16[144,216]{1,0:T(8,128)(2,1)}, bf16[144,216]{1,0:T(8,128)(2,1)S(1)}, u32[]{:S(2)}, u32[]{:S(2)}) collective-permute-start(bf16[144,216]{1,0:T(8,128)(2,1)} %get-tuple-element.20), channel_id=1, source_target_pairs={{0,8},{4,12},{8,0},{12,4},{1,9},{5,13},{9,1},{13,5},{2,10},{6,14},... | collective-permute-start | bytes 186632 | tf_op jit(solution)/shard_map/ppermute | solution.py:516
  23.0 0.9 collective-permute-start.3
  23.9 6.8 %collective-permute-done.2.refs_2_ = bf16[144,216]{1,0:T(8,128)(2,1)S(1)} collective-permute-done((bf16[144,216]{1,0:T(8,128)(2,1)}, bf16[144,216]{1,0:T(8,128)(2,1)S(1)}, u32[]{:S(2)}, u32[]{:S(2)}) %collective-permute-start.2) | collective-permute-done | bytes 62240 | tf_op jit(solution)/shard_map/ppermute | solution.py:516
  31.9 1.2 %collective-permute-done.8.other = bf16[16,32,96]{2,1,0:T(8,128)(2,1)S(1)} collective-permute-done((bf16[16,32,96]{2,1,0:T(8,128)(2,1)S(1)}, bf16[16,32,96]{2,1,0:T(8,128)(2,1)S(1)}, u32[]{:S(2)}, u32[]{:S(2)}) %collective-permute-start.8) | collective-permute-done | bytes 98336 | tf_op jit(solution)/shard_map/ppermute | solution.py:516
  33.2 0.9 copy-done.1
  34.1 0.8 copy-done.2
  34.9 0.7 copy-done.7
  35.6 2.3 %shard_map.159 = (bf16[1024,1152]{1,0:T(8,128)(2,1)S(1)}, bf16[2,16,32,128]{3,2,1,0:T(8,128)(2,1)S(1)}, f32[16,1,256]{2,1,0:T(1,128)S(1)}, f32[2,16,16,128]{3,2,1,0:T(8,128)S(1)}) custom-call(bf16[16,32,96]{2,1,0:T(8,128)(2,1)S(1)} %all-to-all-done.mine, bf16[16,32,96]{2,1,0:T(8,128)(2,1)S(1)} %collective-permute-done.8.other, f32[1,1152]{1,0:T(1,128)S(1)} %copy-done.7, ...), custom_call_target="tpu_custom_call" | custom-call | flops 1000000 | bytes 8000000 | tf_op jit(solution)/shard_map/pallas_call | solution.py:590
  37.9 0.9 copy-done.4
  40.1 6.7 %shard_map.160 = bf16[16,72,240]{2,1,0:T(8,128)(2,1)} custom-call(bf16[144,216]{1,0:T(8,128)(2,1)S(1)} %copy-done.4, bf16[144,216]{1,0:T(8,128)(2,1)S(1)} %collective-permute-done.1.refs_1_, bf16[144,216]{1,0:T(8,128)(2,1)S(1)} %collective-permute-done.2.refs_2_, bf16[144,216]{1,0:T(8,128)(2,1)S(1)} %collective-permute-done.3.refs_3_, ...), custom_call_target="tpu_custom_call" | custom-call | flops 1000000 | bytes 24000000 | tf_op jit(solution)/shard_map/pallas_call | solution.py:602
  46.8 5.4 %all-to-all-start.1 = ((bf16[16,72,240]{2,1,0:T(8,128)(2,1)}), bf16[16,72,240]{2,1,0:T(8,128)(2,1)S(1)}, u32[]{:S(2)}, u32[]{:S(2)}) async-start(bf16[16,72,240]{2,1,0:T(8,128)(2,1)} %shard_map.160), calls=%async_computation.1 | async-start | bytes 1179648 | tf_op jit(solution)/shard_map/all_to_all | solution.py:615
  52.1 1.9 %collective-permute-start.13 = (bf16[288,576]{1,0:T(8,128)(2,1)S(1)}, bf16[288,576]{1,0:T(8,128)(2,1)S(1)}, u32[]{:S(2)}, u32[]{:S(2)}) collective-permute-start(bf16[288,576]{1,0:T(8,128)(2,1)S(1)} %pad_maximum_fusion.refs_8_), channel_id=1, source_target_pairs={{0,2},{2,0},{1,3},{3,1},{4,6},{6,4},{5,7},{7,5},{8,10},{10,8},{9,1... | collective-permute-start | bytes 995336 | tf_op jit(solution)/shard_map/ppermute | solution.py:516
  54.1 1.5 %collective-permute-start.14 = (bf16[288,576]{1,0:T(8,128)(2,1)S(1)}, bf16[288,576]{1,0:T(8,128)(2,1)S(1)}, u32[]{:S(2)}, u32[]{:S(2)}) collective-permute-start(bf16[288,576]{1,0:T(8,128)(2,1)S(1)} %pad_maximum_fusion.refs_8_), channel_id=1, source_target_pairs={{0,16},{16,0},{1,17},{17,1},{2,18},{18,2},{3,19},{19,3},{4,20},{20... | collective-permute-start | bytes 995336 | tf_op jit(solution)/shard_map/ppermute | solution.py:516
  55.7 14.3 %collective-permute-done.13.refs_9_ = bf16[288,576]{1,0:T(8,128)(2,1)S(1)} collective-permute-done((bf16[288,576]{1,0:T(8,128)(2,1)S(1)}, bf16[288,576]{1,0:T(8,128)(2,1)S(1)}, u32[]{:S(2)}, u32[]{:S(2)}) %collective-permute-start.13) | collective-permute-done | bytes 331808 | tf_op jit(solution)/shard_map/ppermute | solution.py:516
  70.5 7.2 %collective-permute-done.15.refs_11_ = bf16[288,576]{1,0:T(8,128)(2,1)S(1)} collective-permute-done((bf16[288,576]{1,0:T(8,128)(2,1)S(1)}, bf16[288,576]{1,0:T(8,128)(2,1)S(1)}, u32[]{:S(2)}, u32[]{:S(2)}) %collective-permute-start.15) | collective-permute-done | bytes 331808 | tf_op jit(solution)/shard_map/ppermute | solution.py:516
  77.7 1.3 %collective-permute-start = (f32[24,48]{1,0:T(8,128)S(1)}, f32[24,48]{1,0:T(8,128)S(1)}, u32[]{:S(2)}, u32[]{:S(2)}) collective-permute-start(f32[24,48]{1,0:T(8,128)S(1)} %copy-done.22), channel_id=1, source_target_pairs={{4,0},{8,4},{12,8},{5,1},{9,5},{13,9},{6,2},{10,6},{14,10},{7,3},{... | collective-permute-start | bytes 13832 | tf_op jit(solution)/shard_map/ppermute | solution.py:573
  79.6 3.7 %collective-permute-done.refs_1_.following = f32[24,48]{1,0:T(8,128)S(1)} collective-permute-done((f32[24,48]{1,0:T(8,128)S(1)}, f32[24,48]{1,0:T(8,128)S(1)}, u32[]{:S(2)}, u32[]{:S(2)}) %collective-permute-start) | collective-permute-done | bytes 4640 | tf_op jit(solution)/shard_map/ppermute | solution.py:573
  83.4 0.7 copy-done.18
  84.2 0.7 copy-done.20
  85.0 0.8 copy-done.13
  85.8 6.2 %shard_map.161 = (f32[8,240]{1,0:T(8,128)}, f32[8,240]{1,0:T(8,128)}) custom-call(f32[24,192]{1,0:T(8,128)} %get-tuple-element.16.refs_0_.packed, f32[24,48]{1,0:T(8,128)} %copy-done.5, f32[1,1152]{1,0:T(1,128)} %refs_2_.1, f32[3,16,1152]{2,1,0:T(8,128)} %bitcast.9, bf16[16,1152]{1,0:T(8,128)(2,1)} %refs_4_.1, f32[1,1152]{1,0:T(1,128)} %broadcast_in_dim.13.refs_5_, ...), custom_call_target="tpu_custom_call" | custom-call | flops 1000000 | bytes 8000000 | tf_op jit(solution)/shard_map/pallas_call | solution.py:635
  92.7 0.7 collective-permute-done.20.partner
  93.4 0.7 copy-done.6
  94.1 0.7 copy-done.8
  94.8 1.3 %shard_map.162 = (f32[4,8,48]{2,1,0:T(8,128)}, f32[4,8,48]{2,1,0:T(8,128)}) custom-call(f32[8,240]{1,0:T(8,128)S(1)} %copy-done.8, f32[8,240]{1,0:T(8,128)S(1)} %collective-permute-done.20.partner, f32[24,192]{1,0:T(8,128)S(1)} %copy-done.3, f32[24,48]{1,0:T(8,128)S(1)} %copy-done.6, f32[8,48]{1,0:T(8,128)S(1)} %copy-done.9, f32[8]{0:T(128)S(1)} %copy-done.12, ...), custom_call_target="tpu_custom_call" | custom-call | flops 1000000 | bytes 1000000 | tf_op jit(solution)/shard_map/pallas_call | solution.py:648
  (68 shorter events, 4.2 us)
Async XLA Ops:
  0.6 12.6 %copy-start = (bf16[576,144]{0,1:T(8,128)(2,1)S(1)}, bf16[576,144]{0,1:T(8,128)(2,1)}, u32[]{:S(2)}) copy-start(bf16[576,144]{0,1:T(8,128)(2,1)} %param.25) | copy-start | bytes 497668
  3.0 28.8 %all-to-all-start = ((bf16[16,32,96]{2,1,0:T(8,128)(2,1)}), bf16[16,32,96]{2,1,0:T(8,128)(2,1)S(1)}, u32[]{:S(2)}, u32[]{:S(2)}) async-start(bf16[16,32,96]{2,1,0:T(8,128)(2,1)} %get-tuple-element.22), calls=%async_computation | async-start | bytes 262144 | tf_op jit(solution)/shard_map/all_to_all | solution.py:570
  11.3 11.7 %collective-permute-start.1 = (bf16[144,216]{1,0:T(8,128)(2,1)}, bf16[144,216]{1,0:T(8,128)(2,1)S(1)}, u32[]{:S(2)}, u32[]{:S(2)}) collective-permute-start(bf16[144,216]{1,0:T(8,128)(2,1)} %get-tuple-element.19), channel_id=1, source_target_pairs={{0,4},{4,0},{8,12},{12,8},{1,5},{5,1},{9,13},{13,9},{2,6},{6,2},{1... | collective-permute-start | bytes 186632 | tf_op jit(solution)/shard_map/ppermute | solution.py:516
  13.3 18.0 %collective-permute-start.10 = (bf16[72,576]{1,0:T(8,128)(2,1)S(1)}, bf16[72,576]{1,0:T(8,128)(2,1)S(1)}, u32[]{:S(2)}, u32[]{:S(2)}) collective-permute-start(bf16[72,576]{1,0:T(8,128)(2,1)S(1)} %dynamic-slice_bitcast_fusion), channel_id=1, source_target_pairs={{0,4},{4,0},{8,12},{12,8},{1,5},{5,1},{9,13},{13,9},{2,6},{6,2},{1... | collective-permute-start | bytes 248840 | tf_op jit(solution)/shard_map/ppermute | solution.py:516
  13.5 17.9 %collective-permute-start.11 = (bf16[72,576]{1,0:T(8,128)(2,1)S(1)}, bf16[72,576]{1,0:T(8,128)(2,1)S(1)}, u32[]{:S(2)}, u32[]{:S(2)}) collective-permute-start(bf16[72,576]{1,0:T(8,128)(2,1)S(1)} %dynamic-slice_bitcast_fusion), channel_id=1, source_target_pairs={{0,8},{4,12},{8,0},{12,4},{1,9},{5,13},{9,1},{13,5},{2,10},{6,14},... | collective-permute-start | bytes 248840 | tf_op jit(solution)/shard_map/ppermute | solution.py:516
  16.3 15.5 %collective-permute-start.12 = (bf16[72,576]{1,0:T(8,128)(2,1)S(1)}, bf16[72,576]{1,0:T(8,128)(2,1)S(1)}, u32[]{:S(2)}, u32[]{:S(2)}) collective-permute-start(bf16[72,576]{1,0:T(8,128)(2,1)S(1)} %dynamic-slice_bitcast_fusion), channel_id=1, source_target_pairs={{0,12},{4,8},{8,4},{12,0},{1,13},{5,9},{9,5},{13,1},{2,14},{6,10},... | collective-permute-start | bytes 248840 | tf_op jit(solution)/shard_map/ppermute | solution.py:516
  17.7 3.8 %collective-permute-start.9 = (f32[1,1152]{1,0:T(1,128)}, f32[1,1152]{1,0:T(1,128)S(1)}, u32[]{:S(2)}, u32[]{:S(2)}) collective-permute-start(f32[1,1152]{1,0:T(1,128)} %refs_2_.1), channel_id=1, source_target_pairs={{0,16},{16,0},{1,17},{17,1},{2,18},{18,2},{3,19},{19,3},{4,20},{20... | collective-permute-start | bytes 13832 | tf_op jit(solution)/shard_map/ppermute | solution.py:516
  21.6 9.2 %collective-permute-start.2 = (bf16[144,216]{1,0:T(8,128)(2,1)}, bf16[144,216]{1,0:T(8,128)(2,1)S(1)}, u32[]{:S(2)}, u32[]{:S(2)}) collective-permute-start(bf16[144,216]{1,0:T(8,128)(2,1)} %get-tuple-element.20), channel_id=1, source_target_pairs={{0,8},{4,12},{8,0},{12,4},{1,9},{5,13},{9,1},{13,5},{2,10},{6,14},... | collective-permute-start | bytes 186632 | tf_op jit(solution)/shard_map/ppermute | solution.py:516
  23.0 7.8 %collective-permute-start.3 = (bf16[144,216]{1,0:T(8,128)(2,1)}, bf16[144,216]{1,0:T(8,128)(2,1)S(1)}, u32[]{:S(2)}, u32[]{:S(2)}) collective-permute-start(bf16[144,216]{1,0:T(8,128)(2,1)} %get-tuple-element.21), channel_id=1, source_target_pairs={{0,12},{4,8},{8,4},{12,0},{1,13},{5,9},{9,5},{13,1},{2,14},{6,10},... | collective-permute-start | bytes 186632 | tf_op jit(solution)/shard_map/ppermute | solution.py:516
  30.8 7.1 %collective-permute-start.4 = (bf16[144,216]{1,0:T(8,128)(2,1)}, bf16[144,216]{1,0:T(8,128)(2,1)S(1)}, u32[]{:S(2)}, u32[]{:S(2)}) collective-permute-start(bf16[144,216]{1,0:T(8,128)(2,1)} %get-tuple-element.18.refs_0_), channel_id=1, source_target_pairs={{0,1},{1,0},{2,3},{3,2},{4,5},{5,4},{6,7},{7,6},{8,9},{9,8},{10,11... | collective-permute-start | bytes 186632 | tf_op jit(solution)/shard_map/ppermute | solution.py:516
  30.8 7.1 %collective-permute-start.5 = (bf16[144,216]{1,0:T(8,128)(2,1)S(1)}, bf16[144,216]{1,0:T(8,128)(2,1)S(1)}, u32[]{:S(2)}, u32[]{:S(2)}) collective-permute-start(bf16[144,216]{1,0:T(8,128)(2,1)S(1)} %collective-permute-done.1.refs_1_), channel_id=1, source_target_pairs={{0,1},{1,0},{2,3},{3,2},{4,5},{5,4},{6,7},{7,6},{8,9},{9,8},{10,11... | collective-permute-start | bytes 186632 | tf_op jit(solution)/shard_map/ppermute | solution.py:516
  31.3 6.6 %collective-permute-start.6 = (bf16[144,216]{1,0:T(8,128)(2,1)S(1)}, bf16[144,216]{1,0:T(8,128)(2,1)S(1)}, u32[]{:S(2)}, u32[]{:S(2)}) collective-permute-start(bf16[144,216]{1,0:T(8,128)(2,1)S(1)} %collective-permute-done.2.refs_2_), channel_id=1, source_target_pairs={{0,1},{1,0},{2,3},{3,2},{4,5},{5,4},{6,7},{7,6},{8,9},{9,8},{10,11... | collective-permute-start | bytes 186632 | tf_op jit(solution)/shard_map/ppermute | solution.py:516
  31.4 6.5 %collective-permute-start.7 = (bf16[144,216]{1,0:T(8,128)(2,1)S(1)}, bf16[144,216]{1,0:T(8,128)(2,1)S(1)}, u32[]{:S(2)}, u32[]{:S(2)}) collective-permute-start(bf16[144,216]{1,0:T(8,128)(2,1)S(1)} %collective-permute-done.3.refs_3_), channel_id=1, source_target_pairs={{0,1},{1,0},{2,3},{3,2},{4,5},{5,4},{6,7},{7,6},{8,9},{9,8},{10,11... | collective-permute-start | bytes 186632 | tf_op jit(solution)/shard_map/ppermute | solution.py:516
  31.8 1.4 %collective-permute-start.8 = (bf16[16,32,96]{2,1,0:T(8,128)(2,1)S(1)}, bf16[16,32,96]{2,1,0:T(8,128)(2,1)S(1)}, u32[]{:S(2)}, u32[]{:S(2)}) collective-permute-start(bf16[16,32,96]{2,1,0:T(8,128)(2,1)S(1)} %all-to-all-done.mine), channel_id=1, source_target_pairs={{0,1},{1,0},{2,3},{3,2},{4,5},{5,4},{6,7},{7,6},{8,9},{9,8},{10,11... | collective-permute-start | bytes 294920 | tf_op jit(solution)/shard_map/ppermute | solution.py:516
  31.9 23.7 %copy-start.14 = (bf16[288,576]{1,0:T(8,128)(2,1)}, bf16[288,576]{1,0:T(8,128)(2,1)S(1)}, u32[]{:S(2)}) copy-start(bf16[288,576]{1,0:T(8,128)(2,1)S(1)} %pad_maximum_fusion.refs_8_) | copy-start | bytes 995332
  40.1 37.6 %copy-start.22 = (f32[24,48]{1,0:T(8,128)S(1)}, f32[24,48]{1,0:T(8,128)}, u32[]{:S(2)}) copy-start(f32[24,48]{1,0:T(8,128)} %get-tuple-element.17) | copy-start | bytes 13828
  40.1 38.9 %copy-start.21 = (f32[1152]{0:T(1024)S(1)}, f32[1152]{0:T(1024)}, u32[]{:S(2)}) copy-start(f32[1152]{0:T(1024)} %param.26) | copy-start | bytes 13828
  46.8 46.7 %copy-start.3 = (f32[24,192]{1,0:T(8,128)S(1)}, f32[24,192]{1,0:T(8,128)}, u32[]{:S(2)}) copy-start(f32[24,192]{1,0:T(8,128)} %get-tuple-element.16.refs_0_.packed) | copy-start | bytes 55300
  46.8 46.7 %copy-start.9 = (f32[8,48]{1,0:T(8,128)S(1)}, f32[8,48]{1,0:T(8,128)}, u32[]{:S(2)}) copy-start(f32[8,48]{1,0:T(8,128)} %noise.1) | copy-start | bytes 4612
  46.8 46.7 %copy-start.12 = (f32[8]{0:T(128)S(1)}, f32[8]{0:T(128)}, u32[]{:S(2)}) copy-start(f32[8]{0:T(128)} %table.1) | copy-start | bytes 100
  46.8 38.2 %all-to-all-start.1 = ((bf16[16,72,240]{2,1,0:T(8,128)(2,1)}), bf16[16,72,240]{2,1,0:T(8,128)(2,1)S(1)}, u32[]{:S(2)}, u32[]{:S(2)}) async-start(bf16[16,72,240]{2,1,0:T(8,128)(2,1)} %shard_map.160), calls=%async_computation.1 | async-start | bytes 1179648 | tf_op jit(solution)/shard_map/all_to_all | solution.py:615
  52.1 17.9 %collective-permute-start.13 = (bf16[288,576]{1,0:T(8,128)(2,1)S(1)}, bf16[288,576]{1,0:T(8,128)(2,1)S(1)}, u32[]{:S(2)}, u32[]{:S(2)}) collective-permute-start(bf16[288,576]{1,0:T(8,128)(2,1)S(1)} %pad_maximum_fusion.refs_8_), channel_id=1, source_target_pairs={{0,2},{2,0},{1,3},{3,1},{4,6},{6,4},{5,7},{7,5},{8,10},{10,8},{9,1... | collective-permute-start | bytes 995336 | tf_op jit(solution)/shard_map/ppermute | solution.py:516
  54.1 16.0 %collective-permute-start.14 = (bf16[288,576]{1,0:T(8,128)(2,1)S(1)}, bf16[288,576]{1,0:T(8,128)(2,1)S(1)}, u32[]{:S(2)}, u32[]{:S(2)}) collective-permute-start(bf16[288,576]{1,0:T(8,128)(2,1)S(1)} %pad_maximum_fusion.refs_8_), channel_id=1, source_target_pairs={{0,16},{16,0},{1,17},{17,1},{2,18},{18,2},{3,19},{19,3},{4,20},{20... | collective-permute-start | bytes 995336 | tf_op jit(solution)/shard_map/ppermute | solution.py:516
  55.5 22.2 %collective-permute-start.15 = (bf16[288,576]{1,0:T(8,128)(2,1)S(1)}, bf16[288,576]{1,0:T(8,128)(2,1)S(1)}, u32[]{:S(2)}, u32[]{:S(2)}) collective-permute-start(bf16[288,576]{1,0:T(8,128)(2,1)S(1)} %pad_maximum_fusion.refs_8_), channel_id=1, source_target_pairs={{0,18},{2,16},{16,2},{18,0},{1,19},{3,17},{17,3},{19,1},{4,22},{6,... | collective-permute-start | bytes 995336 | tf_op jit(solution)/shard_map/ppermute | solution.py:516
  55.7 27.6 %collective-permute-start.16 = (bf16[288,576]{1,0:T(8,128)(2,1)S(1)}, bf16[288,576]{1,0:T(8,128)(2,1)S(1)}, u32[]{:S(2)}, u32[]{:S(2)}) collective-permute-start(bf16[288,576]{1,0:T(8,128)(2,1)S(1)} %pad_maximum_fusion.refs_8_), channel_id=1, source_target_pairs={{0,1},{1,0},{2,3},{3,2},{4,5},{5,4},{6,7},{7,6},{8,9},{9,8},{10,11... | collective-permute-start | bytes 995336 | tf_op jit(solution)/shard_map/ppermute | solution.py:516
  70.0 14.9 %copy-start.15 = (bf16[288,576]{1,0:T(8,128)(2,1)}, bf16[288,576]{1,0:T(8,128)(2,1)S(1)}, u32[]{:S(2)}) copy-start(bf16[288,576]{1,0:T(8,128)(2,1)S(1)} %collective-permute-done.13.refs_9_) | copy-start | bytes 995332
  70.0 13.3 %collective-permute-start.17 = (bf16[288,576]{1,0:T(8,128)(2,1)S(1)}, bf16[288,576]{1,0:T(8,128)(2,1)S(1)}, u32[]{:S(2)}, u32[]{:S(2)}) collective-permute-start(bf16[288,576]{1,0:T(8,128)(2,1)S(1)} %collective-permute-done.13.refs_9_), channel_id=1, source_target_pairs={{0,1},{1,0},{2,3},{3,2},{4,5},{5,4},{6,7},{7,6},{8,9},{9,8},{10,11... | collective-permute-start | bytes 995336 | tf_op jit(solution)/shard_map/ppermute | solution.py:516
  70.0 14.9 %copy-start.16 = (bf16[288,576]{1,0:T(8,128)(2,1)}, bf16[288,576]{1,0:T(8,128)(2,1)S(1)}, u32[]{:S(2)}) copy-start(bf16[288,576]{1,0:T(8,128)(2,1)S(1)} %collective-permute-done.14.refs_10_) | copy-start | bytes 995332
  70.0 13.3 %collective-permute-start.18 = (bf16[288,576]{1,0:T(8,128)(2,1)S(1)}, bf16[288,576]{1,0:T(8,128)(2,1)S(1)}, u32[]{:S(2)}, u32[]{:S(2)}) collective-permute-start(bf16[288,576]{1,0:T(8,128)(2,1)S(1)} %collective-permute-done.14.refs_10_), channel_id=1, source_target_pairs={{0,1},{1,0},{2,3},{3,2},{4,5},{5,4},{6,7},{7,6},{8,9},{9,8},{10,11... | collective-permute-start | bytes 995336 | tf_op jit(solution)/shard_map/ppermute | solution.py:516
  77.7 7.2 %collective-permute-start.19 = (bf16[288,576]{1,0:T(8,128)(2,1)S(1)}, bf16[288,576]{1,0:T(8,128)(2,1)}, u32[]{:S(2)}, u32[]{:S(2)}) collective-permute-start(bf16[288,576]{1,0:T(8,128)(2,1)S(1)} %collective-permute-done.15.refs_11_), channel_id=1, source_target_pairs={{0,1},{1,0},{2,3},{3,2},{4,5},{5,4},{6,7},{7,6},{8,9},{9,8},{10,11... | collective-permute-start | bytes 995336 | tf_op jit(solution)/shard_map/ppermute | solution.py:516
  77.7 5.6 %collective-permute-start = (f32[24,48]{1,0:T(8,128)S(1)}, f32[24,48]{1,0:T(8,128)S(1)}, u32[]{:S(2)}, u32[]{:S(2)}) collective-permute-start(f32[24,48]{1,0:T(8,128)S(1)} %copy-done.22), channel_id=1, source_target_pairs={{4,0},{8,4},{12,8},{5,1},{9,5},{13,9},{6,2},{10,6},{14,10},{7,3},{... | collective-permute-start | bytes 13832 | tf_op jit(solution)/shard_map/ppermute | solution.py:573
  92.0 1.4 %collective-permute-start.20 = (f32[8,240]{1,0:T(8,128)}, f32[8,240]{1,0:T(8,128)S(1)}, u32[]{:S(2)}, u32[]{:S(2)}) collective-permute-start(f32[8,240]{1,0:T(8,128)} %get-tuple-element.29), channel_id=1, source_target_pairs={{0,1},{1,0},{2,3},{3,2},{4,5},{5,4},{6,7},{7,6},{8,9},{9,8},{10,11... | collective-permute-start | bytes 23048 | tf_op jit(solution)/shard_map/ppermute | solution.py:516
  (14 other events, 16.4 us)

commit v5 on v4

--- a/solution.py
+++ b/solution.py
@@ -12,6 +12,7 @@
 LANES = 128
 VMEM_BYTES = 20 * 1024 * 1024
 WHOLE_VMEM = 62 * 1024 * 1024
+HOLD_BYTES = 80_000_000
 F32 = jnp.float32
 BF16 = jnp.bfloat16
 
@@ -228,7 +229,7 @@
     return lax.axis_index(axis)
 
 
-def pack_kernel(head_dim, copies_frames, latents, levels, window_mask, qkv, *outs):
+def pack_kernel(head_dim, copies_frames, latents, levels, window_mask, qkv, out_w, *outs):
     scratch = outs[-1]
     copies, packed, first = outs[-4:-1]
     chunks = outs[:-4]
@@ -238,8 +239,10 @@
         scratch[h] = jnp.concatenate(
             [qkv[part, :, start : start + head_dim] for part in range(3)], axis=1
         )
+    group = out_w.shape[1] // 2
+    half = jnp.where(scene == 0, out_w[:, :group], out_w[:, group:])
     for k, chunk in enumerate(chunks):
-        chunk[...] = scratch[scene * len(chunks) + (q ^ k)]
+        chunk[...] = jnp.concatenate([half, scratch[scene * len(chunks) + (q ^ k)]], axis=1)
     frames, values, tokens = latents.shape
     span = window_mask.shape[1]
     shares = []
@@ -364,7 +367,8 @@
         for side in range(2):
             owner = core if side == 0 else 1 - core
             first = pl.multiple_of(((q_at ^ k) * 2 + owner) * part_rows, 16)
-            whole[pl.ds(first, part_rows), :] = pieces[side * queues + k][...]
+            piece = pieces[side * queues + k]
+            whole[pl.ds(first, part_rows), :] = piece[:, piece.shape[1] - 3 * head_dim :]
     folded = jnp.dot(lhs[...], whole[...], preferred_element_type=F32)
     high, low = split_terms(folded, 2)
     gains = split_terms(gain_q[...] * gain_k[...] * head_dim ** (-0.5), 3)
@@ -421,61 +425,75 @@
                 out[at] = jnp.concatenate(parts, axis=1).astype(BF16)
 
 
+def hold_kernel(*refs):
+    refs[-1][...] = jnp.zeros(refs[-1].shape, F32)
+
+
 def finish_kernel(half, values, queues, *refs):
-    count = 16
-    sources, mine, send, held = refs[:count], refs[count], refs[count + 1], refs[count + 2 : -5]
-    scratch, mixed, emb, gate, sems = refs[-5:]
-    copies = []
-    for i in range(count):
-        source = sources[i].at[2] if i == 3 else sources[i]
-        copies.append(pltpu.make_async_copy(source, held[i], sems.at[i]))
-    for copy in copies:
-        copy.start()
-    for copy in copies[:7]:
-        copy.wait()
-    packed, following, cond, gates, embed, final_gain, final_w, attended = held[:8]
-    parts = held[8:]
+    near = [refs[:queues], refs[queues : 2 * queues]]
+    away = [refs[2 * queues : 2 * queues + 3], refs[2 * queues + 3 : 2 * queues + 6]]
+    (
+        attended,
+        packed,
+        following,
+        cond,
+        level_mod,
+        embed,
+        final_gain,
+        final_w,
+        _,
+        mine,
+        send,
+        scratch,
+        mixed,
+    ) = refs[2 * queues + 6 :]
     scene, q_at, tok, core = (place_of(a) for a in ("scene", "queue", "tok", "cfg"))
-
-    levels_all, width = gates.shape
+    group = away[0][0].shape[1] // queues
+    columns = away[0][0].shape[0]
+    total = None
+    for t in range(2):
+        made = None
+        for y in range(2):
+            if t == y == 0:
+                pieces = [near[c][k][:, :group] for c in range(2) for k in range(queues)]
+            else:
+                pieces = [
+                    away[c][2 * y + t - 1][:, k * group : (k + 1) * group]
+                    for c in range(2)
+                    for k in range(queues)
+                ]
+            first = ((tok ^ t) * 2 + (scene ^ y)) * group
+            rows = attended[pl.ds(pl.multiple_of(first, 16), group), :]
+            term = jnp.dot(jnp.concatenate(pieces, axis=0), rows, preferred_element_type=F32)
+            made = term if made is None else made + term
+        made = made.astype(BF16).astype(F32)
+        total = made if total is None else total + made
+    for c in range(2):
+        for k in range(queues):
+            first = ((q_at ^ k) * 2 + (core ^ c)) * columns
+            at = (c * queues + k) * columns
+            mixed[pl.ds(pl.multiple_of(first, 8), columns), :] = total[at : at + columns]
+
+    levels_all, width = level_mod.shape[1:]
     info = jnp.concatenate([packed[...], following[...]], axis=1)
     lanes = info.shape[1]
     vec = info[:values].astype(BF16)
     ones = jnp.ones((16, lanes), BF16)
     zero = jnp.zeros((13, width), BF16)
     weights = jnp.concatenate([embed[...]] + split_terms(cond[...], 3) + [zero], axis=0)
-    emb[...] = dot_tn(weights, jnp.concatenate([vec, ones], axis=0))
+    emb = dot_tn(weights, jnp.concatenate([vec, ones], axis=0))
     level = info[values : values + 1]
     one_hot = (lax.broadcasted_iota(jnp.int32, (levels_all, lanes), 0).astype(F32) == level).astype(
         F32
     ).astype(BF16)
-    gate_terms = jnp.concatenate(split_terms(gates[...], 3), axis=0)
-    gate[...] = dot_tn(gate_terms, jnp.concatenate([one_hot] * 3, axis=0))
-
-    group = parts[0].shape[1]
-    columns = parts[0].shape[0] // queues
-    copies[7].wait()
-    rows = [attended[pl.ds(pl.multiple_of(at * group, 16), group), :] for at in (tok, 1 - tok)]
-    for n in range(4):
-        owner = core if n // 2 == 0 else 1 - core
-        plane = scene if n % 2 == 0 else 1 - scene
-        total = None
-        for t in range(2):
-            copies[8 + 2 * n + t].wait()
-            made = jnp.dot(parts[2 * n + t][...], rows[t], preferred_element_type=F32)
-            made = made.astype(BF16).astype(F32)
-            total = made if total is None else total + made
-        for k in range(queues):
-            first = (((q_at ^ k) * 2 + owner) * 2 + plane) * columns
-            mixed[pl.ds(pl.multiple_of(first, 8), columns), :] = total[
-                k * columns : (k + 1) * columns
-            ]
-    summed = emb[...] + gate[...] * mixed[...]
+    gate_terms = jnp.concatenate(split_terms(level_mod[2], 3), axis=0)
+    gate = dot_tn(gate_terms, jnp.concatenate([one_hot] * 3, axis=0))
+    gain_terms = jnp.concatenate(split_terms(final_gain[...], 3) + [zero], axis=0)
+    gain = dot_tn(gain_terms, ones)
+    summed = emb + gate * mixed[...]
     center = jnp.mean(summed, axis=0, keepdims=True)
     deviate = summed - center
     spread = jnp.mean(deviate * deviate, axis=0, keepdims=True)
-    gain_terms = jnp.concatenate(split_terms(final_gain[...], 3) + [zero], axis=0)
-    gain = dot_tn(gain_terms, ones)
     final = (deviate * lax.rsqrt(spread + EPS_NORM) * gain).astype(BF16)
     scratch[...] = jnp.dot(final_w[...], final, preferred_element_type=F32)
     own = pl.multiple_of(core * half, half)
@@ -551,7 +569,8 @@
     per_core = frames // 2
     mods = jnp.transpose(level_mod, (1, 0, 2))
 
-    chunk = jax.ShapeDtypeStruct((local_rows, 3 * head_dim), BF16)
+    group = out_weight.shape[0] // scenes
+    chunk = jax.ShapeDtypeStruct((local_rows, group + 3 * head_dim), BF16)
     *chunks, copies, packed, first = kernel_call(
         functools.partial(pack_kernel, head_dim, per_core),
         [chunk] * queues
@@ -560,10 +579,11 @@
             jax.ShapeDtypeStruct((own_rows, frames * tokens), F32),
             jax.ShapeDtypeStruct((own_rows, tokens), F32),
         ],
-        "vvvv",
+        "vvvvv",
         [pltpu.VMEM((local_heads, local_rows, 3 * head_dim), BF16)],
         vmem=WHOLE_VMEM,
-    )(latents, levels[None], window_mask, jnp.transpose(qkv_weight, (1, 0, 2)))
+        bytes_accessed=8_000_000,
+    )(latents, levels[None], window_mask, jnp.transpose(qkv_weight, (1, 0, 2)), out_weight.T)
 
     near = [chunks[0]] + [swapped(chunks[k], "queue", k) for k in range(1, queues)]
     far = [swapped(piece, "cfg", 1) for piece in near]
@@ -572,20 +592,17 @@
     cond_far = swapped(cond_embed, "scene", 1)
     following = lax.ppermute(first, "queue", [(i + 1, i) for i in range(queues - 1)])
 
-    columns = out_weight.shape[1] // scenes
-    out_half = lax.dynamic_slice_in_dim(
-        out_weight.T, lax.axis_index("scene") * columns, columns, 0
-    )
-    part = jnp.concatenate(
-        [out_half] + [swapped(out_half, "queue", k) for k in range(1, queues)], axis=0
-    )
-    parts = [
-        part,
+    part = jnp.concatenate([piece[:, :group] for piece in near], axis=1)
+    away = [
         swapped(part, "tok", 1),
         swapped(part, "scene", 1),
         swapped(part, ("scene", "tok"), 3),
     ]
-    parts = parts + [swapped(piece, "cfg", 1) for piece in parts]
+    token = kernel_call(
+        hold_kernel, jax.ShapeDtypeStruct((8, LANES), F32), "aaa", bytes_accessed=HOLD_BYTES
+    )(*away)
+    *away, token = lax.optimization_barrier((*away, token))
+    away_far = [swapped(piece, "cfg", 1) for piece in away]
 
     lhs, xin, rstd, masks = kernel_call(
         functools.partial(prepare_kernel, frames, values, span),
@@ -598,7 +615,7 @@
         "vvvvvv",
         bytes_accessed=8_000_000,
     )(shares, other_shares, cond_embed, cond_far, mods, embed_weight)
-    lhs, part = lax.optimization_barrier((lhs, part))
+    lhs, part, following = lax.optimization_barrier((lhs, part, following))
     attended = kernel_call(
         functools.partial(attend_kernel, frames, tokens, queues),
         jax.ShapeDtypeStruct((chips, head_dim, row_lanes), BF16),
@@ -617,8 +634,18 @@
 
     half = values // 2
     half_shape = jax.ShapeDtypeStruct((half, row_lanes), F32)
-    wide = pltpu.VMEM((width, row_lanes), F32)
-    operands = (
+    mine, send = kernel_call(
+        functools.partial(finish_kernel, half, values, queues),
+        [half_shape, half_shape],
+        "v" * (2 * queues + 15),
+        [pltpu.VMEM((values, row_lanes), F32), pltpu.VMEM((width, row_lanes), F32)],
+        bytes_accessed=8_000_000,
+    )(
+        *near,
+        *far,
+        *away,
+        *away_far,
+        received,
         packed,
         following,
         cond_embed,
@@ -626,23 +653,8 @@
         embed_weight,
         final_gain[None],
         final_weight.T,
-        received,
-        *parts,
-    )
-    places = [
-        pltpu.VMEM(a.shape[1:] if i == 3 else a.shape, a.dtype) for i, a in enumerate(operands)
-    ]
-    mine, send = kernel_call(
-        functools.partial(finish_kernel, half, values, queues),
-        [half_shape, half_shape],
-        "a" * len(operands),
-        places
-        + [pltpu.VMEM((values, row_lanes), F32)]
-        + [wide] * 3
-        + [pltpu.SemaphoreType.DMA((len(operands),))],
-        vmem=WHOLE_VMEM,
-        bytes_accessed=8_000_000,
-    )(*operands)
+        token,
+    )
     partner = swapped(send, "cfg", 1)
     shape = jax.ShapeDtypeStruct((frames, half, tokens), F32)
     return kernel_call(

time: 96.8 us -> 83.7 us (0.86)
  waiting for transfers between devices: 36.4 us -> 31.8 us
  local copies, waits for them, and re-layouts: 8.99 us -> 5.39 us
  Pallas kernels: 18.8 us -> 15.6 us
  starting transfers between devices: 30.4 us -> 29 us
    unnamed x46 -> x30, local copies, waits for them, and re-layouts: 8.38 us -> 3.46 us
    pallas_call x1, Pallas kernels: 6.19 us -> 2.5 us  [on_device_heads(): kernel_call(functools.partial(finish_kernel, half, values, queues), [half...]
    ppermute x1, waiting for transfers between devices: 3.68 us -> 0.28 us  [on_device_heads(): lax.ppermute(first, 'queue', [(i + 1, i) for i in range(queues - 1)])]
    ppermute x20 -> x16, starting transfers between devices: 15.5 us -> 12.4 us  [swapped(): return lax.ppermute(value, axis, [(i, i ^ mask) for i in range(count)])]
    all_to_all x1, starting transfers between devices: 5.35 us -> 8.16 us  [on_device_heads(): received = lax.all_to_all(attended, ('tok', 'scene', 'queue'), 0, 0)]
    ppermute x20 -> x16, waiting for transfers between devices: 32.7 us -> 30.4 us  [swapped(): return lax.ppermute(value, axis, [(i, i ^ mask) for i in range(count)])]
    all_to_all x1, starting transfers between devices: 8.31 us -> 7.08 us  [on_device_heads(): shares = lax.all_to_all(copies, ('scene', 'queue', 'tok'), 0, 0)]
    all_to_all x1, waiting for transfers between devices: 0.01 us -> 1.13 us  [on_device_heads(): shares = lax.all_to_all(copies, ('scene', 'queue', 'tok'), 0, 0)]
  transfers between devices with their start and end apart: 23 -> 19, of which waited for: 7 -> 10; matrix products, arithmetic and copies ran while one was open for 1% -> 2% of each run, Pallas kernels for 2% -> 3%
where the time goes in v5:
time: 83.7 us; the launch traced here: 83.3 us
  waiting for transfers between devices  31.8 us (38%)
  starting transfers between devices  29 us (35%)
  Pallas kernels  15.6 us (19%)
  local copies, waits for them, and re-layouts  5.39 us (6%)
  between operations  1.51 us (2%)
    ppermute x16, waiting for transfers between devices, swapped(): return lax.ppermute(value, axis, [(i, i ^ mask) for i in range(count)])  30.4 us
    ppermute x16, starting transfers between devices, swapped(): return lax.ppermute(value, axis, [(i, i ^ mask) for i in range(count)])  12.4 us
    all_to_all x1, starting transfers between devices, on_device_heads(): received = lax.all_to_all(attended, ('tok', 'scene', 'queue'), 0, 0)  8.16 us
    all_to_all x1, starting transfers between devices, on_device_heads(): shares = lax.all_to_all(copies, ('scene', 'queue', 'tok'), 0, 0)  7.08 us
    pallas_call x1, Pallas kernels, on_device_heads(): kernel_call(functools.partial(attend_kernel, frames, tokens, queues), jax...  6.84 us
    unnamed x30, local copies, waits for them, and re-layouts  3.46 us
    pallas_call x1, Pallas kernels, on_device_heads(): kernel_call(functools.partial(pack_kernel, head_dim, per_core), [chunk] *...  2.62 us
    pallas_call x1, Pallas kernels, on_device_heads(): kernel_call(functools.partial(finish_kernel, half, values, queues), [half...  2.5 us
  transfers between devices with their start and end apart: 19, of which 10 were waited for; matrix products, arithmetic and copies ran while one was open for 2% of the time, Pallas kernels for 3%

profile of v5, /device:TPU:0, one launch (start us, length us, event | category | flops | bytes accessed | tf_op | source)
XLA Modules:
  0.0 83.3 jit_solution(14893899013309405856)
XLA Ops:
  0.7 2.6 %shard_map.158 = (bf16[144,504]{1,0:T(8,128)(2,1)}, bf16[144,504]{1,0:T(8,128)(2,1)}, bf16[144,504]{1,0:T(8,128)(2,1)}, bf16[144,504]{1,0:T(8,128)(2,1)}, bf16[1...) custom-call(f32[4,16,48]{2,1,0:T(8,128)} %latents.1, s32[1,4]{1,0:T(1,128)} %bitcast.16, ...), custom_call_target="tpu_custom_call" | custom-call | flops 1000000 | bytes 8000000 | tf_op jit(solution)/shard_map/pallas_call | solution.py:574
  3.3 3.0 %collective-permute-start = (bf16[144,504]{1,0:T(8,128)(2,1)}, bf16[144,504]{1,0:T(8,128)(2,1)S(1)}, u32[]{:S(2)}, u32[]{:S(2)}) collective-permute-start(bf16[144,504]{1,0:T(8,128)(2,1)} %get-tuple-element.22), channel_id=1, source_target_pairs={{0,4},{4,0},{8,12},{12,8},{1,5},{5,1},{9,13},{13,9},{2,6},{6,2},{1... | collective-permute-start | bytes 435464 | tf_op jit(solution)/shard_map/ppermute | solution.py:534
  6.3 2.6 %collective-permute-start.1 = (bf16[144,504]{1,0:T(8,128)(2,1)}, bf16[144,504]{1,0:T(8,128)(2,1)S(1)}, u32[]{:S(2)}, u32[]{:S(2)}) collective-permute-start(bf16[144,504]{1,0:T(8,128)(2,1)} %get-tuple-element.23), channel_id=1, source_target_pairs={{0,8},{4,12},{8,0},{12,4},{1,9},{5,13},{9,1},{13,5},{2,10},{6,14},... | collective-permute-start | bytes 435464 | tf_op jit(solution)/shard_map/ppermute | solution.py:534
  8.9 7.1 %all-to-all-start = ((bf16[16,32,96]{2,1,0:T(8,128)(2,1)}), bf16[16,32,96]{2,1,0:T(8,128)(2,1)S(1)}, u32[]{:S(2)}, u32[]{:S(2)}) async-start(bf16[16,32,96]{2,1,0:T(8,128)(2,1)} %get-tuple-element.28), calls=%async_computation | async-start | bytes 262144 | tf_op jit(solution)/shard_map/all_to_all | solution.py:590
  16.1 0.5 collective-permute-start.4
  16.6 4.6 %collective-permute-done.1.refs_2_ = bf16[144,504]{1,0:T(8,128)(2,1)S(1)} collective-permute-done((bf16[144,504]{1,0:T(8,128)(2,1)}, bf16[144,504]{1,0:T(8,128)(2,1)S(1)}, u32[]{:S(2)}, u32[]{:S(2)}) %collective-permute-start.1) | collective-permute-done | bytes 145184 | tf_op jit(solution)/shard_map/ppermute | solution.py:534
  21.3 0.5 collective-permute-start.6
  21.8 1.5 %collective-permute-start.14 = (f32[1,1152]{1,0:T(1,128)}, f32[1,1152]{1,0:T(1,128)S(1)}, u32[]{:S(2)}, u32[]{:S(2)}) collective-permute-start(f32[1,1152]{1,0:T(1,128)} %refs_17_.1), channel_id=1, source_target_pairs={{0,16},{16,0},{1,17},{17,1},{2,18},{18,2},{3,19},{19,3},{4,20},{20... | collective-permute-start | bytes 13832 | tf_op jit(solution)/shard_map/ppermute | solution.py:534
  23.3 2.3 %collective-permute-done.14.cond_far = f32[1,1152]{1,0:T(1,128)S(1)} collective-permute-done((f32[1,1152]{1,0:T(1,128)}, f32[1,1152]{1,0:T(1,128)S(1)}, u32[]{:S(2)}, u32[]{:S(2)}) %collective-permute-start.14) | collective-permute-done | bytes 4640 | tf_op jit(solution)/shard_map/ppermute | solution.py:534
  25.6 1.1 %all-to-all-done.mine = bf16[16,32,96]{2,1,0:T(8,128)(2,1)S(1)} async-done(((bf16[16,32,96]{2,1,0:T(8,128)(2,1)}), bf16[16,32,96]{2,1,0:T(8,128)(2,1)S(1)}, u32[]{:S(2)}, u32[]{:S(2)}) %all-to-all-start) | async-done | bytes 98336 | tf_op jit(solution)/shard_map/all_to_all | solution.py:590
  26.7 1.3 %collective-permute-done.13.other = bf16[16,32,96]{2,1,0:T(8,128)(2,1)S(1)} collective-permute-done((bf16[16,32,96]{2,1,0:T(8,128)(2,1)S(1)}, bf16[16,32,96]{2,1,0:T(8,128)(2,1)S(1)}, u32[]{:S(2)}, u32[]{:S(2)}) %collective-permute-start.13) | collective-permute-done | bytes 98336 | tf_op jit(solution)/shard_map/ppermute | solution.py:534
  28.1 1.3 %collective-permute-start.15 = (f32[24,48]{1,0:T(8,128)}, f32[24,48]{1,0:T(8,128)S(1)}, u32[]{:S(2)}, u32[]{:S(2)}) collective-permute-start(f32[24,48]{1,0:T(8,128)} %get-tuple-element.30), channel_id=1, source_target_pairs={{4,0},{8,4},{12,8},{5,1},{9,5},{13,9},{6,2},{10,6},{14,10},{7,3},{... | collective-permute-start | bytes 13832 | tf_op jit(solution)/shard_map/ppermute | solution.py:593
  29.4 0.9 %slice.12 = bf16[144,288]{1,0:T(8,128)(2,1)S(1)} slice(bf16[144,504]{1,0:T(8,128)(2,1)} %get-tuple-element.21.refs_0_), slice={[0:144], [0:288]} | slice | bytes 165888 | tf_op jit(solution)/shard_map/slice | solution.py:595
  30.3 1.0 %concatenate.3 = bf16[144,1152]{1,0:T(8,128)(2,1)} concatenate(bf16[144,288]{1,0:T(8,128)(2,1)S(1)} %slice.12, bf16[144,288]{1,0:T(8,128)(2,1)S(1)} %slice.16, bf16[144,288]{1,0:T(8,128)(2,1)S(1)} %slice.17, bf16[144,288]{1,0:T(8,128)(2,1)S(1)} %slice.18), dimensions={1} | concatenate | bytes 663552 | tf_op jit(solution)/shard_map/concatenate | solution.py:595
  31.3 2.3 %shard_map.160 = (bf16[1024,1152]{1,0:T(8,128)(2,1)S(1)}, bf16[2,16,32,128]{3,2,1,0:T(8,128)(2,1)S(1)}, f32[16,1,256]{2,1,0:T(1,128)S(1)}, f32[2,16,16,128]{3,2,1,0:T(8,128)S(1)}) custom-call(bf16[16,32,96]{2,1,0:T(8,128)(2,1)S(1)} %all-to-all-done.mine, bf16[16,32,96]{2,1,0:T(8,128)(2,1)S(1)} %collective-permute-done.13.other, f32[1,1152]{1,0:T(1,128)S(1)} %copy-done.9, ...), custom_call_target="tpu_custom_call" | custom-call | flops 1000000 | bytes 8000000 | tf_op jit(solution)/shard_map/pallas_call | solution.py:607
  33.6 0.3 collective-permute-done.15.refs_16_.following
  34.0 6.8 %shard_map.161 = bf16[16,72,240]{2,1,0:T(8,128)(2,1)} custom-call(bf16[144,504]{1,0:T(8,128)(2,1)S(1)} %copy-done, bf16[144,504]{1,0:T(8,128)(2,1)S(1)} %collective-permute-done.refs_1_, bf16[144,504]{1,0:T(8,128)(2,1)S(1)} %collective-permute-done.1.refs_2_, bf16[144,504]{1,0:T(8,128)(2,1)S(1)} %collective-permute-done.2.refs_3_, ...), custom_call_target="tpu_custom_call" | custom-call | flops 1000000 | bytes 24000000 | tf_op jit(solution)/shard_map/pallas_call | solution.py:619
  40.8 8.2 %all-to-all-start.1 = ((bf16[16,72,240]{2,1,0:T(8,128)(2,1)}), bf16[16,72,240]{2,1,0:T(8,128)(2,1)S(1)}, u32[]{:S(2)}, u32[]{:S(2)}) async-start(bf16[16,72,240]{2,1,0:T(8,128)(2,1)} %shard_map.161), calls=%async_computation.1 | async-start | bytes 1179648 | tf_op jit(solution)/shard_map/all_to_all | solution.py:632
  49.0 2.0 %collective-permute-start.7 = (bf16[144,1152]{1,0:T(8,128)(2,1)}, bf16[144,1152]{1,0:T(8,128)(2,1)S(1)}, u32[]{:S(2)}, u32[]{:S(2)}) collective-permute-start(bf16[144,1152]{1,0:T(8,128)(2,1)} %concatenate.3), channel_id=1, source_target_pairs={{0,2},{2,0},{1,3},{3,1},{4,6},{6,4},{5,7},{7,5},{8,10},{10,8},{9,1... | collective-permute-start | bytes 995336 | tf_op jit(solution)/shard_map/ppermute | solution.py:534
  51.0 1.5 %collective-permute-start.8 = (bf16[144,1152]{1,0:T(8,128)(2,1)}, bf16[144,1152]{1,0:T(8,128)(2,1)S(1)}, u32[]{:S(2)}, u32[]{:S(2)}) collective-permute-start(bf16[144,1152]{1,0:T(8,128)(2,1)} %concatenate.3), channel_id=1, source_target_pairs={{0,16},{16,0},{1,17},{17,1},{2,18},{18,2},{3,19},{19,3},{4,20},{20... | collective-permute-start | bytes 995336 | tf_op jit(solution)/shard_map/ppermute | solution.py:534
  52.6 13.6 %collective-permute-done.7.refs_0_.refs_8_ = bf16[144,1152]{1,0:T(8,128)(2,1)S(1)} collective-permute-done((bf16[144,1152]{1,0:T(8,128)(2,1)}, bf16[144,1152]{1,0:T(8,128)(2,1)S(1)}, u32[]{:S(2)}, u32[]{:S(2)}) %collective-permute-start.7) | collective-permute-done | bytes 331808 | tf_op jit(solution)/shard_map/ppermute | solution.py:534
  66.1 6.6 %collective-permute-done.9.refs_2_.refs_10_ = bf16[144,1152]{1,0:T(8,128)(2,1)S(1)} collective-permute-done((bf16[144,1152]{1,0:T(8,128)(2,1)}, bf16[144,1152]{1,0:T(8,128)(2,1)S(1)}, u32[]{:S(2)}, u32[]{:S(2)}) %collective-permute-start.9) | collective-permute-done | bytes 331808 | tf_op jit(solution)/shard_map/ppermute | solution.py:534
  72.7 0.5 collective-permute-start.11
  73.3 1.1 %collective-permute-done.10.refs_11_ = bf16[144,1152]{1,0:T(8,128)(2,1)S(1)} collective-permute-done((bf16[144,1152]{1,0:T(8,128)(2,1)S(1)}, bf16[144,1152]{1,0:T(8,128)(2,1)S(1)}, u32[]{:S(2)}, u32[]{:S(2)}) %collective-permute-start.10) | collective-permute-done | bytes 331808 | tf_op jit(solution)/shard_map/ppermute | solution.py:534
  74.4 0.5 collective-permute-done.11.refs_12_
  74.8 0.7 copy-done.2
  75.6 0.7 copy-done.4
  76.3 1.0 %copy-done.3 = bf16[144,1152]{1,0:T(8,128)(2,1)S(1)} copy-done((bf16[144,1152]{1,0:T(8,128)(2,1)S(1)}, bf16[144,1152]{1,0:T(8,128)(2,1)}, u32[]{:S(2)}) %copy-start.3) | copy-done | bytes 331800
  77.3 1.0 %copy-done.5 = bf16[144,1152]{1,0:T(8,128)(2,1)S(1)} copy-done((bf16[144,1152]{1,0:T(8,128)(2,1)S(1)}, bf16[144,1152]{1,0:T(8,128)(2,1)}, u32[]{:S(2)}) %copy-start.5) | copy-done | bytes 331800
  78.3 2.5 %shard_map.162 = (f32[8,240]{1,0:T(8,128)S(1)}, f32[8,240]{1,0:T(8,128)S(1)}) custom-call(bf16[144,504]{1,0:T(8,128)(2,1)S(1)} %copy-done, bf16[144,504]{1,0:T(8,128)(2,1)S(1)} %collective-permute-done.refs_1_, bf16[144,504]{1,0:T(8,128)(2,1)S(1)} %collective-permute-done.1.refs_2_, bf16[144,504]{1,0:T(8,128)(2,1)S(1)} %collective-permute-done.2.refs_3_, ...), custom_call_target="tpu_custom_call" | custom-call | flops 1000000 | bytes 8000000 | tf_op jit(solution)/shard_map/pallas_call | solution.py:637
  81.6 0.4 collective-permute-done.16.partner
  82.0 1.3 %shard_map.163 = (f32[4,8,48]{2,1,0:T(8,128)}, f32[4,8,48]{2,1,0:T(8,128)}) custom-call(f32[8,240]{1,0:T(8,128)S(1)} %get-tuple-element.38.mine, f32[8,240]{1,0:T(8,128)S(1)} %collective-permute-done.16.partner, f32[24,192]{1,0:T(8,128)S(1)} %copy-done.7, f32[24,48]{1,0:T(8,128)S(1)} %collective-permute-done.15.refs_16_.following, f32[8,48]{1,0:T(8,128)S(1)} %copy-done.10, ...), custom_call_target="tpu_custom_call" | custom-call | flops 1000000 | bytes 1000000 | tf_op jit(solution)/shard_map/pallas_call | solution.py:660
  (48 shorter events, 0.5 us)
Async XLA Ops:
  0.6 30.7 %copy-start.9 = (f32[1,1152]{1,0:T(1,128)S(1)}, f32[1,1152]{1,0:T(1,128)}, u32[]{:S(2)}) copy-start(f32[1,1152]{1,0:T(1,128)} %refs_17_.1) | copy-start | bytes 13828
  0.6 30.7 %copy-start.1 = (f32[16,3,1152]{2,0,1:T(8,128)S(1)}, f32[16,3,1152]{2,0,1:T(8,128)}, u32[]{:S(2)}) copy-start(f32[16,3,1152]{2,0,1:T(8,128)} %param.20) | copy-start | bytes 663556
  0.7 30.7 %copy-start.6 = (bf16[16,1152]{1,0:T(8,128)(2,1)S(1)}, bf16[16,1152]{1,0:T(8,128)(2,1)}, u32[]{:S(2)}) copy-start(bf16[16,1152]{1,0:T(8,128)(2,1)} %refs_19_.1) | copy-start | bytes 110596
  0.7 33.3 %copy-start.11 = (f32[72]{0:T(128)S(1)}, f32[72]{0:T(128)}, u32[]{:S(2)}) copy-start(f32[72]{0:T(128)} %param.23) | copy-start | bytes 868
  0.7 33.3 %copy-start.12 = (f32[72]{0:T(128)S(1)}, f32[72]{0:T(128)}, u32[]{:S(2)}) copy-start(f32[72]{0:T(128)} %param.24) | copy-start | bytes 868
  3.3 30.6 %copy-start = (bf16[144,504]{1,0:T(8,128)(2,1)S(1)}, bf16[144,504]{1,0:T(8,128)(2,1)}, u32[]{:S(2)}) copy-start(bf16[144,504]{1,0:T(8,128)(2,1)} %get-tuple-element.21.refs_0_) | copy-start | bytes 435460
  3.3 12.8 %collective-permute-start = (bf16[144,504]{1,0:T(8,128)(2,1)}, bf16[144,504]{1,0:T(8,128)(2,1)S(1)}, u32[]{:S(2)}, u32[]{:S(2)}) collective-permute-start(bf16[144,504]{1,0:T(8,128)(2,1)} %get-tuple-element.22), channel_id=1, source_target_pairs={{0,4},{4,0},{8,12},{12,8},{1,5},{5,1},{9,13},{13,9},{2,6},{6,2},{1... | collective-permute-start | bytes 435464 | tf_op jit(solution)/shard_map/ppermute | solution.py:534
  6.3 14.9 %collective-permute-start.1 = (bf16[144,504]{1,0:T(8,128)(2,1)}, bf16[144,504]{1,0:T(8,128)(2,1)S(1)}, u32[]{:S(2)}, u32[]{:S(2)}) collective-permute-start(bf16[144,504]{1,0:T(8,128)(2,1)} %get-tuple-element.23), channel_id=1, source_target_pairs={{0,8},{4,12},{8,0},{12,4},{1,9},{5,13},{9,1},{13,5},{2,10},{6,14},... | collective-permute-start | bytes 435464 | tf_op jit(solution)/shard_map/ppermute | solution.py:534
  8.9 12.3 %collective-permute-start.2 = (bf16[144,504]{1,0:T(8,128)(2,1)}, bf16[144,504]{1,0:T(8,128)(2,1)S(1)}, u32[]{:S(2)}, u32[]{:S(2)}) collective-permute-start(bf16[144,504]{1,0:T(8,128)(2,1)} %get-tuple-element.24), channel_id=1, source_target_pairs={{0,12},{4,8},{8,4},{12,0},{1,13},{5,9},{9,5},{13,1},{2,14},{6,10},... | collective-permute-start | bytes 435464 | tf_op jit(solution)/shard_map/ppermute | solution.py:534
  8.9 17.8 %all-to-all-start = ((bf16[16,32,96]{2,1,0:T(8,128)(2,1)}), bf16[16,32,96]{2,1,0:T(8,128)(2,1)S(1)}, u32[]{:S(2)}, u32[]{:S(2)}) async-start(bf16[16,32,96]{2,1,0:T(8,128)(2,1)} %get-tuple-element.28), calls=%async_computation | async-start | bytes 262144 | tf_op jit(solution)/shard_map/all_to_all | solution.py:590
  16.0 17.9 %collective-permute-start.3 = (bf16[144,504]{1,0:T(8,128)(2,1)}, bf16[144,504]{1,0:T(8,128)(2,1)S(1)}, u32[]{:S(2)}, u32[]{:S(2)}) collective-permute-start(bf16[144,504]{1,0:T(8,128)(2,1)} %get-tuple-element.21.refs_0_), channel_id=1, source_target_pairs={{0,1},{1,0},{2,3},{3,2},{4,5},{5,4},{6,7},{7,6},{8,9},{9,8},{10,11... | collective-permute-start | bytes 435464 | tf_op jit(solution)/shard_map/ppermute | solution.py:534
  16.1 17.8 %collective-permute-start.4 = (bf16[144,504]{1,0:T(8,128)(2,1)S(1)}, bf16[144,504]{1,0:T(8,128)(2,1)S(1)}, u32[]{:S(2)}, u32[]{:S(2)}) collective-permute-start(bf16[144,504]{1,0:T(8,128)(2,1)S(1)} %collective-permute-done.refs_1_), channel_id=1, source_target_pairs={{0,1},{1,0},{2,3},{3,2},{4,5},{5,4},{6,7},{7,6},{8,9},{9,8},{10,11... | collective-permute-start | bytes 435464 | tf_op jit(solution)/shard_map/ppermute | solution.py:534
  21.2 12.7 %collective-permute-start.5 = (bf16[144,504]{1,0:T(8,128)(2,1)S(1)}, bf16[144,504]{1,0:T(8,128)(2,1)S(1)}, u32[]{:S(2)}, u32[]{:S(2)}) collective-permute-start(bf16[144,504]{1,0:T(8,128)(2,1)S(1)} %collective-permute-done.1.refs_2_), channel_id=1, source_target_pairs={{0,1},{1,0},{2,3},{3,2},{4,5},{5,4},{6,7},{7,6},{8,9},{9,8},{10,11... | collective-permute-start | bytes 435464 | tf_op jit(solution)/shard_map/ppermute | solution.py:534
  21.3 12.7 %collective-permute-start.6 = (bf16[144,504]{1,0:T(8,128)(2,1)S(1)}, bf16[144,504]{1,0:T(8,128)(2,1)S(1)}, u32[]{:S(2)}, u32[]{:S(2)}) collective-permute-start(bf16[144,504]{1,0:T(8,128)(2,1)S(1)} %collective-permute-done.2.refs_3_), channel_id=1, source_target_pairs={{0,1},{1,0},{2,3},{3,2},{4,5},{5,4},{6,7},{7,6},{8,9},{9,8},{10,11... | collective-permute-start | bytes 435464 | tf_op jit(solution)/shard_map/ppermute | solution.py:534
  21.8 3.8 %collective-permute-start.14 = (f32[1,1152]{1,0:T(1,128)}, f32[1,1152]{1,0:T(1,128)S(1)}, u32[]{:S(2)}, u32[]{:S(2)}) collective-permute-start(f32[1,1152]{1,0:T(1,128)} %refs_17_.1), channel_id=1, source_target_pairs={{0,16},{16,0},{1,17},{17,1},{2,18},{18,2},{3,19},{19,3},{4,20},{20... | collective-permute-start | bytes 13832 | tf_op jit(solution)/shard_map/ppermute | solution.py:534
  26.7 1.3 %collective-permute-start.13 = (bf16[16,32,96]{2,1,0:T(8,128)(2,1)S(1)}, bf16[16,32,96]{2,1,0:T(8,128)(2,1)S(1)}, u32[]{:S(2)}, u32[]{:S(2)}) collective-permute-start(bf16[16,32,96]{2,1,0:T(8,128)(2,1)S(1)} %all-to-all-done.mine), channel_id=1, source_target_pairs={{0,1},{1,0},{2,3},{3,2},{4,5},{5,4},{6,7},{7,6},{8,9},{9,8},{10,11... | collective-permute-start | bytes 294920 | tf_op jit(solution)/shard_map/ppermute | solution.py:534
  28.1 5.8 %collective-permute-start.15 = (f32[24,48]{1,0:T(8,128)}, f32[24,48]{1,0:T(8,128)S(1)}, u32[]{:S(2)}, u32[]{:S(2)}) collective-permute-start(f32[24,48]{1,0:T(8,128)} %get-tuple-element.30), channel_id=1, source_target_pairs={{4,0},{8,4},{12,8},{5,1},{9,5},{13,9},{6,2},{10,6},{14,10},{7,3},{... | collective-permute-start | bytes 13832 | tf_op jit(solution)/shard_map/ppermute | solution.py:593
  34.0 39.3 %copy-start.14 = (f32[1152]{0:T(1024)S(1)}, f32[1152]{0:T(1024)}, u32[]{:S(2)}) copy-start(f32[1152]{0:T(1024)} %param.26) | copy-start | bytes 13828
  34.0 42.3 %copy-start.7 = (f32[24,192]{1,0:T(8,128)S(1)}, f32[24,192]{1,0:T(8,128)}, u32[]{:S(2)}) copy-start(f32[24,192]{1,0:T(8,128)} %get-tuple-element.35.refs_15_.packed) | copy-start | bytes 55300
  34.0 42.3 %copy-start.8 = (bf16[1152,16]{0,1:T(8,128)(2,1)S(1)}, bf16[1152,16]{0,1:T(8,128)(2,1)}, u32[]{:S(2)}) copy-start(bf16[1152,16]{0,1:T(8,128)(2,1)} %param.27) | copy-start | bytes 110596
  40.8 35.5 %all-to-all-start.1 = ((bf16[16,72,240]{2,1,0:T(8,128)(2,1)}), bf16[16,72,240]{2,1,0:T(8,128)(2,1)S(1)}, u32[]{:S(2)}, u32[]{:S(2)}) async-start(bf16[16,72,240]{2,1,0:T(8,128)(2,1)} %shard_map.161), calls=%async_computation.1 | async-start | bytes 1179648 | tf_op jit(solution)/shard_map/all_to_all | solution.py:632
  49.0 33.0 %copy-start.10 = (f32[8,48]{1,0:T(8,128)S(1)}, f32[8,48]{1,0:T(8,128)}, u32[]{:S(2)}) copy-start(f32[8,48]{1,0:T(8,128)} %noise.1) | copy-start | bytes 4612
  49.0 33.0 %copy-start.13 = (f32[8]{0:T(128)S(1)}, f32[8]{0:T(128)}, u32[]{:S(2)}) copy-start(f32[8]{0:T(128)} %table.1) | copy-start | bytes 100
  49.0 17.1 %collective-permute-start.7 = (bf16[144,1152]{1,0:T(8,128)(2,1)}, bf16[144,1152]{1,0:T(8,128)(2,1)S(1)}, u32[]{:S(2)}, u32[]{:S(2)}) collective-permute-start(bf16[144,1152]{1,0:T(8,128)(2,1)} %concatenate.3), channel_id=1, source_target_pairs={{0,2},{2,0},{1,3},{3,1},{4,6},{6,4},{5,7},{7,5},{8,10},{10,8},{9,1... | collective-permute-start | bytes 995336 | tf_op jit(solution)/shard_map/ppermute | solution.py:534
  51.0 15.1 %collective-permute-start.8 = (bf16[144,1152]{1,0:T(8,128)(2,1)}, bf16[144,1152]{1,0:T(8,128)(2,1)S(1)}, u32[]{:S(2)}, u32[]{:S(2)}) collective-permute-start(bf16[144,1152]{1,0:T(8,128)(2,1)} %concatenate.3), channel_id=1, source_target_pairs={{0,16},{16,0},{1,17},{17,1},{2,18},{18,2},{3,19},{19,3},{4,20},{20... | collective-permute-start | bytes 995336 | tf_op jit(solution)/shard_map/ppermute | solution.py:534
  52.5 20.3 %collective-permute-start.9 = (bf16[144,1152]{1,0:T(8,128)(2,1)}, bf16[144,1152]{1,0:T(8,128)(2,1)S(1)}, u32[]{:S(2)}, u32[]{:S(2)}) collective-permute-start(bf16[144,1152]{1,0:T(8,128)(2,1)} %concatenate.3), channel_id=1, source_target_pairs={{0,18},{2,16},{16,2},{18,0},{1,19},{3,17},{17,3},{19,1},{4,22},{6,... | collective-permute-start | bytes 995336 | tf_op jit(solution)/shard_map/ppermute | solution.py:534
  72.7 1.6 %collective-permute-start.10 = (bf16[144,1152]{1,0:T(8,128)(2,1)S(1)}, bf16[144,1152]{1,0:T(8,128)(2,1)S(1)}, u32[]{:S(2)}, u32[]{:S(2)}) collective-permute-start(bf16[144,1152]{1,0:T(8,128)(2,1)S(1)} %collective-permute-done.7.refs_0_.refs_8_), channel_id=1, source_target_pairs={{0,1},{1,0},{2,3},{3,2},{4,5},{5,4},{6,7},{7,6},{8,9},{9,8},{10,11... | collective-permute-start | bytes 995336 | tf_op jit(solution)/shard_map/ppermute | solution.py:534
  72.7 2.1 %collective-permute-start.11 = (bf16[144,1152]{1,0:T(8,128)(2,1)S(1)}, bf16[144,1152]{1,0:T(8,128)(2,1)S(1)}, u32[]{:S(2)}, u32[]{:S(2)}) collective-permute-start(bf16[144,1152]{1,0:T(8,128)(2,1)S(1)} %collective-permute-done.8.refs_1_.refs_9_), channel_id=1, source_target_pairs={{0,1},{1,0},{2,3},{3,2},{4,5},{5,4},{6,7},{7,6},{8,9},{9,8},{10,11... | collective-permute-start | bytes 995336 | tf_op jit(solution)/shard_map/ppermute | solution.py:534
  73.2 2.3 %collective-permute-start.12 = (bf16[144,1152]{1,0:T(8,128)(2,1)S(1)}, bf16[144,1152]{1,0:T(8,128)(2,1)S(1)}, u32[]{:S(2)}, u32[]{:S(2)}) collective-permute-start(bf16[144,1152]{1,0:T(8,128)(2,1)S(1)} %collective-permute-done.9.refs_2_.refs_10_), channel_id=1, source_target_pairs={{0,1},{1,0},{2,3},{3,2},{4,5},{5,4},{6,7},{7,6},{8,9},{9,8},{10,11... | collective-permute-start | bytes 995336 | tf_op jit(solution)/shard_map/ppermute | solution.py:534
  76.3 1.0 %copy-start.3 = (bf16[144,1152]{1,0:T(8,128)(2,1)S(1)}, bf16[144,1152]{1,0:T(8,128)(2,1)}, u32[]{:S(2)}) copy-start(bf16[144,1152]{1,0:T(8,128)(2,1)} %copy-done.2) | copy-start | bytes 995332
  77.3 1.0 %copy-start.5 = (bf16[144,1152]{1,0:T(8,128)(2,1)S(1)}, bf16[144,1152]{1,0:T(8,128)(2,1)}, u32[]{:S(2)}) copy-start(bf16[144,1152]{1,0:T(8,128)(2,1)} %copy-done.4) | copy-start | bytes 995332
  80.8 1.2 %collective-permute-start.16 = (f32[8,240]{1,0:T(8,128)S(1)}, f32[8,240]{1,0:T(8,128)S(1)}, u32[]{:S(2)}, u32[]{:S(2)}) collective-permute-start(f32[8,240]{1,0:T(8,128)S(1)} %get-tuple-element.39), channel_id=1, source_target_pairs={{0,1},{1,0},{2,3},{3,2},{4,5},{5,4},{6,7},{7,6},{8,9},{9,8},{10,11... | collective-permute-start | bytes 23048 | tf_op jit(solution)/shard_map/ppermute | solution.py:534
  (2 other events, 1.5 us)

commit v6 on v5

--- a/solution.py
+++ b/solution.py
@@ -12,7 +12,7 @@
 LANES = 128
 VMEM_BYTES = 20 * 1024 * 1024
 WHOLE_VMEM = 62 * 1024 * 1024
-HOLD_BYTES = 80_000_000
+HOLD_BYTES = 2_000_000_000
 F32 = jnp.float32
 BF16 = jnp.bfloat16
 
@@ -229,11 +229,11 @@
     return lax.axis_index(axis)
 
 
-def pack_kernel(head_dim, copies_frames, latents, levels, window_mask, qkv, out_w, *outs):
+def pack_kernel(head_dim, copies_frames, latents, levels, window_mask, qkv, out_w, cond, *outs):
     scratch = outs[-1]
     copies, packed, first = outs[-4:-1]
     chunks = outs[:-4]
-    scene, q, core = (place_of(a) for a in ("scene", "queue", "cfg"))
+    scene, q, tok, core = (place_of(a) for a in ("scene", "queue", "tok", "cfg"))
     for h in range(scratch.shape[0]):
         start = h * head_dim
         scratch[h] = jnp.concatenate(
@@ -259,7 +259,23 @@
         own.append(jnp.concatenate([latents[f], fill], axis=0))
     lower = jnp.concatenate(shares[:copies_frames], axis=1)
     upper = jnp.concatenate(shares[copies_frames:], axis=1)
-    share = jnp.where(core == 0, lower, upper).astype(BF16)
+    share = jnp.where(core == 0, lower, upper)
+    spots = lax.axis_size("queue") * lax.axis_size("tok")
+    length = cond.shape[1] // spots
+    piece = jnp.zeros((1, length), F32)
+    for i in range(spots):
+        chosen = q * lax.axis_size("tok") + tok == i
+        piece = jnp.where(chosen, cond[:, i * length : (i + 1) * length], piece)
+    row_id = lax.broadcasted_iota(jnp.int32, share.shape, 0)
+    at_row, step = values + span + 1, share.shape[1]
+    for term in split_terms(piece, 3):
+        for start in range(0, length, step):
+            line = term.astype(F32)[:, start : start + step]
+            fill = jnp.zeros((1, step - line.shape[1]), F32)
+            line = jnp.concatenate([line, fill], axis=1) if fill.shape[1] else line
+            share = jnp.where(row_id == at_row, line, share)
+            at_row += 1
+    share = share.astype(BF16)
     for at in range(copies.shape[0]):
         copies[at] = share
     packed[...] = jnp.concatenate(own, axis=1)
@@ -272,8 +288,6 @@
     span,
     mine,
     other,
-    cond,
-    cond_far,
     level_mod,
     embed,
     lhs,
@@ -290,11 +304,19 @@
     core = place_of("cfg")
     weights = embed[...].astype(F32)
     weights = weights - jnp.mean(weights, axis=1, keepdims=True)
-    here, there = cond[...], cond_far[...]
-    is_first = place_of("scene") == 0
-    conds = jnp.concatenate(
-        [jnp.where(is_first, here, there), jnp.where(is_first, there, here)], axis=0
-    )
+    length, step = width // (queues * toks), mine.shape[2]
+    lines = -(-length // step)
+    conds = []
+    for y in range(scenes):
+        pieces = []
+        for at in range(y * queues * toks, (y + 1) * queues * toks):
+            info = mine[at].astype(F32)
+            first = values + span + 1
+            terms = sum(info[first + i * lines : first + (i + 1) * lines] for i in range(3))
+            for i in range(lines):
+                pieces.append(terms[i : i + 1, : min(step, length - i * step)])
+        conds.append(jnp.concatenate(pieces, axis=1))
+    conds = jnp.concatenate(conds, axis=0)
     conds = conds - jnp.mean(conds, axis=1, keepdims=True)
     basis = jnp.concatenate(
         [weights, conds, jnp.zeros((rows - values - scenes, width), F32)], axis=0
@@ -425,13 +447,17 @@
                 out[at] = jnp.concatenate(parts, axis=1).astype(BF16)
 
 
+def side_kernel(group, *refs):
+    for k, piece in enumerate(refs[:-1]):
+        refs[-1][:, k * group : (k + 1) * group] = piece[:, :group]
+
+
 def hold_kernel(*refs):
     refs[-1][...] = jnp.zeros(refs[-1].shape, F32)
 
 
 def finish_kernel(half, values, queues, *refs):
-    near = [refs[:queues], refs[queues : 2 * queues]]
-    away = [refs[2 * queues : 2 * queues + 3], refs[2 * queues + 3 : 2 * queues + 6]]
+    parts = [refs[:4], refs[4:8]]
     (
         attended,
         packed,
@@ -446,22 +472,19 @@
         send,
         scratch,
         mixed,
-    ) = refs[2 * queues + 6 :]
+    ) = refs[8:]
     scene, q_at, tok, core = (place_of(a) for a in ("scene", "queue", "tok", "cfg"))
-    group = away[0][0].shape[1] // queues
-    columns = away[0][0].shape[0]
+    group = parts[0][0].shape[1] // queues
+    columns = parts[0][0].shape[0]
     total = None
     for t in range(2):
         made = None
         for y in range(2):
-            if t == y == 0:
-                pieces = [near[c][k][:, :group] for c in range(2) for k in range(queues)]
-            else:
-                pieces = [
-                    away[c][2 * y + t - 1][:, k * group : (k + 1) * group]
-                    for c in range(2)
-                    for k in range(queues)
-                ]
+            pieces = [
+                parts[c][2 * y + t][:, k * group : (k + 1) * group]
+                for c in range(2)
+                for k in range(queues)
+            ]
             first = ((tok ^ t) * 2 + (scene ^ y)) * group
             rows = attended[pl.ds(pl.multiple_of(first, 16), group), :]
             term = jnp.dot(jnp.concatenate(pieces, axis=0), rows, preferred_element_type=F32)
@@ -560,13 +583,14 @@
     scenes, queues, toks = (lax.axis_size(a) for a in ("scene", "queue", "tok"))
     chips = scenes * queues * toks
     all_frames = queues * frames
-    rows = -(-max(values + scenes + 2, values + span + 1) // 16) * 16
+    per_core = frames // 2
+    cond_rows = 3 * -(-(width // (queues * toks)) // (per_core * tokens))
+    rows = -(-max(values + scenes + 2, values + span + 1 + cond_rows) // 16) * 16
     own_rows = -(-(values + 1) // 8) * 8
     local_rows = qkv_weight.shape[0]
     local_heads = qkv_weight.shape[2] // head_dim
     lanes = scenes * LANES
     row_lanes = (frames + 1) * tokens
-    per_core = frames // 2
     mods = jnp.transpose(level_mod, (1, 0, 2))
 
     group = out_weight.shape[0] // scenes
@@ -579,29 +603,39 @@
             jax.ShapeDtypeStruct((own_rows, frames * tokens), F32),
             jax.ShapeDtypeStruct((own_rows, tokens), F32),
         ],
-        "vvvvv",
+        "vvvvvv",
         [pltpu.VMEM((local_heads, local_rows, 3 * head_dim), BF16)],
         vmem=WHOLE_VMEM,
         bytes_accessed=8_000_000,
-    )(latents, levels[None], window_mask, jnp.transpose(qkv_weight, (1, 0, 2)), out_weight.T)
+    )(
+        latents,
+        levels[None],
+        window_mask,
+        jnp.transpose(qkv_weight, (1, 0, 2)),
+        out_weight.T,
+        cond_embed,
+    )
 
     near = [chunks[0]] + [swapped(chunks[k], "queue", k) for k in range(1, queues)]
     far = [swapped(piece, "cfg", 1) for piece in near]
     shares = lax.all_to_all(copies, ("scene", "queue", "tok"), 0, 0)
     other_shares = swapped(shares, "cfg", 1)
-    cond_far = swapped(cond_embed, "scene", 1)
     following = lax.ppermute(first, "queue", [(i + 1, i) for i in range(queues - 1)])
 
-    part = jnp.concatenate([piece[:, :group] for piece in near], axis=1)
+    part = kernel_call(
+        functools.partial(side_kernel, group),
+        jax.ShapeDtypeStruct((local_rows, queues * group), BF16),
+        "v" * queues,
+    )(*near)
     away = [
         swapped(part, "tok", 1),
         swapped(part, "scene", 1),
         swapped(part, ("scene", "tok"), 3),
     ]
     token = kernel_call(
-        hold_kernel, jax.ShapeDtypeStruct((8, LANES), F32), "aaa", bytes_accessed=HOLD_BYTES
-    )(*away)
-    *away, token = lax.optimization_barrier((*away, token))
+        hold_kernel, jax.ShapeDtypeStruct((8, LANES), F32), "aaaa", bytes_accessed=HOLD_BYTES
+    )(*away, following)
+    *away, token = lax.optimization_barrier((part, *away, token))
     away_far = [swapped(piece, "cfg", 1) for piece in away]
 
     lhs, xin, rstd, masks = kernel_call(
@@ -612,10 +646,10 @@
             jax.ShapeDtypeStruct((all_frames, 1, lanes), F32),
             jax.ShapeDtypeStruct((scenes, all_frames, rows - values, LANES), F32),
         ],
-        "vvvvvv",
+        "vvvv",
         bytes_accessed=8_000_000,
-    )(shares, other_shares, cond_embed, cond_far, mods, embed_weight)
-    lhs, part, following = lax.optimization_barrier((lhs, part, following))
+    )(shares, other_shares, mods, embed_weight)
+    lhs, part = lax.optimization_barrier((lhs, part))
     attended = kernel_call(
         functools.partial(attend_kernel, frames, tokens, queues),
         jax.ShapeDtypeStruct((chips, head_dim, row_lanes), BF16),
@@ -637,12 +671,10 @@
     mine, send = kernel_call(
         functools.partial(finish_kernel, half, values, queues),
         [half_shape, half_shape],
-        "v" * (2 * queues + 15),
+        "v" * 17,
         [pltpu.VMEM((values, row_lanes), F32), pltpu.VMEM((width, row_lanes), F32)],
         bytes_accessed=8_000_000,
     )(
-        *near,
-        *far,
         *away,
         *away_far,
         received,

time: 83.7 us -> 80.5 us (0.962)
  starting transfers between devices: 29 us -> 23.8 us
  local copies, waits for them, and re-layouts: 5.39 us -> 7.63 us
  waiting for transfers between devices: 31.8 us -> 30.9 us
    ppermute x16, waiting for transfers between devices: 30.4 us -> 21.3 us  [swapped(): return lax.ppermute(value, axis, [(i, i ^ mask) for i in range(count)])]
    ppermute x1, waiting for transfers between devices: 0.28 us -> 4.59 us  [on_device_heads(): lax.ppermute(first, 'queue', [(i + 1, i) for i in range(queues - 1)])]
    all_to_all x1, starting transfers between devices: 8.16 us -> 4.02 us  [on_device_heads(): received = lax.all_to_all(attended, ('tok', 'scene', 'queue'), 0, 0)]
    all_to_all x1, waiting for transfers between devices: 1.13 us -> 4.96 us  [on_device_heads(): shares = lax.all_to_all(copies, ('scene', 'queue', 'tok'), 0, 0)]
    unnamed x30 -> x32, local copies, waits for them, and re-layouts: 3.46 us -> 6.93 us
    ppermute x16, starting transfers between devices: 12.4 us -> 11.4 us  [swapped(): return lax.ppermute(value, axis, [(i, i ^ mask) for i in range(count)])]
    concatenate x1 -> x0, local copies, waits for them, and re-layouts: 0.97 us -> none  [on_device_heads(): part = jnp.concatenate([piece[:, :group] for piece in near], axis=1)]
    slice x4 -> x0, local copies, waits for them, and re-layouts: 0.95 us -> none  [on_device_heads(): part = jnp.concatenate([piece[:, :group] for piece in near], axis=1)]
  transfers between devices with their start and end apart: 19 -> 19, of which waited for: 10 -> 10; matrix products, arithmetic and copies ran while one was open for 2% -> 1% of each run, Pallas kernels for 3% -> 3%
where the time goes in v6:
time: 80.5 us; the launch traced here: 79.9 us
  waiting for transfers between devices  30.9 us (38%)
  starting transfers between devices  23.8 us (30%)
  Pallas kernels  16.1 us (20%)
  local copies, waits for them, and re-layouts  7.63 us (9%)
  between operations  1.47 us (2%)
    ppermute x16, waiting for transfers between devices, swapped(): return lax.ppermute(value, axis, [(i, i ^ mask) for i in range(count)])  21.3 us
    ppermute x16, starting transfers between devices, swapped(): return lax.ppermute(value, axis, [(i, i ^ mask) for i in range(count)])  11.4 us
    all_to_all x1, starting transfers between devices, on_device_heads(): shares = lax.all_to_all(copies, ('scene', 'queue', 'tok'), 0, 0)  7.08 us
    unnamed x32, local copies, waits for them, and re-layouts  6.93 us
    pallas_call x1, Pallas kernels, on_device_heads(): kernel_call(functools.partial(attend_kernel, frames, tokens, queues), jax...  6.81 us
    all_to_all x1, waiting for transfers between devices, on_device_heads(): shares = lax.all_to_all(copies, ('scene', 'queue', 'tok'), 0, 0)  4.96 us
    ppermute x1, waiting for transfers between devices, on_device_heads(): lax.ppermute(first, 'queue', [(i + 1, i) for i in range(queues - 1)])  4.59 us
    all_to_all x1, starting transfers between devices, on_device_heads(): received = lax.all_to_all(attended, ('tok', 'scene', 'queue'), 0, 0)  4.02 us
  transfers between devices with their start and end apart: 19, of which 10 were waited for; matrix products, arithmetic and copies ran while one was open for 1% of the time, Pallas kernels for 3%

profile of v6, /device:TPU:0, one launch (start us, length us, event | category | flops | bytes accessed | tf_op | source)
XLA Modules:
  0.0 79.9 jit_solution(11903609172441669333)
XLA Ops:
  0.7 2.9 %shard_map.158 = (bf16[144,504]{1,0:T(8,128)(2,1)}, bf16[144,504]{1,0:T(8,128)(2,1)}, bf16[144,504]{1,0:T(8,128)(2,1)}, bf16[144,504]{1,0:T(8,128)(2,1)}, bf16[1...) custom-call(f32[4,16,48]{2,1,0:T(8,128)} %latents.1, s32[1,4]{1,0:T(1,128)} %bitcast.16, ...), custom_call_target="tpu_custom_call" | custom-call | flops 1000000 | bytes 8000000 | tf_op jit(solution)/shard_map/pallas_call | solution.py:598
  3.6 3.0 %collective-permute-start = (bf16[144,504]{1,0:T(8,128)(2,1)}, bf16[144,504]{1,0:T(8,128)(2,1)S(1)}, u32[]{:S(2)}, u32[]{:S(2)}) collective-permute-start(bf16[144,504]{1,0:T(8,128)(2,1)} %get-tuple-element.22), channel_id=1, source_target_pairs={{0,4},{4,0},{8,12},{12,8},{1,5},{5,1},{9,13},{13,9},{2,6},{6,2},{1... | collective-permute-start | bytes 435464 | tf_op jit(solution)/shard_map/ppermute | solution.py:557
  6.6 2.6 %collective-permute-start.1 = (bf16[144,504]{1,0:T(8,128)(2,1)}, bf16[144,504]{1,0:T(8,128)(2,1)S(1)}, u32[]{:S(2)}, u32[]{:S(2)}) collective-permute-start(bf16[144,504]{1,0:T(8,128)(2,1)} %get-tuple-element.23), channel_id=1, source_target_pairs={{0,8},{4,12},{8,0},{12,4},{1,9},{5,13},{9,1},{13,5},{2,10},{6,14},... | collective-permute-start | bytes 435464 | tf_op jit(solution)/shard_map/ppermute | solution.py:557
  9.2 7.1 %all-to-all-start = ((bf16[16,32,96]{2,1,0:T(8,128)(2,1)}), bf16[16,32,96]{2,1,0:T(8,128)(2,1)S(1)}, u32[]{:S(2)}, u32[]{:S(2)}) async-start(bf16[16,32,96]{2,1,0:T(8,128)(2,1)} %get-tuple-element.30), calls=%async_computation | async-start | bytes 262144 | tf_op jit(solution)/shard_map/all_to_all | solution.py:621
  16.4 0.5 collective-permute-start.12
  16.8 4.6 %collective-permute-done.1.refs_2_ = bf16[144,504]{1,0:T(8,128)(2,1)S(1)} collective-permute-done((bf16[144,504]{1,0:T(8,128)(2,1)}, bf16[144,504]{1,0:T(8,128)(2,1)S(1)}, u32[]{:S(2)}, u32[]{:S(2)}) %collective-permute-start.1) | collective-permute-done | bytes 145184 | tf_op jit(solution)/shard_map/ppermute | solution.py:557
  21.5 0.5 collective-permute-start.14
  22.0 5.0 %all-to-all-done.mine = bf16[16,32,96]{2,1,0:T(8,128)(2,1)S(1)} async-done(((bf16[16,32,96]{2,1,0:T(8,128)(2,1)}), bf16[16,32,96]{2,1,0:T(8,128)(2,1)S(1)}, u32[]{:S(2)}, u32[]{:S(2)}) %all-to-all-start) | async-done | bytes 98336 | tf_op jit(solution)/shard_map/all_to_all | solution.py:621
  27.0 0.9 %copy-done.2 = bf16[144,504]{1,0:T(8,128)(2,1)S(1)} copy-done((bf16[144,504]{1,0:T(8,128)(2,1)S(1)}, bf16[144,504]{1,0:T(8,128)(2,1)}, u32[]{:S(2)}) %copy-start.2) | copy-done | bytes 145176
  28.3 0.9 %copy-done = f32[16,3,1152]{2,0,1:T(8,128)S(1)} copy-done((f32[16,3,1152]{2,0,1:T(8,128)S(1)}, f32[16,3,1152]{2,0,1:T(8,128)}, u32[]{:S(2)}) %copy-start) | copy-done | bytes 221208
  29.3 0.8 copy-done.4
  30.0 2.4 %shard_map.161 = (bf16[1024,1152]{1,0:T(8,128)(2,1)S(1)}, bf16[2,16,32,128]{3,2,1,0:T(8,128)(2,1)S(1)}, f32[16,1,256]{2,1,0:T(1,128)S(1)}, f32[2,16,16,128]{3,2,1,0:T(8,128)S(1)}) custom-call(bf16[16,32,96]{2,1,0:T(8,128)(2,1)S(1)} %all-to-all-done.mine, bf16[16,32,96]{2,1,0:T(8,128)(2,1)S(1)} %collective-permute-done.15.other, f32[3,16,1152]{2,1,0:T(8,128)S(1)} %bitcast.9, ...), custom_call_target="tpu_custom_call" | custom-call | flops 1000000 | bytes 8000000 | tf_op jit(solution)/shard_map/pallas_call | solution.py:641
  32.5 0.9 %copy-done.3 = bf16[144,504]{1,0:T(8,128)(2,1)S(1)} copy-done((bf16[144,504]{1,0:T(8,128)(2,1)S(1)}, bf16[144,504]{1,0:T(8,128)(2,1)}, u32[]{:S(2)}) %copy-start.3) | copy-done | bytes 145176
  33.4 6.8 %shard_map.162 = bf16[16,72,240]{2,1,0:T(8,128)(2,1)} custom-call(bf16[144,504]{1,0:T(8,128)(2,1)S(1)} %copy-done.3, bf16[144,504]{1,0:T(8,128)(2,1)S(1)} %collective-permute-done.refs_1_, bf16[144,504]{1,0:T(8,128)(2,1)S(1)} %collective-permute-done.1.refs_2_, bf16[144,504]{1,0:T(8,128)(2,1)S(1)} %collective-permute-done.2.refs_3_, ...), custom_call_target="tpu_custom_call" | custom-call | flops 1000000 | bytes 24000000 | tf_op jit(solution)/shard_map/pallas_call | solution.py:653
  40.2 4.0 %all-to-all-start.1 = ((bf16[16,72,240]{2,1,0:T(8,128)(2,1)}), bf16[16,72,240]{2,1,0:T(8,128)(2,1)S(1)}, u32[]{:S(2)}, u32[]{:S(2)}) async-start(bf16[16,72,240]{2,1,0:T(8,128)(2,1)} %shard_map.162), calls=%async_computation.1 | async-start | bytes 1179648 | tf_op jit(solution)/shard_map/all_to_all | solution.py:666
  44.3 1.9 %collective-permute-start.3 = (bf16[144,1152]{1,0:T(8,128)(2,1)S(1)}, bf16[144,1152]{1,0:T(8,128)(2,1)S(1)}, u32[]{:S(2)}, u32[]{:S(2)}) collective-permute-start(bf16[144,1152]{1,0:T(8,128)(2,1)S(1)} %shard_map.159.refs_0_), channel_id=1, source_target_pairs={{0,2},{2,0},{1,3},{3,1},{4,6},{6,4},{5,7},{7,5},{8,10},{10,8},{9,1... | collective-permute-start | bytes 995336 | tf_op jit(solution)/shard_map/ppermute | solution.py:557
  46.2 1.5 %collective-permute-start.4 = (bf16[144,1152]{1,0:T(8,128)(2,1)S(1)}, bf16[144,1152]{1,0:T(8,128)(2,1)S(1)}, u32[]{:S(2)}, u32[]{:S(2)}) collective-permute-start(bf16[144,1152]{1,0:T(8,128)(2,1)S(1)} %shard_map.159.refs_0_), channel_id=1, source_target_pairs={{0,16},{16,0},{1,17},{17,1},{2,18},{18,2},{3,19},{19,3},{4,20},{20... | collective-permute-start | bytes 995336 | tf_op jit(solution)/shard_map/ppermute | solution.py:557
  47.8 1.3 %collective-permute-start.6 = (f32[24,48]{1,0:T(8,128)S(1)}, f32[24,48]{1,0:T(8,128)S(1)}, u32[]{:S(2)}, u32[]{:S(2)}) collective-permute-start(f32[24,48]{1,0:T(8,128)S(1)} %copy-done.15), channel_id=1, source_target_pairs={{4,0},{8,4},{12,8},{5,1},{9,5},{13,9},{6,2},{10,6},{14,10},{7,3},{... | collective-permute-start | bytes 13832 | tf_op jit(solution)/shard_map/ppermute | solution.py:623
  49.1 4.6 %collective-permute-done.6.refs_3_.refs_10_.following = f32[24,48]{1,0:T(8,128)S(1)} collective-permute-done((f32[24,48]{1,0:T(8,128)S(1)}, f32[24,48]{1,0:T(8,128)S(1)}, u32[]{:S(2)}, u32[]{:S(2)}) %collective-permute-start.6) | collective-permute-done | bytes 4640 | tf_op jit(solution)/shard_map/ppermute | solution.py:623
  53.7 7.7 %collective-permute-done.3.refs_0_.refs_1_ = bf16[144,1152]{1,0:T(8,128)(2,1)S(1)} collective-permute-done((bf16[144,1152]{1,0:T(8,128)(2,1)S(1)}, bf16[144,1152]{1,0:T(8,128)(2,1)S(1)}, u32[]{:S(2)}, u32[]{:S(2)}) %collective-permute-start.3) | collective-permute-done | bytes 331808 | tf_op jit(solution)/shard_map/ppermute | solution.py:557
  61.4 7.0 %collective-permute-done.5.refs_2_.refs_3_ = bf16[144,1152]{1,0:T(8,128)(2,1)S(1)} collective-permute-done((bf16[144,1152]{1,0:T(8,128)(2,1)S(1)}, bf16[144,1152]{1,0:T(8,128)(2,1)S(1)}, u32[]{:S(2)}, u32[]{:S(2)}) %collective-permute-start.5) | collective-permute-done | bytes 331808 | tf_op jit(solution)/shard_map/ppermute | solution.py:557
  68.4 0.6 copy-done.9
  69.0 0.5 collective-permute-start.7
  69.5 0.5 collective-permute-start.9
  70.0 0.7 broadcast_in_dim.15.refs_14_
  71.6 0.5 collective-permute-done.9.refs_6_
  72.1 0.8 copy-done.7
  72.8 0.7 copy-done.10
  73.5 2.5 %shard_map.163 = (f32[8,240]{1,0:T(8,128)S(1)}, f32[8,240]{1,0:T(8,128)S(1)}) custom-call(bf16[144,1152]{1,0:T(8,128)(2,1)S(1)} %shard_map.159.refs_0_, bf16[144,1152]{1,0:T(8,128)(2,1)S(1)} %collective-permute-done.3.refs_0_.refs_1_, bf16[144,1152]{1,0:T(8,128)(2,1)S(1)} %collective-permute-done.4.refs_1_.refs_2_, ...), custom_call_target="tpu_custom_call" | custom-call | flops 1000000 | bytes 8000000 | tf_op jit(solution)/shard_map/pallas_call | solution.py:671
  77.2 0.7 copy-done.11
  77.9 0.7 copy-done.14
  78.6 1.3 %shard_map.164 = (f32[4,8,48]{2,1,0:T(8,128)}, f32[4,8,48]{2,1,0:T(8,128)}) custom-call(f32[8,240]{1,0:T(8,128)S(1)} %get-tuple-element.38.mine, f32[8,240]{1,0:T(8,128)S(1)} %collective-permute-done.16.partner, f32[24,192]{1,0:T(8,128)S(1)} %copy-done.6, f32[24,48]{1,0:T(8,128)S(1)} %collective-permute-done.6.refs_3_.refs_10_.following, ...), custom_call_target="tpu_custom_call" | custom-call | flops 1000000 | bytes 1000000 | tf_op jit(solution)/shard_map/pallas_call | solution.py:692
  (46 shorter events, 2.1 us)
Async XLA Ops:
  0.6 31.8 %copy-start.12 = (f32[72]{0:T(128)S(1)}, f32[72]{0:T(128)}, u32[]{:S(2)}) copy-start(f32[72]{0:T(128)} %param.23) | copy-start | bytes 868
  0.6 31.8 %copy-start.13 = (f32[72]{0:T(128)S(1)}, f32[72]{0:T(128)}, u32[]{:S(2)}) copy-start(f32[72]{0:T(128)} %param.24) | copy-start | bytes 868
  3.6 12.8 %collective-permute-start = (bf16[144,504]{1,0:T(8,128)(2,1)}, bf16[144,504]{1,0:T(8,128)(2,1)S(1)}, u32[]{:S(2)}, u32[]{:S(2)}) collective-permute-start(bf16[144,504]{1,0:T(8,128)(2,1)} %get-tuple-element.22), channel_id=1, source_target_pairs={{0,4},{4,0},{8,12},{12,8},{1,5},{5,1},{9,13},{13,9},{2,6},{6,2},{1... | collective-permute-start | bytes 435464 | tf_op jit(solution)/shard_map/ppermute | solution.py:557
  6.6 14.9 %collective-permute-start.1 = (bf16[144,504]{1,0:T(8,128)(2,1)}, bf16[144,504]{1,0:T(8,128)(2,1)S(1)}, u32[]{:S(2)}, u32[]{:S(2)}) collective-permute-start(bf16[144,504]{1,0:T(8,128)(2,1)} %get-tuple-element.23), channel_id=1, source_target_pairs={{0,8},{4,12},{8,0},{12,4},{1,9},{5,13},{9,1},{13,5},{2,10},{6,14},... | collective-permute-start | bytes 435464 | tf_op jit(solution)/shard_map/ppermute | solution.py:557
  9.2 12.3 %collective-permute-start.2 = (bf16[144,504]{1,0:T(8,128)(2,1)}, bf16[144,504]{1,0:T(8,128)(2,1)S(1)}, u32[]{:S(2)}, u32[]{:S(2)}) collective-permute-start(bf16[144,504]{1,0:T(8,128)(2,1)} %get-tuple-element.24), channel_id=1, source_target_pairs={{0,12},{4,8},{8,4},{12,0},{1,13},{5,9},{9,5},{13,1},{2,14},{6,10},... | collective-permute-start | bytes 435464 | tf_op jit(solution)/shard_map/ppermute | solution.py:557
  9.2 17.8 %all-to-all-start = ((bf16[16,32,96]{2,1,0:T(8,128)(2,1)}), bf16[16,32,96]{2,1,0:T(8,128)(2,1)S(1)}, u32[]{:S(2)}, u32[]{:S(2)}) async-start(bf16[16,32,96]{2,1,0:T(8,128)(2,1)} %get-tuple-element.30), calls=%async_computation | async-start | bytes 262144 | tf_op jit(solution)/shard_map/all_to_all | solution.py:621
  16.3 16.1 %collective-permute-start.11 = (bf16[144,504]{1,0:T(8,128)(2,1)}, bf16[144,504]{1,0:T(8,128)(2,1)S(1)}, u32[]{:S(2)}, u32[]{:S(2)}) collective-permute-start(bf16[144,504]{1,0:T(8,128)(2,1)} %get-tuple-element.21.refs_0_), channel_id=1, source_target_pairs={{0,1},{1,0},{2,3},{3,2},{4,5},{5,4},{6,7},{7,6},{8,9},{9,8},{10,11... | collective-permute-start | bytes 435464 | tf_op jit(solution)/shard_map/ppermute | solution.py:557
  16.4 16.1 %collective-permute-start.12 = (bf16[144,504]{1,0:T(8,128)(2,1)S(1)}, bf16[144,504]{1,0:T(8,128)(2,1)S(1)}, u32[]{:S(2)}, u32[]{:S(2)}) collective-permute-start(bf16[144,504]{1,0:T(8,128)(2,1)S(1)} %collective-permute-done.refs_1_), channel_id=1, source_target_pairs={{0,1},{1,0},{2,3},{3,2},{4,5},{5,4},{6,7},{7,6},{8,9},{9,8},{10,11... | collective-permute-start | bytes 435464 | tf_op jit(solution)/shard_map/ppermute | solution.py:557
  21.5 10.9 %collective-permute-start.13 = (bf16[144,504]{1,0:T(8,128)(2,1)S(1)}, bf16[144,504]{1,0:T(8,128)(2,1)S(1)}, u32[]{:S(2)}, u32[]{:S(2)}) collective-permute-start(bf16[144,504]{1,0:T(8,128)(2,1)S(1)} %collective-permute-done.1.refs_2_), channel_id=1, source_target_pairs={{0,1},{1,0},{2,3},{3,2},{4,5},{5,4},{6,7},{7,6},{8,9},{9,8},{10,11... | collective-permute-start | bytes 435464 | tf_op jit(solution)/shard_map/ppermute | solution.py:557
  21.5 10.9 %collective-permute-start.14 = (bf16[144,504]{1,0:T(8,128)(2,1)S(1)}, bf16[144,504]{1,0:T(8,128)(2,1)S(1)}, u32[]{:S(2)}, u32[]{:S(2)}) collective-permute-start(bf16[144,504]{1,0:T(8,128)(2,1)S(1)} %collective-permute-done.2.refs_3_), channel_id=1, source_target_pairs={{0,1},{1,0},{2,3},{3,2},{4,5},{5,4},{6,7},{7,6},{8,9},{9,8},{10,11... | collective-permute-start | bytes 435464 | tf_op jit(solution)/shard_map/ppermute | solution.py:557
  27.0 1.3 %collective-permute-start.15 = (bf16[16,32,96]{2,1,0:T(8,128)(2,1)S(1)}, bf16[16,32,96]{2,1,0:T(8,128)(2,1)S(1)}, u32[]{:S(2)}, u32[]{:S(2)}) collective-permute-start(bf16[16,32,96]{2,1,0:T(8,128)(2,1)S(1)} %all-to-all-done.mine), channel_id=1, source_target_pairs={{0,1},{1,0},{2,3},{3,2},{4,5},{5,4},{6,7},{7,6},{8,9},{9,8},{10,11... | collective-permute-start | bytes 294920 | tf_op jit(solution)/shard_map/ppermute | solution.py:557
  27.0 0.9 %copy-start.2 = (bf16[144,504]{1,0:T(8,128)(2,1)S(1)}, bf16[144,504]{1,0:T(8,128)(2,1)}, u32[]{:S(2)}) copy-start(bf16[144,504]{1,0:T(8,128)(2,1)} %get-tuple-element.21.refs_0_) | copy-start | bytes 435460
  28.3 0.9 %copy-start = (f32[16,3,1152]{2,0,1:T(8,128)S(1)}, f32[16,3,1152]{2,0,1:T(8,128)}, u32[]{:S(2)}) copy-start(f32[16,3,1152]{2,0,1:T(8,128)} %param.20) | copy-start | bytes 663556
  29.3 0.8 copy-start.4
  32.5 0.9 %copy-start.3 = (bf16[144,504]{1,0:T(8,128)(2,1)S(1)}, bf16[144,504]{1,0:T(8,128)(2,1)}, u32[]{:S(2)}) copy-start(bf16[144,504]{1,0:T(8,128)(2,1)} %get-tuple-element.21.refs_0_) | copy-start | bytes 435460
  33.4 14.4 %copy-start.15 = (f32[24,48]{1,0:T(8,128)S(1)}, f32[24,48]{1,0:T(8,128)}, u32[]{:S(2)}) copy-start(f32[24,48]{1,0:T(8,128)} %get-tuple-element.25) | copy-start | bytes 13828
  33.4 38.7 %copy-start.1 = (f32[16,3,1152]{2,0,1:T(8,128)S(1)}, f32[16,3,1152]{2,0,1:T(8,128)}, u32[]{:S(2)}) copy-start(f32[16,3,1152]{2,0,1:T(8,128)} %param.20) | copy-start | bytes 663556
  33.4 38.7 %copy-start.5 = (bf16[16,1152]{1,0:T(8,128)(2,1)S(1)}, bf16[16,1152]{1,0:T(8,128)(2,1)}, u32[]{:S(2)}) copy-start(bf16[16,1152]{1,0:T(8,128)(2,1)} %refs_13_.1) | copy-start | bytes 110596
  33.4 38.7 %copy-start.6 = (f32[24,192]{1,0:T(8,128)S(1)}, f32[24,192]{1,0:T(8,128)}, u32[]{:S(2)}) copy-start(f32[24,192]{1,0:T(8,128)} %get-tuple-element.36.refs_9_.packed) | copy-start | bytes 55300
  33.4 38.7 %copy-start.8 = (f32[1,1152]{1,0:T(1,128)S(1)}, f32[1,1152]{1,0:T(1,128)}, u32[]{:S(2)}) copy-start(f32[1,1152]{1,0:T(1,128)} %refs_11_.1) | copy-start | bytes 13828
  40.2 31.8 %all-to-all-start.1 = ((bf16[16,72,240]{2,1,0:T(8,128)(2,1)}), bf16[16,72,240]{2,1,0:T(8,128)(2,1)S(1)}, u32[]{:S(2)}, u32[]{:S(2)}) async-start(bf16[16,72,240]{2,1,0:T(8,128)(2,1)} %shard_map.162), calls=%async_computation.1 | async-start | bytes 1179648 | tf_op jit(solution)/shard_map/all_to_all | solution.py:666
  44.3 17.1 %collective-permute-start.3 = (bf16[144,1152]{1,0:T(8,128)(2,1)S(1)}, bf16[144,1152]{1,0:T(8,128)(2,1)S(1)}, u32[]{:S(2)}, u32[]{:S(2)}) collective-permute-start(bf16[144,1152]{1,0:T(8,128)(2,1)S(1)} %shard_map.159.refs_0_), channel_id=1, source_target_pairs={{0,2},{2,0},{1,3},{3,1},{4,6},{6,4},{5,7},{7,5},{8,10},{10,8},{9,1... | collective-permute-start | bytes 995336 | tf_op jit(solution)/shard_map/ppermute | solution.py:557
  46.2 15.2 %collective-permute-start.4 = (bf16[144,1152]{1,0:T(8,128)(2,1)S(1)}, bf16[144,1152]{1,0:T(8,128)(2,1)S(1)}, u32[]{:S(2)}, u32[]{:S(2)}) collective-permute-start(bf16[144,1152]{1,0:T(8,128)(2,1)S(1)} %shard_map.159.refs_0_), channel_id=1, source_target_pairs={{0,16},{16,0},{1,17},{17,1},{2,18},{18,2},{3,19},{19,3},{4,20},{20... | collective-permute-start | bytes 995336 | tf_op jit(solution)/shard_map/ppermute | solution.py:557
  47.7 20.7 %collective-permute-start.5 = (bf16[144,1152]{1,0:T(8,128)(2,1)S(1)}, bf16[144,1152]{1,0:T(8,128)(2,1)S(1)}, u32[]{:S(2)}, u32[]{:S(2)}) collective-permute-start(bf16[144,1152]{1,0:T(8,128)(2,1)S(1)} %shard_map.159.refs_0_), channel_id=1, source_target_pairs={{0,18},{2,16},{16,2},{18,0},{1,19},{3,17},{17,3},{19,1},{4,22},{6,... | collective-permute-start | bytes 995336 | tf_op jit(solution)/shard_map/ppermute | solution.py:557
  47.8 5.9 %collective-permute-start.6 = (f32[24,48]{1,0:T(8,128)S(1)}, f32[24,48]{1,0:T(8,128)S(1)}, u32[]{:S(2)}, u32[]{:S(2)}) collective-permute-start(f32[24,48]{1,0:T(8,128)S(1)} %copy-done.15), channel_id=1, source_target_pairs={{4,0},{8,4},{12,8},{5,1},{9,5},{13,9},{6,2},{10,6},{14,10},{7,3},{... | collective-permute-start | bytes 13832 | tf_op jit(solution)/shard_map/ppermute | solution.py:623
  69.0 1.7 %collective-permute-start.10 = (bf16[144,1152]{1,0:T(8,128)(2,1)S(1)}, bf16[144,1152]{1,0:T(8,128)(2,1)S(1)}, u32[]{:S(2)}, u32[]{:S(2)}) collective-permute-start(bf16[144,1152]{1,0:T(8,128)(2,1)S(1)} %collective-permute-done.5.refs_2_.refs_3_), channel_id=1, source_target_pairs={{0,1},{1,0},{2,3},{3,2},{4,5},{5,4},{6,7},{7,6},{8,9},{9,8},{10,11... | collective-permute-start | bytes 995336 | tf_op jit(solution)/shard_map/ppermute | solution.py:557
  69.0 2.1 %collective-permute-start.7 = (bf16[144,1152]{1,0:T(8,128)(2,1)S(1)}, bf16[144,1152]{1,0:T(8,128)(2,1)S(1)}, u32[]{:S(2)}, u32[]{:S(2)}) collective-permute-start(bf16[144,1152]{1,0:T(8,128)(2,1)S(1)} %shard_map.159.refs_0_), channel_id=1, source_target_pairs={{0,1},{1,0},{2,3},{3,2},{4,5},{5,4},{6,7},{7,6},{8,9},{9,8},{10,11... | collective-permute-start | bytes 995336 | tf_op jit(solution)/shard_map/ppermute | solution.py:557
  69.5 2.1 %collective-permute-start.8 = (bf16[144,1152]{1,0:T(8,128)(2,1)S(1)}, bf16[144,1152]{1,0:T(8,128)(2,1)S(1)}, u32[]{:S(2)}, u32[]{:S(2)}) collective-permute-start(bf16[144,1152]{1,0:T(8,128)(2,1)S(1)} %collective-permute-done.3.refs_0_.refs_1_), channel_id=1, source_target_pairs={{0,1},{1,0},{2,3},{3,2},{4,5},{5,4},{6,7},{7,6},{8,9},{9,8},{10,11... | collective-permute-start | bytes 995336 | tf_op jit(solution)/shard_map/ppermute | solution.py:557
  69.5 2.5 %collective-permute-start.9 = (bf16[144,1152]{1,0:T(8,128)(2,1)S(1)}, bf16[144,1152]{1,0:T(8,128)(2,1)S(1)}, u32[]{:S(2)}, u32[]{:S(2)}) collective-permute-start(bf16[144,1152]{1,0:T(8,128)(2,1)S(1)} %collective-permute-done.4.refs_1_.refs_2_), channel_id=1, source_target_pairs={{0,1},{1,0},{2,3},{3,2},{4,5},{5,4},{6,7},{7,6},{8,9},{9,8},{10,11... | collective-permute-start | bytes 995336 | tf_op jit(solution)/shard_map/ppermute | solution.py:557
  72.1 0.8 copy-start.7
  76.0 1.2 %collective-permute-start.16 = (f32[8,240]{1,0:T(8,128)S(1)}, f32[8,240]{1,0:T(8,128)S(1)}, u32[]{:S(2)}, u32[]{:S(2)}) collective-permute-start(f32[8,240]{1,0:T(8,128)S(1)} %get-tuple-element.39), channel_id=1, source_target_pairs={{0,1},{1,0},{2,3},{3,2},{4,5},{5,4},{6,7},{7,6},{8,9},{9,8},{10,11... | collective-permute-start | bytes 23048 | tf_op jit(solution)/shard_map/ppermute | solution.py:557
  77.2 0.7 copy-start.11
  (3 other events, 1.9 us)

commit v7 on v6

--- a/solution.py
+++ b/solution.py
@@ -12,7 +12,6 @@
 LANES = 128
 VMEM_BYTES = 20 * 1024 * 1024
 WHOLE_VMEM = 62 * 1024 * 1024
-HOLD_BYTES = 2_000_000_000
 F32 = jnp.float32
 BF16 = jnp.bfloat16
 
@@ -288,12 +287,14 @@
     span,
     mine,
     other,
-    level_mod,
+    level_source,
     embed,
     lhs,
     xin,
     rstd_out,
     mask_out,
+    level_mod,
+    sem,
 ):
     width = embed.shape[1]
     scenes, all_frames, rows, _ = xin.shape
@@ -302,6 +303,8 @@
     per_core = frames // 2
     tokens = mine.shape[2] // per_core
     core = place_of("cfg")
+    copy = pltpu.make_async_copy(level_source.at[pl.ds(0, 2)], level_mod, sem)
+    copy.start()
     weights = embed[...].astype(F32)
     weights = weights - jnp.mean(weights, axis=1, keepdims=True)
     length, step = width // (queues * toks), mine.shape[2]
@@ -333,6 +336,7 @@
     level_id = lax.broadcasted_iota(jnp.int32, (level_mod.shape[1], width), 0).astype(F32)
     shift_row = values + scenes
     fill = LANES - toks * tokens
+    copy.wait()
     for y in range(scenes):
         for q in range(queues):
             first = (y * queues + q) * toks
@@ -376,20 +380,25 @@
 
 def attend_kernel(frames, tokens, queues, *refs):
     pieces = refs[: 2 * queues]
-    lhs, xin, rstd_in, mask_in, gain_q, gain_k, out, whole, proj, kfac, vfac, att = refs[
+    lhs, xin, rstd_in, mask_in, gain_q, gain_k, out, whole, proj, kfac, vfac, att, own, sem = refs[
         2 * queues :
     ]
+    copy = pltpu.make_async_copy(pieces[0], own, sem)
+    copy.start()
     scenes, all_frames, rows, _ = xin.shape
     head_dim = gain_q.shape[1]
     window = (proj.shape[0] - all_frames) // 2
     span = 2 * window + 1
     q_at, core = place_of("queue"), place_of("cfg")
     part_rows = pieces[0].shape[0]
-    for k in range(queues):
-        for side in range(2):
+    for k in reversed(range(queues)):
+        for side in reversed(range(2)):
             owner = core if side == 0 else 1 - core
             first = pl.multiple_of(((q_at ^ k) * 2 + owner) * part_rows, 16)
             piece = pieces[side * queues + k]
+            if k == side == 0:
+                copy.wait()
+                piece = own
             whole[pl.ds(first, part_rows), :] = piece[:, piece.shape[1] - 3 * head_dim :]
     folded = jnp.dot(lhs[...], whole[...], preferred_element_type=F32)
     high, low = split_terms(folded, 2)
@@ -448,8 +457,14 @@
 
 
 def side_kernel(group, *refs):
-    for k, piece in enumerate(refs[:-1]):
-        refs[-1][:, k * group : (k + 1) * group] = piece[:, :group]
+    *pieces, out, own, sem = refs
+    copy = pltpu.make_async_copy(pieces[0], own, sem)
+    copy.start()
+    for k, piece in reversed(list(enumerate(pieces))):
+        if k == 0:
+            copy.wait()
+            piece = own
+        out[:, k * group : (k + 1) * group] = piece[:, :group]
 
 
 def hold_kernel(*refs):
@@ -457,34 +472,37 @@
 
 
 def finish_kernel(half, values, queues, *refs):
-    parts = [refs[:4], refs[4:8]]
-    (
-        attended,
-        packed,
-        following,
-        cond,
-        level_mod,
-        embed,
-        final_gain,
-        final_w,
-        _,
-        mine,
-        send,
-        scratch,
-        mixed,
-    ) = refs[8:]
+    parts = [refs[:5], refs[5:10]]
+    attended, _, table, index = refs[10:14]
+    sources = refs[14:22]
+    mine, send, base, factor, noise_out, guide = refs[22:28]
+    held = refs[28:36]
+    scratch, mixed, sems = refs[36:]
+    copies = []
+    for i, (source, to) in enumerate(zip(sources, held)):
+        source = source.at[2] if i == 3 else source
+        copies.append(pltpu.make_async_copy(source, to, sems.at[i]))
+    for copy in copies:
+        copy.start()
+    packed, following, cond, gates, embed, final_gain, final_w, noise = held
     scene, q_at, tok, core = (place_of(a) for a in ("scene", "queue", "tok", "cfg"))
     group = parts[0][0].shape[1] // queues
     columns = parts[0][0].shape[0]
+
+    def weights_of(c, t, y, k):
+        lane = slice(k * group, (k + 1) * group)
+        if t == y == 1:
+            return [parts[c][3][:, lane], parts[c][4][:, lane]]
+        return [parts[c][2 * y + t][:, lane]]
+
     total = None
     for t in range(2):
         made = None
         for y in range(2):
-            pieces = [
-                parts[c][2 * y + t][:, k * group : (k + 1) * group]
-                for c in range(2)
-                for k in range(queues)
-            ]
+            pieces = []
+            for c in range(2):
+                for k in range(queues):
+                    pieces += weights_of(c, t, y, k)
             first = ((tok ^ t) * 2 + (scene ^ y)) * group
             rows = attended[pl.ds(pl.multiple_of(first, 16), group), :]
             term = jnp.dot(jnp.concatenate(pieces, axis=0), rows, preferred_element_type=F32)
@@ -497,7 +515,9 @@
             at = (c * queues + k) * columns
             mixed[pl.ds(pl.multiple_of(first, 8), columns), :] = total[at : at + columns]
 
-    levels_all, width = level_mod.shape[1:]
+    for copy in copies:
+        copy.wait()
+    levels_all, width = gates.shape
     info = jnp.concatenate([packed[...], following[...]], axis=1)
     lanes = info.shape[1]
     vec = info[:values].astype(BF16)
@@ -509,7 +529,7 @@
     one_hot = (lax.broadcasted_iota(jnp.int32, (levels_all, lanes), 0).astype(F32) == level).astype(
         F32
     ).astype(BF16)
-    gate_terms = jnp.concatenate(split_terms(level_mod[2], 3), axis=0)
+    gate_terms = jnp.concatenate(split_terms(gates[...], 3), axis=0)
     gate = dot_tn(gate_terms, jnp.concatenate([one_hot] * 3, axis=0))
     gain_terms = jnp.concatenate(split_terms(final_gain[...], 3) + [zero], axis=0)
     gain = dot_tn(gain_terms, ones)
@@ -524,25 +544,24 @@
     mine[...] = scratch[pl.ds(own, half), :]
     send[...] = scratch[pl.ds(other, half), :]
 
-
-def update_kernel(
-    values, levels_all, mine, partner, packed, following, noise, table, index, vel, new
-):
-    half = mine.shape[0]
-    frames, _, tokens = vel.shape
-    core = place_of("cfg")
-    own = pl.multiple_of(core * half, half)
-    here, there = mine[...], partner[...]
-    cond = jnp.where(core == 0, here, there)
-    uncond = jnp.where(core == 0, there, here)
-    guided = uncond + table[index[0]] * (cond - uncond)
-    level = jnp.concatenate(
-        [packed[values : values + 1], following[values : values + 1]], axis=1
-    )
     current = noise_sigma((level + 1.0) / levels_all)
     upcoming = noise_sigma(level / levels_all)
-    latents = jnp.concatenate([packed[pl.ds(own, half), :], following[pl.ds(own, half), :]], axis=1)
-    updated = latents + (upcoming - current) * guided
+    factor[...] = jnp.broadcast_to(upcoming - current, factor.shape)
+    base[...] = jnp.concatenate(
+        [packed[pl.ds(own, half), :], following[pl.ds(own, half), :]], axis=1
+    )
+    noise_out[...] = noise[...]
+    guide[...] = jnp.full(guide.shape, table[index[0]], F32)
+
+
+def update_kernel(mine, partner, base, factor, noise, guide, vel, new):
+    frames, _, tokens = vel.shape
+    is_cond = place_of("cfg") == 0
+    here, there = mine[...], partner[...]
+    cond = jnp.where(is_cond, here, there)
+    uncond = jnp.where(is_cond, there, here)
+    guided = uncond + guide[0:1, 0:1] * (cond - uncond)
+    updated = base[...] + factor[...] * guided
     is_last = place_of("queue") == lax.axis_size("queue") - 1
     for f in range(frames):
         vel[f] = guided[:, f * tokens : (f + 1) * tokens]
@@ -620,23 +639,14 @@
     far = [swapped(piece, "cfg", 1) for piece in near]
     shares = lax.all_to_all(copies, ("scene", "queue", "tok"), 0, 0)
     other_shares = swapped(shares, "cfg", 1)
-    following = lax.ppermute(first, "queue", [(i + 1, i) for i in range(queues - 1)])
 
     part = kernel_call(
         functools.partial(side_kernel, group),
         jax.ShapeDtypeStruct((local_rows, queues * group), BF16),
-        "v" * queues,
+        "a" + "v" * (queues - 1),
+        [pltpu.VMEM(chunk.shape, BF16), pltpu.SemaphoreType.DMA],
     )(*near)
-    away = [
-        swapped(part, "tok", 1),
-        swapped(part, "scene", 1),
-        swapped(part, ("scene", "tok"), 3),
-    ]
-    token = kernel_call(
-        hold_kernel, jax.ShapeDtypeStruct((8, LANES), F32), "aaaa", bytes_accessed=HOLD_BYTES
-    )(*away, following)
-    *away, token = lax.optimization_barrier((part, *away, token))
-    away_far = [swapped(piece, "cfg", 1) for piece in away]
+    part_tok, part_scene = swapped(part, "tok", 1), swapped(part, "scene", 1)
 
     lhs, xin, rstd, masks = kernel_call(
         functools.partial(prepare_kernel, frames, values, span),
@@ -646,38 +656,42 @@
             jax.ShapeDtypeStruct((all_frames, 1, lanes), F32),
             jax.ShapeDtypeStruct((scenes, all_frames, rows - values, LANES), F32),
         ],
-        "vvvv",
+        "vvav",
+        [pltpu.VMEM((2, levels_all, width), F32), pltpu.SemaphoreType.DMA],
         bytes_accessed=8_000_000,
     )(shares, other_shares, mods, embed_weight)
-    lhs, part = lax.optimization_barrier((lhs, part))
     attended = kernel_call(
         functools.partial(attend_kernel, frames, tokens, queues),
         jax.ShapeDtypeStruct((chips, head_dim, row_lanes), BF16),
-        "v" * (2 * queues + 6),
+        "a" + "v" * (2 * queues + 5),
         [
             pltpu.VMEM((width, 3 * head_dim), BF16),
             pltpu.VMEM((all_frames + 2 * window, 3 * head_dim, lanes), F32),
             pltpu.VMEM((all_frames + 2 * window, 1, lanes), F32),
             pltpu.VMEM((all_frames + 2 * window, 1, lanes), F32),
             pltpu.VMEM((all_frames, scenes, head_dim, LANES), F32),
+            pltpu.VMEM(chunk.shape, BF16),
+            pltpu.SemaphoreType.DMA,
         ],
-        bytes_accessed=24_000_000,
+        bytes_accessed=100_000_000,
     )(*near, *far, lhs, xin, rstd, masks, query_gain[None], key_gain[None])
+    attended, part, part_tok, part_scene, first = lax.optimization_barrier(
+        (attended, part, part_tok, part_scene, first)
+    )
     received = lax.all_to_all(attended, ("tok", "scene", "queue"), 0, 0)
+    following = lax.ppermute(first, "queue", [(i + 1, i) for i in range(queues - 1)])
+    cut = -(-local_rows // 32) * 16
+    upper = swapped(part_tok[:cut], "scene", 1)
+    lower = swapped(part_scene[cut:], "tok", 1)
+    token = kernel_call(hold_kernel, jax.ShapeDtypeStruct((8, LANES), F32), "a")(following)
+    upper, lower, token = lax.optimization_barrier((upper, lower, token))
+    away = [part, part_tok, part_scene, upper, lower]
+    away_far = [swapped(piece, "cfg", 1) for piece in away]
     received = received.reshape(width, row_lanes)
 
     half = values // 2
     half_shape = jax.ShapeDtypeStruct((half, row_lanes), F32)
-    mine, send = kernel_call(
-        functools.partial(finish_kernel, half, values, queues),
-        [half_shape, half_shape],
-        "v" * 17,
-        [pltpu.VMEM((values, row_lanes), F32), pltpu.VMEM((width, row_lanes), F32)],
-        bytes_accessed=8_000_000,
-    )(
-        *away,
-        *away_far,
-        received,
+    smalls = (
         packed,
         following,
         cond_embed,
@@ -685,13 +699,30 @@
         embed_weight,
         final_gain[None],
         final_weight.T,
-        token,
-    )
+        fresh_noise,
+    )
+    places = [
+        pltpu.VMEM(a.shape[1:] if i == 3 else a.shape, a.dtype) for i, a in enumerate(smalls)
+    ]
+    mine, send, *rest = kernel_call(
+        functools.partial(finish_kernel, half, values, queues),
+        [half_shape] * 4
+        + [
+            jax.ShapeDtypeStruct(fresh_noise.shape, F32),
+            jax.ShapeDtypeStruct((8, LANES), F32),
+        ],
+        "v" * 12 + "ss" + "a" * len(smalls),
+        places
+        + [
+            pltpu.VMEM((values, row_lanes), F32),
+            pltpu.VMEM((width, row_lanes), F32),
+            pltpu.SemaphoreType.DMA((len(smalls),)),
+        ],
+        bytes_accessed=8_000_000,
+    )(*away, *away_far, received, token, guide_table, guide_index, *smalls)
     partner = swapped(send, "cfg", 1)
     shape = jax.ShapeDtypeStruct((frames, half, tokens), F32)
-    return kernel_call(
-        functools.partial(update_kernel, values, levels_all), [shape, shape], "vvvvvss"
-    )(mine, partner, packed, following, fresh_noise, guide_table, guide_index)
+    return kernel_call(update_kernel, [shape, shape], "v" * 6)(mine, partner, *rest)
 
 
 def on_device(*args):

time: 80.5 us -> 74 us (0.919)
  waiting for transfers between devices: 30.9 us -> 18.9 us
  starting transfers between devices: 23.8 us -> 27.6 us
  Pallas kernels: 16.1 us -> 18.7 us
  local copies, waits for them, and re-layouts: 7.63 us -> 6.5 us
    ppermute x16 -> x18, waiting for transfers between devices: 21.3 us -> 10.6 us  [swapped(): return lax.ppermute(value, axis, [(i, i ^ mask) for i in range(count)])]
    all_to_all x1, waiting for transfers between devices: 0.01 us -> 3.5 us  [on_device_heads(): received = lax.all_to_all(attended, ('tok', 'scene', 'queue'), 0, 0)]
    all_to_all x1, waiting for transfers between devices: 4.96 us -> 1.52 us  [on_device_heads(): shares = lax.all_to_all(copies, ('scene', 'queue', 'tok'), 0, 0)]
    ppermute x16 -> x18, starting transfers between devices: 11.4 us -> 14 us  [swapped(): return lax.ppermute(value, axis, [(i, i ^ mask) for i in range(count)])]
    unnamed x32 -> x26, local copies, waits for them, and re-layouts: 6.93 us -> 5.18 us
    pallas_call x1, Pallas kernels: 2.51 us -> 3.82 us  [on_device_heads(): kernel_call(functools.partial(finish_kernel, half, values, queues), [half...]
    ppermute x1, waiting for transfers between devices: 4.59 us -> 3.31 us  [on_device_heads(): lax.ppermute(first, 'queue', [(i + 1, i) for i in range(queues - 1)])]
    all_to_all x1, starting transfers between devices: 4.02 us -> 5.29 us  [on_device_heads(): received = lax.all_to_all(attended, ('tok', 'scene', 'queue'), 0, 0)]
  transfers between devices with their start and end apart: 19 -> 21, of which waited for: 10 -> 7; matrix products, arithmetic and copies ran while one was open for 1% -> 2% of each run, Pallas kernels for 3% -> 15%
where the time goes in v7:
time: 74 us; the launch traced here: 73.3 us
  starting transfers between devices  27.6 us (37%)
  waiting for transfers between devices  18.9 us (26%)
  Pallas kernels  18.7 us (25%)
  local copies, waits for them, and re-layouts  6.5 us (9%)
  between operations  1.55 us (2%)
    ppermute x18, starting transfers between devices, swapped(): return lax.ppermute(value, axis, [(i, i ^ mask) for i in range(count)])  14 us
    ppermute x18, waiting for transfers between devices, swapped(): return lax.ppermute(value, axis, [(i, i ^ mask) for i in range(count)])  10.6 us
    pallas_call x1, Pallas kernels, on_device_heads(): kernel_call(functools.partial(attend_kernel, frames, tokens, queues), jax...  7.7 us
    all_to_all x1, starting transfers between devices, on_device_heads(): shares = lax.all_to_all(copies, ('scene', 'queue', 'tok'), 0, 0)  7.08 us
    all_to_all x1, starting transfers between devices, on_device_heads(): received = lax.all_to_all(attended, ('tok', 'scene', 'queue'), 0, 0)  5.29 us
    unnamed x26, local copies, waits for them, and re-layouts  5.18 us
    pallas_call x1, Pallas kernels, on_device_heads(): kernel_call(functools.partial(finish_kernel, half, values, queues), [half...  3.82 us
    all_to_all x1, waiting for transfers between devices, on_device_heads(): received = lax.all_to_all(attended, ('tok', 'scene', 'queue'), 0, 0)  3.5 us
  transfers between devices with their start and end apart: 21, of which 7 were waited for; matrix products, arithmetic and copies ran while one was open for 2% of the time, Pallas kernels for 15%

profile of v7, /device:TPU:0, one launch (start us, length us, event | category | flops | bytes accessed | tf_op | source)
XLA Modules:
  0.0 73.3 jit_solution(7031246920685950147)
XLA Ops:
  0.7 2.9 %shard_map.158 = (bf16[144,504]{1,0:T(8,128)(2,1)}, bf16[144,504]{1,0:T(8,128)(2,1)}, bf16[144,504]{1,0:T(8,128)(2,1)}, bf16[144,504]{1,0:T(8,128)(2,1)}, bf16[1...) custom-call(f32[4,16,48]{2,1,0:T(8,128)} %latents.1, s32[1,4]{1,0:T(1,128)} %bitcast.16, ...), custom_call_target="tpu_custom_call" | custom-call | flops 1000000 | bytes 8000000 | tf_op jit(solution)/shard_map/pallas_call | solution.py:617
  3.6 3.0 %collective-permute-start = (bf16[144,504]{1,0:T(8,128)(2,1)}, bf16[144,504]{1,0:T(8,128)(2,1)S(1)}, u32[]{:S(2)}, u32[]{:S(2)}) collective-permute-start(bf16[144,504]{1,0:T(8,128)(2,1)} %get-tuple-element.28), channel_id=1, source_target_pairs={{0,4},{4,0},{8,12},{12,8},{1,5},{5,1},{9,13},{13,9},{2,6},{6,2},{1... | collective-permute-start | bytes 435464 | tf_op jit(solution)/shard_map/ppermute | solution.py:576
  6.6 2.6 %collective-permute-start.1 = (bf16[144,504]{1,0:T(8,128)(2,1)}, bf16[144,504]{1,0:T(8,128)(2,1)S(1)}, u32[]{:S(2)}, u32[]{:S(2)}) collective-permute-start(bf16[144,504]{1,0:T(8,128)(2,1)} %get-tuple-element.29), channel_id=1, source_target_pairs={{0,8},{4,12},{8,0},{12,4},{1,9},{5,13},{9,1},{13,5},{2,10},{6,14},... | collective-permute-start | bytes 435464 | tf_op jit(solution)/shard_map/ppermute | solution.py:576
  9.2 7.1 %all-to-all-start = ((bf16[16,32,96]{2,1,0:T(8,128)(2,1)}), bf16[16,32,96]{2,1,0:T(8,128)(2,1)S(1)}, u32[]{:S(2)}, u32[]{:S(2)}) async-start(bf16[16,32,96]{2,1,0:T(8,128)(2,1)} %get-tuple-element.31), calls=%async_computation | async-start | bytes 262144 | tf_op jit(solution)/shard_map/all_to_all | solution.py:640
  16.3 5.2 %collective-permute-done.1.refs_2_ = bf16[144,504]{1,0:T(8,128)(2,1)S(1)} collective-permute-done((bf16[144,504]{1,0:T(8,128)(2,1)}, bf16[144,504]{1,0:T(8,128)(2,1)S(1)}, u32[]{:S(2)}, u32[]{:S(2)}) %collective-permute-start.1) | collective-permute-done | bytes 145184 | tf_op jit(solution)/shard_map/ppermute | solution.py:576
  21.5 0.9 %shard_map.161.refs_0_ = bf16[144,1152]{1,0:T(8,128)(2,1)S(1)} custom-call(bf16[144,504]{1,0:T(8,128)(2,1)} %get-tuple-element.27.refs_0_, bf16[144,504]{1,0:T(8,128)(2,1)S(1)} %collective-permute-done.refs_1_, bf16[144,504]{1,0:T(8,128)(2,1)S(1)} %collective-permute-done.1.refs_2_, bf16[144,504]{1,0:T(8,128)(2,1)S(1)} %collective-permute-done.2.refs_3_), custom_call_target="tpu_custom_call" | custom-call | flops 1000000 | bytes 1000000 | tf_op jit(solution)/shard_map/pallas_call | solution.py:643
  22.4 1.6 %collective-permute-start.8 = (bf16[144,1152]{1,0:T(8,128)(2,1)S(1)}, bf16[144,1152]{1,0:T(8,128)(2,1)S(1)}, u32[]{:S(2)}, u32[]{:S(2)}) collective-permute-start(bf16[144,1152]{1,0:T(8,128)(2,1)S(1)} %shard_map.161.refs_0_), channel_id=1, source_target_pairs={{0,2},{2,0},{1,3},{3,1},{4,6},{6,4},{5,7},{7,5},{8,10},{10,8},{9,1... | collective-permute-start | bytes 995336 | tf_op jit(solution)/shard_map/ppermute | solution.py:576
  24.0 1.5 %collective-permute-start.9 = (bf16[144,1152]{1,0:T(8,128)(2,1)S(1)}, bf16[144,1152]{1,0:T(8,128)(2,1)S(1)}, u32[]{:S(2)}, u32[]{:S(2)}) collective-permute-start(bf16[144,1152]{1,0:T(8,128)(2,1)S(1)} %shard_map.161.refs_0_), channel_id=1, source_target_pairs={{0,16},{16,0},{1,17},{17,1},{2,18},{18,2},{3,19},{19,3},{4,20},{20... | collective-permute-start | bytes 995336 | tf_op jit(solution)/shard_map/ppermute | solution.py:576
  25.5 1.5 %all-to-all-done.mine = bf16[16,32,96]{2,1,0:T(8,128)(2,1)S(1)} async-done(((bf16[16,32,96]{2,1,0:T(8,128)(2,1)}), bf16[16,32,96]{2,1,0:T(8,128)(2,1)S(1)}, u32[]{:S(2)}, u32[]{:S(2)}) %all-to-all-start) | async-done | bytes 98336 | tf_op jit(solution)/shard_map/all_to_all | solution.py:640
  27.1 0.5 collective-permute-start.4
  27.6 0.8 %collective-permute-done.7.other = bf16[16,32,96]{2,1,0:T(8,128)(2,1)S(1)} collective-permute-done((bf16[16,32,96]{2,1,0:T(8,128)(2,1)S(1)}, bf16[16,32,96]{2,1,0:T(8,128)(2,1)S(1)}, u32[]{:S(2)}, u32[]{:S(2)}) %collective-permute-start.7) | collective-permute-done | bytes 98336 | tf_op jit(solution)/shard_map/ppermute | solution.py:576
  28.6 0.9 %copy-done = f32[16,3,1152]{2,0,1:T(8,128)S(1)} copy-done((f32[16,3,1152]{2,0,1:T(8,128)S(1)}, f32[16,3,1152]{2,0,1:T(8,128)}, u32[]{:S(2)}) %copy-start) | copy-done | bytes 221208
  29.5 0.8 %copy-done.2 = bf16[16,1152]{1,0:T(8,128)(2,1)S(1)} copy-done((bf16[16,1152]{1,0:T(8,128)(2,1)S(1)}, bf16[16,1152]{1,0:T(8,128)(2,1)}, u32[]{:S(2)}) %copy-start.2) | copy-done | bytes 36888
  30.3 2.6 %shard_map.159 = (bf16[1024,1152]{1,0:T(8,128)(2,1)S(1)}, bf16[2,16,32,128]{3,2,1,0:T(8,128)(2,1)S(1)}, f32[16,1,256]{2,1,0:T(1,128)S(1)}, f32[2,16,16,128]{3,2,1,0:T(8,128)S(1)}) custom-call(bf16[16,32,96]{2,1,0:T(8,128)(2,1)S(1)} %all-to-all-done.mine, bf16[16,32,96]{2,1,0:T(8,128)(2,1)S(1)} %collective-permute-done.7.other, f32[3,16,1152]{2,1,0:T(8,128)S(1)} %bitcast.9, ...), custom_call_target="tpu_custom_call" | custom-call | flops 1000000 | bytes 8000000 | tf_op jit(solution)/shard_map/pallas_call | solution.py:651
  33.0 7.7 %shard_map.160 = bf16[16,72,240]{2,1,0:T(8,128)(2,1)} custom-call(bf16[144,504]{1,0:T(8,128)(2,1)} %get-tuple-element.27.refs_0_, bf16[144,504]{1,0:T(8,128)(2,1)S(1)} %collective-permute-done.refs_1_, bf16[144,504]{1,0:T(8,128)(2,1)S(1)} %collective-permute-done.1.refs_2_, bf16[144,504]{1,0:T(8,128)(2,1)S(1)} %collective-permute-done.2.refs_3_, ...), custom_call_target="tpu_custom_call" | custom-call | flops 1000000 | bytes 100000000 | tf_op jit(solution)/shard_map/pallas_call | solution.py:663
  40.7 5.3 %all-to-all-start.1 = ((bf16[16,72,240]{2,1,0:T(8,128)(2,1)}), bf16[16,72,240]{2,1,0:T(8,128)(2,1)S(1)}, u32[]{:S(2)}, u32[]{:S(2)}) async-start(bf16[16,72,240]{2,1,0:T(8,128)(2,1)} %shard_map.160), calls=%async_computation.1 | async-start | bytes 1179648 | tf_op jit(solution)/shard_map/all_to_all | solution.py:681
  46.0 2.0 %collective-permute-start.10 = (bf16[80,1152]{1,0:T(8,128)(2,1)S(1)}, bf16[80,1152]{1,0:T(8,128)(2,1)S(1)}, u32[]{:S(2)}, u32[]{:S(2)}) collective-permute-start(bf16[80,1152]{1,0:T(8,128)(2,1)S(1)} %slice.6), channel_id=1, source_target_pairs={{0,16},{16,0},{1,17},{17,1},{2,18},{18,2},{3,19},{19,3},{4,20},{20... | collective-permute-start | bytes 552968 | tf_op jit(solution)/shard_map/ppermute | solution.py:576
  48.0 1.3 %collective-permute-start.12 = (f32[24,48]{1,0:T(8,128)S(1)}, f32[24,48]{1,0:T(8,128)S(1)}, u32[]{:S(2)}, u32[]{:S(2)}) collective-permute-start(f32[24,48]{1,0:T(8,128)S(1)} %copy-done.12), channel_id=1, source_target_pairs={{4,0},{8,4},{12,8},{5,1},{9,5},{13,9},{6,2},{10,6},{14,10},{7,3},{... | collective-permute-start | bytes 13832 | tf_op jit(solution)/shard_map/ppermute | solution.py:682
  49.3 1.5 %collective-permute-start.11 = (bf16[64,1152]{1,0:T(8,128)(2,1)S(1)}, bf16[64,1152]{1,0:T(8,128)(2,1)S(1)}, u32[]{:S(2)}, u32[]{:S(2)}) collective-permute-start(bf16[64,1152]{1,0:T(8,128)(2,1)S(1)} %slice.7), channel_id=1, source_target_pairs={{0,2},{2,0},{1,3},{3,1},{4,6},{6,4},{5,7},{7,5},{8,10},{10,8},{9,1... | collective-permute-start | bytes 442376 | tf_op jit(solution)/shard_map/ppermute | solution.py:576
  51.4 3.3 %collective-permute-done.12.refs_0_.refs_15_ = f32[24,48]{1,0:T(8,128)S(1)} collective-permute-done((f32[24,48]{1,0:T(8,128)S(1)}, f32[24,48]{1,0:T(8,128)S(1)}, u32[]{:S(2)}, u32[]{:S(2)}) %collective-permute-start.12) | collective-permute-done | bytes 4640 | tf_op jit(solution)/shard_map/ppermute | solution.py:682
  54.7 3.3 %collective-permute-done.11.refs_4_ = bf16[64,1152]{1,0:T(8,128)(2,1)S(1)} collective-permute-done((bf16[64,1152]{1,0:T(8,128)(2,1)S(1)}, bf16[64,1152]{1,0:T(8,128)(2,1)S(1)}, u32[]{:S(2)}, u32[]{:S(2)}) %collective-permute-start.11) | collective-permute-done | bytes 147488 | tf_op jit(solution)/shard_map/ppermute | solution.py:576
  58.0 0.5 collective-permute-start.17
  58.6 1.3 %broadcast_in_dim.15.refs_19_ = f32[1,1152]{1,0:T(1,128)} reshape(f32[1152]{0:T(1024)} %param.26) | data formatting | bytes 9216 | tf_op jit(solution)/shard_map/broadcast_in_dim | solution.py:700
  60.5 3.5 %all-to-all-done.1 = bf16[16,72,240]{2,1,0:T(8,128)(2,1)S(1)} async-done(((bf16[16,72,240]{2,1,0:T(8,128)(2,1)}), bf16[16,72,240]{2,1,0:T(8,128)(2,1)S(1)}, u32[]{:S(2)}, u32[]{:S(2)}) %all-to-all-start.1) | async-done | bytes 552992 | tf_op jit(solution)/shard_map/all_to_all | solution.py:681
  64.1 0.7 copy-done.5
  64.8 0.7 copy-done.6
  65.5 0.7 copy-done.7
  66.2 0.7 copy-done.8
  66.9 0.7 copy-done.11
  67.5 3.8 %shard_map.163 = (f32[8,240]{1,0:T(8,128)S(1)}, f32[8,240]{1,0:T(8,128)S(1)}, f32[8,240]{1,0:T(8,128)S(1)}, f32[8,240]{1,0:T(8,128)S(1)}, f32[8,48]{1,0:T(8,128)S(1)}, /*index=5*/f32[8,128]{1,0:T(8,128)S(1)}) custom-call(bf16[144,1152]{1,0:T(8,128)(2,1)S(1)} %shard_map.161.refs_0_, bf16[144,1152]{1,0:T(8,128)(2,1)S(1)} %collective-permute-done.8.refs_1_, ...), custom_call_target="tpu_custom_call" | custom-call | flops 1000000 | bytes 8000000 | tf_op jit(solution)/shard_map/pallas_call | solution.py:707
  71.4 1.2 %collective-permute-done.18.partner = f32[8,240]{1,0:T(8,128)S(1)} collective-permute-done((f32[8,240]{1,0:T(8,128)S(1)}, f32[8,240]{1,0:T(8,128)S(1)}, u32[]{:S(2)}, u32[]{:S(2)}) %collective-permute-start.18) | collective-permute-done | bytes 7712 | tf_op jit(solution)/shard_map/ppermute | solution.py:576
  72.6 0.7 shard_map.164
  (46 shorter events, 0.9 us)
Async XLA Ops:
  0.6 32.3 %copy-start.9 = (f32[72]{0:T(128)S(1)}, f32[72]{0:T(128)}, u32[]{:S(2)}) copy-start(f32[72]{0:T(128)} %param.23) | copy-start | bytes 868
  0.6 32.3 %copy-start.10 = (f32[72]{0:T(128)S(1)}, f32[72]{0:T(128)}, u32[]{:S(2)}) copy-start(f32[72]{0:T(128)} %param.24) | copy-start | bytes 868
  3.6 12.7 %collective-permute-start = (bf16[144,504]{1,0:T(8,128)(2,1)}, bf16[144,504]{1,0:T(8,128)(2,1)S(1)}, u32[]{:S(2)}, u32[]{:S(2)}) collective-permute-start(bf16[144,504]{1,0:T(8,128)(2,1)} %get-tuple-element.28), channel_id=1, source_target_pairs={{0,4},{4,0},{8,12},{12,8},{1,5},{5,1},{9,13},{13,9},{2,6},{6,2},{1... | collective-permute-start | bytes 435464 | tf_op jit(solution)/shard_map/ppermute | solution.py:576
  6.6 14.9 %collective-permute-start.1 = (bf16[144,504]{1,0:T(8,128)(2,1)}, bf16[144,504]{1,0:T(8,128)(2,1)S(1)}, u32[]{:S(2)}, u32[]{:S(2)}) collective-permute-start(bf16[144,504]{1,0:T(8,128)(2,1)} %get-tuple-element.29), channel_id=1, source_target_pairs={{0,8},{4,12},{8,0},{12,4},{1,9},{5,13},{9,1},{13,5},{2,10},{6,14},... | collective-permute-start | bytes 435464 | tf_op jit(solution)/shard_map/ppermute | solution.py:576
  9.2 12.3 %collective-permute-start.2 = (bf16[144,504]{1,0:T(8,128)(2,1)}, bf16[144,504]{1,0:T(8,128)(2,1)S(1)}, u32[]{:S(2)}, u32[]{:S(2)}) collective-permute-start(bf16[144,504]{1,0:T(8,128)(2,1)} %get-tuple-element.30), channel_id=1, source_target_pairs={{0,12},{4,8},{8,4},{12,0},{1,13},{5,9},{9,5},{13,1},{2,14},{6,10},... | collective-permute-start | bytes 435464 | tf_op jit(solution)/shard_map/ppermute | solution.py:576
  9.2 17.9 %all-to-all-start = ((bf16[16,32,96]{2,1,0:T(8,128)(2,1)}), bf16[16,32,96]{2,1,0:T(8,128)(2,1)S(1)}, u32[]{:S(2)}, u32[]{:S(2)}) async-start(bf16[16,32,96]{2,1,0:T(8,128)(2,1)} %get-tuple-element.31), calls=%async_computation | async-start | bytes 262144 | tf_op jit(solution)/shard_map/all_to_all | solution.py:640
  22.4 18.3 %collective-permute-start.8 = (bf16[144,1152]{1,0:T(8,128)(2,1)S(1)}, bf16[144,1152]{1,0:T(8,128)(2,1)S(1)}, u32[]{:S(2)}, u32[]{:S(2)}) collective-permute-start(bf16[144,1152]{1,0:T(8,128)(2,1)S(1)} %shard_map.161.refs_0_), channel_id=1, source_target_pairs={{0,2},{2,0},{1,3},{3,1},{4,6},{6,4},{5,7},{7,5},{8,10},{10,8},{9,1... | collective-permute-start | bytes 995336 | tf_op jit(solution)/shard_map/ppermute | solution.py:576
  24.0 16.7 %collective-permute-start.9 = (bf16[144,1152]{1,0:T(8,128)(2,1)S(1)}, bf16[144,1152]{1,0:T(8,128)(2,1)S(1)}, u32[]{:S(2)}, u32[]{:S(2)}) collective-permute-start(bf16[144,1152]{1,0:T(8,128)(2,1)S(1)} %shard_map.161.refs_0_), channel_id=1, source_target_pairs={{0,16},{16,0},{1,17},{17,1},{2,18},{18,2},{3,19},{19,3},{4,20},{20... | collective-permute-start | bytes 995336 | tf_op jit(solution)/shard_map/ppermute | solution.py:576
  25.5 2.0 %collective-permute-start.3 = (bf16[144,504]{1,0:T(8,128)(2,1)}, bf16[144,504]{1,0:T(8,128)(2,1)S(1)}, u32[]{:S(2)}, u32[]{:S(2)}) collective-permute-start(bf16[144,504]{1,0:T(8,128)(2,1)} %get-tuple-element.27.refs_0_), channel_id=1, source_target_pairs={{0,1},{1,0},{2,3},{3,2},{4,5},{5,4},{6,7},{7,6},{8,9},{9,8},{10,11... | collective-permute-start | bytes 435464 | tf_op jit(solution)/shard_map/ppermute | solution.py:576
  27.1 1.3 %collective-permute-start.7 = (bf16[16,32,96]{2,1,0:T(8,128)(2,1)S(1)}, bf16[16,32,96]{2,1,0:T(8,128)(2,1)S(1)}, u32[]{:S(2)}, u32[]{:S(2)}) collective-permute-start(bf16[16,32,96]{2,1,0:T(8,128)(2,1)S(1)} %all-to-all-done.mine), channel_id=1, source_target_pairs={{0,1},{1,0},{2,3},{3,2},{4,5},{5,4},{6,7},{7,6},{8,9},{9,8},{10,11... | collective-permute-start | bytes 294920 | tf_op jit(solution)/shard_map/ppermute | solution.py:576
  27.1 5.8 %collective-permute-start.4 = (bf16[144,504]{1,0:T(8,128)(2,1)S(1)}, bf16[144,504]{1,0:T(8,128)(2,1)S(1)}, u32[]{:S(2)}, u32[]{:S(2)}) collective-permute-start(bf16[144,504]{1,0:T(8,128)(2,1)S(1)} %collective-permute-done.refs_1_), channel_id=1, source_target_pairs={{0,1},{1,0},{2,3},{3,2},{4,5},{5,4},{6,7},{7,6},{8,9},{9,8},{10,11... | collective-permute-start | bytes 435464 | tf_op jit(solution)/shard_map/ppermute | solution.py:576
  27.6 5.3 %collective-permute-start.5 = (bf16[144,504]{1,0:T(8,128)(2,1)S(1)}, bf16[144,504]{1,0:T(8,128)(2,1)S(1)}, u32[]{:S(2)}, u32[]{:S(2)}) collective-permute-start(bf16[144,504]{1,0:T(8,128)(2,1)S(1)} %collective-permute-done.1.refs_2_), channel_id=1, source_target_pairs={{0,1},{1,0},{2,3},{3,2},{4,5},{5,4},{6,7},{7,6},{8,9},{9,8},{10,11... | collective-permute-start | bytes 435464 | tf_op jit(solution)/shard_map/ppermute | solution.py:576
  28.4 4.5 %collective-permute-start.6 = (bf16[144,504]{1,0:T(8,128)(2,1)S(1)}, bf16[144,504]{1,0:T(8,128)(2,1)S(1)}, u32[]{:S(2)}, u32[]{:S(2)}) collective-permute-start(bf16[144,504]{1,0:T(8,128)(2,1)S(1)} %collective-permute-done.2.refs_3_), channel_id=1, source_target_pairs={{0,1},{1,0},{2,3},{3,2},{4,5},{5,4},{6,7},{7,6},{8,9},{9,8},{10,11... | collective-permute-start | bytes 435464 | tf_op jit(solution)/shard_map/ppermute | solution.py:576
  28.6 0.9 %copy-start = (f32[16,3,1152]{2,0,1:T(8,128)S(1)}, f32[16,3,1152]{2,0,1:T(8,128)}, u32[]{:S(2)}) copy-start(f32[16,3,1152]{2,0,1:T(8,128)} %param.20) | copy-start | bytes 663556
  29.5 0.8 %copy-start.2 = (bf16[16,1152]{1,0:T(8,128)(2,1)S(1)}, bf16[16,1152]{1,0:T(8,128)(2,1)}, u32[]{:S(2)}) copy-start(bf16[16,1152]{1,0:T(8,128)(2,1)} %refs_18_.1) | copy-start | bytes 110596
  32.9 15.1 %copy-start.12 = (f32[24,48]{1,0:T(8,128)S(1)}, f32[24,48]{1,0:T(8,128)}, u32[]{:S(2)}) copy-start(f32[24,48]{1,0:T(8,128)} %get-tuple-element.40) | copy-start | bytes 13828
  33.0 31.1 %copy-start.1 = (f32[16,3,1152]{2,0,1:T(8,128)S(1)}, f32[16,3,1152]{2,0,1:T(8,128)}, u32[]{:S(2)}) copy-start(f32[16,3,1152]{2,0,1:T(8,128)} %param.20) | copy-start | bytes 663556
  33.0 31.1 %copy-start.3 = (bf16[16,1152]{1,0:T(8,128)(2,1)S(1)}, bf16[16,1152]{1,0:T(8,128)(2,1)}, u32[]{:S(2)}) copy-start(bf16[16,1152]{1,0:T(8,128)(2,1)} %refs_18_.1) | copy-start | bytes 110596
  33.0 31.1 %copy-start.4 = (bf16[1152,16]{0,1:T(8,128)(2,1)S(1)}, bf16[1152,16]{0,1:T(8,128)(2,1)}, u32[]{:S(2)}) copy-start(bf16[1152,16]{0,1:T(8,128)(2,1)} %param.27) | copy-start | bytes 110596
  40.7 23.3 %all-to-all-start.1 = ((bf16[16,72,240]{2,1,0:T(8,128)(2,1)}), bf16[16,72,240]{2,1,0:T(8,128)(2,1)S(1)}, u32[]{:S(2)}, u32[]{:S(2)}) async-start(bf16[16,72,240]{2,1,0:T(8,128)(2,1)} %shard_map.160), calls=%async_computation.1 | async-start | bytes 1179648 | tf_op jit(solution)/shard_map/all_to_all | solution.py:681
  46.0 12.0 %collective-permute-start.10 = (bf16[80,1152]{1,0:T(8,128)(2,1)S(1)}, bf16[80,1152]{1,0:T(8,128)(2,1)S(1)}, u32[]{:S(2)}, u32[]{:S(2)}) collective-permute-start(bf16[80,1152]{1,0:T(8,128)(2,1)S(1)} %slice.6), channel_id=1, source_target_pairs={{0,16},{16,0},{1,17},{17,1},{2,18},{18,2},{3,19},{19,3},{4,20},{20... | collective-permute-start | bytes 552968 | tf_op jit(solution)/shard_map/ppermute | solution.py:576
  48.0 6.7 %collective-permute-start.12 = (f32[24,48]{1,0:T(8,128)S(1)}, f32[24,48]{1,0:T(8,128)S(1)}, u32[]{:S(2)}, u32[]{:S(2)}) collective-permute-start(f32[24,48]{1,0:T(8,128)S(1)} %copy-done.12), channel_id=1, source_target_pairs={{4,0},{8,4},{12,8},{5,1},{9,5},{13,9},{6,2},{10,6},{14,10},{7,3},{... | collective-permute-start | bytes 13832 | tf_op jit(solution)/shard_map/ppermute | solution.py:682
  49.3 8.7 %collective-permute-start.11 = (bf16[64,1152]{1,0:T(8,128)(2,1)S(1)}, bf16[64,1152]{1,0:T(8,128)(2,1)S(1)}, u32[]{:S(2)}, u32[]{:S(2)}) collective-permute-start(bf16[64,1152]{1,0:T(8,128)(2,1)S(1)} %slice.7), channel_id=1, source_target_pairs={{0,2},{2,0},{1,3},{3,1},{4,6},{6,4},{5,7},{7,5},{8,10},{10,8},{9,1... | collective-permute-start | bytes 442376 | tf_op jit(solution)/shard_map/ppermute | solution.py:576
  50.9 9.6 %collective-permute-start.14 = (bf16[144,1152]{1,0:T(8,128)(2,1)S(1)}, bf16[144,1152]{1,0:T(8,128)(2,1)S(1)}, u32[]{:S(2)}, u32[]{:S(2)}) collective-permute-start(bf16[144,1152]{1,0:T(8,128)(2,1)S(1)} %collective-permute-done.8.refs_1_), channel_id=1, source_target_pairs={{0,1},{1,0},{2,3},{3,2},{4,5},{5,4},{6,7},{7,6},{8,9},{9,8},{10,11... | collective-permute-start | bytes 995336 | tf_op jit(solution)/shard_map/ppermute | solution.py:576
  50.9 9.6 %collective-permute-start.13 = (bf16[144,1152]{1,0:T(8,128)(2,1)S(1)}, bf16[144,1152]{1,0:T(8,128)(2,1)S(1)}, u32[]{:S(2)}, u32[]{:S(2)}) collective-permute-start(bf16[144,1152]{1,0:T(8,128)(2,1)S(1)} %shard_map.161.refs_0_), channel_id=1, source_target_pairs={{0,1},{1,0},{2,3},{3,2},{4,5},{5,4},{6,7},{7,6},{8,9},{9,8},{10,11... | collective-permute-start | bytes 995336 | tf_op jit(solution)/shard_map/ppermute | solution.py:576
  54.7 5.8 %collective-permute-start.15 = (bf16[144,1152]{1,0:T(8,128)(2,1)S(1)}, bf16[144,1152]{1,0:T(8,128)(2,1)S(1)}, u32[]{:S(2)}, u32[]{:S(2)}) collective-permute-start(bf16[144,1152]{1,0:T(8,128)(2,1)S(1)} %collective-permute-done.9.refs_2_), channel_id=1, source_target_pairs={{0,1},{1,0},{2,3},{3,2},{4,5},{5,4},{6,7},{7,6},{8,9},{9,8},{10,11... | collective-permute-start | bytes 995336 | tf_op jit(solution)/shard_map/ppermute | solution.py:576
  58.0 2.5 %collective-permute-start.16 = (bf16[80,1152]{1,0:T(8,128)(2,1)S(1)}, bf16[80,1152]{1,0:T(8,128)(2,1)S(1)}, u32[]{:S(2)}, u32[]{:S(2)}) collective-permute-start(bf16[80,1152]{1,0:T(8,128)(2,1)S(1)} %collective-permute-done.10.refs_3_), channel_id=1, source_target_pairs={{0,1},{1,0},{2,3},{3,2},{4,5},{5,4},{6,7},{7,6},{8,9},{9,8},{10,11... | collective-permute-start | bytes 552968 | tf_op jit(solution)/shard_map/ppermute | solution.py:576
  58.0 2.5 %collective-permute-start.17 = (bf16[64,1152]{1,0:T(8,128)(2,1)S(1)}, bf16[64,1152]{1,0:T(8,128)(2,1)S(1)}, u32[]{:S(2)}, u32[]{:S(2)}) collective-permute-start(bf16[64,1152]{1,0:T(8,128)(2,1)S(1)} %collective-permute-done.11.refs_4_), channel_id=1, source_target_pairs={{0,1},{1,0},{2,3},{3,2},{4,5},{5,4},{6,7},{7,6},{8,9},{9,8},{10,11... | collective-permute-start | bytes 442376 | tf_op jit(solution)/shard_map/ppermute | solution.py:576
  64.1 0.7 %copy-start.5 = (f32[24,192]{1,0:T(8,128)S(1)}, f32[24,192]{1,0:T(8,128)}, u32[]{:S(2)}) copy-start(f32[24,192]{1,0:T(8,128)} %get-tuple-element.45.refs_14_) | copy-start | bytes 55300
  64.8 0.7 copy-start.6
  65.5 0.7 copy-start.7
  71.4 1.2 %collective-permute-start.18 = (f32[8,240]{1,0:T(8,128)S(1)}, f32[8,240]{1,0:T(8,128)S(1)}, u32[]{:S(2)}, u32[]{:S(2)}) collective-permute-start(f32[8,240]{1,0:T(8,128)S(1)} %get-tuple-element.47), channel_id=1, source_target_pairs={{0,1},{1,0},{2,3},{3,2},{4,5},{5,4},{6,7},{7,6},{8,9},{9,8},{10,11... | collective-permute-start | bytes 23048 | tf_op jit(solution)/shard_map/ppermute | solution.py:576
  (2 other events, 1.3 us)

commit v8 on v7

--- a/solution.py
+++ b/solution.py
@@ -192,6 +192,7 @@
         "v": pl.BlockSpec(),
         "s": pl.BlockSpec(memory_space=pltpu.SMEM),
         "a": pl.BlockSpec(memory_space=pl.ANY),
+        "h": pl.BlockSpec(memory_space=pltpu.HBM),
     }
     many = isinstance(out_shapes, (list, tuple))
     return pl.pallas_call(
@@ -287,14 +288,12 @@
     span,
     mine,
     other,
-    level_source,
+    level_mod,
     embed,
     lhs,
     xin,
     rstd_out,
     mask_out,
-    level_mod,
-    sem,
 ):
     width = embed.shape[1]
     scenes, all_frames, rows, _ = xin.shape
@@ -303,8 +302,6 @@
     per_core = frames // 2
     tokens = mine.shape[2] // per_core
     core = place_of("cfg")
-    copy = pltpu.make_async_copy(level_source.at[pl.ds(0, 2)], level_mod, sem)
-    copy.start()
     weights = embed[...].astype(F32)
     weights = weights - jnp.mean(weights, axis=1, keepdims=True)
     length, step = width // (queues * toks), mine.shape[2]
@@ -336,7 +333,6 @@
     level_id = lax.broadcasted_iota(jnp.int32, (level_mod.shape[1], width), 0).astype(F32)
     shift_row = values + scenes
     fill = LANES - toks * tokens
-    copy.wait()
     for y in range(scenes):
         for q in range(queues):
             first = (y * queues + q) * toks
@@ -380,25 +376,20 @@
 
 def attend_kernel(frames, tokens, queues, *refs):
     pieces = refs[: 2 * queues]
-    lhs, xin, rstd_in, mask_in, gain_q, gain_k, out, whole, proj, kfac, vfac, att, own, sem = refs[
+    lhs, xin, rstd_in, mask_in, gain_q, gain_k, out, whole, proj, kfac, vfac, att = refs[
         2 * queues :
     ]
-    copy = pltpu.make_async_copy(pieces[0], own, sem)
-    copy.start()
     scenes, all_frames, rows, _ = xin.shape
     head_dim = gain_q.shape[1]
     window = (proj.shape[0] - all_frames) // 2
     span = 2 * window + 1
     q_at, core = place_of("queue"), place_of("cfg")
     part_rows = pieces[0].shape[0]
-    for k in reversed(range(queues)):
-        for side in reversed(range(2)):
+    for k in range(queues):
+        for side in range(2):
             owner = core if side == 0 else 1 - core
             first = pl.multiple_of(((q_at ^ k) * 2 + owner) * part_rows, 16)
             piece = pieces[side * queues + k]
-            if k == side == 0:
-                copy.wait()
-                piece = own
             whole[pl.ds(first, part_rows), :] = piece[:, piece.shape[1] - 3 * head_dim :]
     folded = jnp.dot(lhs[...], whole[...], preferred_element_type=F32)
     high, low = split_terms(folded, 2)
@@ -456,35 +447,72 @@
                 out[at] = jnp.concatenate(parts, axis=1).astype(BF16)
 
 
-def side_kernel(group, *refs):
-    *pieces, out, own, sem = refs
-    copy = pltpu.make_async_copy(pieces[0], own, sem)
-    copy.start()
+def stage_kernel(group, *refs):
+    *pieces, level_source, embed_source, out, own, level_mod, embed, sems = refs
+    copies = [
+        pltpu.make_async_copy(pieces[0], own, sems.at[0]),
+        pltpu.make_async_copy(level_source.at[pl.ds(0, 2)], level_mod, sems.at[1]),
+        pltpu.make_async_copy(embed_source, embed, sems.at[2]),
+    ]
+    for copy in copies:
+        copy.start()
     for k, piece in reversed(list(enumerate(pieces))):
         if k == 0:
-            copy.wait()
+            for copy in copies:
+                copy.wait()
             piece = own
         out[:, k * group : (k + 1) * group] = piece[:, :group]
 
 
-def hold_kernel(*refs):
-    refs[-1][...] = jnp.zeros(refs[-1].shape, F32)
-
-
-def finish_kernel(half, values, queues, *refs):
-    parts = [refs[:5], refs[5:10]]
-    attended, _, table, index = refs[10:14]
-    sources = refs[14:22]
-    mine, send, base, factor, noise_out, guide = refs[22:28]
-    held = refs[28:36]
-    scratch, mixed, sems = refs[36:]
+def ready_kernel(values, half, *refs):
+    sources, table, index = refs[:8], refs[8], refs[9]
+    left, right, base, factor, noise_out, guide, final_out = refs[10:17]
+    held, sems = refs[17:25], refs[25]
     copies = []
     for i, (source, to) in enumerate(zip(sources, held)):
         source = source.at[2] if i == 3 else source
         copies.append(pltpu.make_async_copy(source, to, sems.at[i]))
     for copy in copies:
         copy.start()
+    for copy in copies:
+        copy.wait()
     packed, following, cond, gates, embed, final_gain, final_w, noise = held
+    levels_all, width = gates.shape
+    info = jnp.concatenate([packed[...], following[...]], axis=1)
+    lanes = info.shape[1]
+    ones = jnp.ones((16, lanes), BF16)
+    zero = jnp.zeros((13, width), BF16)
+    left[...] = jnp.concatenate(
+        [embed[...]]
+        + split_terms(cond[...], 3)
+        + [zero]
+        + split_terms(gates[...], 3)
+        + split_terms(final_gain[...], 3)
+        + [zero],
+        axis=0,
+    )
+    level = info[values : values + 1]
+    one_hot = (lax.broadcasted_iota(jnp.int32, (levels_all, lanes), 0).astype(F32) == level).astype(
+        F32
+    ).astype(BF16)
+    right[...] = jnp.concatenate(
+        [info[:values].astype(BF16), ones, one_hot, one_hot, one_hot, ones], axis=0
+    )
+    own = pl.multiple_of(place_of("cfg") * half, half)
+    current = noise_sigma((level + 1.0) / levels_all)
+    upcoming = noise_sigma(level / levels_all)
+    factor[...] = jnp.broadcast_to(upcoming - current, factor.shape)
+    base[...] = jnp.concatenate(
+        [packed[pl.ds(own, half), :], following[pl.ds(own, half), :]], axis=1
+    )
+    noise_out[...] = noise[...]
+    final_out[...] = final_w[...]
+    guide[...] = jnp.full(guide.shape, table[index[0]], F32)
+
+
+def finish_kernel(half, values, queues, *refs):
+    parts = [refs[:5], refs[5:10]]
+    attended, left, right, final_w, mine, send, scratch, mixed = refs[10:]
     scene, q_at, tok, core = (place_of(a) for a in ("scene", "queue", "tok", "cfg"))
     group = parts[0][0].shape[1] // queues
     columns = parts[0][0].shape[0]
@@ -515,24 +543,10 @@
             at = (c * queues + k) * columns
             mixed[pl.ds(pl.multiple_of(first, 8), columns), :] = total[at : at + columns]
 
-    for copy in copies:
-        copy.wait()
-    levels_all, width = gates.shape
-    info = jnp.concatenate([packed[...], following[...]], axis=1)
-    lanes = info.shape[1]
-    vec = info[:values].astype(BF16)
-    ones = jnp.ones((16, lanes), BF16)
-    zero = jnp.zeros((13, width), BF16)
-    weights = jnp.concatenate([embed[...]] + split_terms(cond[...], 3) + [zero], axis=0)
-    emb = dot_tn(weights, jnp.concatenate([vec, ones], axis=0))
-    level = info[values : values + 1]
-    one_hot = (lax.broadcasted_iota(jnp.int32, (levels_all, lanes), 0).astype(F32) == level).astype(
-        F32
-    ).astype(BF16)
-    gate_terms = jnp.concatenate(split_terms(gates[...], 3), axis=0)
-    gate = dot_tn(gate_terms, jnp.concatenate([one_hot] * 3, axis=0))
-    gain_terms = jnp.concatenate(split_terms(final_gain[...], 3) + [zero], axis=0)
-    gain = dot_tn(gain_terms, ones)
+    first, last = values + 16, left.shape[0] - 16
+    emb = dot_tn(left[:first], right[:first])
+    gate = dot_tn(left[first:last], right[first:last])
+    gain = dot_tn(left[last:], right[last:])
     summed = emb + gate * mixed[...]
     center = jnp.mean(summed, axis=0, keepdims=True)
     deviate = summed - center
@@ -543,15 +557,6 @@
     other = pl.multiple_of((1 - core) * half, half)
     mine[...] = scratch[pl.ds(own, half), :]
     send[...] = scratch[pl.ds(other, half), :]
-
-    current = noise_sigma((level + 1.0) / levels_all)
-    upcoming = noise_sigma(level / levels_all)
-    factor[...] = jnp.broadcast_to(upcoming - current, factor.shape)
-    base[...] = jnp.concatenate(
-        [packed[pl.ds(own, half), :], following[pl.ds(own, half), :]], axis=1
-    )
-    noise_out[...] = noise[...]
-    guide[...] = jnp.full(guide.shape, table[index[0]], F32)
 
 
 def update_kernel(mine, partner, base, factor, noise, guide, vel, new):
@@ -640,12 +645,17 @@
     shares = lax.all_to_all(copies, ("scene", "queue", "tok"), 0, 0)
     other_shares = swapped(shares, "cfg", 1)
 
-    part = kernel_call(
-        functools.partial(side_kernel, group),
-        jax.ShapeDtypeStruct((local_rows, queues * group), BF16),
-        "a" + "v" * (queues - 1),
-        [pltpu.VMEM(chunk.shape, BF16), pltpu.SemaphoreType.DMA],
-    )(*near)
+    part, own, level_rows, embed_held = kernel_call(
+        functools.partial(stage_kernel, group),
+        [
+            jax.ShapeDtypeStruct((local_rows, queues * group), BF16),
+            chunk,
+            jax.ShapeDtypeStruct((2, levels_all, width), F32),
+            jax.ShapeDtypeStruct(embed_weight.shape, BF16),
+        ],
+        "h" + "v" * (queues - 1) + "hh",
+        [pltpu.SemaphoreType.DMA((3,))],
+    )(*near, mods, embed_weight)
     part_tok, part_scene = swapped(part, "tok", 1), swapped(part, "scene", 1)
 
     lhs, xin, rstd, masks = kernel_call(
@@ -656,25 +666,22 @@
             jax.ShapeDtypeStruct((all_frames, 1, lanes), F32),
             jax.ShapeDtypeStruct((scenes, all_frames, rows - values, LANES), F32),
         ],
-        "vvav",
-        [pltpu.VMEM((2, levels_all, width), F32), pltpu.SemaphoreType.DMA],
+        "vvvv",
         bytes_accessed=8_000_000,
-    )(shares, other_shares, mods, embed_weight)
+    )(shares, other_shares, level_rows, embed_held)
     attended = kernel_call(
         functools.partial(attend_kernel, frames, tokens, queues),
         jax.ShapeDtypeStruct((chips, head_dim, row_lanes), BF16),
-        "a" + "v" * (2 * queues + 5),
+        "v" * (2 * queues + 6),
         [
             pltpu.VMEM((width, 3 * head_dim), BF16),
             pltpu.VMEM((all_frames + 2 * window, 3 * head_dim, lanes), F32),
             pltpu.VMEM((all_frames + 2 * window, 1, lanes), F32),
             pltpu.VMEM((all_frames + 2 * window, 1, lanes), F32),
             pltpu.VMEM((all_frames, scenes, head_dim, LANES), F32),
-            pltpu.VMEM(chunk.shape, BF16),
-            pltpu.SemaphoreType.DMA,
         ],
         bytes_accessed=100_000_000,
-    )(*near, *far, lhs, xin, rstd, masks, query_gain[None], key_gain[None])
+    )(own, *near[1:], *far, lhs, xin, rstd, masks, query_gain[None], key_gain[None])
     attended, part, part_tok, part_scene, first = lax.optimization_barrier(
         (attended, part, part_tok, part_scene, first)
     )
@@ -683,12 +690,6 @@
     cut = -(-local_rows // 32) * 16
     upper = swapped(part_tok[:cut], "scene", 1)
     lower = swapped(part_scene[cut:], "tok", 1)
-    token = kernel_call(hold_kernel, jax.ShapeDtypeStruct((8, LANES), F32), "a")(following)
-    upper, lower, token = lax.optimization_barrier((upper, lower, token))
-    away = [part, part_tok, part_scene, upper, lower]
-    away_far = [swapped(piece, "cfg", 1) for piece in away]
-    received = received.reshape(width, row_lanes)
-
     half = values // 2
     half_shape = jax.ShapeDtypeStruct((half, row_lanes), F32)
     smalls = (
@@ -704,22 +705,33 @@
     places = [
         pltpu.VMEM(a.shape[1:] if i == 3 else a.shape, a.dtype) for i, a in enumerate(smalls)
     ]
-    mine, send, *rest = kernel_call(
-        functools.partial(finish_kernel, half, values, queues),
-        [half_shape] * 4
-        + [
+    terms = values + 16 + 3 * levels_all + 16
+    left, right, *rest, final_held = kernel_call(
+        functools.partial(ready_kernel, values, half),
+        [
+            jax.ShapeDtypeStruct((terms, width), BF16),
+            jax.ShapeDtypeStruct((terms, row_lanes), BF16),
+            half_shape,
+            half_shape,
             jax.ShapeDtypeStruct(fresh_noise.shape, F32),
             jax.ShapeDtypeStruct((8, LANES), F32),
+            jax.ShapeDtypeStruct((values, width), BF16),
         ],
-        "v" * 12 + "ss" + "a" * len(smalls),
-        places
-        + [
-            pltpu.VMEM((values, row_lanes), F32),
-            pltpu.VMEM((width, row_lanes), F32),
-            pltpu.SemaphoreType.DMA((len(smalls),)),
-        ],
+        "ha" + "h" * 6 + "ss",
+        places + [pltpu.SemaphoreType.DMA((len(smalls),))],
+    )(*smalls, guide_table, guide_index)
+    upper, lower, right = lax.optimization_barrier((upper, lower, right))
+    away = [part, part_tok, part_scene, upper, lower]
+    away_far = [swapped(piece, "cfg", 1) for piece in away]
+    received = received.reshape(width, row_lanes)
+
+    mine, send = kernel_call(
+        functools.partial(finish_kernel, half, values, queues),
+        [half_shape] * 2,
+        "v" * 14,
+        [pltpu.VMEM((values, row_lanes), F32), pltpu.VMEM((width, row_lanes), F32)],
         bytes_accessed=8_000_000,
-    )(*away, *away_far, received, token, guide_table, guide_index, *smalls)
+    )(*away, *away_far, received, left, right, final_held)
     partner = swapped(send, "cfg", 1)
     shape = jax.ShapeDtypeStruct((frames, half, tokens), F32)
     return kernel_call(update_kernel, [shape, shape], "v" * 6)(mine, partner, *rest)

time: 74 us -> 71.7 us (0.969)
  the two profiles are of different devices: /device:TPU:0 before, /device:TPU:9 now
where the time goes in v8:
time: 71.7 us; the launch traced here: 71.2 us
  starting transfers between devices  29.8 us (42%)
  Pallas kernels  17.3 us (24%)
  waiting for transfers between devices  16.9 us (24%)
  local copies, waits for them, and re-layouts  5.6 us (8%)
  between operations  1.59 us (2%)
    ppermute x18, starting transfers between devices, swapped(): return lax.ppermute(value, axis, [(i, i ^ mask) for i in range(count)])  16.3 us
    ppermute x18, waiting for transfers between devices, swapped(): return lax.ppermute(value, axis, [(i, i ^ mask) for i in range(count)])  8.85 us
    ppermute x1, waiting for transfers between devices, on_device_heads(): lax.ppermute(first, 'queue', [(i + 1, i) for i in range(queues - 1)])  8.02 us
    all_to_all x1, starting transfers between devices, on_device_heads(): shares = lax.all_to_all(copies, ('scene', 'queue', 'tok'), 0, 0)  7.56 us
    pallas_call x1, Pallas kernels, on_device_heads(): kernel_call(functools.partial(attend_kernel, frames, tokens, queues), jax...  6.8 us
    unnamed x42, local copies, waits for them, and re-layouts  5.57 us
    all_to_all x1, starting transfers between devices, on_device_heads(): received = lax.all_to_all(attended, ('tok', 'scene', 'queue'), 0, 0)  3.76 us
    pallas_call x1, Pallas kernels, on_device_heads(): kernel_call(functools.partial(pack_kernel, head_dim, per_core), [chunk] *...  2.92 us
  transfers between devices with their start and end apart: 21, of which 5 were waited for; matrix products, arithmetic and copies ran while one was open for 0% of the time, Pallas kernels for 16%

profile of v8, /device:TPU:9, one launch (start us, length us, event | category | flops | bytes accessed | tf_op | source)
XLA Modules:
  0.0 71.2 jit_solution(15182661188173346531)
XLA Ops:
  0.7 2.9 %shard_map.158 = (bf16[144,504]{1,0:T(8,128)(2,1)}, bf16[144,504]{1,0:T(8,128)(2,1)}, bf16[144,504]{1,0:T(8,128)(2,1)}, bf16[144,504]{1,0:T(8,128)(2,1)}, bf16[1...) custom-call(f32[4,16,48]{2,1,0:T(8,128)} %latents.1, s32[1,4]{1,0:T(1,128)} %bitcast.16, ...), custom_call_target="tpu_custom_call" | custom-call | flops 1000000 | bytes 8000000 | tf_op jit(solution)/shard_map/pallas_call | solution.py:622
  3.6 2.5 %collective-permute-start.1 = (bf16[144,504]{1,0:T(8,128)(2,1)}, bf16[144,504]{1,0:T(8,128)(2,1)S(1)}, u32[]{:S(2)}, u32[]{:S(2)}) collective-permute-start(bf16[144,504]{1,0:T(8,128)(2,1)} %get-tuple-element.36), channel_id=1, source_target_pairs={{0,8},{4,12},{8,0},{12,4},{1,9},{5,13},{9,1},{13,5},{2,10},{6,14},... | collective-permute-start | bytes 435464 | tf_op jit(solution)/shard_map/ppermute | solution.py:581
  6.2 7.6 %all-to-all-start = ((bf16[16,32,96]{2,1,0:T(8,128)(2,1)}), bf16[16,32,96]{2,1,0:T(8,128)(2,1)S(1)}, u32[]{:S(2)}, u32[]{:S(2)}) async-start(bf16[16,32,96]{2,1,0:T(8,128)(2,1)} %get-tuple-element.39), calls=%async_computation | async-start | bytes 262144 | tf_op jit(solution)/shard_map/all_to_all | solution.py:645
  13.8 5.9 %collective-permute-done.2.refs_3_ = bf16[144,504]{1,0:T(8,128)(2,1)S(1)} collective-permute-done((bf16[144,504]{1,0:T(8,128)(2,1)}, bf16[144,504]{1,0:T(8,128)(2,1)S(1)}, u32[]{:S(2)}, u32[]{:S(2)}) %collective-permute-start.2) | collective-permute-done | bytes 145184 | tf_op jit(solution)/shard_map/ppermute | solution.py:581
  19.7 0.9 %copy-done = f32[16,3,1152]{2,0,1:T(8,128)S(1)} copy-done((f32[16,3,1152]{2,0,1:T(8,128)S(1)}, f32[16,3,1152]{2,0,1:T(8,128)}, u32[]{:S(2)}) %copy-start) | copy-done | bytes 221208
  20.7 0.8 %copy-done.2 = bf16[16,1152]{1,0:T(8,128)(2,1)S(1)} copy-done((bf16[16,1152]{1,0:T(8,128)(2,1)S(1)}, bf16[16,1152]{1,0:T(8,128)(2,1)}, u32[]{:S(2)}) %copy-start.2) | copy-done | bytes 36888
  21.4 0.9 %shard_map.159 = (bf16[144,1152]{1,0:T(8,128)(2,1)S(1)}, bf16[144,504]{1,0:T(8,128)(2,1)S(1)}, f32[2,16,1152]{2,1,0:T(8,128)S(1)}, bf16[16,1152]{1,0:T(8,128)(2,1)S(1)}) custom-call(bf16[144,504]{1,0:T(8,128)(2,1)} %get-tuple-element.34.refs_0_, bf16[144,504]{1,0:T(8,128)(2,1)S(1)} %collective-permute-done.refs_1_, ...), custom_call_target="tpu_custom_call" | custom-call | flops 1000000 | bytes 1000000 | tf_op jit(solution)/shard_map/pallas_call | solution.py:648
  22.4 1.3 %collective-permute-start.8 = (bf16[144,1152]{1,0:T(8,128)(2,1)S(1)}, bf16[144,1152]{1,0:T(8,128)(2,1)S(1)}, u32[]{:S(2)}, u32[]{:S(2)}) collective-permute-start(bf16[144,1152]{1,0:T(8,128)(2,1)S(1)} %get-tuple-element.48.refs_0_), channel_id=1, source_target_pairs={{0,2},{2,0},{1,3},{3,1},{4,6},{6,4},{5,7},{7,5},{8,10},{10,8},{9,1... | collective-permute-start | bytes 995336 | tf_op jit(solution)/shard_map/ppermute | solution.py:581
  23.7 1.4 %collective-permute-start.9 = (bf16[144,1152]{1,0:T(8,128)(2,1)S(1)}, bf16[144,1152]{1,0:T(8,128)(2,1)S(1)}, u32[]{:S(2)}, u32[]{:S(2)}) collective-permute-start(bf16[144,1152]{1,0:T(8,128)(2,1)S(1)} %get-tuple-element.48.refs_0_), channel_id=1, source_target_pairs={{0,16},{16,0},{1,17},{17,1},{2,18},{18,2},{3,19},{19,3},{4,20},{20... | collective-permute-start | bytes 995336 | tf_op jit(solution)/shard_map/ppermute | solution.py:581
  25.1 3.5 %collective-permute-start.3 = (bf16[144,504]{1,0:T(8,128)(2,1)}, bf16[144,504]{1,0:T(8,128)(2,1)S(1)}, u32[]{:S(2)}, u32[]{:S(2)}) collective-permute-start(bf16[144,504]{1,0:T(8,128)(2,1)} %get-tuple-element.34.refs_0_), channel_id=1, source_target_pairs={{0,1},{1,0},{2,3},{3,2},{4,5},{5,4},{6,7},{7,6},{8,9},{9,8},{10,11... | collective-permute-start | bytes 435464 | tf_op jit(solution)/shard_map/ppermute | solution.py:581
  28.6 0.5 collective-permute-start.4
  29.1 0.8 %collective-permute-done.3.refs_4_ = bf16[144,504]{1,0:T(8,128)(2,1)S(1)} collective-permute-done((bf16[144,504]{1,0:T(8,128)(2,1)}, bf16[144,504]{1,0:T(8,128)(2,1)S(1)}, u32[]{:S(2)}, u32[]{:S(2)}) %collective-permute-start.3) | collective-permute-done | bytes 145184 | tf_op jit(solution)/shard_map/ppermute | solution.py:581
  30.5 2.4 %shard_map.160 = (bf16[1024,1152]{1,0:T(8,128)(2,1)S(1)}, bf16[2,16,32,128]{3,2,1,0:T(8,128)(2,1)S(1)}, f32[16,1,256]{2,1,0:T(1,128)S(1)}, f32[2,16,16,128]{3,2,1,0:T(8,128)S(1)}) custom-call(bf16[16,32,96]{2,1,0:T(8,128)(2,1)S(1)} %all-to-all-done.mine, bf16[16,32,96]{2,1,0:T(8,128)(2,1)S(1)} %collective-permute-done.7.other, ...), custom_call_target="tpu_custom_call" | custom-call | flops 1000000 | bytes 8000000 | tf_op jit(solution)/shard_map/pallas_call | solution.py:661
  33.0 6.8 %shard_map.161 = bf16[16,72,240]{2,1,0:T(8,128)(2,1)} custom-call(bf16[144,504]{1,0:T(8,128)(2,1)S(1)} %get-tuple-element.38.refs_0_, bf16[144,504]{1,0:T(8,128)(2,1)S(1)} %collective-permute-done.refs_1_, bf16[144,504]{1,0:T(8,128)(2,1)S(1)} %collective-permute-done.1.refs_2_, bf16[144,504]{1,0:T(8,128)(2,1)S(1)} %collective-permute-done.2.refs_3_, ...), custom_call_target="tpu_custom_call" | custom-call | flops 1000000 | bytes 100000000 | tf_op jit(solution)/shard_map/pallas_call | solution.py:672
  39.8 3.8 %all-to-all-start.1 = ((bf16[16,72,240]{2,1,0:T(8,128)(2,1)}), bf16[16,72,240]{2,1,0:T(8,128)(2,1)S(1)}, u32[]{:S(2)}, u32[]{:S(2)}) async-start(bf16[16,72,240]{2,1,0:T(8,128)(2,1)} %shard_map.161), calls=%async_computation.1 | async-start | bytes 1179648 | tf_op jit(solution)/shard_map/all_to_all | solution.py:688
  43.6 1.2 %collective-permute-start.10 = (bf16[80,1152]{1,0:T(8,128)(2,1)S(1)}, bf16[80,1152]{1,0:T(8,128)(2,1)S(1)}, u32[]{:S(2)}, u32[]{:S(2)}) collective-permute-start(bf16[80,1152]{1,0:T(8,128)(2,1)S(1)} %slice.6), channel_id=1, source_target_pairs={{0,16},{16,0},{1,17},{17,1},{2,18},{18,2},{3,19},{19,3},{4,20},{20... | collective-permute-start | bytes 552968 | tf_op jit(solution)/shard_map/ppermute | solution.py:581
  44.9 2.2 %collective-permute-start.12 = (f32[24,48]{1,0:T(8,128)S(1)}, f32[24,48]{1,0:T(8,128)S(1)}, u32[]{:S(2)}, u32[]{:S(2)}) collective-permute-start(f32[24,48]{1,0:T(8,128)S(1)} %copy-done.20), channel_id=1, source_target_pairs={{4,0},{8,4},{12,8},{5,1},{9,5},{13,9},{6,2},{10,6},{14,10},{7,3},{... | collective-permute-start | bytes 13832 | tf_op jit(solution)/shard_map/ppermute | solution.py:689
  47.1 1.3 %collective-permute-start.11 = (bf16[64,1152]{1,0:T(8,128)(2,1)S(1)}, bf16[64,1152]{1,0:T(8,128)(2,1)S(1)}, u32[]{:S(2)}, u32[]{:S(2)}) collective-permute-start(bf16[64,1152]{1,0:T(8,128)(2,1)S(1)} %slice.7), channel_id=1, source_target_pairs={{0,2},{2,0},{1,3},{3,1},{4,6},{6,4},{5,7},{7,5},{8,10},{10,8},{9,1... | collective-permute-start | bytes 442376 | tf_op jit(solution)/shard_map/ppermute | solution.py:581
  48.3 1.8 %collective-permute-start.14 = (bf16[144,1152]{1,0:T(8,128)(2,1)S(1)}, bf16[144,1152]{1,0:T(8,128)(2,1)S(1)}, u32[]{:S(2)}, u32[]{:S(2)}) collective-permute-start(bf16[144,1152]{1,0:T(8,128)(2,1)S(1)} %collective-permute-done.8.refs_1_), channel_id=1, source_target_pairs={{0,1},{1,0},{2,3},{3,2},{4,5},{5,4},{6,7},{7,6},{8,9},{9,8},{10,11... | collective-permute-start | bytes 995336 | tf_op jit(solution)/shard_map/ppermute | solution.py:581
  50.1 8.0 %collective-permute-done.12.refs_1_ = f32[24,48]{1,0:T(8,128)S(1)} collective-permute-done((f32[24,48]{1,0:T(8,128)S(1)}, f32[24,48]{1,0:T(8,128)S(1)}, u32[]{:S(2)}, u32[]{:S(2)}) %collective-permute-start.12) | collective-permute-done | bytes 4640 | tf_op jit(solution)/shard_map/ppermute | solution.py:689
  58.1 1.4 %collective-permute-start.15 = (bf16[144,1152]{1,0:T(8,128)(2,1)S(1)}, bf16[144,1152]{1,0:T(8,128)(2,1)S(1)}, u32[]{:S(2)}, u32[]{:S(2)}) collective-permute-start(bf16[144,1152]{1,0:T(8,128)(2,1)S(1)} %collective-permute-done.9.refs_2_), channel_id=1, source_target_pairs={{0,1},{1,0},{2,3},{3,2},{4,5},{5,4},{6,7},{7,6},{8,9},{9,8},{10,11... | collective-permute-start | bytes 995336 | tf_op jit(solution)/shard_map/ppermute | solution.py:581
  60.2 0.6 copy-done.18
  60.9 1.0 %shard_map.162 = (bf16[96,1152]{1,0:T(8,128)(2,1)S(1)}, bf16[96,240]{1,0:T(8,128)(2,1)S(1)}, f32[8,240]{1,0:T(8,128)S(1)}, f32[8,240]{1,0:T(8,128)S(1)}, f32[8,4...) custom-call(f32[24,192]{1,0:T(8,128)S(1)} %copy-done.7, ...), custom_call_target="tpu_custom_call" | custom-call | flops 1000000 | bytes 1000000 | tf_op jit(solution)/shard_map/pallas_call | solution.py:709
  61.9 0.6 copy-done.4
  62.5 0.6 copy-done.9
  63.1 0.6 copy-done.11
  63.7 0.6 copy-done.14
  64.8 1.1 %collective-permute-done.17.refs_9_ = bf16[64,1152]{1,0:T(8,128)(2,1)S(1)} collective-permute-done((bf16[64,1152]{1,0:T(8,128)(2,1)S(1)}, bf16[64,1152]{1,0:T(8,128)(2,1)S(1)}, u32[]{:S(2)}, u32[]{:S(2)}) %collective-permute-start.17) | collective-permute-done | bytes 147488 | tf_op jit(solution)/shard_map/ppermute | solution.py:581
  66.0 0.8 %copy-done.5 = bf16[16,1152]{1,0:T(8,128)(2,1)S(1)} copy-done((bf16[16,1152]{1,0:T(8,128)(2,1)S(1)}, bf16[16,1152]{1,0:T(8,128)(2,1)}, u32[]{:S(2)}) %copy-start.5) | copy-done | bytes 36888
  66.7 2.5 %shard_map.163 = (f32[8,240]{1,0:T(8,128)S(1)}, f32[8,240]{1,0:T(8,128)S(1)}) custom-call(bf16[144,1152]{1,0:T(8,128)(2,1)S(1)} %get-tuple-element.48.refs_0_, bf16[144,1152]{1,0:T(8,128)(2,1)S(1)} %collective-permute-done.8.refs_1_, bf16[144,1152]{1,0:T(8,128)(2,1)S(1)} %collective-permute-done.9.refs_2_, ...), custom_call_target="tpu_custom_call" | custom-call | flops 1000000 | bytes 8000000 | tf_op jit(solution)/shard_map/pallas_call | solution.py:728
  69.5 0.9 %collective-permute-done.18.partner = f32[8,240]{1,0:T(8,128)S(1)} collective-permute-done((f32[8,240]{1,0:T(8,128)S(1)}, f32[8,240]{1,0:T(8,128)S(1)}, u32[]{:S(2)}, u32[]{:S(2)}) %collective-permute-start.18) | collective-permute-done | bytes 7712 | tf_op jit(solution)/shard_map/ppermute | solution.py:581
  70.4 0.7 %shard_map.164 = (f32[4,8,48]{2,1,0:T(8,128)}, f32[4,8,48]{2,1,0:T(8,128)}) custom-call(f32[8,240]{1,0:T(8,128)S(1)} %get-tuple-element.60.mine, f32[8,240]{1,0:T(8,128)S(1)} %collective-permute-done.18.partner, f32[8,240]{1,0:T(8,128)S(1)} %copy-done.10, f32[8,240]{1,0:T(8,128)S(1)} %copy-done.12, f32[8,48]{1,0:T(8,128)S(1)} %get-tuple-element.64.noise, ...), custom_call_target="tpu_custom_call" | custom-call | flops 1000000 | bytes 1000000 | tf_op jit(solution)/shard_map/pallas_call | solution.py:737
  (62 shorter events, 1.6 us)
Async XLA Ops:
  0.6 32.3 %copy-start.16 = (f32[72]{0:T(128)S(1)}, f32[72]{0:T(128)}, u32[]{:S(2)}) copy-start(f32[72]{0:T(128)} %param.23) | copy-start | bytes 868
  0.6 32.3 %copy-start.17 = (f32[72]{0:T(128)S(1)}, f32[72]{0:T(128)}, u32[]{:S(2)}) copy-start(f32[72]{0:T(128)} %param.24) | copy-start | bytes 868
  3.6 10.2 %collective-permute-start = (bf16[144,504]{1,0:T(8,128)(2,1)}, bf16[144,504]{1,0:T(8,128)(2,1)S(1)}, u32[]{:S(2)}, u32[]{:S(2)}) collective-permute-start(bf16[144,504]{1,0:T(8,128)(2,1)} %get-tuple-element.35), channel_id=1, source_target_pairs={{0,4},{4,0},{8,12},{12,8},{1,5},{5,1},{9,13},{13,9},{2,6},{6,2},{1... | collective-permute-start | bytes 435464 | tf_op jit(solution)/shard_map/ppermute | solution.py:581
  3.6 10.2 %collective-permute-start.1 = (bf16[144,504]{1,0:T(8,128)(2,1)}, bf16[144,504]{1,0:T(8,128)(2,1)S(1)}, u32[]{:S(2)}, u32[]{:S(2)}) collective-permute-start(bf16[144,504]{1,0:T(8,128)(2,1)} %get-tuple-element.36), channel_id=1, source_target_pairs={{0,8},{4,12},{8,0},{12,4},{1,9},{5,13},{9,1},{13,5},{2,10},{6,14},... | collective-permute-start | bytes 435464 | tf_op jit(solution)/shard_map/ppermute | solution.py:581
  6.1 13.7 %collective-permute-start.2 = (bf16[144,504]{1,0:T(8,128)(2,1)}, bf16[144,504]{1,0:T(8,128)(2,1)S(1)}, u32[]{:S(2)}, u32[]{:S(2)}) collective-permute-start(bf16[144,504]{1,0:T(8,128)(2,1)} %get-tuple-element.37), channel_id=1, source_target_pairs={{0,12},{4,8},{8,4},{12,0},{1,13},{5,9},{9,5},{13,1},{2,14},{6,10},... | collective-permute-start | bytes 435464 | tf_op jit(solution)/shard_map/ppermute | solution.py:581
  6.2 22.4 %all-to-all-start = ((bf16[16,32,96]{2,1,0:T(8,128)(2,1)}), bf16[16,32,96]{2,1,0:T(8,128)(2,1)S(1)}, u32[]{:S(2)}, u32[]{:S(2)}) async-start(bf16[16,32,96]{2,1,0:T(8,128)(2,1)} %get-tuple-element.39), calls=%async_computation | async-start | bytes 262144 | tf_op jit(solution)/shard_map/all_to_all | solution.py:645
  22.4 17.4 %collective-permute-start.8 = (bf16[144,1152]{1,0:T(8,128)(2,1)S(1)}, bf16[144,1152]{1,0:T(8,128)(2,1)S(1)}, u32[]{:S(2)}, u32[]{:S(2)}) collective-permute-start(bf16[144,1152]{1,0:T(8,128)(2,1)S(1)} %get-tuple-element.48.refs_0_), channel_id=1, source_target_pairs={{0,2},{2,0},{1,3},{3,1},{4,6},{6,4},{5,7},{7,5},{8,10},{10,8},{9,1... | collective-permute-start | bytes 995336 | tf_op jit(solution)/shard_map/ppermute | solution.py:581
  23.7 16.2 %collective-permute-start.9 = (bf16[144,1152]{1,0:T(8,128)(2,1)S(1)}, bf16[144,1152]{1,0:T(8,128)(2,1)S(1)}, u32[]{:S(2)}, u32[]{:S(2)}) collective-permute-start(bf16[144,1152]{1,0:T(8,128)(2,1)S(1)} %get-tuple-element.48.refs_0_), channel_id=1, source_target_pairs={{0,16},{16,0},{1,17},{17,1},{2,18},{18,2},{3,19},{19,3},{4,20},{20... | collective-permute-start | bytes 995336 | tf_op jit(solution)/shard_map/ppermute | solution.py:581
  25.1 4.9 %collective-permute-start.3 = (bf16[144,504]{1,0:T(8,128)(2,1)}, bf16[144,504]{1,0:T(8,128)(2,1)S(1)}, u32[]{:S(2)}, u32[]{:S(2)}) collective-permute-start(bf16[144,504]{1,0:T(8,128)(2,1)} %get-tuple-element.34.refs_0_), channel_id=1, source_target_pairs={{0,1},{1,0},{2,3},{3,2},{4,5},{5,4},{6,7},{7,6},{8,9},{9,8},{10,11... | collective-permute-start | bytes 435464 | tf_op jit(solution)/shard_map/ppermute | solution.py:581
  28.6 1.7 %collective-permute-start.7 = (bf16[16,32,96]{2,1,0:T(8,128)(2,1)S(1)}, bf16[16,32,96]{2,1,0:T(8,128)(2,1)S(1)}, u32[]{:S(2)}, u32[]{:S(2)}) collective-permute-start(bf16[16,32,96]{2,1,0:T(8,128)(2,1)S(1)} %all-to-all-done.mine), channel_id=1, source_target_pairs={{0,1},{1,0},{2,3},{3,2},{4,5},{5,4},{6,7},{7,6},{8,9},{9,8},{10,11... | collective-permute-start | bytes 294920 | tf_op jit(solution)/shard_map/ppermute | solution.py:581
  28.6 4.2 %collective-permute-start.4 = (bf16[144,504]{1,0:T(8,128)(2,1)S(1)}, bf16[144,504]{1,0:T(8,128)(2,1)S(1)}, u32[]{:S(2)}, u32[]{:S(2)}) collective-permute-start(bf16[144,504]{1,0:T(8,128)(2,1)S(1)} %collective-permute-done.refs_1_), channel_id=1, source_target_pairs={{0,1},{1,0},{2,3},{3,2},{4,5},{5,4},{6,7},{7,6},{8,9},{9,8},{10,11... | collective-permute-start | bytes 435464 | tf_op jit(solution)/shard_map/ppermute | solution.py:581
  30.0 2.9 %collective-permute-start.5 = (bf16[144,504]{1,0:T(8,128)(2,1)S(1)}, bf16[144,504]{1,0:T(8,128)(2,1)S(1)}, u32[]{:S(2)}, u32[]{:S(2)}) collective-permute-start(bf16[144,504]{1,0:T(8,128)(2,1)S(1)} %collective-permute-done.1.refs_2_), channel_id=1, source_target_pairs={{0,1},{1,0},{2,3},{3,2},{4,5},{5,4},{6,7},{7,6},{8,9},{9,8},{10,11... | collective-permute-start | bytes 435464 | tf_op jit(solution)/shard_map/ppermute | solution.py:581
  30.3 2.6 %collective-permute-start.6 = (bf16[144,504]{1,0:T(8,128)(2,1)S(1)}, bf16[144,504]{1,0:T(8,128)(2,1)S(1)}, u32[]{:S(2)}, u32[]{:S(2)}) collective-permute-start(bf16[144,504]{1,0:T(8,128)(2,1)S(1)} %collective-permute-done.2.refs_3_), channel_id=1, source_target_pairs={{0,1},{1,0},{2,3},{3,2},{4,5},{5,4},{6,7},{7,6},{8,9},{9,8},{10,11... | collective-permute-start | bytes 435464 | tf_op jit(solution)/shard_map/ppermute | solution.py:581
  32.9 11.9 %copy-start.20 = (f32[24,48]{1,0:T(8,128)S(1)}, f32[24,48]{1,0:T(8,128)}, u32[]{:S(2)}) copy-start(f32[24,48]{1,0:T(8,128)} %get-tuple-element.52) | copy-start | bytes 13828
  32.9 26.6 %copy-start.19 = (f32[1152]{0:T(1024)S(1)}, f32[1152]{0:T(1024)}, u32[]{:S(2)}) copy-start(f32[1152]{0:T(1024)} %param.26) | copy-start | bytes 13828
  32.9 27.2 %copy-start.1 = (f32[16,3,1152]{2,0,1:T(8,128)S(1)}, f32[16,3,1152]{2,0,1:T(8,128)}, u32[]{:S(2)}) copy-start(f32[16,3,1152]{2,0,1:T(8,128)} %param.20) | copy-start | bytes 663556
  33.0 27.2 %copy-start.3 = (bf16[16,1152]{1,0:T(8,128)(2,1)S(1)}, bf16[16,1152]{1,0:T(8,128)(2,1)}, u32[]{:S(2)}) copy-start(bf16[16,1152]{1,0:T(8,128)(2,1)} %refs_4_.1) | copy-start | bytes 110596
  33.0 27.2 %copy-start.6 = (bf16[1152,16]{0,1:T(8,128)(2,1)S(1)}, bf16[1152,16]{0,1:T(8,128)(2,1)}, u32[]{:S(2)}) copy-start(bf16[1152,16]{0,1:T(8,128)(2,1)} %param.27) | copy-start | bytes 110596
  33.0 27.2 %copy-start.7 = (f32[24,192]{1,0:T(8,128)S(1)}, f32[24,192]{1,0:T(8,128)}, u32[]{:S(2)}) copy-start(f32[24,192]{1,0:T(8,128)} %get-tuple-element.51.refs_0_) | copy-start | bytes 55300
  33.0 27.2 %copy-start.8 = (f32[1,1152]{1,0:T(1,128)S(1)}, f32[1,1152]{1,0:T(1,128)}, u32[]{:S(2)}) copy-start(f32[1,1152]{1,0:T(1,128)} %refs_2_.1) | copy-start | bytes 13828
  33.0 27.2 %copy-start.13 = (f32[8,48]{1,0:T(8,128)S(1)}, f32[8,48]{1,0:T(8,128)}, u32[]{:S(2)}) copy-start(f32[8,48]{1,0:T(8,128)} %refs_7_.1) | copy-start | bytes 4612
  39.8 26.1 %all-to-all-start.1 = ((bf16[16,72,240]{2,1,0:T(8,128)(2,1)}), bf16[16,72,240]{2,1,0:T(8,128)(2,1)S(1)}, u32[]{:S(2)}, u32[]{:S(2)}) async-start(bf16[16,72,240]{2,1,0:T(8,128)(2,1)} %shard_map.161), calls=%async_computation.1 | async-start | bytes 1179648 | tf_op jit(solution)/shard_map/all_to_all | solution.py:688
  43.6 20.7 %collective-permute-start.10 = (bf16[80,1152]{1,0:T(8,128)(2,1)S(1)}, bf16[80,1152]{1,0:T(8,128)(2,1)S(1)}, u32[]{:S(2)}, u32[]{:S(2)}) collective-permute-start(bf16[80,1152]{1,0:T(8,128)(2,1)S(1)} %slice.6), channel_id=1, source_target_pairs={{0,16},{16,0},{1,17},{17,1},{2,18},{18,2},{3,19},{19,3},{4,20},{20... | collective-permute-start | bytes 552968 | tf_op jit(solution)/shard_map/ppermute | solution.py:581
  44.9 13.3 %collective-permute-start.12 = (f32[24,48]{1,0:T(8,128)S(1)}, f32[24,48]{1,0:T(8,128)S(1)}, u32[]{:S(2)}, u32[]{:S(2)}) collective-permute-start(f32[24,48]{1,0:T(8,128)S(1)} %copy-done.20), channel_id=1, source_target_pairs={{4,0},{8,4},{12,8},{5,1},{9,5},{13,9},{6,2},{10,6},{14,10},{7,3},{... | collective-permute-start | bytes 13832 | tf_op jit(solution)/shard_map/ppermute | solution.py:689
  47.1 17.2 %collective-permute-start.11 = (bf16[64,1152]{1,0:T(8,128)(2,1)S(1)}, bf16[64,1152]{1,0:T(8,128)(2,1)S(1)}, u32[]{:S(2)}, u32[]{:S(2)}) collective-permute-start(bf16[64,1152]{1,0:T(8,128)(2,1)S(1)} %slice.7), channel_id=1, source_target_pairs={{0,2},{2,0},{1,3},{3,1},{4,6},{6,4},{5,7},{7,5},{8,10},{10,8},{9,1... | collective-permute-start | bytes 442376 | tf_op jit(solution)/shard_map/ppermute | solution.py:581
  48.3 17.6 %collective-permute-start.14 = (bf16[144,1152]{1,0:T(8,128)(2,1)S(1)}, bf16[144,1152]{1,0:T(8,128)(2,1)S(1)}, u32[]{:S(2)}, u32[]{:S(2)}) collective-permute-start(bf16[144,1152]{1,0:T(8,128)(2,1)S(1)} %collective-permute-done.8.refs_1_), channel_id=1, source_target_pairs={{0,1},{1,0},{2,3},{3,2},{4,5},{5,4},{6,7},{7,6},{8,9},{9,8},{10,11... | collective-permute-start | bytes 995336 | tf_op jit(solution)/shard_map/ppermute | solution.py:581
  50.1 15.8 %collective-permute-start.13 = (bf16[144,1152]{1,0:T(8,128)(2,1)S(1)}, bf16[144,1152]{1,0:T(8,128)(2,1)S(1)}, u32[]{:S(2)}, u32[]{:S(2)}) collective-permute-start(bf16[144,1152]{1,0:T(8,128)(2,1)S(1)} %get-tuple-element.48.refs_0_), channel_id=1, source_target_pairs={{0,1},{1,0},{2,3},{3,2},{4,5},{5,4},{6,7},{7,6},{8,9},{9,8},{10,11... | collective-permute-start | bytes 995336 | tf_op jit(solution)/shard_map/ppermute | solution.py:581
  58.1 7.8 %collective-permute-start.15 = (bf16[144,1152]{1,0:T(8,128)(2,1)S(1)}, bf16[144,1152]{1,0:T(8,128)(2,1)S(1)}, u32[]{:S(2)}, u32[]{:S(2)}) collective-permute-start(bf16[144,1152]{1,0:T(8,128)(2,1)S(1)} %collective-permute-done.9.refs_2_), channel_id=1, source_target_pairs={{0,1},{1,0},{2,3},{3,2},{4,5},{5,4},{6,7},{7,6},{8,9},{9,8},{10,11... | collective-permute-start | bytes 995336 | tf_op jit(solution)/shard_map/ppermute | solution.py:581
  64.3 1.7 %collective-permute-start.16 = (bf16[80,1152]{1,0:T(8,128)(2,1)S(1)}, bf16[80,1152]{1,0:T(8,128)(2,1)S(1)}, u32[]{:S(2)}, u32[]{:S(2)}) collective-permute-start(bf16[80,1152]{1,0:T(8,128)(2,1)S(1)} %collective-permute-done.10.refs_3_), channel_id=1, source_target_pairs={{0,1},{1,0},{2,3},{3,2},{4,5},{5,4},{6,7},{7,6},{8,9},{9,8},{10,11... | collective-permute-start | bytes 552968 | tf_op jit(solution)/shard_map/ppermute | solution.py:581
  64.3 1.6 %collective-permute-start.17 = (bf16[64,1152]{1,0:T(8,128)(2,1)S(1)}, bf16[64,1152]{1,0:T(8,128)(2,1)S(1)}, u32[]{:S(2)}, u32[]{:S(2)}) collective-permute-start(bf16[64,1152]{1,0:T(8,128)(2,1)S(1)} %collective-permute-done.11.refs_4_), channel_id=1, source_target_pairs={{0,1},{1,0},{2,3},{3,2},{4,5},{5,4},{6,7},{7,6},{8,9},{9,8},{10,11... | collective-permute-start | bytes 442376 | tf_op jit(solution)/shard_map/ppermute | solution.py:581
  65.9 4.5 %copy-start.15 = (f32[8,128]{1,0:T(8,128)S(1)}, f32[8,128]{1,0:T(8,128)}, u32[]{:S(2)}) copy-start(f32[8,128]{1,0:T(8,128)} %copy-done.14) | copy-start | bytes 12292
  69.2 1.2 %collective-permute-start.18 = (f32[8,240]{1,0:T(8,128)S(1)}, f32[8,240]{1,0:T(8,128)S(1)}, u32[]{:S(2)}, u32[]{:S(2)}) collective-permute-start(f32[8,240]{1,0:T(8,128)S(1)} %get-tuple-element.61), channel_id=1, source_target_pairs={{0,1},{1,0},{2,3},{3,2},{4,5},{5,4},{6,7},{7,6},{8,9},{9,8},{10,11... | collective-permute-start | bytes 23048 | tf_op jit(solution)/shard_map/ppermute | solution.py:581
  (10 other events, 12.9 us)

commit v9 on v8

--- a/solution.py
+++ b/solution.py
@@ -296,7 +296,8 @@
     mask_out,
 ):
     width = embed.shape[1]
-    scenes, all_frames, rows, _ = xin.shape
+    scenes, all_frames = mask_out.shape[:2]
+    rows = xin.shape[1] // scenes
     queues = all_frames // frames
     toks = mine.shape[0] // (scenes * queues)
     per_core = frames // 2
@@ -350,7 +351,7 @@
                 scale = jnp.sum(jnp.where(chosen, level_mod[1], 0.0), axis=0, keepdims=True)
                 block = basis * (1.0 + scale)
                 block = jnp.where((wide_id == shift_row) | (wide_id == shift_row + 1), shift, block)
-                to = (y * all_frames + f) * rows
+                to = (f * scenes + y) * rows
                 lhs[to : to + rows, :] = block.astype(BF16)
                 info = jnp.concatenate(info + [jnp.ones((info[0].shape[0], fill), F32)], axis=1)
                 mask_out[y, f] = info[values : values + mask_out.shape[2]]
@@ -370,7 +371,9 @@
                 high = std.astype(BF16).astype(F32)
                 vec = jnp.where(row_id == shift_row, high, vec)
                 vec = jnp.where(row_id == shift_row + 1, std - high, vec)
-                xin[y, f] = vec.astype(BF16)
+                blank = jnp.zeros(vec.shape, F32)
+                blocks = [vec if n == y else blank for n in range(scenes)]
+                xin[f, y * rows : (y + 1) * rows] = jnp.concatenate(blocks, axis=1).astype(BF16)
                 rstd_out[f, :, y * LANES : (y + 1) * LANES] = rstd
 
 
@@ -379,7 +382,8 @@
     lhs, xin, rstd_in, mask_in, gain_q, gain_k, out, whole, proj, kfac, vfac, att = refs[
         2 * queues :
     ]
-    scenes, all_frames, rows, _ = xin.shape
+    scenes, all_frames = mask_in.shape[:2]
+    rows = xin.shape[1]
     head_dim = gain_q.shape[1]
     window = (proj.shape[0] - all_frames) // 2
     span = 2 * window + 1
@@ -401,18 +405,18 @@
             proj[at] = jnp.zeros(proj.shape[1:], F32)
             kfac[at] = jnp.zeros(kfac.shape[1:], F32)
             vfac[at] = jnp.zeros(vfac.shape[1:], F32)
-    for y in range(scenes):
-        lane = slice(y * LANES, (y + 1) * LANES)
-        for f in range(all_frames):
-            first = (y * all_frames + f) * rows
-            piece = slice(first, first + rows)
-            made = dot_tn(high[piece], xin[y, f]) + dot_tn(low[piece], xin[y, f])
-            proj[f + window, :, lane] = made
-            rstd = rstd_in[f, :, lane]
-            keys = made[head_dim : 2 * head_dim]
-            square = jnp.mean(keys * keys, axis=0, keepdims=True)
-            kfac[f + window, :, lane] = rstd * lax.rsqrt(rstd * rstd * square + EPS_NORM)
-            vfac[f + window, :, lane] = rstd
+    for f in range(all_frames):
+        piece = slice(f * rows, (f + 1) * rows)
+        made = dot_tn(
+            jnp.concatenate([high[piece], low[piece]], axis=0),
+            jnp.concatenate([xin[f], xin[f]], axis=0),
+        )
+        proj[f + window] = made
+        rstd = rstd_in[f]
+        keys = made[head_dim : 2 * head_dim]
+        square = jnp.mean(keys * keys, axis=0, keepdims=True)
+        kfac[f + window] = rstd * lax.rsqrt(rstd * rstd * square + EPS_NORM)
+        vfac[f + window] = rstd
 
     def one_frame(f, carry):
         for y in range(scenes):
@@ -431,7 +435,7 @@
                 part = jnp.exp(score) * mask_in[y, f, o : o + 1, :]
                 norm = norm + part
                 total = total + (part * vfac[f + o, :, lane]) * proj[f + o, 2 * head_dim :, lane]
-            att[f, y] = total / norm
+            att[f, y] = total * (1.0 / norm)
         return carry
 
     lax.fori_loop(0, all_frames, one_frame, 0)
@@ -443,7 +447,7 @@
                     att[min(q * frames + i, all_frames - 1), y, :, t * tokens : (t + 1) * tokens]
                     for i in range(frames + 1)
                 ]
-                at = (t * scenes + y) * queues + q
+                at = (t * queues + q) * scenes + y
                 out[at] = jnp.concatenate(parts, axis=1).astype(BF16)
 
 
@@ -531,8 +535,11 @@
             for c in range(2):
                 for k in range(queues):
                     pieces += weights_of(c, t, y, k)
-            first = ((tok ^ t) * 2 + (scene ^ y)) * group
-            rows = attended[pl.ds(pl.multiple_of(first, 16), group), :]
+            rows = [
+                attended[((tok ^ t) * queues + k) * 2 + (scene ^ y)].astype(F32)
+                for k in range(queues)
+            ]
+            rows = jnp.concatenate(rows, axis=0).astype(BF16)
             term = jnp.dot(jnp.concatenate(pieces, axis=0), rows, preferred_element_type=F32)
             made = term if made is None else made + term
         made = made.astype(BF16).astype(F32)
@@ -662,7 +669,7 @@
         functools.partial(prepare_kernel, frames, values, span),
         [
             jax.ShapeDtypeStruct((scenes * all_frames * rows, width), BF16),
-            jax.ShapeDtypeStruct((scenes, all_frames, rows, LANES), BF16),
+            jax.ShapeDtypeStruct((all_frames, scenes * rows, lanes), BF16),
             jax.ShapeDtypeStruct((all_frames, 1, lanes), F32),
             jax.ShapeDtypeStruct((scenes, all_frames, rows - values, LANES), F32),
         ],
@@ -685,7 +692,7 @@
     attended, part, part_tok, part_scene, first = lax.optimization_barrier(
         (attended, part, part_tok, part_scene, first)
     )
-    received = lax.all_to_all(attended, ("tok", "scene", "queue"), 0, 0)
+    received = lax.all_to_all(attended, ("tok", "queue", "scene"), 0, 0)
     following = lax.ppermute(first, "queue", [(i + 1, i) for i in range(queues - 1)])
     cut = -(-local_rows // 32) * 16
     upper = swapped(part_tok[:cut], "scene", 1)
@@ -723,7 +730,6 @@
     upper, lower, right = lax.optimization_barrier((upper, lower, right))
     away = [part, part_tok, part_scene, upper, lower]
     away_far = [swapped(piece, "cfg", 1) for piece in away]
-    received = received.reshape(width, row_lanes)
 
     mine, send = kernel_call(
         functools.partial(finish_kernel, half, values, queues),

time: 71.7 us -> 71 us (level)
  transfers between devices with their start and end apart: 21 -> 21, of which waited for: 5 -> 5; matrix products, arithmetic and copies ran while one was open for 0% -> 0% of each run, Pallas kernels for 16% -> 15%
where the time goes in v9:
time: 71 us; the launch traced here: 70.5 us
  starting transfers between devices  30.1 us (42%)
  Pallas kernels  16.6 us (23%)
  waiting for transfers between devices  16.6 us (23%)
  local copies, waits for them, and re-layouts  5.6 us (8%)
  between operations  1.58 us (2%)
    ppermute x18, starting transfers between devices, swapped(): return lax.ppermute(value, axis, [(i, i ^ mask) for i in range(count)])  16.6 us
    ppermute x18, waiting for transfers between devices, swapped(): return lax.ppermute(value, axis, [(i, i ^ mask) for i in range(count)])  8.85 us
    ppermute x1, waiting for transfers between devices, on_device_heads(): lax.ppermute(first, 'queue', [(i + 1, i) for i in range(queues - 1)])  7.72 us
    all_to_all x1, starting transfers between devices, on_device_heads(): shares = lax.all_to_all(copies, ('scene', 'queue', 'tok'), 0, 0)  7.56 us
    pallas_call x1, Pallas kernels, on_device_heads(): kernel_call(functools.partial(attend_kernel, frames, tokens, queues), jax...  6.12 us
    unnamed x42, local copies, waits for them, and re-layouts  5.57 us
    all_to_all x1, starting transfers between devices, on_device_heads(): received = lax.all_to_all(attended, ('tok', 'queue', 'scene'), 0, 0)  3.75 us
    pallas_call x1, Pallas kernels, on_device_heads(): kernel_call(functools.partial(pack_kernel, head_dim, per_core), [chunk] *...  2.92 us
  transfers between devices with their start and end apart: 21, of which 5 were waited for; matrix products, arithmetic and copies ran while one was open for 0% of the time, Pallas kernels for 15%

profile of v9, /device:TPU:9, one launch (start us, length us, event | category | flops | bytes accessed | tf_op | source)
XLA Modules:
  0.0 70.5 jit_solution(3649867229973632384)
XLA Ops:
  0.7 2.9 %shard_map.158 = (bf16[144,504]{1,0:T(8,128)(2,1)}, bf16[144,504]{1,0:T(8,128)(2,1)}, bf16[144,504]{1,0:T(8,128)(2,1)}, bf16[144,504]{1,0:T(8,128)(2,1)}, bf16[1...) custom-call(f32[4,16,48]{2,1,0:T(8,128)} %latents.1, s32[1,4]{1,0:T(1,128)} %bitcast.14, ...), custom_call_target="tpu_custom_call" | custom-call | flops 1000000 | bytes 8000000 | tf_op jit(solution)/shard_map/pallas_call | solution.py:629
  3.6 2.5 %collective-permute-start.1 = (bf16[144,504]{1,0:T(8,128)(2,1)}, bf16[144,504]{1,0:T(8,128)(2,1)S(1)}, u32[]{:S(2)}, u32[]{:S(2)}) collective-permute-start(bf16[144,504]{1,0:T(8,128)(2,1)} %get-tuple-element.36), channel_id=1, source_target_pairs={{0,8},{4,12},{8,0},{12,4},{1,9},{5,13},{9,1},{13,5},{2,10},{6,14},... | collective-permute-start | bytes 435464 | tf_op jit(solution)/shard_map/ppermute | solution.py:588
  6.2 7.6 %all-to-all-start = ((bf16[16,32,96]{2,1,0:T(8,128)(2,1)}), bf16[16,32,96]{2,1,0:T(8,128)(2,1)S(1)}, u32[]{:S(2)}, u32[]{:S(2)}) async-start(bf16[16,32,96]{2,1,0:T(8,128)(2,1)} %get-tuple-element.39), calls=%async_computation | async-start | bytes 262144 | tf_op jit(solution)/shard_map/all_to_all | solution.py:652
  13.8 5.9 %collective-permute-done.2.refs_3_ = bf16[144,504]{1,0:T(8,128)(2,1)S(1)} collective-permute-done((bf16[144,504]{1,0:T(8,128)(2,1)}, bf16[144,504]{1,0:T(8,128)(2,1)S(1)}, u32[]{:S(2)}, u32[]{:S(2)}) %collective-permute-start.2) | collective-permute-done | bytes 145184 | tf_op jit(solution)/shard_map/ppermute | solution.py:588
  19.7 0.9 %copy-done = f32[16,3,1152]{2,0,1:T(8,128)S(1)} copy-done((f32[16,3,1152]{2,0,1:T(8,128)S(1)}, f32[16,3,1152]{2,0,1:T(8,128)}, u32[]{:S(2)}) %copy-start) | copy-done | bytes 221208
  20.7 0.8 %copy-done.2 = bf16[16,1152]{1,0:T(8,128)(2,1)S(1)} copy-done((bf16[16,1152]{1,0:T(8,128)(2,1)S(1)}, bf16[16,1152]{1,0:T(8,128)(2,1)}, u32[]{:S(2)}) %copy-start.2) | copy-done | bytes 36888
  21.4 0.9 %shard_map.159 = (bf16[144,1152]{1,0:T(8,128)(2,1)S(1)}, bf16[144,504]{1,0:T(8,128)(2,1)S(1)}, f32[2,16,1152]{2,1,0:T(8,128)S(1)}, bf16[16,1152]{1,0:T(8,128)(2,1)S(1)}) custom-call(bf16[144,504]{1,0:T(8,128)(2,1)} %get-tuple-element.34.refs_0_, bf16[144,504]{1,0:T(8,128)(2,1)S(1)} %collective-permute-done.refs_1_, ...), custom_call_target="tpu_custom_call" | custom-call | flops 1000000 | bytes 1000000 | tf_op jit(solution)/shard_map/pallas_call | solution.py:655
  22.4 1.3 %collective-permute-start.8 = (bf16[144,1152]{1,0:T(8,128)(2,1)S(1)}, bf16[144,1152]{1,0:T(8,128)(2,1)S(1)}, u32[]{:S(2)}, u32[]{:S(2)}) collective-permute-start(bf16[144,1152]{1,0:T(8,128)(2,1)S(1)} %get-tuple-element.48.refs_0_), channel_id=1, source_target_pairs={{0,2},{2,0},{1,3},{3,1},{4,6},{6,4},{5,7},{7,5},{8,10},{10,8},{9,1... | collective-permute-start | bytes 995336 | tf_op jit(solution)/shard_map/ppermute | solution.py:588
  23.7 1.4 %collective-permute-start.9 = (bf16[144,1152]{1,0:T(8,128)(2,1)S(1)}, bf16[144,1152]{1,0:T(8,128)(2,1)S(1)}, u32[]{:S(2)}, u32[]{:S(2)}) collective-permute-start(bf16[144,1152]{1,0:T(8,128)(2,1)S(1)} %get-tuple-element.48.refs_0_), channel_id=1, source_target_pairs={{0,16},{16,0},{1,17},{17,1},{2,18},{18,2},{3,19},{19,3},{4,20},{20... | collective-permute-start | bytes 995336 | tf_op jit(solution)/shard_map/ppermute | solution.py:588
  25.1 3.5 %collective-permute-start.3 = (bf16[144,504]{1,0:T(8,128)(2,1)}, bf16[144,504]{1,0:T(8,128)(2,1)S(1)}, u32[]{:S(2)}, u32[]{:S(2)}) collective-permute-start(bf16[144,504]{1,0:T(8,128)(2,1)} %get-tuple-element.34.refs_0_), channel_id=1, source_target_pairs={{0,1},{1,0},{2,3},{3,2},{4,5},{5,4},{6,7},{7,6},{8,9},{9,8},{10,11... | collective-permute-start | bytes 435464 | tf_op jit(solution)/shard_map/ppermute | solution.py:588
  28.6 0.5 collective-permute-start.4
  29.1 0.8 %collective-permute-done.3.refs_4_ = bf16[144,504]{1,0:T(8,128)(2,1)S(1)} collective-permute-done((bf16[144,504]{1,0:T(8,128)(2,1)}, bf16[144,504]{1,0:T(8,128)(2,1)S(1)}, u32[]{:S(2)}, u32[]{:S(2)}) %collective-permute-start.3) | collective-permute-done | bytes 145184 | tf_op jit(solution)/shard_map/ppermute | solution.py:588
  30.5 2.4 %shard_map.160 = (bf16[1024,1152]{1,0:T(8,128)(2,1)S(1)}, bf16[16,64,256]{2,1,0:T(8,128)(2,1)S(1)}, f32[16,1,256]{2,1,0:T(1,128)S(1)}, f32[2,16,16,128]{3,2,1,0:T(8,128)S(1)}) custom-call(bf16[16,32,96]{2,1,0:T(8,128)(2,1)S(1)} %all-to-all-done.mine, bf16[16,32,96]{2,1,0:T(8,128)(2,1)S(1)} %collective-permute-done.7.other, ...), custom_call_target="tpu_custom_call" | custom-call | flops 1000000 | bytes 8000000 | tf_op jit(solution)/shard_map/pallas_call | solution.py:668
  33.0 6.1 %shard_map.161 = bf16[16,72,240]{2,1,0:T(8,128)(2,1)} custom-call(bf16[144,504]{1,0:T(8,128)(2,1)S(1)} %get-tuple-element.38.refs_0_, bf16[144,504]{1,0:T(8,128)(2,1)S(1)} %collective-permute-done.refs_1_, bf16[144,504]{1,0:T(8,128)(2,1)S(1)} %collective-permute-done.1.refs_2_, bf16[144,504]{1,0:T(8,128)(2,1)S(1)} %collective-permute-done.2.refs_3_, ...), custom_call_target="tpu_custom_call" | custom-call | flops 1000000 | bytes 100000000 | tf_op jit(solution)/shard_map/pallas_call | solution.py:679
  39.2 3.8 %all-to-all-start.1 = ((bf16[16,72,240]{2,1,0:T(8,128)(2,1)}), bf16[16,72,240]{2,1,0:T(8,128)(2,1)S(1)}, u32[]{:S(2)}, u32[]{:S(2)}) async-start(bf16[16,72,240]{2,1,0:T(8,128)(2,1)} %shard_map.161), calls=%async_computation.1 | async-start | bytes 1179648 | tf_op jit(solution)/shard_map/all_to_all | solution.py:695
  42.9 1.2 %collective-permute-start.10 = (bf16[80,1152]{1,0:T(8,128)(2,1)S(1)}, bf16[80,1152]{1,0:T(8,128)(2,1)S(1)}, u32[]{:S(2)}, u32[]{:S(2)}) collective-permute-start(bf16[80,1152]{1,0:T(8,128)(2,1)S(1)} %slice.6), channel_id=1, source_target_pairs={{0,16},{16,0},{1,17},{17,1},{2,18},{18,2},{3,19},{19,3},{4,20},{20... | collective-permute-start | bytes 552968 | tf_op jit(solution)/shard_map/ppermute | solution.py:588
  44.2 2.2 %collective-permute-start.12 = (f32[24,48]{1,0:T(8,128)S(1)}, f32[24,48]{1,0:T(8,128)S(1)}, u32[]{:S(2)}, u32[]{:S(2)}) collective-permute-start(f32[24,48]{1,0:T(8,128)S(1)} %copy-done.20), channel_id=1, source_target_pairs={{4,0},{8,4},{12,8},{5,1},{9,5},{13,9},{6,2},{10,6},{14,10},{7,3},{... | collective-permute-start | bytes 13832 | tf_op jit(solution)/shard_map/ppermute | solution.py:696
  46.4 1.3 %collective-permute-start.11 = (bf16[64,1152]{1,0:T(8,128)(2,1)S(1)}, bf16[64,1152]{1,0:T(8,128)(2,1)S(1)}, u32[]{:S(2)}, u32[]{:S(2)}) collective-permute-start(bf16[64,1152]{1,0:T(8,128)(2,1)S(1)} %slice.7), channel_id=1, source_target_pairs={{0,2},{2,0},{1,3},{3,1},{4,6},{6,4},{5,7},{7,5},{8,10},{10,8},{9,1... | collective-permute-start | bytes 442376 | tf_op jit(solution)/shard_map/ppermute | solution.py:588
  47.6 1.8 %collective-permute-start.14 = (bf16[144,1152]{1,0:T(8,128)(2,1)S(1)}, bf16[144,1152]{1,0:T(8,128)(2,1)S(1)}, u32[]{:S(2)}, u32[]{:S(2)}) collective-permute-start(bf16[144,1152]{1,0:T(8,128)(2,1)S(1)} %collective-permute-done.8.refs_1_), channel_id=1, source_target_pairs={{0,1},{1,0},{2,3},{3,2},{4,5},{5,4},{6,7},{7,6},{8,9},{9,8},{10,11... | collective-permute-start | bytes 995336 | tf_op jit(solution)/shard_map/ppermute | solution.py:588
  49.4 7.7 %collective-permute-done.12.refs_1_ = f32[24,48]{1,0:T(8,128)S(1)} collective-permute-done((f32[24,48]{1,0:T(8,128)S(1)}, f32[24,48]{1,0:T(8,128)S(1)}, u32[]{:S(2)}, u32[]{:S(2)}) %collective-permute-start.12) | collective-permute-done | bytes 4640 | tf_op jit(solution)/shard_map/ppermute | solution.py:696
  57.1 1.7 %collective-permute-start.15 = (bf16[144,1152]{1,0:T(8,128)(2,1)S(1)}, bf16[144,1152]{1,0:T(8,128)(2,1)S(1)}, u32[]{:S(2)}, u32[]{:S(2)}) collective-permute-start(bf16[144,1152]{1,0:T(8,128)(2,1)S(1)} %collective-permute-done.9.refs_2_), channel_id=1, source_target_pairs={{0,1},{1,0},{2,3},{3,2},{4,5},{5,4},{6,7},{7,6},{8,9},{9,8},{10,11... | collective-permute-start | bytes 995336 | tf_op jit(solution)/shard_map/ppermute | solution.py:588
  59.6 0.6 copy-done.16
  60.2 1.0 %shard_map.162 = (bf16[96,1152]{1,0:T(8,128)(2,1)S(1)}, bf16[96,240]{1,0:T(8,128)(2,1)S(1)}, f32[8,240]{1,0:T(8,128)S(1)}, f32[8,240]{1,0:T(8,128)S(1)}, f32[8,4...) custom-call(f32[24,192]{1,0:T(8,128)S(1)} %copy-done.7, ...), custom_call_target="tpu_custom_call" | custom-call | flops 1000000 | bytes 1000000 | tf_op jit(solution)/shard_map/pallas_call | solution.py:716
  61.2 0.6 copy-done.4
  61.8 0.6 copy-done.9
  62.4 0.6 copy-done.11
  63.0 0.6 copy-done.14
  64.1 1.1 %collective-permute-done.17.refs_9_ = bf16[64,1152]{1,0:T(8,128)(2,1)S(1)} collective-permute-done((bf16[64,1152]{1,0:T(8,128)(2,1)S(1)}, bf16[64,1152]{1,0:T(8,128)(2,1)S(1)}, u32[]{:S(2)}, u32[]{:S(2)}) %collective-permute-start.17) | collective-permute-done | bytes 147488 | tf_op jit(solution)/shard_map/ppermute | solution.py:588
  65.3 0.8 %copy-done.5 = bf16[16,1152]{1,0:T(8,128)(2,1)S(1)} copy-done((bf16[16,1152]{1,0:T(8,128)(2,1)S(1)}, bf16[16,1152]{1,0:T(8,128)(2,1)}, u32[]{:S(2)}) %copy-start.5) | copy-done | bytes 36888
  66.0 2.5 %shard_map.163 = (f32[8,240]{1,0:T(8,128)S(1)}, f32[8,240]{1,0:T(8,128)S(1)}) custom-call(bf16[144,1152]{1,0:T(8,128)(2,1)S(1)} %get-tuple-element.48.refs_0_, bf16[144,1152]{1,0:T(8,128)(2,1)S(1)} %collective-permute-done.8.refs_1_, bf16[144,1152]{1,0:T(8,128)(2,1)S(1)} %collective-permute-done.9.refs_2_, ...), custom_call_target="tpu_custom_call" | custom-call | flops 1000000 | bytes 8000000 | tf_op jit(solution)/shard_map/pallas_call | solution.py:734
  68.8 0.9 %collective-permute-done.18.partner = f32[8,240]{1,0:T(8,128)S(1)} collective-permute-done((f32[8,240]{1,0:T(8,128)S(1)}, f32[8,240]{1,0:T(8,128)S(1)}, u32[]{:S(2)}, u32[]{:S(2)}) %collective-permute-start.18) | collective-permute-done | bytes 7712 | tf_op jit(solution)/shard_map/ppermute | solution.py:588
  69.7 0.7 %shard_map.164 = (f32[4,8,48]{2,1,0:T(8,128)}, f32[4,8,48]{2,1,0:T(8,128)}) custom-call(f32[8,240]{1,0:T(8,128)S(1)} %get-tuple-element.60.mine, f32[8,240]{1,0:T(8,128)S(1)} %collective-permute-done.18.partner, f32[8,240]{1,0:T(8,128)S(1)} %copy-done.10, f32[8,240]{1,0:T(8,128)S(1)} %copy-done.12, f32[8,48]{1,0:T(8,128)S(1)} %get-tuple-element.64.noise, ...), custom_call_target="tpu_custom_call" | custom-call | flops 1000000 | bytes 1000000 | tf_op jit(solution)/shard_map/pallas_call | solution.py:743
  (62 shorter events, 1.6 us)
Async XLA Ops:
  0.6 32.3 %copy-start.17 = (f32[72]{0:T(128)S(1)}, f32[72]{0:T(128)}, u32[]{:S(2)}) copy-start(f32[72]{0:T(128)} %param.23) | copy-start | bytes 868
  0.6 32.3 %copy-start.18 = (f32[72]{0:T(128)S(1)}, f32[72]{0:T(128)}, u32[]{:S(2)}) copy-start(f32[72]{0:T(128)} %param.24) | copy-start | bytes 868
  3.6 10.2 %collective-permute-start = (bf16[144,504]{1,0:T(8,128)(2,1)}, bf16[144,504]{1,0:T(8,128)(2,1)S(1)}, u32[]{:S(2)}, u32[]{:S(2)}) collective-permute-start(bf16[144,504]{1,0:T(8,128)(2,1)} %get-tuple-element.35), channel_id=1, source_target_pairs={{0,4},{4,0},{8,12},{12,8},{1,5},{5,1},{9,13},{13,9},{2,6},{6,2},{1... | collective-permute-start | bytes 435464 | tf_op jit(solution)/shard_map/ppermute | solution.py:588
  3.6 10.2 %collective-permute-start.1 = (bf16[144,504]{1,0:T(8,128)(2,1)}, bf16[144,504]{1,0:T(8,128)(2,1)S(1)}, u32[]{:S(2)}, u32[]{:S(2)}) collective-permute-start(bf16[144,504]{1,0:T(8,128)(2,1)} %get-tuple-element.36), channel_id=1, source_target_pairs={{0,8},{4,12},{8,0},{12,4},{1,9},{5,13},{9,1},{13,5},{2,10},{6,14},... | collective-permute-start | bytes 435464 | tf_op jit(solution)/shard_map/ppermute | solution.py:588
  6.1 13.7 %collective-permute-start.2 = (bf16[144,504]{1,0:T(8,128)(2,1)}, bf16[144,504]{1,0:T(8,128)(2,1)S(1)}, u32[]{:S(2)}, u32[]{:S(2)}) collective-permute-start(bf16[144,504]{1,0:T(8,128)(2,1)} %get-tuple-element.37), channel_id=1, source_target_pairs={{0,12},{4,8},{8,4},{12,0},{1,13},{5,9},{9,5},{13,1},{2,14},{6,10},... | collective-permute-start | bytes 435464 | tf_op jit(solution)/shard_map/ppermute | solution.py:588
  6.2 22.4 %all-to-all-start = ((bf16[16,32,96]{2,1,0:T(8,128)(2,1)}), bf16[16,32,96]{2,1,0:T(8,128)(2,1)S(1)}, u32[]{:S(2)}, u32[]{:S(2)}) async-start(bf16[16,32,96]{2,1,0:T(8,128)(2,1)} %get-tuple-element.39), calls=%async_computation | async-start | bytes 262144 | tf_op jit(solution)/shard_map/all_to_all | solution.py:652
  22.4 16.8 %collective-permute-start.8 = (bf16[144,1152]{1,0:T(8,128)(2,1)S(1)}, bf16[144,1152]{1,0:T(8,128)(2,1)S(1)}, u32[]{:S(2)}, u32[]{:S(2)}) collective-permute-start(bf16[144,1152]{1,0:T(8,128)(2,1)S(1)} %get-tuple-element.48.refs_0_), channel_id=1, source_target_pairs={{0,2},{2,0},{1,3},{3,1},{4,6},{6,4},{5,7},{7,5},{8,10},{10,8},{9,1... | collective-permute-start | bytes 995336 | tf_op jit(solution)/shard_map/ppermute | solution.py:588
  23.7 15.5 %collective-permute-start.9 = (bf16[144,1152]{1,0:T(8,128)(2,1)S(1)}, bf16[144,1152]{1,0:T(8,128)(2,1)S(1)}, u32[]{:S(2)}, u32[]{:S(2)}) collective-permute-start(bf16[144,1152]{1,0:T(8,128)(2,1)S(1)} %get-tuple-element.48.refs_0_), channel_id=1, source_target_pairs={{0,16},{16,0},{1,17},{17,1},{2,18},{18,2},{3,19},{19,3},{4,20},{20... | collective-permute-start | bytes 995336 | tf_op jit(solution)/shard_map/ppermute | solution.py:588
  25.1 4.9 %collective-permute-start.3 = (bf16[144,504]{1,0:T(8,128)(2,1)}, bf16[144,504]{1,0:T(8,128)(2,1)S(1)}, u32[]{:S(2)}, u32[]{:S(2)}) collective-permute-start(bf16[144,504]{1,0:T(8,128)(2,1)} %get-tuple-element.34.refs_0_), channel_id=1, source_target_pairs={{0,1},{1,0},{2,3},{3,2},{4,5},{5,4},{6,7},{7,6},{8,9},{9,8},{10,11... | collective-permute-start | bytes 435464 | tf_op jit(solution)/shard_map/ppermute | solution.py:588
  28.6 1.7 %collective-permute-start.7 = (bf16[16,32,96]{2,1,0:T(8,128)(2,1)S(1)}, bf16[16,32,96]{2,1,0:T(8,128)(2,1)S(1)}, u32[]{:S(2)}, u32[]{:S(2)}) collective-permute-start(bf16[16,32,96]{2,1,0:T(8,128)(2,1)S(1)} %all-to-all-done.mine), channel_id=1, source_target_pairs={{0,1},{1,0},{2,3},{3,2},{4,5},{5,4},{6,7},{7,6},{8,9},{9,8},{10,11... | collective-permute-start | bytes 294920 | tf_op jit(solution)/shard_map/ppermute | solution.py:588
  28.6 4.3 %collective-permute-start.4 = (bf16[144,504]{1,0:T(8,128)(2,1)S(1)}, bf16[144,504]{1,0:T(8,128)(2,1)S(1)}, u32[]{:S(2)}, u32[]{:S(2)}) collective-permute-start(bf16[144,504]{1,0:T(8,128)(2,1)S(1)} %collective-permute-done.refs_1_), channel_id=1, source_target_pairs={{0,1},{1,0},{2,3},{3,2},{4,5},{5,4},{6,7},{7,6},{8,9},{9,8},{10,11... | collective-permute-start | bytes 435464 | tf_op jit(solution)/shard_map/ppermute | solution.py:588
  30.0 2.9 %collective-permute-start.5 = (bf16[144,504]{1,0:T(8,128)(2,1)S(1)}, bf16[144,504]{1,0:T(8,128)(2,1)S(1)}, u32[]{:S(2)}, u32[]{:S(2)}) collective-permute-start(bf16[144,504]{1,0:T(8,128)(2,1)S(1)} %collective-permute-done.1.refs_2_), channel_id=1, source_target_pairs={{0,1},{1,0},{2,3},{3,2},{4,5},{5,4},{6,7},{7,6},{8,9},{9,8},{10,11... | collective-permute-start | bytes 435464 | tf_op jit(solution)/shard_map/ppermute | solution.py:588
  30.3 2.6 %collective-permute-start.6 = (bf16[144,504]{1,0:T(8,128)(2,1)S(1)}, bf16[144,504]{1,0:T(8,128)(2,1)S(1)}, u32[]{:S(2)}, u32[]{:S(2)}) collective-permute-start(bf16[144,504]{1,0:T(8,128)(2,1)S(1)} %collective-permute-done.2.refs_3_), channel_id=1, source_target_pairs={{0,1},{1,0},{2,3},{3,2},{4,5},{5,4},{6,7},{7,6},{8,9},{9,8},{10,11... | collective-permute-start | bytes 435464 | tf_op jit(solution)/shard_map/ppermute | solution.py:588
  32.9 11.2 %copy-start.20 = (f32[24,48]{1,0:T(8,128)S(1)}, f32[24,48]{1,0:T(8,128)}, u32[]{:S(2)}) copy-start(f32[24,48]{1,0:T(8,128)} %get-tuple-element.52) | copy-start | bytes 13828
  32.9 25.9 %copy-start.19 = (f32[1152]{0:T(1024)S(1)}, f32[1152]{0:T(1024)}, u32[]{:S(2)}) copy-start(f32[1152]{0:T(1024)} %param.26) | copy-start | bytes 13828
  33.0 26.5 %copy-start.1 = (f32[16,3,1152]{2,0,1:T(8,128)S(1)}, f32[16,3,1152]{2,0,1:T(8,128)}, u32[]{:S(2)}) copy-start(f32[16,3,1152]{2,0,1:T(8,128)} %param.20) | copy-start | bytes 663556
  33.0 26.5 %copy-start.3 = (bf16[16,1152]{1,0:T(8,128)(2,1)S(1)}, bf16[16,1152]{1,0:T(8,128)(2,1)}, u32[]{:S(2)}) copy-start(bf16[16,1152]{1,0:T(8,128)(2,1)} %refs_4_.1) | copy-start | bytes 110596
  33.0 26.5 %copy-start.6 = (bf16[1152,16]{0,1:T(8,128)(2,1)S(1)}, bf16[1152,16]{0,1:T(8,128)(2,1)}, u32[]{:S(2)}) copy-start(bf16[1152,16]{0,1:T(8,128)(2,1)} %param.27) | copy-start | bytes 110596
  33.0 26.5 %copy-start.7 = (f32[24,192]{1,0:T(8,128)S(1)}, f32[24,192]{1,0:T(8,128)}, u32[]{:S(2)}) copy-start(f32[24,192]{1,0:T(8,128)} %get-tuple-element.51.refs_0_) | copy-start | bytes 55300
  33.0 26.5 %copy-start.8 = (f32[1,1152]{1,0:T(1,128)S(1)}, f32[1,1152]{1,0:T(1,128)}, u32[]{:S(2)}) copy-start(f32[1,1152]{1,0:T(1,128)} %refs_2_.1) | copy-start | bytes 13828
  33.0 26.5 %copy-start.13 = (f32[8,48]{1,0:T(8,128)S(1)}, f32[8,48]{1,0:T(8,128)}, u32[]{:S(2)}) copy-start(f32[8,48]{1,0:T(8,128)} %refs_7_.1) | copy-start | bytes 4612
  39.2 26.1 %all-to-all-start.1 = ((bf16[16,72,240]{2,1,0:T(8,128)(2,1)}), bf16[16,72,240]{2,1,0:T(8,128)(2,1)S(1)}, u32[]{:S(2)}, u32[]{:S(2)}) async-start(bf16[16,72,240]{2,1,0:T(8,128)(2,1)} %shard_map.161), calls=%async_computation.1 | async-start | bytes 1179648 | tf_op jit(solution)/shard_map/all_to_all | solution.py:695
  42.9 20.7 %collective-permute-start.10 = (bf16[80,1152]{1,0:T(8,128)(2,1)S(1)}, bf16[80,1152]{1,0:T(8,128)(2,1)S(1)}, u32[]{:S(2)}, u32[]{:S(2)}) collective-permute-start(bf16[80,1152]{1,0:T(8,128)(2,1)S(1)} %slice.6), channel_id=1, source_target_pairs={{0,16},{16,0},{1,17},{17,1},{2,18},{18,2},{3,19},{19,3},{4,20},{20... | collective-permute-start | bytes 552968 | tf_op jit(solution)/shard_map/ppermute | solution.py:588
  44.2 13.0 %collective-permute-start.12 = (f32[24,48]{1,0:T(8,128)S(1)}, f32[24,48]{1,0:T(8,128)S(1)}, u32[]{:S(2)}, u32[]{:S(2)}) collective-permute-start(f32[24,48]{1,0:T(8,128)S(1)} %copy-done.20), channel_id=1, source_target_pairs={{4,0},{8,4},{12,8},{5,1},{9,5},{13,9},{6,2},{10,6},{14,10},{7,3},{... | collective-permute-start | bytes 13832 | tf_op jit(solution)/shard_map/ppermute | solution.py:696
  46.4 17.2 %collective-permute-start.11 = (bf16[64,1152]{1,0:T(8,128)(2,1)S(1)}, bf16[64,1152]{1,0:T(8,128)(2,1)S(1)}, u32[]{:S(2)}, u32[]{:S(2)}) collective-permute-start(bf16[64,1152]{1,0:T(8,128)(2,1)S(1)} %slice.7), channel_id=1, source_target_pairs={{0,2},{2,0},{1,3},{3,1},{4,6},{6,4},{5,7},{7,5},{8,10},{10,8},{9,1... | collective-permute-start | bytes 442376 | tf_op jit(solution)/shard_map/ppermute | solution.py:588
  47.6 17.6 %collective-permute-start.14 = (bf16[144,1152]{1,0:T(8,128)(2,1)S(1)}, bf16[144,1152]{1,0:T(8,128)(2,1)S(1)}, u32[]{:S(2)}, u32[]{:S(2)}) collective-permute-start(bf16[144,1152]{1,0:T(8,128)(2,1)S(1)} %collective-permute-done.8.refs_1_), channel_id=1, source_target_pairs={{0,1},{1,0},{2,3},{3,2},{4,5},{5,4},{6,7},{7,6},{8,9},{9,8},{10,11... | collective-permute-start | bytes 995336 | tf_op jit(solution)/shard_map/ppermute | solution.py:588
  49.4 15.8 %collective-permute-start.13 = (bf16[144,1152]{1,0:T(8,128)(2,1)S(1)}, bf16[144,1152]{1,0:T(8,128)(2,1)S(1)}, u32[]{:S(2)}, u32[]{:S(2)}) collective-permute-start(bf16[144,1152]{1,0:T(8,128)(2,1)S(1)} %get-tuple-element.48.refs_0_), channel_id=1, source_target_pairs={{0,1},{1,0},{2,3},{3,2},{4,5},{5,4},{6,7},{7,6},{8,9},{9,8},{10,11... | collective-permute-start | bytes 995336 | tf_op jit(solution)/shard_map/ppermute | solution.py:588
  57.1 8.1 %collective-permute-start.15 = (bf16[144,1152]{1,0:T(8,128)(2,1)S(1)}, bf16[144,1152]{1,0:T(8,128)(2,1)S(1)}, u32[]{:S(2)}, u32[]{:S(2)}) collective-permute-start(bf16[144,1152]{1,0:T(8,128)(2,1)S(1)} %collective-permute-done.9.refs_2_), channel_id=1, source_target_pairs={{0,1},{1,0},{2,3},{3,2},{4,5},{5,4},{6,7},{7,6},{8,9},{9,8},{10,11... | collective-permute-start | bytes 995336 | tf_op jit(solution)/shard_map/ppermute | solution.py:588
  63.6 1.7 %collective-permute-start.16 = (bf16[80,1152]{1,0:T(8,128)(2,1)S(1)}, bf16[80,1152]{1,0:T(8,128)(2,1)S(1)}, u32[]{:S(2)}, u32[]{:S(2)}) collective-permute-start(bf16[80,1152]{1,0:T(8,128)(2,1)S(1)} %collective-permute-done.10.refs_3_), channel_id=1, source_target_pairs={{0,1},{1,0},{2,3},{3,2},{4,5},{5,4},{6,7},{7,6},{8,9},{9,8},{10,11... | collective-permute-start | bytes 552968 | tf_op jit(solution)/shard_map/ppermute | solution.py:588
  63.6 1.6 %collective-permute-start.17 = (bf16[64,1152]{1,0:T(8,128)(2,1)S(1)}, bf16[64,1152]{1,0:T(8,128)(2,1)S(1)}, u32[]{:S(2)}, u32[]{:S(2)}) collective-permute-start(bf16[64,1152]{1,0:T(8,128)(2,1)S(1)} %collective-permute-done.11.refs_4_), channel_id=1, source_target_pairs={{0,1},{1,0},{2,3},{3,2},{4,5},{5,4},{6,7},{7,6},{8,9},{9,8},{10,11... | collective-permute-start | bytes 442376 | tf_op jit(solution)/shard_map/ppermute | solution.py:588
  66.0 3.7 %copy-start.15 = (f32[8,128]{1,0:T(8,128)S(1)}, f32[8,128]{1,0:T(8,128)}, u32[]{:S(2)}) copy-start(f32[8,128]{1,0:T(8,128)} %copy-done.14) | copy-start | bytes 12292
  68.5 1.2 %collective-permute-start.18 = (f32[8,240]{1,0:T(8,128)S(1)}, f32[8,240]{1,0:T(8,128)S(1)}, u32[]{:S(2)}, u32[]{:S(2)}) collective-permute-start(f32[8,240]{1,0:T(8,128)S(1)} %get-tuple-element.61), channel_id=1, source_target_pairs={{0,1},{1,0},{2,3},{3,2},{4,5},{5,4},{6,7},{7,6},{8,9},{9,8},{10,11... | collective-permute-start | bytes 23048 | tf_op jit(solution)/shard_map/ppermute | solution.py:588
  (10 other events, 12.9 us)

commit v10 on v9

--- a/solution.py
+++ b/solution.py
@@ -451,21 +451,21 @@
                 out[at] = jnp.concatenate(parts, axis=1).astype(BF16)
 
 
-def stage_kernel(group, *refs):
-    *pieces, level_source, embed_source, out, own, level_mod, embed, sems = refs
+def stage_kernel(own_source, level_source, embed_source, own, level_mod, embed, sems):
     copies = [
-        pltpu.make_async_copy(pieces[0], own, sems.at[0]),
+        pltpu.make_async_copy(own_source, own, sems.at[0]),
         pltpu.make_async_copy(level_source.at[pl.ds(0, 2)], level_mod, sems.at[1]),
         pltpu.make_async_copy(embed_source, embed, sems.at[2]),
     ]
     for copy in copies:
         copy.start()
-    for k, piece in reversed(list(enumerate(pieces))):
-        if k == 0:
-            for copy in copies:
-                copy.wait()
-            piece = own
-        out[:, k * group : (k + 1) * group] = piece[:, :group]
+    for copy in copies:
+        copy.wait()
+
+
+def side_kernel(group, *refs):
+    for k, piece in enumerate(refs[:-1]):
+        refs[-1][:, k * group : (k + 1) * group] = piece[:, :group]
 
 
 def ready_kernel(values, half, *refs):
@@ -652,17 +652,23 @@
     shares = lax.all_to_all(copies, ("scene", "queue", "tok"), 0, 0)
     other_shares = swapped(shares, "cfg", 1)
 
-    part, own, level_rows, embed_held = kernel_call(
-        functools.partial(stage_kernel, group),
+    own, level_rows, embed_held = kernel_call(
+        stage_kernel,
         [
-            jax.ShapeDtypeStruct((local_rows, queues * group), BF16),
             chunk,
             jax.ShapeDtypeStruct((2, levels_all, width), F32),
             jax.ShapeDtypeStruct(embed_weight.shape, BF16),
         ],
-        "h" + "v" * (queues - 1) + "hh",
+        "hhh",
         [pltpu.SemaphoreType.DMA((3,))],
-    )(*near, mods, embed_weight)
+    )(chunks[0], mods, embed_weight)
+    following = lax.ppermute(first, "queue", [(i + 1, i) for i in range(queues - 1)])
+    near[-1], following, *far[:-1] = lax.optimization_barrier((near[-1], following, *far[:-1]))
+    part = kernel_call(
+        functools.partial(side_kernel, group),
+        jax.ShapeDtypeStruct((local_rows, queues * group), BF16),
+        "v" * queues,
+    )(own, *near[1:])
     part_tok, part_scene = swapped(part, "tok", 1), swapped(part, "scene", 1)
 
     lhs, xin, rstd, masks = kernel_call(
@@ -689,11 +695,10 @@
         ],
         bytes_accessed=100_000_000,
     )(own, *near[1:], *far, lhs, xin, rstd, masks, query_gain[None], key_gain[None])
-    attended, part, part_tok, part_scene, first = lax.optimization_barrier(
-        (attended, part, part_tok, part_scene, first)
+    attended, part, part_tok, part_scene = lax.optimization_barrier(
+        (attended, part, part_tok, part_scene)
     )
     received = lax.all_to_all(attended, ("tok", "queue", "scene"), 0, 0)
-    following = lax.ppermute(first, "queue", [(i + 1, i) for i in range(queues - 1)])
     cut = -(-local_rows // 32) * 16
     upper = swapped(part_tok[:cut], "scene", 1)
     lower = swapped(part_scene[cut:], "tok", 1)

time: 71 us -> 77.4 us (1.090)
  the two profiles are of different devices: /device:TPU:9 before, /device:TPU:0 now
where the time goes in v10:
time: 77.4 us; the launch traced here: 76.9 us
  waiting for transfers between devices  30.2 us (39%)
  starting transfers between devices  21.6 us (28%)
  Pallas kernels  16.3 us (21%)
  local copies, waits for them, and re-layouts  7.22 us (9%)
  between operations  1.58 us (2%)
    ppermute x18, waiting for transfers between devices, swapped(): return lax.ppermute(value, axis, [(i, i ^ mask) for i in range(count)])  16.5 us
    ppermute x18, starting transfers between devices, swapped(): return lax.ppermute(value, axis, [(i, i ^ mask) for i in range(count)])  13.2 us
    all_to_all x1, waiting for transfers between devices, on_device_heads(): shares = lax.all_to_all(copies, ('scene', 'queue', 'tok'), 0, 0)  7.69 us
    unnamed x46, local copies, waits for them, and re-layouts  7.19 us
    pallas_call x1, Pallas kernels, on_device_heads(): kernel_call(functools.partial(attend_kernel, frames, tokens, queues), jax...  6.13 us
    all_to_all x1, waiting for transfers between devices, on_device_heads(): received = lax.all_to_all(attended, ('tok', 'queue', 'scene'), 0, 0)  4.58 us
    all_to_all x1, starting transfers between devices, on_device_heads(): received = lax.all_to_all(attended, ('tok', 'queue', 'scene'), 0, 0)  3.58 us
    all_to_all x1, starting transfers between devices, on_device_heads(): shares = lax.all_to_all(copies, ('scene', 'queue', 'tok'), 0, 0)  3.51 us
  transfers between devices with their start and end apart: 21, of which 9 were waited for; matrix products, arithmetic and copies ran while one was open for 0% of the time, Pallas kernels for 13%

profile of v10, /device:TPU:0, one launch (start us, length us, event | category | flops | bytes accessed | tf_op | source)
XLA Modules:
  0.0 76.9 jit_solution(8713937063845822087)
XLA Ops:
  0.7 2.9 %shard_map.158 = (bf16[144,504]{1,0:T(8,128)(2,1)}, bf16[144,504]{1,0:T(8,128)(2,1)}, bf16[144,504]{1,0:T(8,128)(2,1)}, bf16[144,504]{1,0:T(8,128)(2,1)}, bf16[1...) custom-call(f32[4,16,48]{2,1,0:T(8,128)} %latents.1, s32[1,4]{1,0:T(1,128)} %bitcast.14, ...), custom_call_target="tpu_custom_call" | custom-call | flops 1000000 | bytes 8000000 | tf_op jit(solution)/shard_map/pallas_call | solution.py:629
  3.6 3.0 %collective-permute-start = (bf16[144,504]{1,0:T(8,128)(2,1)}, bf16[144,504]{1,0:T(8,128)(2,1)S(1)}, u32[]{:S(2)}, u32[]{:S(2)}) collective-permute-start(bf16[144,504]{1,0:T(8,128)(2,1)} %get-tuple-element.39), channel_id=1, source_target_pairs={{0,4},{4,0},{8,12},{12,8},{1,5},{5,1},{9,13},{13,9},{2,6},{6,2},{1... | collective-permute-start | bytes 435464 | tf_op jit(solution)/shard_map/ppermute | solution.py:588
  6.6 2.6 %collective-permute-start.1 = (bf16[144,504]{1,0:T(8,128)(2,1)}, bf16[144,504]{1,0:T(8,128)(2,1)S(1)}, u32[]{:S(2)}, u32[]{:S(2)}) collective-permute-start(bf16[144,504]{1,0:T(8,128)(2,1)} %get-tuple-element.40), channel_id=1, source_target_pairs={{0,8},{4,12},{8,0},{12,4},{1,9},{5,13},{9,1},{13,5},{2,10},{6,14},... | collective-permute-start | bytes 435464 | tf_op jit(solution)/shard_map/ppermute | solution.py:588
  9.2 3.5 %collective-permute-done.refs_1_ = bf16[144,504]{1,0:T(8,128)(2,1)S(1)} collective-permute-done((bf16[144,504]{1,0:T(8,128)(2,1)}, bf16[144,504]{1,0:T(8,128)(2,1)S(1)}, u32[]{:S(2)}, u32[]{:S(2)}) %collective-permute-start) | collective-permute-done | bytes 145184 | tf_op jit(solution)/shard_map/ppermute | solution.py:588
  12.7 8.1 %collective-permute-done.1.refs_2_ = bf16[144,504]{1,0:T(8,128)(2,1)S(1)} collective-permute-done((bf16[144,504]{1,0:T(8,128)(2,1)}, bf16[144,504]{1,0:T(8,128)(2,1)S(1)}, u32[]{:S(2)}, u32[]{:S(2)}) %collective-permute-start.1) | collective-permute-done | bytes 145184 | tf_op jit(solution)/shard_map/ppermute | solution.py:588
  20.8 1.3 %collective-permute-start.3 = (f32[24,48]{1,0:T(8,128)}, f32[24,48]{1,0:T(8,128)S(1)}, u32[]{:S(2)}, u32[]{:S(2)}) collective-permute-start(f32[24,48]{1,0:T(8,128)} %get-tuple-element.42), channel_id=1, source_target_pairs={{4,0},{8,4},{12,8},{5,1},{9,5},{13,9},{6,2},{10,6},{14,10},{7,3},{... | collective-permute-start | bytes 13832 | tf_op jit(solution)/shard_map/ppermute | solution.py:665
  22.1 0.9 %copy-done = f32[16,3,1152]{2,0,1:T(8,128)S(1)} copy-done((f32[16,3,1152]{2,0,1:T(8,128)S(1)}, f32[16,3,1152]{2,0,1:T(8,128)}, u32[]{:S(2)}) %copy-start) | copy-done | bytes 221208
  23.0 0.9 %copy-done.2 = bf16[144,504]{1,0:T(8,128)(2,1)S(1)} copy-done((bf16[144,504]{1,0:T(8,128)(2,1)S(1)}, bf16[144,504]{1,0:T(8,128)(2,1)}, u32[]{:S(2)}) %copy-start.2) | copy-done | bytes 145176
  24.0 0.8 copy-done.3
  25.2 1.5 %collective-permute-done.3.refs_1_ = f32[24,48]{1,0:T(8,128)S(1)} collective-permute-done((f32[24,48]{1,0:T(8,128)}, f32[24,48]{1,0:T(8,128)S(1)}, u32[]{:S(2)}, u32[]{:S(2)}) %collective-permute-start.3) | collective-permute-done | bytes 4640 | tf_op jit(solution)/shard_map/ppermute | solution.py:665
  26.8 1.6 %collective-permute-start.10 = (bf16[144,1152]{1,0:T(8,128)(2,1)S(1)}, bf16[144,1152]{1,0:T(8,128)(2,1)S(1)}, u32[]{:S(2)}, u32[]{:S(2)}) collective-permute-start(bf16[144,1152]{1,0:T(8,128)(2,1)S(1)} %shard_map.162.refs_0_), channel_id=1, source_target_pairs={{0,16},{16,0},{1,17},{17,1},{2,18},{18,2},{3,19},{19,3},{4,20},{20... | collective-permute-start | bytes 995336 | tf_op jit(solution)/shard_map/ppermute | solution.py:588
  28.4 1.5 %collective-permute-start.9 = (bf16[144,1152]{1,0:T(8,128)(2,1)S(1)}, bf16[144,1152]{1,0:T(8,128)(2,1)S(1)}, u32[]{:S(2)}, u32[]{:S(2)}) collective-permute-start(bf16[144,1152]{1,0:T(8,128)(2,1)S(1)} %shard_map.162.refs_0_), channel_id=1, source_target_pairs={{0,2},{2,0},{1,3},{3,1},{4,6},{6,4},{5,7},{7,5},{8,10},{10,8},{9,1... | collective-permute-start | bytes 995336 | tf_op jit(solution)/shard_map/ppermute | solution.py:588
  29.9 3.5 %all-to-all-start = ((bf16[16,32,96]{2,1,0:T(8,128)(2,1)}), bf16[16,32,96]{2,1,0:T(8,128)(2,1)S(1)}, u32[]{:S(2)}, u32[]{:S(2)}) async-start(bf16[16,32,96]{2,1,0:T(8,128)(2,1)} %get-tuple-element.47), calls=%async_computation | async-start | bytes 262144 | tf_op jit(solution)/shard_map/all_to_all | solution.py:652
  33.5 7.7 %all-to-all-done.mine = bf16[16,32,96]{2,1,0:T(8,128)(2,1)S(1)} async-done(((bf16[16,32,96]{2,1,0:T(8,128)(2,1)}), bf16[16,32,96]{2,1,0:T(8,128)(2,1)S(1)}, u32[]{:S(2)}, u32[]{:S(2)}) %all-to-all-start) | async-done | bytes 98336 | tf_op jit(solution)/shard_map/all_to_all | solution.py:652
  41.2 1.3 %collective-permute-done.8.other = bf16[16,32,96]{2,1,0:T(8,128)(2,1)S(1)} collective-permute-done((bf16[16,32,96]{2,1,0:T(8,128)(2,1)S(1)}, bf16[16,32,96]{2,1,0:T(8,128)(2,1)S(1)}, u32[]{:S(2)}, u32[]{:S(2)}) %collective-permute-start.8) | collective-permute-done | bytes 98336 | tf_op jit(solution)/shard_map/ppermute | solution.py:588
  42.5 2.4 %shard_map.160 = (bf16[1024,1152]{1,0:T(8,128)(2,1)S(1)}, bf16[16,64,256]{2,1,0:T(8,128)(2,1)S(1)}, f32[16,1,256]{2,1,0:T(1,128)S(1)}, f32[2,16,16,128]{3,2,1,0:T(8,128)S(1)}) custom-call(bf16[16,32,96]{2,1,0:T(8,128)(2,1)S(1)} %all-to-all-done.mine, bf16[16,32,96]{2,1,0:T(8,128)(2,1)S(1)} %collective-permute-done.8.other, ...), custom_call_target="tpu_custom_call" | custom-call | flops 1000000 | bytes 8000000 | tf_op jit(solution)/shard_map/pallas_call | solution.py:674
  45.0 6.1 %shard_map.161 = bf16[16,72,240]{2,1,0:T(8,128)(2,1)} custom-call(bf16[144,504]{1,0:T(8,128)(2,1)S(1)} %get-tuple-element.38.refs_0_, bf16[144,504]{1,0:T(8,128)(2,1)S(1)} %collective-permute-done.refs_1_, bf16[144,504]{1,0:T(8,128)(2,1)S(1)} %collective-permute-done.1.refs_2_, bf16[144,504]{1,0:T(8,128)(2,1)S(1)} %collective-permute-done.2.refs_3_, ...), custom_call_target="tpu_custom_call" | custom-call | flops 1000000 | bytes 100000000 | tf_op jit(solution)/shard_map/pallas_call | solution.py:685
  51.2 3.6 %all-to-all-start.1 = ((bf16[16,72,240]{2,1,0:T(8,128)(2,1)}), bf16[16,72,240]{2,1,0:T(8,128)(2,1)S(1)}, u32[]{:S(2)}, u32[]{:S(2)}) async-start(bf16[16,72,240]{2,1,0:T(8,128)(2,1)} %shard_map.161), calls=%async_computation.1 | async-start | bytes 1179648 | tf_op jit(solution)/shard_map/all_to_all | solution.py:701
  54.8 1.9 %collective-permute-start.11 = (bf16[80,1152]{1,0:T(8,128)(2,1)S(1)}, bf16[80,1152]{1,0:T(8,128)(2,1)S(1)}, u32[]{:S(2)}, u32[]{:S(2)}) collective-permute-start(bf16[80,1152]{1,0:T(8,128)(2,1)S(1)} %slice.6), channel_id=1, source_target_pairs={{0,16},{16,0},{1,17},{17,1},{2,18},{18,2},{3,19},{19,3},{4,20},{20... | collective-permute-start | bytes 552968 | tf_op jit(solution)/shard_map/ppermute | solution.py:588
  56.7 1.6 %collective-permute-start.12 = (bf16[64,1152]{1,0:T(8,128)(2,1)S(1)}, bf16[64,1152]{1,0:T(8,128)(2,1)S(1)}, u32[]{:S(2)}, u32[]{:S(2)}) collective-permute-start(bf16[64,1152]{1,0:T(8,128)(2,1)S(1)} %slice.7), channel_id=1, source_target_pairs={{0,2},{2,0},{1,3},{3,1},{4,6},{6,4},{5,7},{7,5},{8,10},{10,8},{9,1... | collective-permute-start | bytes 442376 | tf_op jit(solution)/shard_map/ppermute | solution.py:588
  59.5 0.7 copy-done.11
  60.2 0.7 copy-done.19
  60.9 1.0 %shard_map.163 = (bf16[96,1152]{1,0:T(8,128)(2,1)S(1)}, bf16[96,240]{1,0:T(8,128)(2,1)S(1)}, f32[8,240]{1,0:T(8,128)S(1)}, f32[8,240]{1,0:T(8,128)S(1)}, f32[8,4...) custom-call(f32[24,192]{1,0:T(8,128)S(1)} %copy-done.8, f32[24,48]{1,0:T(8,128)S(1)} %copy-done.11, ...), custom_call_target="tpu_custom_call" | custom-call | flops 1000000 | bytes 1000000 | tf_op jit(solution)/shard_map/pallas_call | solution.py:721
  61.9 0.6 copy-done.5
  62.5 0.6 copy-done.12
  64.2 1.2 %collective-permute-done.12.refs_4_ = bf16[64,1152]{1,0:T(8,128)(2,1)S(1)} collective-permute-done((bf16[64,1152]{1,0:T(8,128)(2,1)S(1)}, bf16[64,1152]{1,0:T(8,128)(2,1)S(1)}, u32[]{:S(2)}, u32[]{:S(2)}) %collective-permute-start.12) | collective-permute-done | bytes 147488 | tf_op jit(solution)/shard_map/ppermute | solution.py:588
  65.9 1.1 %collective-permute-done.17.refs_9_ = bf16[64,1152]{1,0:T(8,128)(2,1)S(1)} collective-permute-done((bf16[64,1152]{1,0:T(8,128)(2,1)S(1)}, bf16[64,1152]{1,0:T(8,128)(2,1)S(1)}, u32[]{:S(2)}, u32[]{:S(2)}) %collective-permute-start.17) | collective-permute-done | bytes 147488 | tf_op jit(solution)/shard_map/ppermute | solution.py:588
  67.1 4.6 %all-to-all-done.1.refs_10_ = bf16[16,72,240]{2,1,0:T(8,128)(2,1)S(1)} async-done(((bf16[16,72,240]{2,1,0:T(8,128)(2,1)}), bf16[16,72,240]{2,1,0:T(8,128)(2,1)S(1)}, u32[]{:S(2)}, u32[]{:S(2)}) %all-to-all-start.1) | async-done | bytes 552992 | tf_op jit(solution)/shard_map/all_to_all | solution.py:701
  71.7 0.8 copy-done.6
  72.4 2.5 %shard_map.164 = (f32[8,240]{1,0:T(8,128)S(1)}, f32[8,240]{1,0:T(8,128)S(1)}) custom-call(bf16[144,1152]{1,0:T(8,128)(2,1)S(1)} %shard_map.162.refs_0_, bf16[144,1152]{1,0:T(8,128)(2,1)S(1)} %collective-permute-done.9.refs_1_, bf16[144,1152]{1,0:T(8,128)(2,1)S(1)} %collective-permute-done.10.refs_2_, bf16[80,1152]{1,0:T(8,128)(2,1)S(1)} %collective-permute-done.11.refs_3_, ...), custom_call_target="tpu_custom_call" | custom-call | flops 1000000 | bytes 8000000 | tf_op jit(solution)/shard_map/pallas_call | solution.py:739
  74.9 1.2 %collective-permute-done.18.partner = f32[8,240]{1,0:T(8,128)S(1)} collective-permute-done((f32[8,240]{1,0:T(8,128)S(1)}, f32[8,240]{1,0:T(8,128)S(1)}, u32[]{:S(2)}, u32[]{:S(2)}) %collective-permute-start.18) | collective-permute-done | bytes 7712 | tf_op jit(solution)/shard_map/ppermute | solution.py:588
  76.1 0.7 shard_map.165
  (67 shorter events, 3.0 us)
Async XLA Ops:
  0.6 44.3 %copy-start.20 = (f32[72]{0:T(128)S(1)}, f32[72]{0:T(128)}, u32[]{:S(2)}) copy-start(f32[72]{0:T(128)} %param.23) | copy-start | bytes 868
  0.6 44.3 %copy-start.21 = (f32[72]{0:T(128)S(1)}, f32[72]{0:T(128)}, u32[]{:S(2)}) copy-start(f32[72]{0:T(128)} %param.24) | copy-start | bytes 868
  3.6 9.1 %collective-permute-start = (bf16[144,504]{1,0:T(8,128)(2,1)}, bf16[144,504]{1,0:T(8,128)(2,1)S(1)}, u32[]{:S(2)}, u32[]{:S(2)}) collective-permute-start(bf16[144,504]{1,0:T(8,128)(2,1)} %get-tuple-element.39), channel_id=1, source_target_pairs={{0,4},{4,0},{8,12},{12,8},{1,5},{5,1},{9,13},{13,9},{2,6},{6,2},{1... | collective-permute-start | bytes 435464 | tf_op jit(solution)/shard_map/ppermute | solution.py:588
  6.6 14.2 %collective-permute-start.1 = (bf16[144,504]{1,0:T(8,128)(2,1)}, bf16[144,504]{1,0:T(8,128)(2,1)S(1)}, u32[]{:S(2)}, u32[]{:S(2)}) collective-permute-start(bf16[144,504]{1,0:T(8,128)(2,1)} %get-tuple-element.40), channel_id=1, source_target_pairs={{0,8},{4,12},{8,0},{12,4},{1,9},{5,13},{9,1},{13,5},{2,10},{6,14},... | collective-permute-start | bytes 435464 | tf_op jit(solution)/shard_map/ppermute | solution.py:588
  9.2 17.4 %collective-permute-start.2 = (bf16[144,504]{1,0:T(8,128)(2,1)}, bf16[144,504]{1,0:T(8,128)(2,1)S(1)}, u32[]{:S(2)}, u32[]{:S(2)}) collective-permute-start(bf16[144,504]{1,0:T(8,128)(2,1)} %get-tuple-element.41), channel_id=1, source_target_pairs={{0,12},{4,8},{8,4},{12,0},{1,13},{5,9},{9,5},{13,1},{2,14},{6,10},... | collective-permute-start | bytes 435464 | tf_op jit(solution)/shard_map/ppermute | solution.py:588
  9.2 17.4 %collective-permute-start.4 = (bf16[144,504]{1,0:T(8,128)(2,1)}, bf16[144,504]{1,0:T(8,128)(2,1)S(1)}, u32[]{:S(2)}, u32[]{:S(2)}) collective-permute-start(bf16[144,504]{1,0:T(8,128)(2,1)} %get-tuple-element.37.own_source), channel_id=1, source_target_pairs={{0,1},{1,0},{2,3},{3,2},{4,5},{5,4},{6,7},{7,6},{8,9},{9,8},{10,11... | collective-permute-start | bytes 435464 | tf_op jit(solution)/shard_map/ppermute | solution.py:588
  12.7 13.9 %collective-permute-start.5 = (bf16[144,504]{1,0:T(8,128)(2,1)S(1)}, bf16[144,504]{1,0:T(8,128)(2,1)S(1)}, u32[]{:S(2)}, u32[]{:S(2)}) collective-permute-start(bf16[144,504]{1,0:T(8,128)(2,1)S(1)} %collective-permute-done.refs_1_), channel_id=1, source_target_pairs={{0,1},{1,0},{2,3},{3,2},{4,5},{5,4},{6,7},{7,6},{8,9},{9,8},{10,11... | collective-permute-start | bytes 435464 | tf_op jit(solution)/shard_map/ppermute | solution.py:588
  20.8 5.8 %collective-permute-start.6 = (bf16[144,504]{1,0:T(8,128)(2,1)S(1)}, bf16[144,504]{1,0:T(8,128)(2,1)S(1)}, u32[]{:S(2)}, u32[]{:S(2)}) collective-permute-start(bf16[144,504]{1,0:T(8,128)(2,1)S(1)} %collective-permute-done.1.refs_2_), channel_id=1, source_target_pairs={{0,1},{1,0},{2,3},{3,2},{4,5},{5,4},{6,7},{7,6},{8,9},{9,8},{10,11... | collective-permute-start | bytes 435464 | tf_op jit(solution)/shard_map/ppermute | solution.py:588
  20.8 5.8 %collective-permute-start.3 = (f32[24,48]{1,0:T(8,128)}, f32[24,48]{1,0:T(8,128)S(1)}, u32[]{:S(2)}, u32[]{:S(2)}) collective-permute-start(f32[24,48]{1,0:T(8,128)} %get-tuple-element.42), channel_id=1, source_target_pairs={{4,0},{8,4},{12,8},{5,1},{9,5},{13,9},{6,2},{10,6},{14,10},{7,3},{... | collective-permute-start | bytes 13832 | tf_op jit(solution)/shard_map/ppermute | solution.py:665
  26.8 24.4 %collective-permute-start.10 = (bf16[144,1152]{1,0:T(8,128)(2,1)S(1)}, bf16[144,1152]{1,0:T(8,128)(2,1)S(1)}, u32[]{:S(2)}, u32[]{:S(2)}) collective-permute-start(bf16[144,1152]{1,0:T(8,128)(2,1)S(1)} %shard_map.162.refs_0_), channel_id=1, source_target_pairs={{0,16},{16,0},{1,17},{17,1},{2,18},{18,2},{3,19},{19,3},{4,20},{20... | collective-permute-start | bytes 995336 | tf_op jit(solution)/shard_map/ppermute | solution.py:588
  28.4 22.8 %collective-permute-start.9 = (bf16[144,1152]{1,0:T(8,128)(2,1)S(1)}, bf16[144,1152]{1,0:T(8,128)(2,1)S(1)}, u32[]{:S(2)}, u32[]{:S(2)}) collective-permute-start(bf16[144,1152]{1,0:T(8,128)(2,1)S(1)} %shard_map.162.refs_0_), channel_id=1, source_target_pairs={{0,2},{2,0},{1,3},{3,1},{4,6},{6,4},{5,7},{7,5},{8,10},{10,8},{9,1... | collective-permute-start | bytes 995336 | tf_op jit(solution)/shard_map/ppermute | solution.py:588
  29.9 11.3 %all-to-all-start = ((bf16[16,32,96]{2,1,0:T(8,128)(2,1)}), bf16[16,32,96]{2,1,0:T(8,128)(2,1)S(1)}, u32[]{:S(2)}, u32[]{:S(2)}) async-start(bf16[16,32,96]{2,1,0:T(8,128)(2,1)} %get-tuple-element.47), calls=%async_computation | async-start | bytes 262144 | tf_op jit(solution)/shard_map/all_to_all | solution.py:652
  33.4 11.5 %collective-permute-start.7 = (bf16[144,504]{1,0:T(8,128)(2,1)S(1)}, bf16[144,504]{1,0:T(8,128)(2,1)S(1)}, u32[]{:S(2)}, u32[]{:S(2)}) collective-permute-start(bf16[144,504]{1,0:T(8,128)(2,1)S(1)} %collective-permute-done.2.refs_3_), channel_id=1, source_target_pairs={{0,1},{1,0},{2,3},{3,2},{4,5},{5,4},{6,7},{7,6},{8,9},{9,8},{10,11... | collective-permute-start | bytes 435464 | tf_op jit(solution)/shard_map/ppermute | solution.py:588
  41.2 1.3 %collective-permute-start.8 = (bf16[16,32,96]{2,1,0:T(8,128)(2,1)S(1)}, bf16[16,32,96]{2,1,0:T(8,128)(2,1)S(1)}, u32[]{:S(2)}, u32[]{:S(2)}) collective-permute-start(bf16[16,32,96]{2,1,0:T(8,128)(2,1)S(1)} %all-to-all-done.mine), channel_id=1, source_target_pairs={{0,1},{1,0},{2,3},{3,2},{4,5},{5,4},{6,7},{7,6},{8,9},{9,8},{10,11... | collective-permute-start | bytes 294920 | tf_op jit(solution)/shard_map/ppermute | solution.py:588
  45.0 13.8 %copy-start.22 = (f32[1152]{0:T(1024)S(1)}, f32[1152]{0:T(1024)}, u32[]{:S(2)}) copy-start(f32[1152]{0:T(1024)} %param.26) | copy-start | bytes 13828
  45.0 14.5 %copy-start.1 = (f32[16,3,1152]{2,0,1:T(8,128)S(1)}, f32[16,3,1152]{2,0,1:T(8,128)}, u32[]{:S(2)}) copy-start(f32[16,3,1152]{2,0,1:T(8,128)} %param.20) | copy-start | bytes 663556
  45.0 14.5 %copy-start.4 = (bf16[16,1152]{1,0:T(8,128)(2,1)S(1)}, bf16[16,1152]{1,0:T(8,128)(2,1)}, u32[]{:S(2)}) copy-start(bf16[16,1152]{1,0:T(8,128)(2,1)} %refs_4_.1) | copy-start | bytes 110596
  45.0 14.5 %copy-start.7 = (bf16[1152,16]{0,1:T(8,128)(2,1)S(1)}, bf16[1152,16]{0,1:T(8,128)(2,1)}, u32[]{:S(2)}) copy-start(bf16[1152,16]{0,1:T(8,128)(2,1)} %param.27) | copy-start | bytes 110596
  45.0 14.5 %copy-start.8 = (f32[24,192]{1,0:T(8,128)S(1)}, f32[24,192]{1,0:T(8,128)}, u32[]{:S(2)}) copy-start(f32[24,192]{1,0:T(8,128)} %get-tuple-element.57.refs_0_) | copy-start | bytes 55300
  45.0 14.5 %copy-start.9 = (f32[1,1152]{1,0:T(1,128)S(1)}, f32[1,1152]{1,0:T(1,128)}, u32[]{:S(2)}) copy-start(f32[1,1152]{1,0:T(1,128)} %refs_2_.1) | copy-start | bytes 13828
  45.0 14.5 %copy-start.16 = (f32[8,48]{1,0:T(8,128)S(1)}, f32[8,48]{1,0:T(8,128)}, u32[]{:S(2)}) copy-start(f32[8,48]{1,0:T(8,128)} %refs_7_.1) | copy-start | bytes 4612
  51.2 20.5 %all-to-all-start.1 = ((bf16[16,72,240]{2,1,0:T(8,128)(2,1)}), bf16[16,72,240]{2,1,0:T(8,128)(2,1)S(1)}, u32[]{:S(2)}, u32[]{:S(2)}) async-start(bf16[16,72,240]{2,1,0:T(8,128)(2,1)} %shard_map.161), calls=%async_computation.1 | async-start | bytes 1179648 | tf_op jit(solution)/shard_map/all_to_all | solution.py:701
  54.8 10.6 %collective-permute-start.11 = (bf16[80,1152]{1,0:T(8,128)(2,1)S(1)}, bf16[80,1152]{1,0:T(8,128)(2,1)S(1)}, u32[]{:S(2)}, u32[]{:S(2)}) collective-permute-start(bf16[80,1152]{1,0:T(8,128)(2,1)S(1)} %slice.6), channel_id=1, source_target_pairs={{0,16},{16,0},{1,17},{17,1},{2,18},{18,2},{3,19},{19,3},{4,20},{20... | collective-permute-start | bytes 552968 | tf_op jit(solution)/shard_map/ppermute | solution.py:588
  56.7 8.7 %collective-permute-start.12 = (bf16[64,1152]{1,0:T(8,128)(2,1)S(1)}, bf16[64,1152]{1,0:T(8,128)(2,1)S(1)}, u32[]{:S(2)}, u32[]{:S(2)}) collective-permute-start(bf16[64,1152]{1,0:T(8,128)(2,1)S(1)} %slice.7), channel_id=1, source_target_pairs={{0,2},{2,0},{1,3},{3,1},{4,6},{6,4},{5,7},{7,5},{8,10},{10,8},{9,1... | collective-permute-start | bytes 442376 | tf_op jit(solution)/shard_map/ppermute | solution.py:588
  58.3 8.8 %collective-permute-start.13 = (bf16[144,1152]{1,0:T(8,128)(2,1)S(1)}, bf16[144,1152]{1,0:T(8,128)(2,1)S(1)}, u32[]{:S(2)}, u32[]{:S(2)}) collective-permute-start(bf16[144,1152]{1,0:T(8,128)(2,1)S(1)} %shard_map.162.refs_0_), channel_id=1, source_target_pairs={{0,1},{1,0},{2,3},{3,2},{4,5},{5,4},{6,7},{7,6},{8,9},{9,8},{10,11... | collective-permute-start | bytes 995336 | tf_op jit(solution)/shard_map/ppermute | solution.py:588
  58.3 8.8 %collective-permute-start.14 = (bf16[144,1152]{1,0:T(8,128)(2,1)S(1)}, bf16[144,1152]{1,0:T(8,128)(2,1)S(1)}, u32[]{:S(2)}, u32[]{:S(2)}) collective-permute-start(bf16[144,1152]{1,0:T(8,128)(2,1)S(1)} %collective-permute-done.9.refs_1_), channel_id=1, source_target_pairs={{0,1},{1,0},{2,3},{3,2},{4,5},{5,4},{6,7},{7,6},{8,9},{9,8},{10,11... | collective-permute-start | bytes 995336 | tf_op jit(solution)/shard_map/ppermute | solution.py:588
  58.8 8.3 %collective-permute-start.15 = (bf16[144,1152]{1,0:T(8,128)(2,1)S(1)}, bf16[144,1152]{1,0:T(8,128)(2,1)S(1)}, u32[]{:S(2)}, u32[]{:S(2)}) collective-permute-start(bf16[144,1152]{1,0:T(8,128)(2,1)S(1)} %collective-permute-done.10.refs_2_), channel_id=1, source_target_pairs={{0,1},{1,0},{2,3},{3,2},{4,5},{5,4},{6,7},{7,6},{8,9},{9,8},{10,11... | collective-permute-start | bytes 995336 | tf_op jit(solution)/shard_map/ppermute | solution.py:588
  65.4 1.7 %collective-permute-start.16 = (bf16[80,1152]{1,0:T(8,128)(2,1)S(1)}, bf16[80,1152]{1,0:T(8,128)(2,1)S(1)}, u32[]{:S(2)}, u32[]{:S(2)}) collective-permute-start(bf16[80,1152]{1,0:T(8,128)(2,1)S(1)} %collective-permute-done.11.refs_3_), channel_id=1, source_target_pairs={{0,1},{1,0},{2,3},{3,2},{4,5},{5,4},{6,7},{7,6},{8,9},{9,8},{10,11... | collective-permute-start | bytes 552968 | tf_op jit(solution)/shard_map/ppermute | solution.py:588
  65.4 1.6 %collective-permute-start.17 = (bf16[64,1152]{1,0:T(8,128)(2,1)S(1)}, bf16[64,1152]{1,0:T(8,128)(2,1)S(1)}, u32[]{:S(2)}, u32[]{:S(2)}) collective-permute-start(bf16[64,1152]{1,0:T(8,128)(2,1)S(1)} %collective-permute-done.12.refs_4_), channel_id=1, source_target_pairs={{0,1},{1,0},{2,3},{3,2},{4,5},{5,4},{6,7},{7,6},{8,9},{9,8},{10,11... | collective-permute-start | bytes 442376 | tf_op jit(solution)/shard_map/ppermute | solution.py:588
  72.4 3.7 %copy-start.15 = (f32[8,240]{1,0:T(8,128)S(1)}, f32[8,240]{1,0:T(8,128)}, u32[]{:S(2)}) copy-start(f32[8,240]{1,0:T(8,128)} %copy-done.14) | copy-start | bytes 23044
  72.4 3.7 %copy-start.18 = (f32[8,128]{1,0:T(8,128)S(1)}, f32[8,128]{1,0:T(8,128)}, u32[]{:S(2)}) copy-start(f32[8,128]{1,0:T(8,128)} %copy-done.17) | copy-start | bytes 12292
  74.9 1.2 %collective-permute-start.18 = (f32[8,240]{1,0:T(8,128)S(1)}, f32[8,240]{1,0:T(8,128)S(1)}, u32[]{:S(2)}, u32[]{:S(2)}) collective-permute-start(f32[8,240]{1,0:T(8,128)S(1)} %get-tuple-element.67), channel_id=1, source_target_pairs={{0,1},{1,0},{2,3},{3,2},{4,5},{5,4},{6,7},{7,6},{8,9},{9,8},{10,11... | collective-permute-start | bytes 23048 | tf_op jit(solution)/shard_map/ppermute | solution.py:588
  (12 other events, 14.1 us)

commit v11 on v10

--- a/solution.py
+++ b/solution.py
@@ -663,7 +663,9 @@
         [pltpu.SemaphoreType.DMA((3,))],
     )(chunks[0], mods, embed_weight)
     following = lax.ppermute(first, "queue", [(i + 1, i) for i in range(queues - 1)])
-    near[-1], following, *far[:-1] = lax.optimization_barrier((near[-1], following, *far[:-1]))
+    near[-1], following, shares, *far[:-1] = lax.optimization_barrier(
+        (near[-1], following, shares, *far[:-1])
+    )
     part = kernel_call(
         functools.partial(side_kernel, group),
         jax.ShapeDtypeStruct((local_rows, queues * group), BF16),

time: 77.4 us -> 67 us (0.87)
  waiting for transfers between devices: 30.2 us -> 12.8 us
  starting transfers between devices: 21.6 us -> 28 us
    ppermute x18, waiting for transfers between devices: 16.5 us -> 4.87 us  [swapped(): return lax.ppermute(value, axis, [(i, i ^ mask) for i in range(count)])]
    all_to_all x1, waiting for transfers between devices: 7.69 us -> 0.01 us  [on_device_heads(): shares = lax.all_to_all(copies, ('scene', 'queue', 'tok'), 0, 0)]
    ppermute x18, starting transfers between devices: 13.2 us -> 18 us  [swapped(): return lax.ppermute(value, axis, [(i, i ^ mask) for i in range(count)])]
    ppermute x1, waiting for transfers between devices: 1.45 us -> 3.74 us  [on_device_heads(): lax.ppermute(first, 'queue', [(i + 1, i) for i in range(queues - 1)])]
    all_to_all x1, starting transfers between devices: 3.58 us -> 4.81 us  [on_device_heads(): received = lax.all_to_all(attended, ('tok', 'queue', 'scene'), 0, 0)]
  transfers between devices with their start and end apart: 21 -> 21, of which waited for: 9 -> 6; matrix products, arithmetic and copies ran while one was open for 0% -> 0% of each run, Pallas kernels for 13% -> 15%
where the time goes in v11:
time: 67 us; the launch traced here: 66.4 us
  starting transfers between devices  28 us (42%)
  Pallas kernels  16.2 us (24%)
  waiting for transfers between devices  12.8 us (19%)
  local copies, waits for them, and re-layouts  7.81 us (12%)
  between operations  1.58 us (2%)
    ppermute x18, starting transfers between devices, swapped(): return lax.ppermute(value, axis, [(i, i ^ mask) for i in range(count)])  18 us
    unnamed x46, local copies, waits for them, and re-layouts  7.78 us
    pallas_call x1, Pallas kernels, on_device_heads(): kernel_call(functools.partial(attend_kernel, frames, tokens, queues), jax...  6.13 us
    ppermute x18, waiting for transfers between devices, swapped(): return lax.ppermute(value, axis, [(i, i ^ mask) for i in range(count)])  4.87 us
    all_to_all x1, starting transfers between devices, on_device_heads(): received = lax.all_to_all(attended, ('tok', 'queue', 'scene'), 0, 0)  4.81 us
    all_to_all x1, waiting for transfers between devices, on_device_heads(): received = lax.all_to_all(attended, ('tok', 'queue', 'scene'), 0, 0)  4.22 us
    all_to_all x1, starting transfers between devices, on_device_heads(): shares = lax.all_to_all(copies, ('scene', 'queue', 'tok'), 0, 0)  3.83 us
    ppermute x1, waiting for transfers between devices, on_device_heads(): lax.ppermute(first, 'queue', [(i + 1, i) for i in range(queues - 1)])  3.74 us
  transfers between devices with their start and end apart: 21, of which 6 were waited for; matrix products, arithmetic and copies ran while one was open for 0% of the time, Pallas kernels for 15%

profile of v11, /device:TPU:0, one launch (start us, length us, event | category | flops | bytes accessed | tf_op | source)
XLA Modules:
  0.0 66.4 jit_solution(11357999586844941114)
XLA Ops:
  0.7 2.9 %shard_map.158 = (bf16[144,504]{1,0:T(8,128)(2,1)}, bf16[144,504]{1,0:T(8,128)(2,1)}, bf16[144,504]{1,0:T(8,128)(2,1)}, bf16[144,504]{1,0:T(8,128)(2,1)}, bf16[1...) custom-call(f32[4,16,48]{2,1,0:T(8,128)} %latents.1, s32[1,4]{1,0:T(1,128)} %bitcast.14, ...), custom_call_target="tpu_custom_call" | custom-call | flops 1000000 | bytes 8000000 | tf_op jit(solution)/shard_map/pallas_call | solution.py:629
  3.6 3.0 %collective-permute-start = (bf16[144,504]{1,0:T(8,128)(2,1)}, bf16[144,504]{1,0:T(8,128)(2,1)S(1)}, u32[]{:S(2)}, u32[]{:S(2)}) collective-permute-start(bf16[144,504]{1,0:T(8,128)(2,1)} %get-tuple-element.40), channel_id=1, source_target_pairs={{0,4},{4,0},{8,12},{12,8},{1,5},{5,1},{9,13},{13,9},{2,6},{6,2},{1... | collective-permute-start | bytes 435464 | tf_op jit(solution)/shard_map/ppermute | solution.py:588
  6.6 2.6 %collective-permute-start.1 = (bf16[144,504]{1,0:T(8,128)(2,1)}, bf16[144,504]{1,0:T(8,128)(2,1)S(1)}, u32[]{:S(2)}, u32[]{:S(2)}) collective-permute-start(bf16[144,504]{1,0:T(8,128)(2,1)} %get-tuple-element.41), channel_id=1, source_target_pairs={{0,8},{4,12},{8,0},{12,4},{1,9},{5,13},{9,1},{13,5},{2,10},{6,14},... | collective-permute-start | bytes 435464 | tf_op jit(solution)/shard_map/ppermute | solution.py:588
  9.2 3.8 %all-to-all-start = ((bf16[16,32,96]{2,1,0:T(8,128)(2,1)}), bf16[16,32,96]{2,1,0:T(8,128)(2,1)S(1)}, u32[]{:S(2)}, u32[]{:S(2)}) async-start(bf16[16,32,96]{2,1,0:T(8,128)(2,1)} %get-tuple-element.44), calls=%async_computation | async-start | bytes 262144 | tf_op jit(solution)/shard_map/all_to_all | solution.py:652
  13.0 3.7 %collective-permute-start.2 = (bf16[144,504]{1,0:T(8,128)(2,1)}, bf16[144,504]{1,0:T(8,128)(2,1)S(1)}, u32[]{:S(2)}, u32[]{:S(2)}) collective-permute-start(bf16[144,504]{1,0:T(8,128)(2,1)} %get-tuple-element.42), channel_id=1, source_target_pairs={{0,12},{4,8},{8,4},{12,0},{1,13},{5,9},{9,5},{13,1},{2,14},{6,10},... | collective-permute-start | bytes 435464 | tf_op jit(solution)/shard_map/ppermute | solution.py:588
  17.3 1.3 %collective-permute-start.3 = (f32[24,48]{1,0:T(8,128)}, f32[24,48]{1,0:T(8,128)S(1)}, u32[]{:S(2)}, u32[]{:S(2)}) collective-permute-start(f32[24,48]{1,0:T(8,128)} %get-tuple-element.43), channel_id=1, source_target_pairs={{4,0},{8,4},{12,8},{5,1},{9,5},{13,9},{6,2},{10,6},{14,10},{7,3},{... | collective-permute-start | bytes 13832 | tf_op jit(solution)/shard_map/ppermute | solution.py:665
  18.6 0.9 %copy-done = f32[16,3,1152]{2,0,1:T(8,128)S(1)} copy-done((f32[16,3,1152]{2,0,1:T(8,128)S(1)}, f32[16,3,1152]{2,0,1:T(8,128)}, u32[]{:S(2)}) %copy-start) | copy-done | bytes 221208
  19.6 0.9 %copy-done.2 = bf16[144,504]{1,0:T(8,128)(2,1)S(1)} copy-done((bf16[144,504]{1,0:T(8,128)(2,1)S(1)}, bf16[144,504]{1,0:T(8,128)(2,1)}, u32[]{:S(2)}) %copy-start.2) | copy-done | bytes 145176
  20.5 0.8 %copy-done.3 = bf16[16,1152]{1,0:T(8,128)(2,1)S(1)} copy-done((bf16[16,1152]{1,0:T(8,128)(2,1)S(1)}, bf16[16,1152]{1,0:T(8,128)(2,1)}, u32[]{:S(2)}) %copy-start.3) | copy-done | bytes 36888
  21.7 3.7 %collective-permute-done.3.refs_1_ = f32[24,48]{1,0:T(8,128)S(1)} collective-permute-done((f32[24,48]{1,0:T(8,128)}, f32[24,48]{1,0:T(8,128)S(1)}, u32[]{:S(2)}, u32[]{:S(2)}) %collective-permute-start.3) | collective-permute-done | bytes 4640 | tf_op jit(solution)/shard_map/ppermute | solution.py:665
  25.4 0.6 copy-done.10
  26.2 1.6 %collective-permute-start.10 = (bf16[144,1152]{1,0:T(8,128)(2,1)S(1)}, bf16[144,1152]{1,0:T(8,128)(2,1)S(1)}, u32[]{:S(2)}, u32[]{:S(2)}) collective-permute-start(bf16[144,1152]{1,0:T(8,128)(2,1)S(1)} %shard_map.162.refs_0_), channel_id=1, source_target_pairs={{0,16},{16,0},{1,17},{17,1},{2,18},{18,2},{3,19},{19,3},{4,20},{20... | collective-permute-start | bytes 995336 | tf_op jit(solution)/shard_map/ppermute | solution.py:588
  27.8 1.5 %collective-permute-start.9 = (bf16[144,1152]{1,0:T(8,128)(2,1)S(1)}, bf16[144,1152]{1,0:T(8,128)(2,1)S(1)}, u32[]{:S(2)}, u32[]{:S(2)}) collective-permute-start(bf16[144,1152]{1,0:T(8,128)(2,1)S(1)} %shard_map.162.refs_0_), channel_id=1, source_target_pairs={{0,2},{2,0},{1,3},{3,1},{4,6},{6,4},{5,7},{7,5},{8,10},{10,8},{9,1... | collective-permute-start | bytes 995336 | tf_op jit(solution)/shard_map/ppermute | solution.py:588
  29.8 1.0 %collective-permute-done.8.other = bf16[16,32,96]{2,1,0:T(8,128)(2,1)S(1)} collective-permute-done((bf16[16,32,96]{2,1,0:T(8,128)(2,1)S(1)}, bf16[16,32,96]{2,1,0:T(8,128)(2,1)S(1)}, u32[]{:S(2)}, u32[]{:S(2)}) %collective-permute-start.8) | collective-permute-done | bytes 98336 | tf_op jit(solution)/shard_map/ppermute | solution.py:588
  30.9 2.4 %shard_map.160 = (bf16[1024,1152]{1,0:T(8,128)(2,1)S(1)}, bf16[16,64,256]{2,1,0:T(8,128)(2,1)S(1)}, f32[16,1,256]{2,1,0:T(1,128)S(1)}, f32[2,16,16,128]{3,2,1,0:T(8,128)S(1)}) custom-call(bf16[16,32,96]{2,1,0:T(8,128)(2,1)S(1)} %all-to-all-done.mine, bf16[16,32,96]{2,1,0:T(8,128)(2,1)S(1)} %collective-permute-done.8.other, ...), custom_call_target="tpu_custom_call" | custom-call | flops 1000000 | bytes 8000000 | tf_op jit(solution)/shard_map/pallas_call | solution.py:676
  33.4 6.1 %shard_map.161 = bf16[16,72,240]{2,1,0:T(8,128)(2,1)} custom-call(bf16[144,504]{1,0:T(8,128)(2,1)S(1)} %get-tuple-element.39.refs_0_, bf16[144,504]{1,0:T(8,128)(2,1)S(1)} %collective-permute-done.refs_1_, bf16[144,504]{1,0:T(8,128)(2,1)S(1)} %collective-permute-done.1.refs_2_, bf16[144,504]{1,0:T(8,128)(2,1)S(1)} %collective-permute-done.2.refs_3_, ...), custom_call_target="tpu_custom_call" | custom-call | flops 1000000 | bytes 100000000 | tf_op jit(solution)/shard_map/pallas_call | solution.py:687
  39.5 4.8 %all-to-all-start.1 = ((bf16[16,72,240]{2,1,0:T(8,128)(2,1)}), bf16[16,72,240]{2,1,0:T(8,128)(2,1)S(1)}, u32[]{:S(2)}, u32[]{:S(2)}) async-start(bf16[16,72,240]{2,1,0:T(8,128)(2,1)} %shard_map.161), calls=%async_computation.1 | async-start | bytes 1179648 | tf_op jit(solution)/shard_map/all_to_all | solution.py:703
  44.4 2.0 %collective-permute-start.11 = (bf16[80,1152]{1,0:T(8,128)(2,1)S(1)}, bf16[80,1152]{1,0:T(8,128)(2,1)S(1)}, u32[]{:S(2)}, u32[]{:S(2)}) collective-permute-start(bf16[80,1152]{1,0:T(8,128)(2,1)S(1)} %slice.6), channel_id=1, source_target_pairs={{0,16},{16,0},{1,17},{17,1},{2,18},{18,2},{3,19},{19,3},{4,20},{20... | collective-permute-start | bytes 552968 | tf_op jit(solution)/shard_map/ppermute | solution.py:588
  46.4 1.5 %collective-permute-start.12 = (bf16[64,1152]{1,0:T(8,128)(2,1)S(1)}, bf16[64,1152]{1,0:T(8,128)(2,1)S(1)}, u32[]{:S(2)}, u32[]{:S(2)}) collective-permute-start(bf16[64,1152]{1,0:T(8,128)(2,1)S(1)} %slice.7), channel_id=1, source_target_pairs={{0,2},{2,0},{1,3},{3,1},{4,6},{6,4},{5,7},{7,5},{8,10},{10,8},{9,1... | collective-permute-start | bytes 442376 | tf_op jit(solution)/shard_map/ppermute | solution.py:588
  49.1 0.7 %copy-done.11 = f32[24,48]{1,0:T(8,128)S(1)} copy-done((f32[24,48]{1,0:T(8,128)S(1)}, f32[24,48]{1,0:T(8,128)}, u32[]{:S(2)}) %copy-start.11) | copy-done | bytes 4632
  49.8 0.7 copy-done.19
  50.5 1.0 %shard_map.163 = (bf16[96,1152]{1,0:T(8,128)(2,1)S(1)}, bf16[96,240]{1,0:T(8,128)(2,1)S(1)}, f32[8,240]{1,0:T(8,128)S(1)}, f32[8,240]{1,0:T(8,128)S(1)}, f32[8,4...) custom-call(f32[24,192]{1,0:T(8,128)S(1)} %copy-done.8, f32[24,48]{1,0:T(8,128)S(1)} %copy-done.11, ...), custom_call_target="tpu_custom_call" | custom-call | flops 1000000 | bytes 1000000 | tf_op jit(solution)/shard_map/pallas_call | solution.py:723
  51.5 0.6 copy-done.5
  52.1 0.6 copy-done.12
  52.7 0.6 copy-done.14
  53.9 1.5 %collective-permute-done.12.refs_4_ = bf16[64,1152]{1,0:T(8,128)(2,1)S(1)} collective-permute-done((bf16[64,1152]{1,0:T(8,128)(2,1)S(1)}, bf16[64,1152]{1,0:T(8,128)(2,1)S(1)}, u32[]{:S(2)}, u32[]{:S(2)}) %collective-permute-start.12) | collective-permute-done | bytes 147488 | tf_op jit(solution)/shard_map/ppermute | solution.py:588
  55.9 1.1 %collective-permute-done.17.refs_9_ = bf16[64,1152]{1,0:T(8,128)(2,1)S(1)} collective-permute-done((bf16[64,1152]{1,0:T(8,128)(2,1)S(1)}, bf16[64,1152]{1,0:T(8,128)(2,1)S(1)}, u32[]{:S(2)}, u32[]{:S(2)}) %collective-permute-start.17) | collective-permute-done | bytes 147488 | tf_op jit(solution)/shard_map/ppermute | solution.py:588
  57.0 4.2 %all-to-all-done.1.refs_10_ = bf16[16,72,240]{2,1,0:T(8,128)(2,1)S(1)} async-done(((bf16[16,72,240]{2,1,0:T(8,128)(2,1)}), bf16[16,72,240]{2,1,0:T(8,128)(2,1)S(1)}, u32[]{:S(2)}, u32[]{:S(2)}) %all-to-all-start.1) | async-done | bytes 552992 | tf_op jit(solution)/shard_map/all_to_all | solution.py:703
  61.2 0.8 %copy-done.6 = bf16[16,1152]{1,0:T(8,128)(2,1)S(1)} copy-done((bf16[16,1152]{1,0:T(8,128)(2,1)S(1)}, bf16[16,1152]{1,0:T(8,128)(2,1)}, u32[]{:S(2)}) %copy-start.6) | copy-done | bytes 36888
  62.0 2.5 %shard_map.164 = (f32[8,240]{1,0:T(8,128)S(1)}, f32[8,240]{1,0:T(8,128)S(1)}) custom-call(bf16[144,1152]{1,0:T(8,128)(2,1)S(1)} %shard_map.162.refs_0_, bf16[144,1152]{1,0:T(8,128)(2,1)S(1)} %collective-permute-done.9.refs_1_, bf16[144,1152]{1,0:T(8,128)(2,1)S(1)} %collective-permute-done.10.refs_2_, bf16[80,1152]{1,0:T(8,128)(2,1)S(1)} %collective-permute-done.11.refs_3_, ...), custom_call_target="tpu_custom_call" | custom-call | flops 1000000 | bytes 8000000 | tf_op jit(solution)/shard_map/pallas_call | solution.py:741
  64.5 1.2 %collective-permute-done.18.partner = f32[8,240]{1,0:T(8,128)S(1)} collective-permute-done((f32[8,240]{1,0:T(8,128)S(1)}, f32[8,240]{1,0:T(8,128)S(1)}, u32[]{:S(2)}, u32[]{:S(2)}) %collective-permute-start.18) | collective-permute-done | bytes 7712 | tf_op jit(solution)/shard_map/ppermute | solution.py:588
  65.7 0.7 %shard_map.165 = (f32[4,8,48]{2,1,0:T(8,128)}, f32[4,8,48]{2,1,0:T(8,128)}) custom-call(f32[8,240]{1,0:T(8,128)S(1)} %get-tuple-element.68.mine, f32[8,240]{1,0:T(8,128)S(1)} %collective-permute-done.18.partner, f32[8,240]{1,0:T(8,128)S(1)} %copy-done.13, f32[8,240]{1,0:T(8,128)S(1)} %copy-done.15, f32[8,48]{1,0:T(8,128)S(1)} %get-tuple-element.72.noise, ...), custom_call_target="tpu_custom_call" | custom-call | flops 1000000 | bytes 1000000 | tf_op jit(solution)/shard_map/pallas_call | solution.py:750
  (67 shorter events, 3.5 us)
Async XLA Ops:
  0.6 32.7 %copy-start.20 = (f32[72]{0:T(128)S(1)}, f32[72]{0:T(128)}, u32[]{:S(2)}) copy-start(f32[72]{0:T(128)} %param.23) | copy-start | bytes 868
  0.6 32.7 %copy-start.21 = (f32[72]{0:T(128)S(1)}, f32[72]{0:T(128)}, u32[]{:S(2)}) copy-start(f32[72]{0:T(128)} %param.24) | copy-start | bytes 868
  3.6 13.2 %collective-permute-start = (bf16[144,504]{1,0:T(8,128)(2,1)}, bf16[144,504]{1,0:T(8,128)(2,1)S(1)}, u32[]{:S(2)}, u32[]{:S(2)}) collective-permute-start(bf16[144,504]{1,0:T(8,128)(2,1)} %get-tuple-element.40), channel_id=1, source_target_pairs={{0,4},{4,0},{8,12},{12,8},{1,5},{5,1},{9,13},{13,9},{2,6},{6,2},{1... | collective-permute-start | bytes 435464 | tf_op jit(solution)/shard_map/ppermute | solution.py:588
  6.6 10.7 %collective-permute-start.1 = (bf16[144,504]{1,0:T(8,128)(2,1)}, bf16[144,504]{1,0:T(8,128)(2,1)S(1)}, u32[]{:S(2)}, u32[]{:S(2)}) collective-permute-start(bf16[144,504]{1,0:T(8,128)(2,1)} %get-tuple-element.41), channel_id=1, source_target_pairs={{0,8},{4,12},{8,0},{12,4},{1,9},{5,13},{9,1},{13,5},{2,10},{6,14},... | collective-permute-start | bytes 435464 | tf_op jit(solution)/shard_map/ppermute | solution.py:588
  9.2 16.8 %all-to-all-start = ((bf16[16,32,96]{2,1,0:T(8,128)(2,1)}), bf16[16,32,96]{2,1,0:T(8,128)(2,1)S(1)}, u32[]{:S(2)}, u32[]{:S(2)}) async-start(bf16[16,32,96]{2,1,0:T(8,128)(2,1)} %get-tuple-element.44), calls=%async_computation | async-start | bytes 262144 | tf_op jit(solution)/shard_map/all_to_all | solution.py:652
  13.0 13.0 %collective-permute-start.2 = (bf16[144,504]{1,0:T(8,128)(2,1)}, bf16[144,504]{1,0:T(8,128)(2,1)S(1)}, u32[]{:S(2)}, u32[]{:S(2)}) collective-permute-start(bf16[144,504]{1,0:T(8,128)(2,1)} %get-tuple-element.42), channel_id=1, source_target_pairs={{0,12},{4,8},{8,4},{12,0},{1,13},{5,9},{9,5},{13,1},{2,14},{6,10},... | collective-permute-start | bytes 435464 | tf_op jit(solution)/shard_map/ppermute | solution.py:588
  16.8 9.3 %collective-permute-start.4 = (bf16[144,504]{1,0:T(8,128)(2,1)}, bf16[144,504]{1,0:T(8,128)(2,1)S(1)}, u32[]{:S(2)}, u32[]{:S(2)}) collective-permute-start(bf16[144,504]{1,0:T(8,128)(2,1)} %get-tuple-element.38.own_source), channel_id=1, source_target_pairs={{0,1},{1,0},{2,3},{3,2},{4,5},{5,4},{6,7},{7,6},{8,9},{9,8},{10,11... | collective-permute-start | bytes 435464 | tf_op jit(solution)/shard_map/ppermute | solution.py:588
  16.8 9.3 %collective-permute-start.5 = (bf16[144,504]{1,0:T(8,128)(2,1)S(1)}, bf16[144,504]{1,0:T(8,128)(2,1)S(1)}, u32[]{:S(2)}, u32[]{:S(2)}) collective-permute-start(bf16[144,504]{1,0:T(8,128)(2,1)S(1)} %collective-permute-done.refs_1_), channel_id=1, source_target_pairs={{0,1},{1,0},{2,3},{3,2},{4,5},{5,4},{6,7},{7,6},{8,9},{9,8},{10,11... | collective-permute-start | bytes 435464 | tf_op jit(solution)/shard_map/ppermute | solution.py:588
  17.3 8.8 %collective-permute-start.6 = (bf16[144,504]{1,0:T(8,128)(2,1)S(1)}, bf16[144,504]{1,0:T(8,128)(2,1)S(1)}, u32[]{:S(2)}, u32[]{:S(2)}) collective-permute-start(bf16[144,504]{1,0:T(8,128)(2,1)S(1)} %collective-permute-done.1.refs_2_), channel_id=1, source_target_pairs={{0,1},{1,0},{2,3},{3,2},{4,5},{5,4},{6,7},{7,6},{8,9},{9,8},{10,11... | collective-permute-start | bytes 435464 | tf_op jit(solution)/shard_map/ppermute | solution.py:588
  17.3 8.1 %collective-permute-start.3 = (f32[24,48]{1,0:T(8,128)}, f32[24,48]{1,0:T(8,128)S(1)}, u32[]{:S(2)}, u32[]{:S(2)}) collective-permute-start(f32[24,48]{1,0:T(8,128)} %get-tuple-element.43), channel_id=1, source_target_pairs={{4,0},{8,4},{12,8},{5,1},{9,5},{13,9},{6,2},{10,6},{14,10},{7,3},{... | collective-permute-start | bytes 13832 | tf_op jit(solution)/shard_map/ppermute | solution.py:665
  26.2 13.3 %collective-permute-start.10 = (bf16[144,1152]{1,0:T(8,128)(2,1)S(1)}, bf16[144,1152]{1,0:T(8,128)(2,1)S(1)}, u32[]{:S(2)}, u32[]{:S(2)}) collective-permute-start(bf16[144,1152]{1,0:T(8,128)(2,1)S(1)} %shard_map.162.refs_0_), channel_id=1, source_target_pairs={{0,16},{16,0},{1,17},{17,1},{2,18},{18,2},{3,19},{19,3},{4,20},{20... | collective-permute-start | bytes 995336 | tf_op jit(solution)/shard_map/ppermute | solution.py:588
  27.8 11.7 %collective-permute-start.9 = (bf16[144,1152]{1,0:T(8,128)(2,1)S(1)}, bf16[144,1152]{1,0:T(8,128)(2,1)S(1)}, u32[]{:S(2)}, u32[]{:S(2)}) collective-permute-start(bf16[144,1152]{1,0:T(8,128)(2,1)S(1)} %shard_map.162.refs_0_), channel_id=1, source_target_pairs={{0,2},{2,0},{1,3},{3,1},{4,6},{6,4},{5,7},{7,5},{8,10},{10,8},{9,1... | collective-permute-start | bytes 995336 | tf_op jit(solution)/shard_map/ppermute | solution.py:588
  29.3 4.0 %collective-permute-start.7 = (bf16[144,504]{1,0:T(8,128)(2,1)S(1)}, bf16[144,504]{1,0:T(8,128)(2,1)S(1)}, u32[]{:S(2)}, u32[]{:S(2)}) collective-permute-start(bf16[144,504]{1,0:T(8,128)(2,1)S(1)} %collective-permute-done.2.refs_3_), channel_id=1, source_target_pairs={{0,1},{1,0},{2,3},{3,2},{4,5},{5,4},{6,7},{7,6},{8,9},{9,8},{10,11... | collective-permute-start | bytes 435464 | tf_op jit(solution)/shard_map/ppermute | solution.py:588
  29.3 1.6 %collective-permute-start.8 = (bf16[16,32,96]{2,1,0:T(8,128)(2,1)S(1)}, bf16[16,32,96]{2,1,0:T(8,128)(2,1)S(1)}, u32[]{:S(2)}, u32[]{:S(2)}) collective-permute-start(bf16[16,32,96]{2,1,0:T(8,128)(2,1)S(1)} %all-to-all-done.mine), channel_id=1, source_target_pairs={{0,1},{1,0},{2,3},{3,2},{4,5},{5,4},{6,7},{7,6},{8,9},{9,8},{10,11... | collective-permute-start | bytes 294920 | tf_op jit(solution)/shard_map/ppermute | solution.py:588
  33.3 15.1 %copy-start.22 = (f32[1152]{0:T(1024)S(1)}, f32[1152]{0:T(1024)}, u32[]{:S(2)}) copy-start(f32[1152]{0:T(1024)} %param.26) | copy-start | bytes 13828
  33.3 15.8 %copy-start.1 = (f32[16,3,1152]{2,0,1:T(8,128)S(1)}, f32[16,3,1152]{2,0,1:T(8,128)}, u32[]{:S(2)}) copy-start(f32[16,3,1152]{2,0,1:T(8,128)} %param.20) | copy-start | bytes 663556
  33.3 15.8 %copy-start.4 = (bf16[16,1152]{1,0:T(8,128)(2,1)S(1)}, bf16[16,1152]{1,0:T(8,128)(2,1)}, u32[]{:S(2)}) copy-start(bf16[16,1152]{1,0:T(8,128)(2,1)} %refs_4_.1) | copy-start | bytes 110596
  33.3 15.8 %copy-start.7 = (bf16[1152,16]{0,1:T(8,128)(2,1)S(1)}, bf16[1152,16]{0,1:T(8,128)(2,1)}, u32[]{:S(2)}) copy-start(bf16[1152,16]{0,1:T(8,128)(2,1)} %param.27) | copy-start | bytes 110596
  33.4 15.7 %copy-start.8 = (f32[24,192]{1,0:T(8,128)S(1)}, f32[24,192]{1,0:T(8,128)}, u32[]{:S(2)}) copy-start(f32[24,192]{1,0:T(8,128)} %get-tuple-element.59.refs_0_) | copy-start | bytes 55300
  33.4 15.7 %copy-start.9 = (f32[1,1152]{1,0:T(1,128)S(1)}, f32[1,1152]{1,0:T(1,128)}, u32[]{:S(2)}) copy-start(f32[1,1152]{1,0:T(1,128)} %refs_2_.1) | copy-start | bytes 13828
  33.4 15.7 %copy-start.16 = (f32[8,48]{1,0:T(8,128)S(1)}, f32[8,48]{1,0:T(8,128)}, u32[]{:S(2)}) copy-start(f32[8,48]{1,0:T(8,128)} %refs_7_.1) | copy-start | bytes 4612
  39.5 21.7 %all-to-all-start.1 = ((bf16[16,72,240]{2,1,0:T(8,128)(2,1)}), bf16[16,72,240]{2,1,0:T(8,128)(2,1)S(1)}, u32[]{:S(2)}, u32[]{:S(2)}) async-start(bf16[16,72,240]{2,1,0:T(8,128)(2,1)} %shard_map.161), calls=%async_computation.1 | async-start | bytes 1179648 | tf_op jit(solution)/shard_map/all_to_all | solution.py:703
  44.4 11.0 %collective-permute-start.11 = (bf16[80,1152]{1,0:T(8,128)(2,1)S(1)}, bf16[80,1152]{1,0:T(8,128)(2,1)S(1)}, u32[]{:S(2)}, u32[]{:S(2)}) collective-permute-start(bf16[80,1152]{1,0:T(8,128)(2,1)S(1)} %slice.6), channel_id=1, source_target_pairs={{0,16},{16,0},{1,17},{17,1},{2,18},{18,2},{3,19},{19,3},{4,20},{20... | collective-permute-start | bytes 552968 | tf_op jit(solution)/shard_map/ppermute | solution.py:588
  46.4 9.0 %collective-permute-start.12 = (bf16[64,1152]{1,0:T(8,128)(2,1)S(1)}, bf16[64,1152]{1,0:T(8,128)(2,1)S(1)}, u32[]{:S(2)}, u32[]{:S(2)}) collective-permute-start(bf16[64,1152]{1,0:T(8,128)(2,1)S(1)} %slice.7), channel_id=1, source_target_pairs={{0,2},{2,0},{1,3},{3,1},{4,6},{6,4},{5,7},{7,5},{8,10},{10,8},{9,1... | collective-permute-start | bytes 442376 | tf_op jit(solution)/shard_map/ppermute | solution.py:588
  47.9 9.1 %collective-permute-start.13 = (bf16[144,1152]{1,0:T(8,128)(2,1)S(1)}, bf16[144,1152]{1,0:T(8,128)(2,1)S(1)}, u32[]{:S(2)}, u32[]{:S(2)}) collective-permute-start(bf16[144,1152]{1,0:T(8,128)(2,1)S(1)} %shard_map.162.refs_0_), channel_id=1, source_target_pairs={{0,1},{1,0},{2,3},{3,2},{4,5},{5,4},{6,7},{7,6},{8,9},{9,8},{10,11... | collective-permute-start | bytes 995336 | tf_op jit(solution)/shard_map/ppermute | solution.py:588
  47.9 9.1 %collective-permute-start.14 = (bf16[144,1152]{1,0:T(8,128)(2,1)S(1)}, bf16[144,1152]{1,0:T(8,128)(2,1)S(1)}, u32[]{:S(2)}, u32[]{:S(2)}) collective-permute-start(bf16[144,1152]{1,0:T(8,128)(2,1)S(1)} %collective-permute-done.9.refs_1_), channel_id=1, source_target_pairs={{0,1},{1,0},{2,3},{3,2},{4,5},{5,4},{6,7},{7,6},{8,9},{9,8},{10,11... | collective-permute-start | bytes 995336 | tf_op jit(solution)/shard_map/ppermute | solution.py:588
  48.4 8.6 %collective-permute-start.15 = (bf16[144,1152]{1,0:T(8,128)(2,1)S(1)}, bf16[144,1152]{1,0:T(8,128)(2,1)S(1)}, u32[]{:S(2)}, u32[]{:S(2)}) collective-permute-start(bf16[144,1152]{1,0:T(8,128)(2,1)S(1)} %collective-permute-done.10.refs_2_), channel_id=1, source_target_pairs={{0,1},{1,0},{2,3},{3,2},{4,5},{5,4},{6,7},{7,6},{8,9},{9,8},{10,11... | collective-permute-start | bytes 995336 | tf_op jit(solution)/shard_map/ppermute | solution.py:588
  55.3 1.7 %collective-permute-start.16 = (bf16[80,1152]{1,0:T(8,128)(2,1)S(1)}, bf16[80,1152]{1,0:T(8,128)(2,1)S(1)}, u32[]{:S(2)}, u32[]{:S(2)}) collective-permute-start(bf16[80,1152]{1,0:T(8,128)(2,1)S(1)} %collective-permute-done.11.refs_3_), channel_id=1, source_target_pairs={{0,1},{1,0},{2,3},{3,2},{4,5},{5,4},{6,7},{7,6},{8,9},{9,8},{10,11... | collective-permute-start | bytes 552968 | tf_op jit(solution)/shard_map/ppermute | solution.py:588
  55.4 1.6 %collective-permute-start.17 = (bf16[64,1152]{1,0:T(8,128)(2,1)S(1)}, bf16[64,1152]{1,0:T(8,128)(2,1)S(1)}, u32[]{:S(2)}, u32[]{:S(2)}) collective-permute-start(bf16[64,1152]{1,0:T(8,128)(2,1)S(1)} %collective-permute-done.12.refs_4_), channel_id=1, source_target_pairs={{0,1},{1,0},{2,3},{3,2},{4,5},{5,4},{6,7},{7,6},{8,9},{9,8},{10,11... | collective-permute-start | bytes 442376 | tf_op jit(solution)/shard_map/ppermute | solution.py:588
  62.0 3.7 %copy-start.15 = (f32[8,240]{1,0:T(8,128)S(1)}, f32[8,240]{1,0:T(8,128)}, u32[]{:S(2)}) copy-start(f32[8,240]{1,0:T(8,128)} %copy-done.14) | copy-start | bytes 23044
  62.0 3.7 %copy-start.18 = (f32[8,128]{1,0:T(8,128)S(1)}, f32[8,128]{1,0:T(8,128)}, u32[]{:S(2)}) copy-start(f32[8,128]{1,0:T(8,128)} %copy-done.17) | copy-start | bytes 12292
  64.5 1.2 %collective-permute-start.18 = (f32[8,240]{1,0:T(8,128)S(1)}, f32[8,240]{1,0:T(8,128)S(1)}, u32[]{:S(2)}, u32[]{:S(2)}) collective-permute-start(f32[8,240]{1,0:T(8,128)S(1)} %get-tuple-element.69), channel_id=1, source_target_pairs={{0,1},{1,0},{2,3},{3,2},{4,5},{5,4},{6,7},{7,6},{8,9},{9,8},{10,11... | collective-permute-start | bytes 23048 | tf_op jit(solution)/shard_map/ppermute | solution.py:588
  (12 other events, 11.4 us)

commit v12 on v11

--- a/solution.py
+++ b/solution.py
@@ -470,8 +470,8 @@
 
 def ready_kernel(values, half, *refs):
     sources, table, index = refs[:8], refs[8], refs[9]
-    left, right, base, factor, noise_out, guide, final_out = refs[10:17]
-    held, sems = refs[17:25], refs[25]
+    left, right, base, factor, noise_out, guide = refs[10:16]
+    held, sems = refs[16:24], refs[24]
     copies = []
     for i, (source, to) in enumerate(zip(sources, held)):
         source = source.at[2] if i == 3 else source
@@ -492,7 +492,7 @@
         + [zero]
         + split_terms(gates[...], 3)
         + split_terms(final_gain[...], 3)
-        + [zero],
+        + [zero, final_w[...]],
         axis=0,
     )
     level = info[values : values + 1]
@@ -510,13 +510,12 @@
         [packed[pl.ds(own, half), :], following[pl.ds(own, half), :]], axis=1
     )
     noise_out[...] = noise[...]
-    final_out[...] = final_w[...]
     guide[...] = jnp.full(guide.shape, table[index[0]], F32)
 
 
 def finish_kernel(half, values, queues, *refs):
     parts = [refs[:5], refs[5:10]]
-    attended, left, right, final_w, mine, send, scratch, mixed = refs[10:]
+    attended, left, right, mine, send, scratch, mixed = refs[10:]
     scene, q_at, tok, core = (place_of(a) for a in ("scene", "queue", "tok", "cfg"))
     group = parts[0][0].shape[1] // queues
     columns = parts[0][0].shape[0]
@@ -550,16 +549,17 @@
             at = (c * queues + k) * columns
             mixed[pl.ds(pl.multiple_of(first, 8), columns), :] = total[at : at + columns]
 
-    first, last = values + 16, left.shape[0] - 16
+    first, terms = values + 16, right.shape[0]
+    last = terms - 16
     emb = dot_tn(left[:first], right[:first])
     gate = dot_tn(left[first:last], right[first:last])
-    gain = dot_tn(left[last:], right[last:])
+    gain = dot_tn(left[last:terms], right[last:])
     summed = emb + gate * mixed[...]
     center = jnp.mean(summed, axis=0, keepdims=True)
     deviate = summed - center
     spread = jnp.mean(deviate * deviate, axis=0, keepdims=True)
     final = (deviate * lax.rsqrt(spread + EPS_NORM) * gain).astype(BF16)
-    scratch[...] = jnp.dot(final_w[...], final, preferred_element_type=F32)
+    scratch[...] = jnp.dot(left[terms:], final, preferred_element_type=F32)
     own = pl.multiple_of(core * half, half)
     other = pl.multiple_of((1 - core) * half, half)
     mine[...] = scratch[pl.ds(own, half), :]
@@ -648,10 +648,6 @@
     )
 
     near = [chunks[0]] + [swapped(chunks[k], "queue", k) for k in range(1, queues)]
-    far = [swapped(piece, "cfg", 1) for piece in near]
-    shares = lax.all_to_all(copies, ("scene", "queue", "tok"), 0, 0)
-    other_shares = swapped(shares, "cfg", 1)
-
     own, level_rows, embed_held = kernel_call(
         stage_kernel,
         [
@@ -662,6 +658,13 @@
         "hhh",
         [pltpu.SemaphoreType.DMA((3,))],
     )(chunks[0], mods, embed_weight)
+    near[1], own, level_rows, embed_held = lax.optimization_barrier(
+        (near[1], own, level_rows, embed_held)
+    )
+    far = [swapped(piece, "cfg", 1) for piece in near]
+    shares = lax.all_to_all(copies, ("scene", "queue", "tok"), 0, 0)
+    other_shares = swapped(shares, "cfg", 1)
+
     following = lax.ppermute(first, "queue", [(i + 1, i) for i in range(queues - 1)])
     near[-1], following, shares, *far[:-1] = lax.optimization_barrier(
         (near[-1], following, shares, *far[:-1])
@@ -720,16 +723,15 @@
         pltpu.VMEM(a.shape[1:] if i == 3 else a.shape, a.dtype) for i, a in enumerate(smalls)
     ]
     terms = values + 16 + 3 * levels_all + 16
-    left, right, *rest, final_held = kernel_call(
+    left, right, *rest = kernel_call(
         functools.partial(ready_kernel, values, half),
         [
-            jax.ShapeDtypeStruct((terms, width), BF16),
+            jax.ShapeDtypeStruct((terms + values, width), BF16),
             jax.ShapeDtypeStruct((terms, row_lanes), BF16),
             half_shape,
             half_shape,
             jax.ShapeDtypeStruct(fresh_noise.shape, F32),
             jax.ShapeDtypeStruct((8, LANES), F32),
-            jax.ShapeDtypeStruct((values, width), BF16),
         ],
         "ha" + "h" * 6 + "ss",
         places + [pltpu.SemaphoreType.DMA((len(smalls),))],
@@ -741,10 +743,10 @@
     mine, send = kernel_call(
         functools.partial(finish_kernel, half, values, queues),
         [half_shape] * 2,
-        "v" * 14,
+        "v" * 13,
         [pltpu.VMEM((values, row_lanes), F32), pltpu.VMEM((width, row_lanes), F32)],
         bytes_accessed=8_000_000,
-    )(*away, *away_far, received, left, right, final_held)
+    )(*away, *away_far, received, left, right)
     partner = swapped(send, "cfg", 1)
     shape = jax.ShapeDtypeStruct((frames, half, tokens), F32)
     return kernel_call(update_kernel, [shape, shape], "v" * 6)(mine, partner, *rest)

time: 67 us -> 66 us (0.985)
  waiting for transfers between devices: 12.8 us -> 15.7 us
  local copies, waits for them, and re-layouts: 7.81 us -> 5.3 us
  starting transfers between devices: 28 us -> 26.7 us
    unnamed x46 -> x38, local copies, waits for them, and re-layouts: 7.78 us -> 5.26 us
    ppermute x18, waiting for transfers between devices: 4.87 us -> 6.5 us  [swapped(): return lax.ppermute(value, axis, [(i, i ^ mask) for i in range(count)])]
    all_to_all x1, starting transfers between devices: 4.81 us -> 3.58 us  [on_device_heads(): received = lax.all_to_all(attended, ('tok', 'queue', 'scene'), 0, 0)]
    ppermute x1, waiting for transfers between devices: 3.74 us -> 4.5 us  [on_device_heads(): lax.ppermute(first, 'queue', [(i + 1, i) for i in range(queues - 1)])]
where the time goes in v12:
time: 66 us; the launch traced here: 65.5 us
  starting transfers between devices  26.7 us (40%)
  Pallas kernels  16.2 us (25%)
  waiting for transfers between devices  15.7 us (24%)
  local copies, waits for them, and re-layouts  5.3 us (8%)
  between operations  1.57 us (2%)
    ppermute x18, starting transfers between devices, swapped(): return lax.ppermute(value, axis, [(i, i ^ mask) for i in range(count)])  18 us
    ppermute x18, waiting for transfers between devices, swapped(): return lax.ppermute(value, axis, [(i, i ^ mask) for i in range(count)])  6.5 us
    pallas_call x1, Pallas kernels, on_device_heads(): kernel_call(functools.partial(attend_kernel, frames, tokens, queues), jax...  6.13 us
    unnamed x38, local copies, waits for them, and re-layouts  5.26 us
    all_to_all x1, waiting for transfers between devices, on_device_heads(): received = lax.all_to_all(attended, ('tok', 'queue', 'scene'), 0, 0)  4.68 us
    ppermute x1, waiting for transfers between devices, on_device_heads(): lax.ppermute(first, 'queue', [(i + 1, i) for i in range(queues - 1)])  4.5 us
    all_to_all x1, starting transfers between devices, on_device_heads(): shares = lax.all_to_all(copies, ('scene', 'queue', 'tok'), 0, 0)  3.83 us
    all_to_all x1, starting transfers between devices, on_device_heads(): received = lax.all_to_all(attended, ('tok', 'queue', 'scene'), 0, 0)  3.58 us
  transfers between devices with their start and end apart: 21, of which 6 were waited for; matrix products, arithmetic and copies ran while one was open for 0% of the time, Pallas kernels for 15%

profile of v12, /device:TPU:0, one launch (start us, length us, event | category | flops | bytes accessed | tf_op | source)
XLA Modules:
  0.0 65.5 jit_solution(14648671502992829213)
XLA Ops:
  0.7 2.9 %shard_map.158 = (bf16[144,504]{1,0:T(8,128)(2,1)}, bf16[144,504]{1,0:T(8,128)(2,1)}, bf16[144,504]{1,0:T(8,128)(2,1)}, bf16[144,504]{1,0:T(8,128)(2,1)}, bf16[1...) custom-call(f32[4,16,48]{2,1,0:T(8,128)} %latents.1, s32[1,4]{1,0:T(1,128)} %bitcast.14, ...), custom_call_target="tpu_custom_call" | custom-call | flops 1000000 | bytes 8000000 | tf_op jit(solution)/shard_map/pallas_call | solution.py:629
  3.6 3.0 %collective-permute-start = (bf16[144,504]{1,0:T(8,128)(2,1)}, bf16[144,504]{1,0:T(8,128)(2,1)S(1)}, u32[]{:S(2)}, u32[]{:S(2)}) collective-permute-start(bf16[144,504]{1,0:T(8,128)(2,1)} %get-tuple-element.41), channel_id=1, source_target_pairs={{0,4},{4,0},{8,12},{12,8},{1,5},{5,1},{9,13},{13,9},{2,6},{6,2},{1... | collective-permute-start | bytes 435464 | tf_op jit(solution)/shard_map/ppermute | solution.py:588
  6.6 2.6 %collective-permute-start.1 = (bf16[144,504]{1,0:T(8,128)(2,1)}, bf16[144,504]{1,0:T(8,128)(2,1)S(1)}, u32[]{:S(2)}, u32[]{:S(2)}) collective-permute-start(bf16[144,504]{1,0:T(8,128)(2,1)} %get-tuple-element.48), channel_id=1, source_target_pairs={{0,8},{4,12},{8,0},{12,4},{1,9},{5,13},{9,1},{13,5},{2,10},{6,14},... | collective-permute-start | bytes 435464 | tf_op jit(solution)/shard_map/ppermute | solution.py:588
  9.2 3.8 %all-to-all-start = ((bf16[16,32,96]{2,1,0:T(8,128)(2,1)}), bf16[16,32,96]{2,1,0:T(8,128)(2,1)S(1)}, u32[]{:S(2)}, u32[]{:S(2)}) async-start(bf16[16,32,96]{2,1,0:T(8,128)(2,1)} %get-tuple-element.51), calls=%async_computation | async-start | bytes 262144 | tf_op jit(solution)/shard_map/all_to_all | solution.py:665
  13.0 3.7 %collective-permute-start.2 = (bf16[144,504]{1,0:T(8,128)(2,1)}, bf16[144,504]{1,0:T(8,128)(2,1)S(1)}, u32[]{:S(2)}, u32[]{:S(2)}) collective-permute-start(bf16[144,504]{1,0:T(8,128)(2,1)} %get-tuple-element.49), channel_id=1, source_target_pairs={{0,12},{4,8},{8,4},{12,0},{1,13},{5,9},{9,5},{13,1},{2,14},{6,10},... | collective-permute-start | bytes 435464 | tf_op jit(solution)/shard_map/ppermute | solution.py:588
  16.8 0.9 %copy-done = f32[16,3,1152]{2,0,1:T(8,128)S(1)} copy-done((f32[16,3,1152]{2,0,1:T(8,128)S(1)}, f32[16,3,1152]{2,0,1:T(8,128)}, u32[]{:S(2)}) %copy-start) | copy-done | bytes 221208
  17.7 0.9 %copy-done.2 = bf16[144,504]{1,0:T(8,128)(2,1)S(1)} copy-done((bf16[144,504]{1,0:T(8,128)(2,1)S(1)}, bf16[144,504]{1,0:T(8,128)(2,1)}, u32[]{:S(2)}) %copy-start.2) | copy-done | bytes 145176
  18.6 0.8 %copy-done.3 = bf16[16,1152]{1,0:T(8,128)(2,1)S(1)} copy-done((bf16[16,1152]{1,0:T(8,128)(2,1)S(1)}, bf16[16,1152]{1,0:T(8,128)(2,1)}, u32[]{:S(2)}) %copy-start.3) | copy-done | bytes 36888
  19.8 0.6 collective-permute-start.5
  20.5 1.3 %collective-permute-start.3 = (f32[24,48]{1,0:T(8,128)}, f32[24,48]{1,0:T(8,128)S(1)}, u32[]{:S(2)}, u32[]{:S(2)}) collective-permute-start(f32[24,48]{1,0:T(8,128)} %get-tuple-element.50), channel_id=1, source_target_pairs={{4,0},{8,4},{12,8},{5,1},{9,5},{13,9},{6,2},{10,6},{14,10},{7,3},{... | collective-permute-start | bytes 13832 | tf_op jit(solution)/shard_map/ppermute | solution.py:668
  21.8 4.5 %collective-permute-done.3.refs_1_ = f32[24,48]{1,0:T(8,128)S(1)} collective-permute-done((f32[24,48]{1,0:T(8,128)}, f32[24,48]{1,0:T(8,128)S(1)}, u32[]{:S(2)}, u32[]{:S(2)}) %collective-permute-start.3) | collective-permute-done | bytes 4640 | tf_op jit(solution)/shard_map/ppermute | solution.py:668
  26.5 1.5 %collective-permute-start.9 = (bf16[144,1152]{1,0:T(8,128)(2,1)S(1)}, bf16[144,1152]{1,0:T(8,128)(2,1)S(1)}, u32[]{:S(2)}, u32[]{:S(2)}) collective-permute-start(bf16[144,1152]{1,0:T(8,128)(2,1)S(1)} %shard_map.162.refs_0_), channel_id=1, source_target_pairs={{0,2},{2,0},{1,3},{3,1},{4,6},{6,4},{5,7},{7,5},{8,10},{10,8},{9,1... | collective-permute-start | bytes 995336 | tf_op jit(solution)/shard_map/ppermute | solution.py:588
  28.0 1.5 %collective-permute-start.10 = (bf16[144,1152]{1,0:T(8,128)(2,1)S(1)}, bf16[144,1152]{1,0:T(8,128)(2,1)S(1)}, u32[]{:S(2)}, u32[]{:S(2)}) collective-permute-start(bf16[144,1152]{1,0:T(8,128)(2,1)S(1)} %shard_map.162.refs_0_), channel_id=1, source_target_pairs={{0,16},{16,0},{1,17},{17,1},{2,18},{18,2},{3,19},{19,3},{4,20},{20... | collective-permute-start | bytes 995336 | tf_op jit(solution)/shard_map/ppermute | solution.py:588
  30.0 1.0 %collective-permute-done.8.other = bf16[16,32,96]{2,1,0:T(8,128)(2,1)S(1)} collective-permute-done((bf16[16,32,96]{2,1,0:T(8,128)(2,1)S(1)}, bf16[16,32,96]{2,1,0:T(8,128)(2,1)S(1)}, u32[]{:S(2)}, u32[]{:S(2)}) %collective-permute-start.8) | collective-permute-done | bytes 98336 | tf_op jit(solution)/shard_map/ppermute | solution.py:588
  31.0 2.4 %shard_map.160 = (bf16[1024,1152]{1,0:T(8,128)(2,1)S(1)}, bf16[16,64,256]{2,1,0:T(8,128)(2,1)S(1)}, f32[16,1,256]{2,1,0:T(1,128)S(1)}, f32[2,16,16,128]{3,2,1,0:T(8,128)S(1)}) custom-call(bf16[16,32,96]{2,1,0:T(8,128)(2,1)S(1)} %all-to-all-done.mine, bf16[16,32,96]{2,1,0:T(8,128)(2,1)S(1)} %collective-permute-done.8.other, ...), custom_call_target="tpu_custom_call" | custom-call | flops 1000000 | bytes 8000000 | tf_op jit(solution)/shard_map/pallas_call | solution.py:679
  33.6 6.1 %shard_map.161 = bf16[16,72,240]{2,1,0:T(8,128)(2,1)} custom-call(bf16[144,504]{1,0:T(8,128)(2,1)S(1)} %get-tuple-element.46.refs_0_, bf16[144,504]{1,0:T(8,128)(2,1)S(1)} %collective-permute-done.refs_1_, bf16[144,504]{1,0:T(8,128)(2,1)S(1)} %collective-permute-done.1.refs_2_, bf16[144,504]{1,0:T(8,128)(2,1)S(1)} %collective-permute-done.2.refs_3_, ...), custom_call_target="tpu_custom_call" | custom-call | flops 1000000 | bytes 100000000 | tf_op jit(solution)/shard_map/pallas_call | solution.py:690
  39.7 3.6 %all-to-all-start.1 = ((bf16[16,72,240]{2,1,0:T(8,128)(2,1)}), bf16[16,72,240]{2,1,0:T(8,128)(2,1)S(1)}, u32[]{:S(2)}, u32[]{:S(2)}) async-start(bf16[16,72,240]{2,1,0:T(8,128)(2,1)} %shard_map.161), calls=%async_computation.1 | async-start | bytes 1179648 | tf_op jit(solution)/shard_map/all_to_all | solution.py:706
  43.3 1.9 %collective-permute-start.11 = (bf16[80,1152]{1,0:T(8,128)(2,1)S(1)}, bf16[80,1152]{1,0:T(8,128)(2,1)S(1)}, u32[]{:S(2)}, u32[]{:S(2)}) collective-permute-start(bf16[80,1152]{1,0:T(8,128)(2,1)S(1)} %slice.6), channel_id=1, source_target_pairs={{0,16},{16,0},{1,17},{17,1},{2,18},{18,2},{3,19},{19,3},{4,20},{20... | collective-permute-start | bytes 552968 | tf_op jit(solution)/shard_map/ppermute | solution.py:588
  45.2 1.6 %collective-permute-start.12 = (bf16[64,1152]{1,0:T(8,128)(2,1)S(1)}, bf16[64,1152]{1,0:T(8,128)(2,1)S(1)}, u32[]{:S(2)}, u32[]{:S(2)}) collective-permute-start(bf16[64,1152]{1,0:T(8,128)(2,1)S(1)} %slice.7), channel_id=1, source_target_pairs={{0,2},{2,0},{1,3},{3,1},{4,6},{6,4},{5,7},{7,5},{8,10},{10,8},{9,1... | collective-permute-start | bytes 442376 | tf_op jit(solution)/shard_map/ppermute | solution.py:588
  46.8 0.5 collective-permute-start.14
  48.0 1.0 %shard_map.163 = (bf16[112,1152]{1,0:T(8,128)(2,1)S(1)}, bf16[96,240]{1,0:T(8,128)(2,1)S(1)}, f32[8,240]{1,0:T(8,128)S(1)}, f32[8,240]{1,0:T(8,128)S(1)}, f32[8,48]{1,0:T(8,128)S(1)}, /*index=5*/f32[8,128]{1,0:T(8,128)S(1)}) custom-call(f32[24,192]{1,0:T(8,128)S(1)} %copy-done.8, f32[24,48]{1,0:T(8,128)S(1)} %collective-permute-done.3.refs_1_, ...), custom_call_target="tpu_custom_call" | custom-call | flops 1000000 | bytes 1000000 | tf_op jit(solution)/shard_map/pallas_call | solution.py:726
  49.0 0.6 copy-done.5
  49.6 0.6 copy-done.11
  50.2 0.6 copy-done.13
  50.8 3.1 %collective-permute-done.12.refs_4_ = bf16[64,1152]{1,0:T(8,128)(2,1)S(1)} collective-permute-done((bf16[64,1152]{1,0:T(8,128)(2,1)S(1)}, bf16[64,1152]{1,0:T(8,128)(2,1)S(1)}, u32[]{:S(2)}, u32[]{:S(2)}) %collective-permute-start.12) | collective-permute-done | bytes 147488 | tf_op jit(solution)/shard_map/ppermute | solution.py:588
  53.9 0.5 collective-permute-start.17
  54.4 1.1 %collective-permute-done.17.refs_9_ = bf16[64,1152]{1,0:T(8,128)(2,1)S(1)} collective-permute-done((bf16[64,1152]{1,0:T(8,128)(2,1)S(1)}, bf16[64,1152]{1,0:T(8,128)(2,1)S(1)}, u32[]{:S(2)}, u32[]{:S(2)}) %collective-permute-start.17) | collective-permute-done | bytes 147488 | tf_op jit(solution)/shard_map/ppermute | solution.py:588
  55.6 4.7 %all-to-all-done.1.refs_10_ = bf16[16,72,240]{2,1,0:T(8,128)(2,1)S(1)} async-done(((bf16[16,72,240]{2,1,0:T(8,128)(2,1)}), bf16[16,72,240]{2,1,0:T(8,128)(2,1)S(1)}, u32[]{:S(2)}, u32[]{:S(2)}) %all-to-all-start.1) | async-done | bytes 552992 | tf_op jit(solution)/shard_map/all_to_all | solution.py:706
  60.2 0.8 %copy-done.6 = bf16[96,240]{1,0:T(8,128)(2,1)S(1)} copy-done((bf16[96,240]{1,0:T(8,128)(2,1)S(1)}, bf16[96,240]{1,0:T(8,128)(2,1)}, u32[]{:S(2)}) %copy-start.6) | copy-done | bytes 46104
  61.0 2.5 %shard_map.164 = (f32[8,240]{1,0:T(8,128)S(1)}, f32[8,240]{1,0:T(8,128)S(1)}) custom-call(bf16[144,1152]{1,0:T(8,128)(2,1)S(1)} %shard_map.162.refs_0_, bf16[144,1152]{1,0:T(8,128)(2,1)S(1)} %collective-permute-done.9.refs_1_, bf16[144,1152]{1,0:T(8,128)(2,1)S(1)} %collective-permute-done.10.refs_2_, bf16[80,1152]{1,0:T(8,128)(2,1)S(1)} %collective-permute-done.11.refs_3_, ...), custom_call_target="tpu_custom_call" | custom-call | flops 1000000 | bytes 8000000 | tf_op jit(solution)/shard_map/pallas_call | solution.py:743
  63.5 1.2 %collective-permute-done.18.partner = f32[8,240]{1,0:T(8,128)S(1)} collective-permute-done((f32[8,240]{1,0:T(8,128)S(1)}, f32[8,240]{1,0:T(8,128)S(1)}, u32[]{:S(2)}, u32[]{:S(2)}) %collective-permute-start.18) | collective-permute-done | bytes 7712 | tf_op jit(solution)/shard_map/ppermute | solution.py:588
  64.7 0.7 %shard_map.165 = (f32[4,8,48]{2,1,0:T(8,128)}, f32[4,8,48]{2,1,0:T(8,128)}) custom-call(f32[8,240]{1,0:T(8,128)S(1)} %get-tuple-element.74.mine, f32[8,240]{1,0:T(8,128)S(1)} %collective-permute-done.18.partner, f32[8,240]{1,0:T(8,128)S(1)} %get-tuple-element.76.base, f32[8,240]{1,0:T(8,128)S(1)} %get-tuple-element.77.factor, f32[8,48]{1,0:T(8,128)S(1)} %copy-done.12, ...), custom_call_target="tpu_custom_call" | custom-call | flops 1000000 | bytes 1000000 | tf_op jit(solution)/shard_map/pallas_call | solution.py:752
  (59 shorter events, 1.4 us)
Async XLA Ops:
  0.6 32.8 %copy-start.16 = (f32[72]{0:T(128)S(1)}, f32[72]{0:T(128)}, u32[]{:S(2)}) copy-start(f32[72]{0:T(128)} %param.23) | copy-start | bytes 868
  0.6 32.8 %copy-start.17 = (f32[72]{0:T(128)S(1)}, f32[72]{0:T(128)}, u32[]{:S(2)}) copy-start(f32[72]{0:T(128)} %param.24) | copy-start | bytes 868
  3.6 16.2 %collective-permute-start = (bf16[144,504]{1,0:T(8,128)(2,1)}, bf16[144,504]{1,0:T(8,128)(2,1)S(1)}, u32[]{:S(2)}, u32[]{:S(2)}) collective-permute-start(bf16[144,504]{1,0:T(8,128)(2,1)} %get-tuple-element.41), channel_id=1, source_target_pairs={{0,4},{4,0},{8,12},{12,8},{1,5},{5,1},{9,13},{13,9},{2,6},{6,2},{1... | collective-permute-start | bytes 435464 | tf_op jit(solution)/shard_map/ppermute | solution.py:588
  6.6 13.8 %collective-permute-start.1 = (bf16[144,504]{1,0:T(8,128)(2,1)}, bf16[144,504]{1,0:T(8,128)(2,1)S(1)}, u32[]{:S(2)}, u32[]{:S(2)}) collective-permute-start(bf16[144,504]{1,0:T(8,128)(2,1)} %get-tuple-element.48), channel_id=1, source_target_pairs={{0,8},{4,12},{8,0},{12,4},{1,9},{5,13},{9,1},{13,5},{2,10},{6,14},... | collective-permute-start | bytes 435464 | tf_op jit(solution)/shard_map/ppermute | solution.py:588
  9.2 17.1 %all-to-all-start = ((bf16[16,32,96]{2,1,0:T(8,128)(2,1)}), bf16[16,32,96]{2,1,0:T(8,128)(2,1)S(1)}, u32[]{:S(2)}, u32[]{:S(2)}) async-start(bf16[16,32,96]{2,1,0:T(8,128)(2,1)} %get-tuple-element.51), calls=%async_computation | async-start | bytes 262144 | tf_op jit(solution)/shard_map/all_to_all | solution.py:665
  13.0 13.2 %collective-permute-start.2 = (bf16[144,504]{1,0:T(8,128)(2,1)}, bf16[144,504]{1,0:T(8,128)(2,1)S(1)}, u32[]{:S(2)}, u32[]{:S(2)}) collective-permute-start(bf16[144,504]{1,0:T(8,128)(2,1)} %get-tuple-element.49), channel_id=1, source_target_pairs={{0,12},{4,8},{8,4},{12,0},{1,13},{5,9},{9,5},{13,1},{2,14},{6,10},... | collective-permute-start | bytes 435464 | tf_op jit(solution)/shard_map/ppermute | solution.py:588
  16.8 9.5 %collective-permute-start.4 = (bf16[144,504]{1,0:T(8,128)(2,1)}, bf16[144,504]{1,0:T(8,128)(2,1)S(1)}, u32[]{:S(2)}, u32[]{:S(2)}) collective-permute-start(bf16[144,504]{1,0:T(8,128)(2,1)} %get-tuple-element.42.own_source), channel_id=1, source_target_pairs={{0,1},{1,0},{2,3},{3,2},{4,5},{5,4},{6,7},{7,6},{8,9},{9,8},{10,11... | collective-permute-start | bytes 435464 | tf_op jit(solution)/shard_map/ppermute | solution.py:588
  19.8 6.5 %collective-permute-start.5 = (bf16[144,504]{1,0:T(8,128)(2,1)S(1)}, bf16[144,504]{1,0:T(8,128)(2,1)S(1)}, u32[]{:S(2)}, u32[]{:S(2)}) collective-permute-start(bf16[144,504]{1,0:T(8,128)(2,1)S(1)} %collective-permute-done.refs_1_), channel_id=1, source_target_pairs={{0,1},{1,0},{2,3},{3,2},{4,5},{5,4},{6,7},{7,6},{8,9},{9,8},{10,11... | collective-permute-start | bytes 435464 | tf_op jit(solution)/shard_map/ppermute | solution.py:588
  20.4 5.9 %collective-permute-start.6 = (bf16[144,504]{1,0:T(8,128)(2,1)S(1)}, bf16[144,504]{1,0:T(8,128)(2,1)S(1)}, u32[]{:S(2)}, u32[]{:S(2)}) collective-permute-start(bf16[144,504]{1,0:T(8,128)(2,1)S(1)} %collective-permute-done.1.refs_2_), channel_id=1, source_target_pairs={{0,1},{1,0},{2,3},{3,2},{4,5},{5,4},{6,7},{7,6},{8,9},{9,8},{10,11... | collective-permute-start | bytes 435464 | tf_op jit(solution)/shard_map/ppermute | solution.py:588
  20.5 5.8 %collective-permute-start.3 = (f32[24,48]{1,0:T(8,128)}, f32[24,48]{1,0:T(8,128)S(1)}, u32[]{:S(2)}, u32[]{:S(2)}) collective-permute-start(f32[24,48]{1,0:T(8,128)} %get-tuple-element.50), channel_id=1, source_target_pairs={{4,0},{8,4},{12,8},{5,1},{9,5},{13,9},{6,2},{10,6},{14,10},{7,3},{... | collective-permute-start | bytes 13832 | tf_op jit(solution)/shard_map/ppermute | solution.py:668
  26.5 13.2 %collective-permute-start.9 = (bf16[144,1152]{1,0:T(8,128)(2,1)S(1)}, bf16[144,1152]{1,0:T(8,128)(2,1)S(1)}, u32[]{:S(2)}, u32[]{:S(2)}) collective-permute-start(bf16[144,1152]{1,0:T(8,128)(2,1)S(1)} %shard_map.162.refs_0_), channel_id=1, source_target_pairs={{0,2},{2,0},{1,3},{3,1},{4,6},{6,4},{5,7},{7,5},{8,10},{10,8},{9,1... | collective-permute-start | bytes 995336 | tf_op jit(solution)/shard_map/ppermute | solution.py:588
  28.0 11.7 %collective-permute-start.10 = (bf16[144,1152]{1,0:T(8,128)(2,1)S(1)}, bf16[144,1152]{1,0:T(8,128)(2,1)S(1)}, u32[]{:S(2)}, u32[]{:S(2)}) collective-permute-start(bf16[144,1152]{1,0:T(8,128)(2,1)S(1)} %shard_map.162.refs_0_), channel_id=1, source_target_pairs={{0,16},{16,0},{1,17},{17,1},{2,18},{18,2},{3,19},{19,3},{4,20},{20... | collective-permute-start | bytes 995336 | tf_op jit(solution)/shard_map/ppermute | solution.py:588
  29.5 4.0 %collective-permute-start.7 = (bf16[144,504]{1,0:T(8,128)(2,1)S(1)}, bf16[144,504]{1,0:T(8,128)(2,1)S(1)}, u32[]{:S(2)}, u32[]{:S(2)}) collective-permute-start(bf16[144,504]{1,0:T(8,128)(2,1)S(1)} %collective-permute-done.2.refs_3_), channel_id=1, source_target_pairs={{0,1},{1,0},{2,3},{3,2},{4,5},{5,4},{6,7},{7,6},{8,9},{9,8},{10,11... | collective-permute-start | bytes 435464 | tf_op jit(solution)/shard_map/ppermute | solution.py:588
  29.5 1.6 %collective-permute-start.8 = (bf16[16,32,96]{2,1,0:T(8,128)(2,1)S(1)}, bf16[16,32,96]{2,1,0:T(8,128)(2,1)S(1)}, u32[]{:S(2)}, u32[]{:S(2)}) collective-permute-start(bf16[16,32,96]{2,1,0:T(8,128)(2,1)S(1)} %all-to-all-done.mine), channel_id=1, source_target_pairs={{0,1},{1,0},{2,3},{3,2},{4,5},{5,4},{6,7},{7,6},{8,9},{9,8},{10,11... | collective-permute-start | bytes 294920 | tf_op jit(solution)/shard_map/ppermute | solution.py:588
  33.5 13.8 %copy-start.18 = (f32[1152]{0:T(1024)S(1)}, f32[1152]{0:T(1024)}, u32[]{:S(2)}) copy-start(f32[1152]{0:T(1024)} %param.26) | copy-start | bytes 13828
  33.5 14.5 %copy-start.1 = (f32[16,3,1152]{2,0,1:T(8,128)S(1)}, f32[16,3,1152]{2,0,1:T(8,128)}, u32[]{:S(2)}) copy-start(f32[16,3,1152]{2,0,1:T(8,128)} %param.20) | copy-start | bytes 663556
  33.5 14.5 %copy-start.4 = (bf16[16,1152]{1,0:T(8,128)(2,1)S(1)}, bf16[16,1152]{1,0:T(8,128)(2,1)}, u32[]{:S(2)}) copy-start(bf16[16,1152]{1,0:T(8,128)(2,1)} %refs_4_.1) | copy-start | bytes 110596
  33.5 14.5 %copy-start.7 = (bf16[1152,16]{0,1:T(8,128)(2,1)S(1)}, bf16[1152,16]{0,1:T(8,128)(2,1)}, u32[]{:S(2)}) copy-start(bf16[1152,16]{0,1:T(8,128)(2,1)} %param.27) | copy-start | bytes 110596
  33.5 14.5 %copy-start.8 = (f32[24,192]{1,0:T(8,128)S(1)}, f32[24,192]{1,0:T(8,128)}, u32[]{:S(2)}) copy-start(f32[24,192]{1,0:T(8,128)} %get-tuple-element.66.refs_0_) | copy-start | bytes 55300
  33.5 14.5 %copy-start.9 = (f32[1,1152]{1,0:T(1,128)S(1)}, f32[1,1152]{1,0:T(1,128)}, u32[]{:S(2)}) copy-start(f32[1,1152]{1,0:T(1,128)} %refs_2_.1) | copy-start | bytes 13828
  33.5 14.5 %copy-start.10 = (f32[8,48]{1,0:T(8,128)S(1)}, f32[8,48]{1,0:T(8,128)}, u32[]{:S(2)}) copy-start(f32[8,48]{1,0:T(8,128)} %refs_7_.1) | copy-start | bytes 4612
  33.6 14.5 %copy-start.15 = (f32[8]{0:T(128)S(1)}, f32[8]{0:T(128)}, u32[]{:S(2)}) copy-start(f32[8]{0:T(128)} %refs_8_.1) | copy-start | bytes 100
  39.7 20.5 %all-to-all-start.1 = ((bf16[16,72,240]{2,1,0:T(8,128)(2,1)}), bf16[16,72,240]{2,1,0:T(8,128)(2,1)S(1)}, u32[]{:S(2)}, u32[]{:S(2)}) async-start(bf16[16,72,240]{2,1,0:T(8,128)(2,1)} %shard_map.161), calls=%async_computation.1 | async-start | bytes 1179648 | tf_op jit(solution)/shard_map/all_to_all | solution.py:706
  43.3 10.6 %collective-permute-start.11 = (bf16[80,1152]{1,0:T(8,128)(2,1)S(1)}, bf16[80,1152]{1,0:T(8,128)(2,1)S(1)}, u32[]{:S(2)}, u32[]{:S(2)}) collective-permute-start(bf16[80,1152]{1,0:T(8,128)(2,1)S(1)} %slice.6), channel_id=1, source_target_pairs={{0,16},{16,0},{1,17},{17,1},{2,18},{18,2},{3,19},{19,3},{4,20},{20... | collective-permute-start | bytes 552968 | tf_op jit(solution)/shard_map/ppermute | solution.py:588
  45.2 8.7 %collective-permute-start.12 = (bf16[64,1152]{1,0:T(8,128)(2,1)S(1)}, bf16[64,1152]{1,0:T(8,128)(2,1)S(1)}, u32[]{:S(2)}, u32[]{:S(2)}) collective-permute-start(bf16[64,1152]{1,0:T(8,128)(2,1)S(1)} %slice.7), channel_id=1, source_target_pairs={{0,2},{2,0},{1,3},{3,1},{4,6},{6,4},{5,7},{7,5},{8,10},{10,8},{9,1... | collective-permute-start | bytes 442376 | tf_op jit(solution)/shard_map/ppermute | solution.py:588
  46.8 7.7 %collective-permute-start.13 = (bf16[144,1152]{1,0:T(8,128)(2,1)S(1)}, bf16[144,1152]{1,0:T(8,128)(2,1)S(1)}, u32[]{:S(2)}, u32[]{:S(2)}) collective-permute-start(bf16[144,1152]{1,0:T(8,128)(2,1)S(1)} %shard_map.162.refs_0_), channel_id=1, source_target_pairs={{0,1},{1,0},{2,3},{3,2},{4,5},{5,4},{6,7},{7,6},{8,9},{9,8},{10,11... | collective-permute-start | bytes 995336 | tf_op jit(solution)/shard_map/ppermute | solution.py:588
  46.8 7.7 %collective-permute-start.14 = (bf16[144,1152]{1,0:T(8,128)(2,1)S(1)}, bf16[144,1152]{1,0:T(8,128)(2,1)S(1)}, u32[]{:S(2)}, u32[]{:S(2)}) collective-permute-start(bf16[144,1152]{1,0:T(8,128)(2,1)S(1)} %collective-permute-done.9.refs_1_), channel_id=1, source_target_pairs={{0,1},{1,0},{2,3},{3,2},{4,5},{5,4},{6,7},{7,6},{8,9},{9,8},{10,11... | collective-permute-start | bytes 995336 | tf_op jit(solution)/shard_map/ppermute | solution.py:588
  47.3 7.1 %collective-permute-start.15 = (bf16[144,1152]{1,0:T(8,128)(2,1)S(1)}, bf16[144,1152]{1,0:T(8,128)(2,1)S(1)}, u32[]{:S(2)}, u32[]{:S(2)}) collective-permute-start(bf16[144,1152]{1,0:T(8,128)(2,1)S(1)} %collective-permute-done.10.refs_2_), channel_id=1, source_target_pairs={{0,1},{1,0},{2,3},{3,2},{4,5},{5,4},{6,7},{7,6},{8,9},{9,8},{10,11... | collective-permute-start | bytes 995336 | tf_op jit(solution)/shard_map/ppermute | solution.py:588
  53.9 1.6 %collective-permute-start.16 = (bf16[80,1152]{1,0:T(8,128)(2,1)S(1)}, bf16[80,1152]{1,0:T(8,128)(2,1)S(1)}, u32[]{:S(2)}, u32[]{:S(2)}) collective-permute-start(bf16[80,1152]{1,0:T(8,128)(2,1)S(1)} %collective-permute-done.11.refs_3_), channel_id=1, source_target_pairs={{0,1},{1,0},{2,3},{3,2},{4,5},{5,4},{6,7},{7,6},{8,9},{9,8},{10,11... | collective-permute-start | bytes 552968 | tf_op jit(solution)/shard_map/ppermute | solution.py:588
  53.9 1.6 %collective-permute-start.17 = (bf16[64,1152]{1,0:T(8,128)(2,1)S(1)}, bf16[64,1152]{1,0:T(8,128)(2,1)S(1)}, u32[]{:S(2)}, u32[]{:S(2)}) collective-permute-start(bf16[64,1152]{1,0:T(8,128)(2,1)S(1)} %collective-permute-done.12.refs_4_), channel_id=1, source_target_pairs={{0,1},{1,0},{2,3},{3,2},{4,5},{5,4},{6,7},{7,6},{8,9},{9,8},{10,11... | collective-permute-start | bytes 442376 | tf_op jit(solution)/shard_map/ppermute | solution.py:588
  61.0 3.7 %copy-start.14 = (f32[8,128]{1,0:T(8,128)S(1)}, f32[8,128]{1,0:T(8,128)}, u32[]{:S(2)}) copy-start(f32[8,128]{1,0:T(8,128)} %copy-done.13) | copy-start | bytes 12292
  63.5 1.2 %collective-permute-start.18 = (f32[8,240]{1,0:T(8,128)S(1)}, f32[8,240]{1,0:T(8,128)S(1)}, u32[]{:S(2)}, u32[]{:S(2)}) collective-permute-start(f32[8,240]{1,0:T(8,128)S(1)} %get-tuple-element.75), channel_id=1, source_target_pairs={{0,1},{1,0},{2,3},{3,2},{4,5},{5,4},{6,7},{7,6},{8,9},{9,8},{10,11... | collective-permute-start | bytes 23048 | tf_op jit(solution)/shard_map/ppermute | solution.py:588
  (8 other events, 8.9 us)

commit v13 on v12

--- a/solution.py
+++ b/solution.py
@@ -438,7 +438,7 @@
             att[f, y] = total * (1.0 / norm)
         return carry
 
-    lax.fori_loop(0, all_frames, one_frame, 0)
+    lax.fori_loop(0, all_frames, one_frame, 0, unroll=2)
     toks = out.shape[0] // (scenes * queues)
     for t in range(toks):
         for y in range(scenes):

time: 66 us -> 65.9 us (level)
  no operation moved by 1% of the time
where the time goes in v13:
time: 65.9 us; the launch traced here: 65.4 us
  starting transfers between devices  26.7 us (41%)
  Pallas kernels  16.2 us (25%)
  waiting for transfers between devices  15.7 us (24%)
  local copies, waits for them, and re-layouts  5.3 us (8%)
  between operations  1.57 us (2%)
    ppermute x18, starting transfers between devices, swapped(): return lax.ppermute(value, axis, [(i, i ^ mask) for i in range(count)])  18 us
    ppermute x18, waiting for transfers between devices, swapped(): return lax.ppermute(value, axis, [(i, i ^ mask) for i in range(count)])  6.5 us
    pallas_call x1, Pallas kernels, on_device_heads(): kernel_call(functools.partial(attend_kernel, frames, tokens, queues), jax...  6.05 us
    unnamed x38, local copies, waits for them, and re-layouts  5.26 us
    all_to_all x1, waiting for transfers between devices, on_device_heads(): received = lax.all_to_all(attended, ('tok', 'queue', 'scene'), 0, 0)  4.68 us
    ppermute x1, waiting for transfers between devices, on_device_heads(): lax.ppermute(first, 'queue', [(i + 1, i) for i in range(queues - 1)])  4.5 us
    all_to_all x1, starting transfers between devices, on_device_heads(): shares = lax.all_to_all(copies, ('scene', 'queue', 'tok'), 0, 0)  3.83 us
    all_to_all x1, starting transfers between devices, on_device_heads(): received = lax.all_to_all(attended, ('tok', 'queue', 'scene'), 0, 0)  3.58 us
  transfers between devices with their start and end apart: 21, of which 6 were waited for; matrix products, arithmetic and copies ran while one was open for 0% of the time, Pallas kernels for 15%

profile of v13, /device:TPU:0, one launch (start us, length us, event | category | flops | bytes accessed | tf_op | source)
XLA Modules:
  0.0 65.4 jit_solution(10465662429384160688)
XLA Ops:
  0.7 2.9 %shard_map.158 = (bf16[144,504]{1,0:T(8,128)(2,1)}, bf16[144,504]{1,0:T(8,128)(2,1)}, bf16[144,504]{1,0:T(8,128)(2,1)}, bf16[144,504]{1,0:T(8,128)(2,1)}, bf16[1...) custom-call(f32[4,16,48]{2,1,0:T(8,128)} %latents.1, s32[1,4]{1,0:T(1,128)} %bitcast.14, ...), custom_call_target="tpu_custom_call" | custom-call | flops 1000000 | bytes 8000000 | tf_op jit(solution)/shard_map/pallas_call | solution.py:629
  3.6 3.0 %collective-permute-start = (bf16[144,504]{1,0:T(8,128)(2,1)}, bf16[144,504]{1,0:T(8,128)(2,1)S(1)}, u32[]{:S(2)}, u32[]{:S(2)}) collective-permute-start(bf16[144,504]{1,0:T(8,128)(2,1)} %get-tuple-element.41), channel_id=1, source_target_pairs={{0,4},{4,0},{8,12},{12,8},{1,5},{5,1},{9,13},{13,9},{2,6},{6,2},{1... | collective-permute-start | bytes 435464 | tf_op jit(solution)/shard_map/ppermute | solution.py:588
  6.6 2.6 %collective-permute-start.1 = (bf16[144,504]{1,0:T(8,128)(2,1)}, bf16[144,504]{1,0:T(8,128)(2,1)S(1)}, u32[]{:S(2)}, u32[]{:S(2)}) collective-permute-start(bf16[144,504]{1,0:T(8,128)(2,1)} %get-tuple-element.48), channel_id=1, source_target_pairs={{0,8},{4,12},{8,0},{12,4},{1,9},{5,13},{9,1},{13,5},{2,10},{6,14},... | collective-permute-start | bytes 435464 | tf_op jit(solution)/shard_map/ppermute | solution.py:588
  9.2 3.8 %all-to-all-start = ((bf16[16,32,96]{2,1,0:T(8,128)(2,1)}), bf16[16,32,96]{2,1,0:T(8,128)(2,1)S(1)}, u32[]{:S(2)}, u32[]{:S(2)}) async-start(bf16[16,32,96]{2,1,0:T(8,128)(2,1)} %get-tuple-element.51), calls=%async_computation | async-start | bytes 262144 | tf_op jit(solution)/shard_map/all_to_all | solution.py:665
  13.0 3.7 %collective-permute-start.2 = (bf16[144,504]{1,0:T(8,128)(2,1)}, bf16[144,504]{1,0:T(8,128)(2,1)S(1)}, u32[]{:S(2)}, u32[]{:S(2)}) collective-permute-start(bf16[144,504]{1,0:T(8,128)(2,1)} %get-tuple-element.49), channel_id=1, source_target_pairs={{0,12},{4,8},{8,4},{12,0},{1,13},{5,9},{9,5},{13,1},{2,14},{6,10},... | collective-permute-start | bytes 435464 | tf_op jit(solution)/shard_map/ppermute | solution.py:588
  16.8 0.9 %copy-done = f32[16,3,1152]{2,0,1:T(8,128)S(1)} copy-done((f32[16,3,1152]{2,0,1:T(8,128)S(1)}, f32[16,3,1152]{2,0,1:T(8,128)}, u32[]{:S(2)}) %copy-start) | copy-done | bytes 221208
  17.7 0.9 %copy-done.2 = bf16[144,504]{1,0:T(8,128)(2,1)S(1)} copy-done((bf16[144,504]{1,0:T(8,128)(2,1)S(1)}, bf16[144,504]{1,0:T(8,128)(2,1)}, u32[]{:S(2)}) %copy-start.2) | copy-done | bytes 145176
  18.6 0.8 %copy-done.3 = bf16[16,1152]{1,0:T(8,128)(2,1)S(1)} copy-done((bf16[16,1152]{1,0:T(8,128)(2,1)S(1)}, bf16[16,1152]{1,0:T(8,128)(2,1)}, u32[]{:S(2)}) %copy-start.3) | copy-done | bytes 36888
  19.8 0.6 collective-permute-start.5
  20.5 1.3 %collective-permute-start.3 = (f32[24,48]{1,0:T(8,128)}, f32[24,48]{1,0:T(8,128)S(1)}, u32[]{:S(2)}, u32[]{:S(2)}) collective-permute-start(f32[24,48]{1,0:T(8,128)} %get-tuple-element.50), channel_id=1, source_target_pairs={{4,0},{8,4},{12,8},{5,1},{9,5},{13,9},{6,2},{10,6},{14,10},{7,3},{... | collective-permute-start | bytes 13832 | tf_op jit(solution)/shard_map/ppermute | solution.py:668
  21.8 4.5 %collective-permute-done.3.refs_1_ = f32[24,48]{1,0:T(8,128)S(1)} collective-permute-done((f32[24,48]{1,0:T(8,128)}, f32[24,48]{1,0:T(8,128)S(1)}, u32[]{:S(2)}, u32[]{:S(2)}) %collective-permute-start.3) | collective-permute-done | bytes 4640 | tf_op jit(solution)/shard_map/ppermute | solution.py:668
  26.5 1.5 %collective-permute-start.9 = (bf16[144,1152]{1,0:T(8,128)(2,1)S(1)}, bf16[144,1152]{1,0:T(8,128)(2,1)S(1)}, u32[]{:S(2)}, u32[]{:S(2)}) collective-permute-start(bf16[144,1152]{1,0:T(8,128)(2,1)S(1)} %shard_map.162.refs_0_), channel_id=1, source_target_pairs={{0,2},{2,0},{1,3},{3,1},{4,6},{6,4},{5,7},{7,5},{8,10},{10,8},{9,1... | collective-permute-start | bytes 995336 | tf_op jit(solution)/shard_map/ppermute | solution.py:588
  28.0 1.5 %collective-permute-start.10 = (bf16[144,1152]{1,0:T(8,128)(2,1)S(1)}, bf16[144,1152]{1,0:T(8,128)(2,1)S(1)}, u32[]{:S(2)}, u32[]{:S(2)}) collective-permute-start(bf16[144,1152]{1,0:T(8,128)(2,1)S(1)} %shard_map.162.refs_0_), channel_id=1, source_target_pairs={{0,16},{16,0},{1,17},{17,1},{2,18},{18,2},{3,19},{19,3},{4,20},{20... | collective-permute-start | bytes 995336 | tf_op jit(solution)/shard_map/ppermute | solution.py:588
  29.5 0.5 collective-permute-start.8
  30.0 1.0 %collective-permute-done.8.other = bf16[16,32,96]{2,1,0:T(8,128)(2,1)S(1)} collective-permute-done((bf16[16,32,96]{2,1,0:T(8,128)(2,1)S(1)}, bf16[16,32,96]{2,1,0:T(8,128)(2,1)S(1)}, u32[]{:S(2)}, u32[]{:S(2)}) %collective-permute-start.8) | collective-permute-done | bytes 98336 | tf_op jit(solution)/shard_map/ppermute | solution.py:588
  31.0 2.4 %shard_map.160 = (bf16[1024,1152]{1,0:T(8,128)(2,1)S(1)}, bf16[16,64,256]{2,1,0:T(8,128)(2,1)S(1)}, f32[16,1,256]{2,1,0:T(1,128)S(1)}, f32[2,16,16,128]{3,2,1,0:T(8,128)S(1)}) custom-call(bf16[16,32,96]{2,1,0:T(8,128)(2,1)S(1)} %all-to-all-done.mine, bf16[16,32,96]{2,1,0:T(8,128)(2,1)S(1)} %collective-permute-done.8.other, ...), custom_call_target="tpu_custom_call" | custom-call | flops 1000000 | bytes 8000000 | tf_op jit(solution)/shard_map/pallas_call | solution.py:679
  33.6 6.0 %shard_map.161 = bf16[16,72,240]{2,1,0:T(8,128)(2,1)} custom-call(bf16[144,504]{1,0:T(8,128)(2,1)S(1)} %get-tuple-element.46.refs_0_, bf16[144,504]{1,0:T(8,128)(2,1)S(1)} %collective-permute-done.refs_1_, bf16[144,504]{1,0:T(8,128)(2,1)S(1)} %collective-permute-done.1.refs_2_, bf16[144,504]{1,0:T(8,128)(2,1)S(1)} %collective-permute-done.2.refs_3_, ...), custom_call_target="tpu_custom_call" | custom-call | flops 1000000 | bytes 100000000 | tf_op jit(solution)/shard_map/pallas_call | solution.py:690
  39.6 3.6 %all-to-all-start.1 = ((bf16[16,72,240]{2,1,0:T(8,128)(2,1)}), bf16[16,72,240]{2,1,0:T(8,128)(2,1)S(1)}, u32[]{:S(2)}, u32[]{:S(2)}) async-start(bf16[16,72,240]{2,1,0:T(8,128)(2,1)} %shard_map.161), calls=%async_computation.1 | async-start | bytes 1179648 | tf_op jit(solution)/shard_map/all_to_all | solution.py:706
  43.2 1.9 %collective-permute-start.11 = (bf16[80,1152]{1,0:T(8,128)(2,1)S(1)}, bf16[80,1152]{1,0:T(8,128)(2,1)S(1)}, u32[]{:S(2)}, u32[]{:S(2)}) collective-permute-start(bf16[80,1152]{1,0:T(8,128)(2,1)S(1)} %slice.6), channel_id=1, source_target_pairs={{0,16},{16,0},{1,17},{17,1},{2,18},{18,2},{3,19},{19,3},{4,20},{20... | collective-permute-start | bytes 552968 | tf_op jit(solution)/shard_map/ppermute | solution.py:588
  45.1 1.6 %collective-permute-start.12 = (bf16[64,1152]{1,0:T(8,128)(2,1)S(1)}, bf16[64,1152]{1,0:T(8,128)(2,1)S(1)}, u32[]{:S(2)}, u32[]{:S(2)}) collective-permute-start(bf16[64,1152]{1,0:T(8,128)(2,1)S(1)} %slice.7), channel_id=1, source_target_pairs={{0,2},{2,0},{1,3},{3,1},{4,6},{6,4},{5,7},{7,5},{8,10},{10,8},{9,1... | collective-permute-start | bytes 442376 | tf_op jit(solution)/shard_map/ppermute | solution.py:588
  47.9 1.0 %shard_map.163 = (bf16[112,1152]{1,0:T(8,128)(2,1)S(1)}, bf16[96,240]{1,0:T(8,128)(2,1)S(1)}, f32[8,240]{1,0:T(8,128)S(1)}, f32[8,240]{1,0:T(8,128)S(1)}, f32[8,48]{1,0:T(8,128)S(1)}, /*index=5*/f32[8,128]{1,0:T(8,128)S(1)}) custom-call(f32[24,192]{1,0:T(8,128)S(1)} %copy-done.8, f32[24,48]{1,0:T(8,128)S(1)} %collective-permute-done.3.refs_1_, ...), custom_call_target="tpu_custom_call" | custom-call | flops 1000000 | bytes 1000000 | tf_op jit(solution)/shard_map/pallas_call | solution.py:726
  48.9 0.6 copy-done.5
  49.5 0.6 copy-done.11
  50.1 0.6 copy-done.13
  50.7 3.1 %collective-permute-done.12.refs_4_ = bf16[64,1152]{1,0:T(8,128)(2,1)S(1)} collective-permute-done((bf16[64,1152]{1,0:T(8,128)(2,1)S(1)}, bf16[64,1152]{1,0:T(8,128)(2,1)S(1)}, u32[]{:S(2)}, u32[]{:S(2)}) %collective-permute-start.12) | collective-permute-done | bytes 147488 | tf_op jit(solution)/shard_map/ppermute | solution.py:588
  53.8 0.5 collective-permute-start.17
  54.4 1.1 %collective-permute-done.17.refs_9_ = bf16[64,1152]{1,0:T(8,128)(2,1)S(1)} collective-permute-done((bf16[64,1152]{1,0:T(8,128)(2,1)S(1)}, bf16[64,1152]{1,0:T(8,128)(2,1)S(1)}, u32[]{:S(2)}, u32[]{:S(2)}) %collective-permute-start.17) | collective-permute-done | bytes 147488 | tf_op jit(solution)/shard_map/ppermute | solution.py:588
  55.5 4.7 %all-to-all-done.1.refs_10_ = bf16[16,72,240]{2,1,0:T(8,128)(2,1)S(1)} async-done(((bf16[16,72,240]{2,1,0:T(8,128)(2,1)}), bf16[16,72,240]{2,1,0:T(8,128)(2,1)S(1)}, u32[]{:S(2)}, u32[]{:S(2)}) %all-to-all-start.1) | async-done | bytes 552992 | tf_op jit(solution)/shard_map/all_to_all | solution.py:706
  60.2 0.8 %copy-done.6 = bf16[96,240]{1,0:T(8,128)(2,1)S(1)} copy-done((bf16[96,240]{1,0:T(8,128)(2,1)S(1)}, bf16[96,240]{1,0:T(8,128)(2,1)}, u32[]{:S(2)}) %copy-start.6) | copy-done | bytes 46104
  61.0 2.5 %shard_map.164 = (f32[8,240]{1,0:T(8,128)S(1)}, f32[8,240]{1,0:T(8,128)S(1)}) custom-call(bf16[144,1152]{1,0:T(8,128)(2,1)S(1)} %shard_map.162.refs_0_, bf16[144,1152]{1,0:T(8,128)(2,1)S(1)} %collective-permute-done.9.refs_1_, bf16[144,1152]{1,0:T(8,128)(2,1)S(1)} %collective-permute-done.10.refs_2_, bf16[80,1152]{1,0:T(8,128)(2,1)S(1)} %collective-permute-done.11.refs_3_, ...), custom_call_target="tpu_custom_call" | custom-call | flops 1000000 | bytes 8000000 | tf_op jit(solution)/shard_map/pallas_call | solution.py:743
  63.5 1.2 %collective-permute-done.18.partner = f32[8,240]{1,0:T(8,128)S(1)} collective-permute-done((f32[8,240]{1,0:T(8,128)S(1)}, f32[8,240]{1,0:T(8,128)S(1)}, u32[]{:S(2)}, u32[]{:S(2)}) %collective-permute-start.18) | collective-permute-done | bytes 7712 | tf_op jit(solution)/shard_map/ppermute | solution.py:588
  64.7 0.7 %shard_map.165 = (f32[4,8,48]{2,1,0:T(8,128)}, f32[4,8,48]{2,1,0:T(8,128)}) custom-call(f32[8,240]{1,0:T(8,128)S(1)} %get-tuple-element.74.mine, f32[8,240]{1,0:T(8,128)S(1)} %collective-permute-done.18.partner, f32[8,240]{1,0:T(8,128)S(1)} %get-tuple-element.76.base, f32[8,240]{1,0:T(8,128)S(1)} %get-tuple-element.77.factor, f32[8,48]{1,0:T(8,128)S(1)} %copy-done.12, ...), custom_call_target="tpu_custom_call" | custom-call | flops 1000000 | bytes 1000000 | tf_op jit(solution)/shard_map/pallas_call | solution.py:752
  (59 shorter events, 1.4 us)
Async XLA Ops:
  0.6 32.8 %copy-start.16 = (f32[72]{0:T(128)S(1)}, f32[72]{0:T(128)}, u32[]{:S(2)}) copy-start(f32[72]{0:T(128)} %param.23) | copy-start | bytes 868
  0.6 32.8 %copy-start.17 = (f32[72]{0:T(128)S(1)}, f32[72]{0:T(128)}, u32[]{:S(2)}) copy-start(f32[72]{0:T(128)} %param.24) | copy-start | bytes 868
  3.6 16.2 %collective-permute-start = (bf16[144,504]{1,0:T(8,128)(2,1)}, bf16[144,504]{1,0:T(8,128)(2,1)S(1)}, u32[]{:S(2)}, u32[]{:S(2)}) collective-permute-start(bf16[144,504]{1,0:T(8,128)(2,1)} %get-tuple-element.41), channel_id=1, source_target_pairs={{0,4},{4,0},{8,12},{12,8},{1,5},{5,1},{9,13},{13,9},{2,6},{6,2},{1... | collective-permute-start | bytes 435464 | tf_op jit(solution)/shard_map/ppermute | solution.py:588
  6.6 13.8 %collective-permute-start.1 = (bf16[144,504]{1,0:T(8,128)(2,1)}, bf16[144,504]{1,0:T(8,128)(2,1)S(1)}, u32[]{:S(2)}, u32[]{:S(2)}) collective-permute-start(bf16[144,504]{1,0:T(8,128)(2,1)} %get-tuple-element.48), channel_id=1, source_target_pairs={{0,8},{4,12},{8,0},{12,4},{1,9},{5,13},{9,1},{13,5},{2,10},{6,14},... | collective-permute-start | bytes 435464 | tf_op jit(solution)/shard_map/ppermute | solution.py:588
  9.2 17.1 %all-to-all-start = ((bf16[16,32,96]{2,1,0:T(8,128)(2,1)}), bf16[16,32,96]{2,1,0:T(8,128)(2,1)S(1)}, u32[]{:S(2)}, u32[]{:S(2)}) async-start(bf16[16,32,96]{2,1,0:T(8,128)(2,1)} %get-tuple-element.51), calls=%async_computation | async-start | bytes 262144 | tf_op jit(solution)/shard_map/all_to_all | solution.py:665
  13.0 13.2 %collective-permute-start.2 = (bf16[144,504]{1,0:T(8,128)(2,1)}, bf16[144,504]{1,0:T(8,128)(2,1)S(1)}, u32[]{:S(2)}, u32[]{:S(2)}) collective-permute-start(bf16[144,504]{1,0:T(8,128)(2,1)} %get-tuple-element.49), channel_id=1, source_target_pairs={{0,12},{4,8},{8,4},{12,0},{1,13},{5,9},{9,5},{13,1},{2,14},{6,10},... | collective-permute-start | bytes 435464 | tf_op jit(solution)/shard_map/ppermute | solution.py:588
  16.8 9.5 %collective-permute-start.4 = (bf16[144,504]{1,0:T(8,128)(2,1)}, bf16[144,504]{1,0:T(8,128)(2,1)S(1)}, u32[]{:S(2)}, u32[]{:S(2)}) collective-permute-start(bf16[144,504]{1,0:T(8,128)(2,1)} %get-tuple-element.42.own_source), channel_id=1, source_target_pairs={{0,1},{1,0},{2,3},{3,2},{4,5},{5,4},{6,7},{7,6},{8,9},{9,8},{10,11... | collective-permute-start | bytes 435464 | tf_op jit(solution)/shard_map/ppermute | solution.py:588
  19.8 6.5 %collective-permute-start.5 = (bf16[144,504]{1,0:T(8,128)(2,1)S(1)}, bf16[144,504]{1,0:T(8,128)(2,1)S(1)}, u32[]{:S(2)}, u32[]{:S(2)}) collective-permute-start(bf16[144,504]{1,0:T(8,128)(2,1)S(1)} %collective-permute-done.refs_1_), channel_id=1, source_target_pairs={{0,1},{1,0},{2,3},{3,2},{4,5},{5,4},{6,7},{7,6},{8,9},{9,8},{10,11... | collective-permute-start | bytes 435464 | tf_op jit(solution)/shard_map/ppermute | solution.py:588
  20.4 5.9 %collective-permute-start.6 = (bf16[144,504]{1,0:T(8,128)(2,1)S(1)}, bf16[144,504]{1,0:T(8,128)(2,1)S(1)}, u32[]{:S(2)}, u32[]{:S(2)}) collective-permute-start(bf16[144,504]{1,0:T(8,128)(2,1)S(1)} %collective-permute-done.1.refs_2_), channel_id=1, source_target_pairs={{0,1},{1,0},{2,3},{3,2},{4,5},{5,4},{6,7},{7,6},{8,9},{9,8},{10,11... | collective-permute-start | bytes 435464 | tf_op jit(solution)/shard_map/ppermute | solution.py:588
  20.5 5.8 %collective-permute-start.3 = (f32[24,48]{1,0:T(8,128)}, f32[24,48]{1,0:T(8,128)S(1)}, u32[]{:S(2)}, u32[]{:S(2)}) collective-permute-start(f32[24,48]{1,0:T(8,128)} %get-tuple-element.50), channel_id=1, source_target_pairs={{4,0},{8,4},{12,8},{5,1},{9,5},{13,9},{6,2},{10,6},{14,10},{7,3},{... | collective-permute-start | bytes 13832 | tf_op jit(solution)/shard_map/ppermute | solution.py:668
  26.5 13.1 %collective-permute-start.9 = (bf16[144,1152]{1,0:T(8,128)(2,1)S(1)}, bf16[144,1152]{1,0:T(8,128)(2,1)S(1)}, u32[]{:S(2)}, u32[]{:S(2)}) collective-permute-start(bf16[144,1152]{1,0:T(8,128)(2,1)S(1)} %shard_map.162.refs_0_), channel_id=1, source_target_pairs={{0,2},{2,0},{1,3},{3,1},{4,6},{6,4},{5,7},{7,5},{8,10},{10,8},{9,1... | collective-permute-start | bytes 995336 | tf_op jit(solution)/shard_map/ppermute | solution.py:588
  28.0 11.6 %collective-permute-start.10 = (bf16[144,1152]{1,0:T(8,128)(2,1)S(1)}, bf16[144,1152]{1,0:T(8,128)(2,1)S(1)}, u32[]{:S(2)}, u32[]{:S(2)}) collective-permute-start(bf16[144,1152]{1,0:T(8,128)(2,1)S(1)} %shard_map.162.refs_0_), channel_id=1, source_target_pairs={{0,16},{16,0},{1,17},{17,1},{2,18},{18,2},{3,19},{19,3},{4,20},{20... | collective-permute-start | bytes 995336 | tf_op jit(solution)/shard_map/ppermute | solution.py:588
  29.5 4.0 %collective-permute-start.7 = (bf16[144,504]{1,0:T(8,128)(2,1)S(1)}, bf16[144,504]{1,0:T(8,128)(2,1)S(1)}, u32[]{:S(2)}, u32[]{:S(2)}) collective-permute-start(bf16[144,504]{1,0:T(8,128)(2,1)S(1)} %collective-permute-done.2.refs_3_), channel_id=1, source_target_pairs={{0,1},{1,0},{2,3},{3,2},{4,5},{5,4},{6,7},{7,6},{8,9},{9,8},{10,11... | collective-permute-start | bytes 435464 | tf_op jit(solution)/shard_map/ppermute | solution.py:588
  29.5 1.6 %collective-permute-start.8 = (bf16[16,32,96]{2,1,0:T(8,128)(2,1)S(1)}, bf16[16,32,96]{2,1,0:T(8,128)(2,1)S(1)}, u32[]{:S(2)}, u32[]{:S(2)}) collective-permute-start(bf16[16,32,96]{2,1,0:T(8,128)(2,1)S(1)} %all-to-all-done.mine), channel_id=1, source_target_pairs={{0,1},{1,0},{2,3},{3,2},{4,5},{5,4},{6,7},{7,6},{8,9},{9,8},{10,11... | collective-permute-start | bytes 294920 | tf_op jit(solution)/shard_map/ppermute | solution.py:588
  33.5 13.7 %copy-start.18 = (f32[1152]{0:T(1024)S(1)}, f32[1152]{0:T(1024)}, u32[]{:S(2)}) copy-start(f32[1152]{0:T(1024)} %param.26) | copy-start | bytes 13828
  33.5 14.4 %copy-start.1 = (f32[16,3,1152]{2,0,1:T(8,128)S(1)}, f32[16,3,1152]{2,0,1:T(8,128)}, u32[]{:S(2)}) copy-start(f32[16,3,1152]{2,0,1:T(8,128)} %param.20) | copy-start | bytes 663556
  33.5 14.4 %copy-start.4 = (bf16[16,1152]{1,0:T(8,128)(2,1)S(1)}, bf16[16,1152]{1,0:T(8,128)(2,1)}, u32[]{:S(2)}) copy-start(bf16[16,1152]{1,0:T(8,128)(2,1)} %refs_4_.1) | copy-start | bytes 110596
  33.5 14.4 %copy-start.7 = (bf16[1152,16]{0,1:T(8,128)(2,1)S(1)}, bf16[1152,16]{0,1:T(8,128)(2,1)}, u32[]{:S(2)}) copy-start(bf16[1152,16]{0,1:T(8,128)(2,1)} %param.27) | copy-start | bytes 110596
  33.5 14.4 %copy-start.8 = (f32[24,192]{1,0:T(8,128)S(1)}, f32[24,192]{1,0:T(8,128)}, u32[]{:S(2)}) copy-start(f32[24,192]{1,0:T(8,128)} %get-tuple-element.66.refs_0_) | copy-start | bytes 55300
  33.5 14.4 %copy-start.9 = (f32[1,1152]{1,0:T(1,128)S(1)}, f32[1,1152]{1,0:T(1,128)}, u32[]{:S(2)}) copy-start(f32[1,1152]{1,0:T(1,128)} %refs_2_.1) | copy-start | bytes 13828
  33.5 14.4 %copy-start.10 = (f32[8,48]{1,0:T(8,128)S(1)}, f32[8,48]{1,0:T(8,128)}, u32[]{:S(2)}) copy-start(f32[8,48]{1,0:T(8,128)} %refs_7_.1) | copy-start | bytes 4612
  33.6 14.4 %copy-start.15 = (f32[8]{0:T(128)S(1)}, f32[8]{0:T(128)}, u32[]{:S(2)}) copy-start(f32[8]{0:T(128)} %refs_8_.1) | copy-start | bytes 100
  39.6 20.5 %all-to-all-start.1 = ((bf16[16,72,240]{2,1,0:T(8,128)(2,1)}), bf16[16,72,240]{2,1,0:T(8,128)(2,1)S(1)}, u32[]{:S(2)}, u32[]{:S(2)}) async-start(bf16[16,72,240]{2,1,0:T(8,128)(2,1)} %shard_map.161), calls=%async_computation.1 | async-start | bytes 1179648 | tf_op jit(solution)/shard_map/all_to_all | solution.py:706
  43.2 10.6 %collective-permute-start.11 = (bf16[80,1152]{1,0:T(8,128)(2,1)S(1)}, bf16[80,1152]{1,0:T(8,128)(2,1)S(1)}, u32[]{:S(2)}, u32[]{:S(2)}) collective-permute-start(bf16[80,1152]{1,0:T(8,128)(2,1)S(1)} %slice.6), channel_id=1, source_target_pairs={{0,16},{16,0},{1,17},{17,1},{2,18},{18,2},{3,19},{19,3},{4,20},{20... | collective-permute-start | bytes 552968 | tf_op jit(solution)/shard_map/ppermute | solution.py:588
  45.1 8.7 %collective-permute-start.12 = (bf16[64,1152]{1,0:T(8,128)(2,1)S(1)}, bf16[64,1152]{1,0:T(8,128)(2,1)S(1)}, u32[]{:S(2)}, u32[]{:S(2)}) collective-permute-start(bf16[64,1152]{1,0:T(8,128)(2,1)S(1)} %slice.7), channel_id=1, source_target_pairs={{0,2},{2,0},{1,3},{3,1},{4,6},{6,4},{5,7},{7,5},{8,10},{10,8},{9,1... | collective-permute-start | bytes 442376 | tf_op jit(solution)/shard_map/ppermute | solution.py:588
  46.7 7.7 %collective-permute-start.13 = (bf16[144,1152]{1,0:T(8,128)(2,1)S(1)}, bf16[144,1152]{1,0:T(8,128)(2,1)S(1)}, u32[]{:S(2)}, u32[]{:S(2)}) collective-permute-start(bf16[144,1152]{1,0:T(8,128)(2,1)S(1)} %shard_map.162.refs_0_), channel_id=1, source_target_pairs={{0,1},{1,0},{2,3},{3,2},{4,5},{5,4},{6,7},{7,6},{8,9},{9,8},{10,11... | collective-permute-start | bytes 995336 | tf_op jit(solution)/shard_map/ppermute | solution.py:588
  46.7 7.7 %collective-permute-start.14 = (bf16[144,1152]{1,0:T(8,128)(2,1)S(1)}, bf16[144,1152]{1,0:T(8,128)(2,1)S(1)}, u32[]{:S(2)}, u32[]{:S(2)}) collective-permute-start(bf16[144,1152]{1,0:T(8,128)(2,1)S(1)} %collective-permute-done.9.refs_1_), channel_id=1, source_target_pairs={{0,1},{1,0},{2,3},{3,2},{4,5},{5,4},{6,7},{7,6},{8,9},{9,8},{10,11... | collective-permute-start | bytes 995336 | tf_op jit(solution)/shard_map/ppermute | solution.py:588
  47.2 7.1 %collective-permute-start.15 = (bf16[144,1152]{1,0:T(8,128)(2,1)S(1)}, bf16[144,1152]{1,0:T(8,128)(2,1)S(1)}, u32[]{:S(2)}, u32[]{:S(2)}) collective-permute-start(bf16[144,1152]{1,0:T(8,128)(2,1)S(1)} %collective-permute-done.10.refs_2_), channel_id=1, source_target_pairs={{0,1},{1,0},{2,3},{3,2},{4,5},{5,4},{6,7},{7,6},{8,9},{9,8},{10,11... | collective-permute-start | bytes 995336 | tf_op jit(solution)/shard_map/ppermute | solution.py:588
  53.8 1.6 %collective-permute-start.16 = (bf16[80,1152]{1,0:T(8,128)(2,1)S(1)}, bf16[80,1152]{1,0:T(8,128)(2,1)S(1)}, u32[]{:S(2)}, u32[]{:S(2)}) collective-permute-start(bf16[80,1152]{1,0:T(8,128)(2,1)S(1)} %collective-permute-done.11.refs_3_), channel_id=1, source_target_pairs={{0,1},{1,0},{2,3},{3,2},{4,5},{5,4},{6,7},{7,6},{8,9},{9,8},{10,11... | collective-permute-start | bytes 552968 | tf_op jit(solution)/shard_map/ppermute | solution.py:588
  53.8 1.6 %collective-permute-start.17 = (bf16[64,1152]{1,0:T(8,128)(2,1)S(1)}, bf16[64,1152]{1,0:T(8,128)(2,1)S(1)}, u32[]{:S(2)}, u32[]{:S(2)}) collective-permute-start(bf16[64,1152]{1,0:T(8,128)(2,1)S(1)} %collective-permute-done.12.refs_4_), channel_id=1, source_target_pairs={{0,1},{1,0},{2,3},{3,2},{4,5},{5,4},{6,7},{7,6},{8,9},{9,8},{10,11... | collective-permute-start | bytes 442376 | tf_op jit(solution)/shard_map/ppermute | solution.py:588
  61.0 3.7 %copy-start.14 = (f32[8,128]{1,0:T(8,128)S(1)}, f32[8,128]{1,0:T(8,128)}, u32[]{:S(2)}) copy-start(f32[8,128]{1,0:T(8,128)} %copy-done.13) | copy-start | bytes 12292
  63.5 1.2 %collective-permute-start.18 = (f32[8,240]{1,0:T(8,128)S(1)}, f32[8,240]{1,0:T(8,128)S(1)}, u32[]{:S(2)}, u32[]{:S(2)}) collective-permute-start(f32[8,240]{1,0:T(8,128)S(1)} %get-tuple-element.75), channel_id=1, source_target_pairs={{0,1},{1,0},{2,3},{3,2},{4,5},{5,4},{6,7},{7,6},{8,9},{9,8},{10,11... | collective-permute-start | bytes 23048 | tf_op jit(solution)/shard_map/ppermute | solution.py:588
  (8 other events, 8.9 us)

commit v14 on v12

--- a/solution.py
+++ b/solution.py
@@ -329,6 +329,7 @@
         preferred_element_type=F32,
         precision=lax.Precision.HIGHEST,
     ) * (1.0 / width)
+    gram = jnp.concatenate(split_terms(gram, 3), axis=1)
     row_id = lax.broadcasted_iota(jnp.int32, (rows, LANES), 0)
     wide_id = lax.broadcasted_iota(jnp.int32, (rows, width), 0)
     level_id = lax.broadcasted_iota(jnp.int32, (level_mod.shape[1], width), 0).astype(F32)
@@ -357,14 +358,13 @@
                 mask_out[y, f] = info[values : values + mask_out.shape[2]]
                 vec = jnp.where(row_id < values, info[:rows], 0.0)
                 vec = jnp.where(row_id == values + y, 1.0, vec)
-                spread = jnp.sum(
-                    vec
-                    * jnp.dot(
-                        gram, vec, preferred_element_type=F32, precision=lax.Precision.HIGHEST
-                    ),
-                    axis=0,
-                    keepdims=True,
+                short = vec.astype(BF16)
+                met = jnp.dot(
+                    gram,
+                    jnp.concatenate([short, short, short], axis=0),
+                    preferred_element_type=F32,
                 )
+                spread = jnp.sum(vec * met, axis=0, keepdims=True)
                 spread = jnp.maximum(spread, 0.0) + EPS_NORM
                 rstd = lax.rsqrt(spread)
                 std = spread * rstd

time: 66 us -> 65.5 us (level)
  transfers between devices with their start and end apart: 21 -> 21, of which waited for: 6 -> 6; matrix products, arithmetic and copies ran while one was open for 0% -> 0% of each run, Pallas kernels for 15% -> 14%
where the time goes in v14:
time: 65.5 us; the launch traced here: 64.9 us
  starting transfers between devices  26.7 us (41%)
  Pallas kernels  15.7 us (24%)
  waiting for transfers between devices  15.7 us (24%)
  local copies, waits for them, and re-layouts  5.3 us (8%)
  between operations  1.57 us (2%)
    ppermute x18, starting transfers between devices, swapped(): return lax.ppermute(value, axis, [(i, i ^ mask) for i in range(count)])  18 us
    ppermute x18, waiting for transfers between devices, swapped(): return lax.ppermute(value, axis, [(i, i ^ mask) for i in range(count)])  6.49 us
    pallas_call x1, Pallas kernels, on_device_heads(): kernel_call(functools.partial(attend_kernel, frames, tokens, queues), jax...  6.13 us
    unnamed x38, local copies, waits for them, and re-layouts  5.26 us
    all_to_all x1, waiting for transfers between devices, on_device_heads(): received = lax.all_to_all(attended, ('tok', 'queue', 'scene'), 0, 0)  4.69 us
    ppermute x1, waiting for transfers between devices, on_device_heads(): lax.ppermute(first, 'queue', [(i + 1, i) for i in range(queues - 1)])  4.5 us
    all_to_all x1, starting transfers between devices, on_device_heads(): shares = lax.all_to_all(copies, ('scene', 'queue', 'tok'), 0, 0)  3.83 us
    all_to_all x1, starting transfers between devices, on_device_heads(): received = lax.all_to_all(attended, ('tok', 'queue', 'scene'), 0, 0)  3.58 us
  transfers between devices with their start and end apart: 21, of which 6 were waited for; matrix products, arithmetic and copies ran while one was open for 0% of the time, Pallas kernels for 14%

profile of v14, /device:TPU:0, one launch (start us, length us, event | category | flops | bytes accessed | tf_op | source)
XLA Modules:
  0.0 64.9 jit_solution(5895856036932285598)
XLA Ops:
  0.7 2.9 %shard_map.158 = (bf16[144,504]{1,0:T(8,128)(2,1)}, bf16[144,504]{1,0:T(8,128)(2,1)}, bf16[144,504]{1,0:T(8,128)(2,1)}, bf16[144,504]{1,0:T(8,128)(2,1)}, bf16[1...) custom-call(f32[4,16,48]{2,1,0:T(8,128)} %latents.1, s32[1,4]{1,0:T(1,128)} %bitcast.14, ...), custom_call_target="tpu_custom_call" | custom-call | flops 1000000 | bytes 8000000 | tf_op jit(solution)/shard_map/pallas_call | solution.py:629
  3.6 3.0 %collective-permute-start = (bf16[144,504]{1,0:T(8,128)(2,1)}, bf16[144,504]{1,0:T(8,128)(2,1)S(1)}, u32[]{:S(2)}, u32[]{:S(2)}) collective-permute-start(bf16[144,504]{1,0:T(8,128)(2,1)} %get-tuple-element.41), channel_id=1, source_target_pairs={{0,4},{4,0},{8,12},{12,8},{1,5},{5,1},{9,13},{13,9},{2,6},{6,2},{1... | collective-permute-start | bytes 435464 | tf_op jit(solution)/shard_map/ppermute | solution.py:588
  6.6 2.6 %collective-permute-start.1 = (bf16[144,504]{1,0:T(8,128)(2,1)}, bf16[144,504]{1,0:T(8,128)(2,1)S(1)}, u32[]{:S(2)}, u32[]{:S(2)}) collective-permute-start(bf16[144,504]{1,0:T(8,128)(2,1)} %get-tuple-element.48), channel_id=1, source_target_pairs={{0,8},{4,12},{8,0},{12,4},{1,9},{5,13},{9,1},{13,5},{2,10},{6,14},... | collective-permute-start | bytes 435464 | tf_op jit(solution)/shard_map/ppermute | solution.py:588
  9.2 3.8 %all-to-all-start = ((bf16[16,32,96]{2,1,0:T(8,128)(2,1)}), bf16[16,32,96]{2,1,0:T(8,128)(2,1)S(1)}, u32[]{:S(2)}, u32[]{:S(2)}) async-start(bf16[16,32,96]{2,1,0:T(8,128)(2,1)} %get-tuple-element.51), calls=%async_computation | async-start | bytes 262144 | tf_op jit(solution)/shard_map/all_to_all | solution.py:665
  13.0 3.7 %collective-permute-start.2 = (bf16[144,504]{1,0:T(8,128)(2,1)}, bf16[144,504]{1,0:T(8,128)(2,1)S(1)}, u32[]{:S(2)}, u32[]{:S(2)}) collective-permute-start(bf16[144,504]{1,0:T(8,128)(2,1)} %get-tuple-element.49), channel_id=1, source_target_pairs={{0,12},{4,8},{8,4},{12,0},{1,13},{5,9},{9,5},{13,1},{2,14},{6,10},... | collective-permute-start | bytes 435464 | tf_op jit(solution)/shard_map/ppermute | solution.py:588
  16.8 0.9 %copy-done = f32[16,3,1152]{2,0,1:T(8,128)S(1)} copy-done((f32[16,3,1152]{2,0,1:T(8,128)S(1)}, f32[16,3,1152]{2,0,1:T(8,128)}, u32[]{:S(2)}) %copy-start) | copy-done | bytes 221208
  17.7 0.9 %copy-done.2 = bf16[144,504]{1,0:T(8,128)(2,1)S(1)} copy-done((bf16[144,504]{1,0:T(8,128)(2,1)S(1)}, bf16[144,504]{1,0:T(8,128)(2,1)}, u32[]{:S(2)}) %copy-start.2) | copy-done | bytes 145176
  18.6 0.8 %copy-done.3 = bf16[16,1152]{1,0:T(8,128)(2,1)S(1)} copy-done((bf16[16,1152]{1,0:T(8,128)(2,1)S(1)}, bf16[16,1152]{1,0:T(8,128)(2,1)}, u32[]{:S(2)}) %copy-start.3) | copy-done | bytes 36888
  19.8 0.6 collective-permute-start.5
  20.5 1.3 %collective-permute-start.3 = (f32[24,48]{1,0:T(8,128)}, f32[24,48]{1,0:T(8,128)S(1)}, u32[]{:S(2)}, u32[]{:S(2)}) collective-permute-start(f32[24,48]{1,0:T(8,128)} %get-tuple-element.50), channel_id=1, source_target_pairs={{4,0},{8,4},{12,8},{5,1},{9,5},{13,9},{6,2},{10,6},{14,10},{7,3},{... | collective-permute-start | bytes 13832 | tf_op jit(solution)/shard_map/ppermute | solution.py:668
  21.8 4.5 %collective-permute-done.3.refs_1_ = f32[24,48]{1,0:T(8,128)S(1)} collective-permute-done((f32[24,48]{1,0:T(8,128)}, f32[24,48]{1,0:T(8,128)S(1)}, u32[]{:S(2)}, u32[]{:S(2)}) %collective-permute-start.3) | collective-permute-done | bytes 4640 | tf_op jit(solution)/shard_map/ppermute | solution.py:668
  26.5 1.5 %collective-permute-start.9 = (bf16[144,1152]{1,0:T(8,128)(2,1)S(1)}, bf16[144,1152]{1,0:T(8,128)(2,1)S(1)}, u32[]{:S(2)}, u32[]{:S(2)}) collective-permute-start(bf16[144,1152]{1,0:T(8,128)(2,1)S(1)} %shard_map.162.refs_0_), channel_id=1, source_target_pairs={{0,2},{2,0},{1,3},{3,1},{4,6},{6,4},{5,7},{7,5},{8,10},{10,8},{9,1... | collective-permute-start | bytes 995336 | tf_op jit(solution)/shard_map/ppermute | solution.py:588
  28.0 1.5 %collective-permute-start.10 = (bf16[144,1152]{1,0:T(8,128)(2,1)S(1)}, bf16[144,1152]{1,0:T(8,128)(2,1)S(1)}, u32[]{:S(2)}, u32[]{:S(2)}) collective-permute-start(bf16[144,1152]{1,0:T(8,128)(2,1)S(1)} %shard_map.162.refs_0_), channel_id=1, source_target_pairs={{0,16},{16,0},{1,17},{17,1},{2,18},{18,2},{3,19},{19,3},{4,20},{20... | collective-permute-start | bytes 995336 | tf_op jit(solution)/shard_map/ppermute | solution.py:588
  29.5 0.5 collective-permute-start.8
  30.0 1.0 %collective-permute-done.8.other = bf16[16,32,96]{2,1,0:T(8,128)(2,1)S(1)} collective-permute-done((bf16[16,32,96]{2,1,0:T(8,128)(2,1)S(1)}, bf16[16,32,96]{2,1,0:T(8,128)(2,1)S(1)}, u32[]{:S(2)}, u32[]{:S(2)}) %collective-permute-start.8) | collective-permute-done | bytes 98336 | tf_op jit(solution)/shard_map/ppermute | solution.py:588
  31.0 1.9 %shard_map.160 = (bf16[1024,1152]{1,0:T(8,128)(2,1)S(1)}, bf16[16,64,256]{2,1,0:T(8,128)(2,1)S(1)}, f32[16,1,256]{2,1,0:T(1,128)S(1)}, f32[2,16,16,128]{3,2,1,0:T(8,128)S(1)}) custom-call(bf16[16,32,96]{2,1,0:T(8,128)(2,1)S(1)} %all-to-all-done.mine, bf16[16,32,96]{2,1,0:T(8,128)(2,1)S(1)} %collective-permute-done.8.other, ...), custom_call_target="tpu_custom_call" | custom-call | flops 1000000 | bytes 8000000 | tf_op jit(solution)/shard_map/pallas_call | solution.py:679
  33.0 6.1 %shard_map.161 = bf16[16,72,240]{2,1,0:T(8,128)(2,1)} custom-call(bf16[144,504]{1,0:T(8,128)(2,1)S(1)} %get-tuple-element.46.refs_0_, bf16[144,504]{1,0:T(8,128)(2,1)S(1)} %collective-permute-done.refs_1_, bf16[144,504]{1,0:T(8,128)(2,1)S(1)} %collective-permute-done.1.refs_2_, bf16[144,504]{1,0:T(8,128)(2,1)S(1)} %collective-permute-done.2.refs_3_, ...), custom_call_target="tpu_custom_call" | custom-call | flops 1000000 | bytes 100000000 | tf_op jit(solution)/shard_map/pallas_call | solution.py:690
  39.2 3.6 %all-to-all-start.1 = ((bf16[16,72,240]{2,1,0:T(8,128)(2,1)}), bf16[16,72,240]{2,1,0:T(8,128)(2,1)S(1)}, u32[]{:S(2)}, u32[]{:S(2)}) async-start(bf16[16,72,240]{2,1,0:T(8,128)(2,1)} %shard_map.161), calls=%async_computation.1 | async-start | bytes 1179648 | tf_op jit(solution)/shard_map/all_to_all | solution.py:706
  42.8 1.9 %collective-permute-start.11 = (bf16[80,1152]{1,0:T(8,128)(2,1)S(1)}, bf16[80,1152]{1,0:T(8,128)(2,1)S(1)}, u32[]{:S(2)}, u32[]{:S(2)}) collective-permute-start(bf16[80,1152]{1,0:T(8,128)(2,1)S(1)} %slice.6), channel_id=1, source_target_pairs={{0,16},{16,0},{1,17},{17,1},{2,18},{18,2},{3,19},{19,3},{4,20},{20... | collective-permute-start | bytes 552968 | tf_op jit(solution)/shard_map/ppermute | solution.py:588
  44.7 1.6 %collective-permute-start.12 = (bf16[64,1152]{1,0:T(8,128)(2,1)S(1)}, bf16[64,1152]{1,0:T(8,128)(2,1)S(1)}, u32[]{:S(2)}, u32[]{:S(2)}) collective-permute-start(bf16[64,1152]{1,0:T(8,128)(2,1)S(1)} %slice.7), channel_id=1, source_target_pairs={{0,2},{2,0},{1,3},{3,1},{4,6},{6,4},{5,7},{7,5},{8,10},{10,8},{9,1... | collective-permute-start | bytes 442376 | tf_op jit(solution)/shard_map/ppermute | solution.py:588
  47.5 1.0 %shard_map.163 = (bf16[112,1152]{1,0:T(8,128)(2,1)S(1)}, bf16[96,240]{1,0:T(8,128)(2,1)S(1)}, f32[8,240]{1,0:T(8,128)S(1)}, f32[8,240]{1,0:T(8,128)S(1)}, f32[8,48]{1,0:T(8,128)S(1)}, /*index=5*/f32[8,128]{1,0:T(8,128)S(1)}) custom-call(f32[24,192]{1,0:T(8,128)S(1)} %copy-done.8, f32[24,48]{1,0:T(8,128)S(1)} %collective-permute-done.3.refs_1_, ...), custom_call_target="tpu_custom_call" | custom-call | flops 1000000 | bytes 1000000 | tf_op jit(solution)/shard_map/pallas_call | solution.py:726
  48.5 0.6 copy-done.5
  49.1 0.6 copy-done.11
  49.7 0.6 copy-done.13
  50.3 3.1 %collective-permute-done.12.refs_4_ = bf16[64,1152]{1,0:T(8,128)(2,1)S(1)} collective-permute-done((bf16[64,1152]{1,0:T(8,128)(2,1)S(1)}, bf16[64,1152]{1,0:T(8,128)(2,1)S(1)}, u32[]{:S(2)}, u32[]{:S(2)}) %collective-permute-start.12) | collective-permute-done | bytes 147488 | tf_op jit(solution)/shard_map/ppermute | solution.py:588
  53.4 0.5 collective-permute-start.17
  53.9 1.1 %collective-permute-done.17.refs_9_ = bf16[64,1152]{1,0:T(8,128)(2,1)S(1)} collective-permute-done((bf16[64,1152]{1,0:T(8,128)(2,1)S(1)}, bf16[64,1152]{1,0:T(8,128)(2,1)S(1)}, u32[]{:S(2)}, u32[]{:S(2)}) %collective-permute-start.17) | collective-permute-done | bytes 147488 | tf_op jit(solution)/shard_map/ppermute | solution.py:588
  55.0 4.7 %all-to-all-done.1.refs_10_ = bf16[16,72,240]{2,1,0:T(8,128)(2,1)S(1)} async-done(((bf16[16,72,240]{2,1,0:T(8,128)(2,1)}), bf16[16,72,240]{2,1,0:T(8,128)(2,1)S(1)}, u32[]{:S(2)}, u32[]{:S(2)}) %all-to-all-start.1) | async-done | bytes 552992 | tf_op jit(solution)/shard_map/all_to_all | solution.py:706
  59.7 0.8 %copy-done.6 = bf16[96,240]{1,0:T(8,128)(2,1)S(1)} copy-done((bf16[96,240]{1,0:T(8,128)(2,1)S(1)}, bf16[96,240]{1,0:T(8,128)(2,1)}, u32[]{:S(2)}) %copy-start.6) | copy-done | bytes 46104
  60.5 2.5 %shard_map.164 = (f32[8,240]{1,0:T(8,128)S(1)}, f32[8,240]{1,0:T(8,128)S(1)}) custom-call(bf16[144,1152]{1,0:T(8,128)(2,1)S(1)} %shard_map.162.refs_0_, bf16[144,1152]{1,0:T(8,128)(2,1)S(1)} %collective-permute-done.9.refs_1_, bf16[144,1152]{1,0:T(8,128)(2,1)S(1)} %collective-permute-done.10.refs_2_, bf16[80,1152]{1,0:T(8,128)(2,1)S(1)} %collective-permute-done.11.refs_3_, ...), custom_call_target="tpu_custom_call" | custom-call | flops 1000000 | bytes 8000000 | tf_op jit(solution)/shard_map/pallas_call | solution.py:743
  63.0 1.2 %collective-permute-done.18.partner = f32[8,240]{1,0:T(8,128)S(1)} collective-permute-done((f32[8,240]{1,0:T(8,128)S(1)}, f32[8,240]{1,0:T(8,128)S(1)}, u32[]{:S(2)}, u32[]{:S(2)}) %collective-permute-start.18) | collective-permute-done | bytes 7712 | tf_op jit(solution)/shard_map/ppermute | solution.py:588
  64.2 0.7 %shard_map.165 = (f32[4,8,48]{2,1,0:T(8,128)}, f32[4,8,48]{2,1,0:T(8,128)}) custom-call(f32[8,240]{1,0:T(8,128)S(1)} %get-tuple-element.74.mine, f32[8,240]{1,0:T(8,128)S(1)} %collective-permute-done.18.partner, f32[8,240]{1,0:T(8,128)S(1)} %get-tuple-element.76.base, f32[8,240]{1,0:T(8,128)S(1)} %get-tuple-element.77.factor, f32[8,48]{1,0:T(8,128)S(1)} %copy-done.12, ...), custom_call_target="tpu_custom_call" | custom-call | flops 1000000 | bytes 1000000 | tf_op jit(solution)/shard_map/pallas_call | solution.py:752
  (59 shorter events, 1.4 us)
Async XLA Ops:
  0.6 32.3 %copy-start.16 = (f32[72]{0:T(128)S(1)}, f32[72]{0:T(128)}, u32[]{:S(2)}) copy-start(f32[72]{0:T(128)} %param.23) | copy-start | bytes 868
  0.6 32.3 %copy-start.17 = (f32[72]{0:T(128)S(1)}, f32[72]{0:T(128)}, u32[]{:S(2)}) copy-start(f32[72]{0:T(128)} %param.24) | copy-start | bytes 868
  3.6 16.2 %collective-permute-start = (bf16[144,504]{1,0:T(8,128)(2,1)}, bf16[144,504]{1,0:T(8,128)(2,1)S(1)}, u32[]{:S(2)}, u32[]{:S(2)}) collective-permute-start(bf16[144,504]{1,0:T(8,128)(2,1)} %get-tuple-element.41), channel_id=1, source_target_pairs={{0,4},{4,0},{8,12},{12,8},{1,5},{5,1},{9,13},{13,9},{2,6},{6,2},{1... | collective-permute-start | bytes 435464 | tf_op jit(solution)/shard_map/ppermute | solution.py:588
  6.6 13.8 %collective-permute-start.1 = (bf16[144,504]{1,0:T(8,128)(2,1)}, bf16[144,504]{1,0:T(8,128)(2,1)S(1)}, u32[]{:S(2)}, u32[]{:S(2)}) collective-permute-start(bf16[144,504]{1,0:T(8,128)(2,1)} %get-tuple-element.48), channel_id=1, source_target_pairs={{0,8},{4,12},{8,0},{12,4},{1,9},{5,13},{9,1},{13,5},{2,10},{6,14},... | collective-permute-start | bytes 435464 | tf_op jit(solution)/shard_map/ppermute | solution.py:588
  9.2 17.1 %all-to-all-start = ((bf16[16,32,96]{2,1,0:T(8,128)(2,1)}), bf16[16,32,96]{2,1,0:T(8,128)(2,1)S(1)}, u32[]{:S(2)}, u32[]{:S(2)}) async-start(bf16[16,32,96]{2,1,0:T(8,128)(2,1)} %get-tuple-element.51), calls=%async_computation | async-start | bytes 262144 | tf_op jit(solution)/shard_map/all_to_all | solution.py:665
  13.0 13.2 %collective-permute-start.2 = (bf16[144,504]{1,0:T(8,128)(2,1)}, bf16[144,504]{1,0:T(8,128)(2,1)S(1)}, u32[]{:S(2)}, u32[]{:S(2)}) collective-permute-start(bf16[144,504]{1,0:T(8,128)(2,1)} %get-tuple-element.49), channel_id=1, source_target_pairs={{0,12},{4,8},{8,4},{12,0},{1,13},{5,9},{9,5},{13,1},{2,14},{6,10},... | collective-permute-start | bytes 435464 | tf_op jit(solution)/shard_map/ppermute | solution.py:588
  16.8 9.5 %collective-permute-start.4 = (bf16[144,504]{1,0:T(8,128)(2,1)}, bf16[144,504]{1,0:T(8,128)(2,1)S(1)}, u32[]{:S(2)}, u32[]{:S(2)}) collective-permute-start(bf16[144,504]{1,0:T(8,128)(2,1)} %get-tuple-element.42.own_source), channel_id=1, source_target_pairs={{0,1},{1,0},{2,3},{3,2},{4,5},{5,4},{6,7},{7,6},{8,9},{9,8},{10,11... | collective-permute-start | bytes 435464 | tf_op jit(solution)/shard_map/ppermute | solution.py:588
  19.8 6.5 %collective-permute-start.5 = (bf16[144,504]{1,0:T(8,128)(2,1)S(1)}, bf16[144,504]{1,0:T(8,128)(2,1)S(1)}, u32[]{:S(2)}, u32[]{:S(2)}) collective-permute-start(bf16[144,504]{1,0:T(8,128)(2,1)S(1)} %collective-permute-done.refs_1_), channel_id=1, source_target_pairs={{0,1},{1,0},{2,3},{3,2},{4,5},{5,4},{6,7},{7,6},{8,9},{9,8},{10,11... | collective-permute-start | bytes 435464 | tf_op jit(solution)/shard_map/ppermute | solution.py:588
  20.4 5.9 %collective-permute-start.6 = (bf16[144,504]{1,0:T(8,128)(2,1)S(1)}, bf16[144,504]{1,0:T(8,128)(2,1)S(1)}, u32[]{:S(2)}, u32[]{:S(2)}) collective-permute-start(bf16[144,504]{1,0:T(8,128)(2,1)S(1)} %collective-permute-done.1.refs_2_), channel_id=1, source_target_pairs={{0,1},{1,0},{2,3},{3,2},{4,5},{5,4},{6,7},{7,6},{8,9},{9,8},{10,11... | collective-permute-start | bytes 435464 | tf_op jit(solution)/shard_map/ppermute | solution.py:588
  20.5 5.8 %collective-permute-start.3 = (f32[24,48]{1,0:T(8,128)}, f32[24,48]{1,0:T(8,128)S(1)}, u32[]{:S(2)}, u32[]{:S(2)}) collective-permute-start(f32[24,48]{1,0:T(8,128)} %get-tuple-element.50), channel_id=1, source_target_pairs={{4,0},{8,4},{12,8},{5,1},{9,5},{13,9},{6,2},{10,6},{14,10},{7,3},{... | collective-permute-start | bytes 13832 | tf_op jit(solution)/shard_map/ppermute | solution.py:668
  26.5 12.7 %collective-permute-start.9 = (bf16[144,1152]{1,0:T(8,128)(2,1)S(1)}, bf16[144,1152]{1,0:T(8,128)(2,1)S(1)}, u32[]{:S(2)}, u32[]{:S(2)}) collective-permute-start(bf16[144,1152]{1,0:T(8,128)(2,1)S(1)} %shard_map.162.refs_0_), channel_id=1, source_target_pairs={{0,2},{2,0},{1,3},{3,1},{4,6},{6,4},{5,7},{7,5},{8,10},{10,8},{9,1... | collective-permute-start | bytes 995336 | tf_op jit(solution)/shard_map/ppermute | solution.py:588
  28.0 11.2 %collective-permute-start.10 = (bf16[144,1152]{1,0:T(8,128)(2,1)S(1)}, bf16[144,1152]{1,0:T(8,128)(2,1)S(1)}, u32[]{:S(2)}, u32[]{:S(2)}) collective-permute-start(bf16[144,1152]{1,0:T(8,128)(2,1)S(1)} %shard_map.162.refs_0_), channel_id=1, source_target_pairs={{0,16},{16,0},{1,17},{17,1},{2,18},{18,2},{3,19},{19,3},{4,20},{20... | collective-permute-start | bytes 995336 | tf_op jit(solution)/shard_map/ppermute | solution.py:588
  29.5 3.4 %collective-permute-start.7 = (bf16[144,504]{1,0:T(8,128)(2,1)S(1)}, bf16[144,504]{1,0:T(8,128)(2,1)S(1)}, u32[]{:S(2)}, u32[]{:S(2)}) collective-permute-start(bf16[144,504]{1,0:T(8,128)(2,1)S(1)} %collective-permute-done.2.refs_3_), channel_id=1, source_target_pairs={{0,1},{1,0},{2,3},{3,2},{4,5},{5,4},{6,7},{7,6},{8,9},{9,8},{10,11... | collective-permute-start | bytes 435464 | tf_op jit(solution)/shard_map/ppermute | solution.py:588
  29.5 1.6 %collective-permute-start.8 = (bf16[16,32,96]{2,1,0:T(8,128)(2,1)S(1)}, bf16[16,32,96]{2,1,0:T(8,128)(2,1)S(1)}, u32[]{:S(2)}, u32[]{:S(2)}) collective-permute-start(bf16[16,32,96]{2,1,0:T(8,128)(2,1)S(1)} %all-to-all-done.mine), channel_id=1, source_target_pairs={{0,1},{1,0},{2,3},{3,2},{4,5},{5,4},{6,7},{7,6},{8,9},{9,8},{10,11... | collective-permute-start | bytes 294920 | tf_op jit(solution)/shard_map/ppermute | solution.py:588
  33.0 13.8 %copy-start.18 = (f32[1152]{0:T(1024)S(1)}, f32[1152]{0:T(1024)}, u32[]{:S(2)}) copy-start(f32[1152]{0:T(1024)} %param.26) | copy-start | bytes 13828
  33.0 14.5 %copy-start.1 = (f32[16,3,1152]{2,0,1:T(8,128)S(1)}, f32[16,3,1152]{2,0,1:T(8,128)}, u32[]{:S(2)}) copy-start(f32[16,3,1152]{2,0,1:T(8,128)} %param.20) | copy-start | bytes 663556
  33.0 14.5 %copy-start.4 = (bf16[16,1152]{1,0:T(8,128)(2,1)S(1)}, bf16[16,1152]{1,0:T(8,128)(2,1)}, u32[]{:S(2)}) copy-start(bf16[16,1152]{1,0:T(8,128)(2,1)} %refs_4_.1) | copy-start | bytes 110596
  33.0 14.5 %copy-start.7 = (bf16[1152,16]{0,1:T(8,128)(2,1)S(1)}, bf16[1152,16]{0,1:T(8,128)(2,1)}, u32[]{:S(2)}) copy-start(bf16[1152,16]{0,1:T(8,128)(2,1)} %param.27) | copy-start | bytes 110596
  33.0 14.5 %copy-start.8 = (f32[24,192]{1,0:T(8,128)S(1)}, f32[24,192]{1,0:T(8,128)}, u32[]{:S(2)}) copy-start(f32[24,192]{1,0:T(8,128)} %get-tuple-element.66.refs_0_) | copy-start | bytes 55300
  33.0 14.5 %copy-start.9 = (f32[1,1152]{1,0:T(1,128)S(1)}, f32[1,1152]{1,0:T(1,128)}, u32[]{:S(2)}) copy-start(f32[1,1152]{1,0:T(1,128)} %refs_2_.1) | copy-start | bytes 13828
  33.0 14.5 %copy-start.10 = (f32[8,48]{1,0:T(8,128)S(1)}, f32[8,48]{1,0:T(8,128)}, u32[]{:S(2)}) copy-start(f32[8,48]{1,0:T(8,128)} %refs_7_.1) | copy-start | bytes 4612
  33.0 14.5 %copy-start.15 = (f32[8]{0:T(128)S(1)}, f32[8]{0:T(128)}, u32[]{:S(2)}) copy-start(f32[8]{0:T(128)} %refs_8_.1) | copy-start | bytes 100
  39.2 20.5 %all-to-all-start.1 = ((bf16[16,72,240]{2,1,0:T(8,128)(2,1)}), bf16[16,72,240]{2,1,0:T(8,128)(2,1)S(1)}, u32[]{:S(2)}, u32[]{:S(2)}) async-start(bf16[16,72,240]{2,1,0:T(8,128)(2,1)} %shard_map.161), calls=%async_computation.1 | async-start | bytes 1179648 | tf_op jit(solution)/shard_map/all_to_all | solution.py:706
  42.8 10.6 %collective-permute-start.11 = (bf16[80,1152]{1,0:T(8,128)(2,1)S(1)}, bf16[80,1152]{1,0:T(8,128)(2,1)S(1)}, u32[]{:S(2)}, u32[]{:S(2)}) collective-permute-start(bf16[80,1152]{1,0:T(8,128)(2,1)S(1)} %slice.6), channel_id=1, source_target_pairs={{0,16},{16,0},{1,17},{17,1},{2,18},{18,2},{3,19},{19,3},{4,20},{20... | collective-permute-start | bytes 552968 | tf_op jit(solution)/shard_map/ppermute | solution.py:588
  44.7 8.7 %collective-permute-start.12 = (bf16[64,1152]{1,0:T(8,128)(2,1)S(1)}, bf16[64,1152]{1,0:T(8,128)(2,1)S(1)}, u32[]{:S(2)}, u32[]{:S(2)}) collective-permute-start(bf16[64,1152]{1,0:T(8,128)(2,1)S(1)} %slice.7), channel_id=1, source_target_pairs={{0,2},{2,0},{1,3},{3,1},{4,6},{6,4},{5,7},{7,5},{8,10},{10,8},{9,1... | collective-permute-start | bytes 442376 | tf_op jit(solution)/shard_map/ppermute | solution.py:588
  46.3 7.6 %collective-permute-start.13 = (bf16[144,1152]{1,0:T(8,128)(2,1)S(1)}, bf16[144,1152]{1,0:T(8,128)(2,1)S(1)}, u32[]{:S(2)}, u32[]{:S(2)}) collective-permute-start(bf16[144,1152]{1,0:T(8,128)(2,1)S(1)} %shard_map.162.refs_0_), channel_id=1, source_target_pairs={{0,1},{1,0},{2,3},{3,2},{4,5},{5,4},{6,7},{7,6},{8,9},{9,8},{10,11... | collective-permute-start | bytes 995336 | tf_op jit(solution)/shard_map/ppermute | solution.py:588
  46.3 7.6 %collective-permute-start.14 = (bf16[144,1152]{1,0:T(8,128)(2,1)S(1)}, bf16[144,1152]{1,0:T(8,128)(2,1)S(1)}, u32[]{:S(2)}, u32[]{:S(2)}) collective-permute-start(bf16[144,1152]{1,0:T(8,128)(2,1)S(1)} %collective-permute-done.9.refs_1_), channel_id=1, source_target_pairs={{0,1},{1,0},{2,3},{3,2},{4,5},{5,4},{6,7},{7,6},{8,9},{9,8},{10,11... | collective-permute-start | bytes 995336 | tf_op jit(solution)/shard_map/ppermute | solution.py:588
  46.8 7.1 %collective-permute-start.15 = (bf16[144,1152]{1,0:T(8,128)(2,1)S(1)}, bf16[144,1152]{1,0:T(8,128)(2,1)S(1)}, u32[]{:S(2)}, u32[]{:S(2)}) collective-permute-start(bf16[144,1152]{1,0:T(8,128)(2,1)S(1)} %collective-permute-done.10.refs_2_), channel_id=1, source_target_pairs={{0,1},{1,0},{2,3},{3,2},{4,5},{5,4},{6,7},{7,6},{8,9},{9,8},{10,11... | collective-permute-start | bytes 995336 | tf_op jit(solution)/shard_map/ppermute | solution.py:588
  53.4 1.6 %collective-permute-start.16 = (bf16[80,1152]{1,0:T(8,128)(2,1)S(1)}, bf16[80,1152]{1,0:T(8,128)(2,1)S(1)}, u32[]{:S(2)}, u32[]{:S(2)}) collective-permute-start(bf16[80,1152]{1,0:T(8,128)(2,1)S(1)} %collective-permute-done.11.refs_3_), channel_id=1, source_target_pairs={{0,1},{1,0},{2,3},{3,2},{4,5},{5,4},{6,7},{7,6},{8,9},{9,8},{10,11... | collective-permute-start | bytes 552968 | tf_op jit(solution)/shard_map/ppermute | solution.py:588
  53.4 1.6 %collective-permute-start.17 = (bf16[64,1152]{1,0:T(8,128)(2,1)S(1)}, bf16[64,1152]{1,0:T(8,128)(2,1)S(1)}, u32[]{:S(2)}, u32[]{:S(2)}) collective-permute-start(bf16[64,1152]{1,0:T(8,128)(2,1)S(1)} %collective-permute-done.12.refs_4_), channel_id=1, source_target_pairs={{0,1},{1,0},{2,3},{3,2},{4,5},{5,4},{6,7},{7,6},{8,9},{9,8},{10,11... | collective-permute-start | bytes 442376 | tf_op jit(solution)/shard_map/ppermute | solution.py:588
  60.5 3.7 %copy-start.14 = (f32[8,128]{1,0:T(8,128)S(1)}, f32[8,128]{1,0:T(8,128)}, u32[]{:S(2)}) copy-start(f32[8,128]{1,0:T(8,128)} %copy-done.13) | copy-start | bytes 12292
  63.0 1.2 %collective-permute-start.18 = (f32[8,240]{1,0:T(8,128)S(1)}, f32[8,240]{1,0:T(8,128)S(1)}, u32[]{:S(2)}, u32[]{:S(2)}) collective-permute-start(f32[8,240]{1,0:T(8,128)S(1)} %get-tuple-element.75), channel_id=1, source_target_pairs={{0,1},{1,0},{2,3},{3,2},{4,5},{5,4},{6,7},{7,6},{8,9},{9,8},{10,11... | collective-permute-start | bytes 23048 | tf_op jit(solution)/shard_map/ppermute | solution.py:588
  (8 other events, 8.9 us)

commit v15 on v14

--- a/solution.py
+++ b/solution.py
@@ -470,8 +470,8 @@
 
 def ready_kernel(values, half, *refs):
     sources, table, index = refs[:8], refs[8], refs[9]
-    left, right, base, factor, noise_out, guide = refs[10:16]
-    held, sems = refs[16:24], refs[24]
+    both, base, factor, noise_out, guide = refs[10:15]
+    held, sems = refs[15:23], refs[23]
     copies = []
     for i, (source, to) in enumerate(zip(sources, held)):
         source = source.at[2] if i == 3 else source
@@ -486,7 +486,7 @@
     lanes = info.shape[1]
     ones = jnp.ones((16, lanes), BF16)
     zero = jnp.zeros((13, width), BF16)
-    left[...] = jnp.concatenate(
+    both[:, :width] = jnp.concatenate(
         [embed[...]]
         + split_terms(cond[...], 3)
         + [zero]
@@ -499,8 +499,9 @@
     one_hot = (lax.broadcasted_iota(jnp.int32, (levels_all, lanes), 0).astype(F32) == level).astype(
         F32
     ).astype(BF16)
-    right[...] = jnp.concatenate(
-        [info[:values].astype(BF16), ones, one_hot, one_hot, one_hot, ones], axis=0
+    unused = jnp.zeros((final_w.shape[0], lanes), BF16)
+    both[:, width:] = jnp.concatenate(
+        [info[:values].astype(BF16), ones, one_hot, one_hot, one_hot, ones, unused], axis=0
     )
     own = pl.multiple_of(place_of("cfg") * half, half)
     current = noise_sigma((level + 1.0) / levels_all)
@@ -515,7 +516,7 @@
 
 def finish_kernel(half, values, queues, *refs):
     parts = [refs[:5], refs[5:10]]
-    attended, left, right, mine, send, scratch, mixed = refs[10:]
+    attended, both, mine, send, scratch, mixed = refs[10:]
     scene, q_at, tok, core = (place_of(a) for a in ("scene", "queue", "tok", "cfg"))
     group = parts[0][0].shape[1] // queues
     columns = parts[0][0].shape[0]
@@ -549,17 +550,17 @@
             at = (c * queues + k) * columns
             mixed[pl.ds(pl.multiple_of(first, 8), columns), :] = total[at : at + columns]
 
-    first, terms = values + 16, right.shape[0]
-    last = terms - 16
-    emb = dot_tn(left[:first], right[:first])
-    gate = dot_tn(left[first:last], right[first:last])
-    gain = dot_tn(left[last:terms], right[last:])
+    width, terms = mixed.shape[0], both.shape[0] - values
+    first, last = values + 16, terms - 16
+    emb = dot_tn(both[:first, :width], both[:first, width:])
+    gate = dot_tn(both[first:last, :width], both[first:last, width:])
+    gain = dot_tn(both[last:terms, :width], both[last:terms, width:])
     summed = emb + gate * mixed[...]
     center = jnp.mean(summed, axis=0, keepdims=True)
     deviate = summed - center
     spread = jnp.mean(deviate * deviate, axis=0, keepdims=True)
     final = (deviate * lax.rsqrt(spread + EPS_NORM) * gain).astype(BF16)
-    scratch[...] = jnp.dot(left[terms:], final, preferred_element_type=F32)
+    scratch[...] = jnp.dot(both[terms:, :width], final, preferred_element_type=F32)
     own = pl.multiple_of(core * half, half)
     other = pl.multiple_of((1 - core) * half, half)
     mine[...] = scratch[pl.ds(own, half), :]
@@ -723,11 +724,10 @@
         pltpu.VMEM(a.shape[1:] if i == 3 else a.shape, a.dtype) for i, a in enumerate(smalls)
     ]
     terms = values + 16 + 3 * levels_all + 16
-    left, right, *rest = kernel_call(
+    both, *rest = kernel_call(
         functools.partial(ready_kernel, values, half),
         [
-            jax.ShapeDtypeStruct((terms + values, width), BF16),
-            jax.ShapeDtypeStruct((terms, row_lanes), BF16),
+            jax.ShapeDtypeStruct((terms + values, width + row_lanes), BF16),
             half_shape,
             half_shape,
             jax.ShapeDtypeStruct(fresh_noise.shape, F32),
@@ -736,17 +736,17 @@
         "ha" + "h" * 6 + "ss",
         places + [pltpu.SemaphoreType.DMA((len(smalls),))],
     )(*smalls, guide_table, guide_index)
-    upper, lower, right = lax.optimization_barrier((upper, lower, right))
+    upper, lower, both = lax.optimization_barrier((upper, lower, both))
     away = [part, part_tok, part_scene, upper, lower]
     away_far = [swapped(piece, "cfg", 1) for piece in away]
 
     mine, send = kernel_call(
         functools.partial(finish_kernel, half, values, queues),
         [half_shape] * 2,
-        "v" * 13,
+        "v" * 12,
         [pltpu.VMEM((values, row_lanes), F32), pltpu.VMEM((width, row_lanes), F32)],
         bytes_accessed=8_000_000,
-    )(*away, *away_far, received, left, right)
+    )(*away, *away_far, received, both)
     partner = swapped(send, "cfg", 1)
     shape = jax.ShapeDtypeStruct((frames, half, tokens), F32)
     return kernel_call(update_kernel, [shape, shape], "v" * 6)(mine, partner, *rest)

time: 65.5 us -> 66.2 us (1.011)
  local copies, waits for them, and re-layouts: 5.3 us -> 9.29 us
  waiting for transfers between devices: 15.7 us -> 12.4 us
    unnamed x38 -> x50, local copies, waits for them, and re-layouts: 5.26 us -> 9.26 us
    ppermute x18, waiting for transfers between devices: 6.49 us -> 3.89 us  [swapped(): return lax.ppermute(value, axis, [(i, i ^ mask) for i in range(count)])]
    all_to_all x1, waiting for transfers between devices: 4.69 us -> 4.02 us  [on_device_heads(): received = lax.all_to_all(attended, ('tok', 'queue', 'scene'), 0, 0)]
where the time goes in v15:
time: 66.2 us; the launch traced here: 65.7 us
  starting transfers between devices  26.7 us (40%)
  Pallas kernels  15.7 us (24%)
  waiting for transfers between devices  12.4 us (19%)
  local copies, waits for them, and re-layouts  9.29 us (14%)
  between operations  1.56 us (2%)
    ppermute x18, starting transfers between devices, swapped(): return lax.ppermute(value, axis, [(i, i ^ mask) for i in range(count)])  18 us
    unnamed x50, local copies, waits for them, and re-layouts  9.26 us
    pallas_call x1, Pallas kernels, on_device_heads(): kernel_call(functools.partial(attend_kernel, frames, tokens, queues), jax...  6.13 us
    ppermute x1, waiting for transfers between devices, on_device_heads(): lax.ppermute(first, 'queue', [(i + 1, i) for i in range(queues - 1)])  4.5 us
    all_to_all x1, waiting for transfers between devices, on_device_heads(): received = lax.all_to_all(attended, ('tok', 'queue', 'scene'), 0, 0)  4.02 us
    ppermute x18, waiting for transfers between devices, swapped(): return lax.ppermute(value, axis, [(i, i ^ mask) for i in range(count)])  3.89 us
    all_to_all x1, starting transfers between devices, on_device_heads(): shares = lax.all_to_all(copies, ('scene', 'queue', 'tok'), 0, 0)  3.83 us
    all_to_all x1, starting transfers between devices, on_device_heads(): received = lax.all_to_all(attended, ('tok', 'queue', 'scene'), 0, 0)  3.58 us
  transfers between devices with their start and end apart: 21, of which 6 were waited for; matrix products, arithmetic and copies ran while one was open for 0% of the time, Pallas kernels for 14%

profile of v15, /device:TPU:0, one launch (start us, length us, event | category | flops | bytes accessed | tf_op | source)
XLA Modules:
  0.0 65.7 jit_solution(13120861709451632768)
XLA Ops:
  0.7 2.9 %shard_map.158 = (bf16[144,504]{1,0:T(8,128)(2,1)}, bf16[144,504]{1,0:T(8,128)(2,1)}, bf16[144,504]{1,0:T(8,128)(2,1)}, bf16[144,504]{1,0:T(8,128)(2,1)}, bf16[1...) custom-call(f32[4,16,48]{2,1,0:T(8,128)} %latents.1, s32[1,4]{1,0:T(1,128)} %bitcast.14, ...), custom_call_target="tpu_custom_call" | custom-call | flops 1000000 | bytes 8000000 | tf_op jit(solution)/shard_map/pallas_call | solution.py:630
  3.6 3.0 %collective-permute-start = (bf16[144,504]{1,0:T(8,128)(2,1)}, bf16[144,504]{1,0:T(8,128)(2,1)S(1)}, u32[]{:S(2)}, u32[]{:S(2)}) collective-permute-start(bf16[144,504]{1,0:T(8,128)(2,1)} %get-tuple-element.40), channel_id=1, source_target_pairs={{0,4},{4,0},{8,12},{12,8},{1,5},{5,1},{9,13},{13,9},{2,6},{6,2},{1... | collective-permute-start | bytes 435464 | tf_op jit(solution)/shard_map/ppermute | solution.py:589
  6.6 2.6 %collective-permute-start.1 = (bf16[144,504]{1,0:T(8,128)(2,1)}, bf16[144,504]{1,0:T(8,128)(2,1)S(1)}, u32[]{:S(2)}, u32[]{:S(2)}) collective-permute-start(bf16[144,504]{1,0:T(8,128)(2,1)} %get-tuple-element.47), channel_id=1, source_target_pairs={{0,8},{4,12},{8,0},{12,4},{1,9},{5,13},{9,1},{13,5},{2,10},{6,14},... | collective-permute-start | bytes 435464 | tf_op jit(solution)/shard_map/ppermute | solution.py:589
  9.2 3.8 %all-to-all-start = ((bf16[16,32,96]{2,1,0:T(8,128)(2,1)}), bf16[16,32,96]{2,1,0:T(8,128)(2,1)S(1)}, u32[]{:S(2)}, u32[]{:S(2)}) async-start(bf16[16,32,96]{2,1,0:T(8,128)(2,1)} %get-tuple-element.50), calls=%async_computation | async-start | bytes 262144 | tf_op jit(solution)/shard_map/all_to_all | solution.py:666
  13.0 3.7 %collective-permute-start.2 = (bf16[144,504]{1,0:T(8,128)(2,1)}, bf16[144,504]{1,0:T(8,128)(2,1)S(1)}, u32[]{:S(2)}, u32[]{:S(2)}) collective-permute-start(bf16[144,504]{1,0:T(8,128)(2,1)} %get-tuple-element.48), channel_id=1, source_target_pairs={{0,12},{4,8},{8,4},{12,0},{1,13},{5,9},{9,5},{13,1},{2,14},{6,10},... | collective-permute-start | bytes 435464 | tf_op jit(solution)/shard_map/ppermute | solution.py:589
  16.8 0.9 %copy-done = f32[16,3,1152]{2,0,1:T(8,128)S(1)} copy-done((f32[16,3,1152]{2,0,1:T(8,128)S(1)}, f32[16,3,1152]{2,0,1:T(8,128)}, u32[]{:S(2)}) %copy-start) | copy-done | bytes 221208
  17.7 0.9 %copy-done.4 = bf16[144,504]{1,0:T(8,128)(2,1)S(1)} copy-done((bf16[144,504]{1,0:T(8,128)(2,1)S(1)}, bf16[144,504]{1,0:T(8,128)(2,1)}, u32[]{:S(2)}) %copy-start.4) | copy-done | bytes 145176
  18.6 0.8 %copy-done.5 = bf16[16,1152]{1,0:T(8,128)(2,1)S(1)} copy-done((bf16[16,1152]{1,0:T(8,128)(2,1)S(1)}, bf16[16,1152]{1,0:T(8,128)(2,1)}, u32[]{:S(2)}) %copy-start.5) | copy-done | bytes 36888
  20.5 1.3 %collective-permute-start.3 = (f32[24,48]{1,0:T(8,128)}, f32[24,48]{1,0:T(8,128)S(1)}, u32[]{:S(2)}, u32[]{:S(2)}) collective-permute-start(f32[24,48]{1,0:T(8,128)} %get-tuple-element.49), channel_id=1, source_target_pairs={{4,0},{8,4},{12,8},{5,1},{9,5},{13,9},{6,2},{10,6},{14,10},{7,3},{... | collective-permute-start | bytes 13832 | tf_op jit(solution)/shard_map/ppermute | solution.py:669
  21.8 4.5 %collective-permute-done.3.refs_1_ = f32[24,48]{1,0:T(8,128)S(1)} collective-permute-done((f32[24,48]{1,0:T(8,128)}, f32[24,48]{1,0:T(8,128)S(1)}, u32[]{:S(2)}, u32[]{:S(2)}) %collective-permute-start.3) | collective-permute-done | bytes 4640 | tf_op jit(solution)/shard_map/ppermute | solution.py:669
  26.3 0.6 copy-done.10
  27.1 1.5 %collective-permute-start.9 = (bf16[144,1152]{1,0:T(8,128)(2,1)S(1)}, bf16[144,1152]{1,0:T(8,128)(2,1)S(1)}, u32[]{:S(2)}, u32[]{:S(2)}) collective-permute-start(bf16[144,1152]{1,0:T(8,128)(2,1)S(1)} %shard_map.162.refs_0_), channel_id=1, source_target_pairs={{0,2},{2,0},{1,3},{3,1},{4,6},{6,4},{5,7},{7,5},{8,10},{10,8},{9,1... | collective-permute-start | bytes 995336 | tf_op jit(solution)/shard_map/ppermute | solution.py:589
  28.6 1.5 %collective-permute-start.10 = (bf16[144,1152]{1,0:T(8,128)(2,1)S(1)}, bf16[144,1152]{1,0:T(8,128)(2,1)S(1)}, u32[]{:S(2)}, u32[]{:S(2)}) collective-permute-start(bf16[144,1152]{1,0:T(8,128)(2,1)S(1)} %shard_map.162.refs_0_), channel_id=1, source_target_pairs={{0,16},{16,0},{1,17},{17,1},{2,18},{18,2},{3,19},{19,3},{4,20},{20... | collective-permute-start | bytes 995336 | tf_op jit(solution)/shard_map/ppermute | solution.py:589
  30.6 1.0 %collective-permute-done.8.other = bf16[16,32,96]{2,1,0:T(8,128)(2,1)S(1)} collective-permute-done((bf16[16,32,96]{2,1,0:T(8,128)(2,1)S(1)}, bf16[16,32,96]{2,1,0:T(8,128)(2,1)S(1)}, u32[]{:S(2)}, u32[]{:S(2)}) %collective-permute-start.8) | collective-permute-done | bytes 98336 | tf_op jit(solution)/shard_map/ppermute | solution.py:589
  31.6 1.9 %shard_map.160 = (bf16[1024,1152]{1,0:T(8,128)(2,1)S(1)}, bf16[16,64,256]{2,1,0:T(8,128)(2,1)S(1)}, f32[16,1,256]{2,1,0:T(1,128)S(1)}, f32[2,16,16,128]{3,2,1,0:T(8,128)S(1)}) custom-call(bf16[16,32,96]{2,1,0:T(8,128)(2,1)S(1)} %all-to-all-done.mine, bf16[16,32,96]{2,1,0:T(8,128)(2,1)S(1)} %collective-permute-done.8.other, ...), custom_call_target="tpu_custom_call" | custom-call | flops 1000000 | bytes 8000000 | tf_op jit(solution)/shard_map/pallas_call | solution.py:680
  33.6 6.1 %shard_map.161 = bf16[16,72,240]{2,1,0:T(8,128)(2,1)} custom-call(bf16[144,504]{1,0:T(8,128)(2,1)S(1)} %get-tuple-element.45.refs_0_, bf16[144,504]{1,0:T(8,128)(2,1)S(1)} %collective-permute-done.refs_1_, bf16[144,504]{1,0:T(8,128)(2,1)S(1)} %collective-permute-done.1.refs_2_, bf16[144,504]{1,0:T(8,128)(2,1)S(1)} %collective-permute-done.2.refs_3_, ...), custom_call_target="tpu_custom_call" | custom-call | flops 1000000 | bytes 100000000 | tf_op jit(solution)/shard_map/pallas_call | solution.py:691
  39.8 3.6 %all-to-all-start.1 = ((bf16[16,72,240]{2,1,0:T(8,128)(2,1)}), bf16[16,72,240]{2,1,0:T(8,128)(2,1)S(1)}, u32[]{:S(2)}, u32[]{:S(2)}) async-start(bf16[16,72,240]{2,1,0:T(8,128)(2,1)} %shard_map.161), calls=%async_computation.1 | async-start | bytes 1179648 | tf_op jit(solution)/shard_map/all_to_all | solution.py:707
  43.4 1.9 %collective-permute-start.11 = (bf16[80,1152]{1,0:T(8,128)(2,1)S(1)}, bf16[80,1152]{1,0:T(8,128)(2,1)S(1)}, u32[]{:S(2)}, u32[]{:S(2)}) collective-permute-start(bf16[80,1152]{1,0:T(8,128)(2,1)S(1)} %slice.6), channel_id=1, source_target_pairs={{0,16},{16,0},{1,17},{17,1},{2,18},{18,2},{3,19},{19,3},{4,20},{20... | collective-permute-start | bytes 552968 | tf_op jit(solution)/shard_map/ppermute | solution.py:589
  45.3 1.6 %collective-permute-start.12 = (bf16[64,1152]{1,0:T(8,128)(2,1)S(1)}, bf16[64,1152]{1,0:T(8,128)(2,1)S(1)}, u32[]{:S(2)}, u32[]{:S(2)}) collective-permute-start(bf16[64,1152]{1,0:T(8,128)(2,1)S(1)} %slice.7), channel_id=1, source_target_pairs={{0,2},{2,0},{1,3},{3,1},{4,6},{6,4},{5,7},{7,5},{8,10},{10,8},{9,1... | collective-permute-start | bytes 442376 | tf_op jit(solution)/shard_map/ppermute | solution.py:589
  48.1 0.7 %copy-done.11 = f32[24,48]{1,0:T(8,128)S(1)} copy-done((f32[24,48]{1,0:T(8,128)S(1)}, f32[24,48]{1,0:T(8,128)}, u32[]{:S(2)}) %copy-start.11) | copy-done | bytes 4632
  48.8 0.7 %copy-done.16 = f32[8,48]{1,0:T(8,128)S(1)} copy-done((f32[8,48]{1,0:T(8,128)S(1)}, f32[8,48]{1,0:T(8,128)}, u32[]{:S(2)}) %copy-start.16) | copy-done | bytes 1560
  49.5 0.7 copy-done.21
  50.1 1.0 %shard_map.163 = (bf16[112,1392]{1,0:T(8,128)(2,1)S(1)}, f32[8,240]{1,0:T(8,128)S(1)}, f32[8,240]{1,0:T(8,128)S(1)}, f32[8,48]{1,0:T(8,128)S(1)}, f32[8,128]{1,0:T(8,128)S(1)}) custom-call(f32[24,192]{1,0:T(8,128)S(1)} %copy-done.8, f32[24,48]{1,0:T(8,128)S(1)} %copy-done.11, f32[1,1152]{1,0:T(1,128)S(1)} %copy-done.9, f32[3,16,1152]{2,1,0:T(8,128)S(1)} %bitcast.8, ...), custom_call_target="tpu_custom_call" | custom-call | flops 1000000 | bytes 1000000 | tf_op jit(solution)/shard_map/pallas_call | solution.py:727
  51.1 0.6 copy-done.12
  51.7 0.6 copy-done.14
  54.5 1.1 %collective-permute-done.17.refs_9_ = bf16[64,1152]{1,0:T(8,128)(2,1)S(1)} collective-permute-done((bf16[64,1152]{1,0:T(8,128)(2,1)S(1)}, bf16[64,1152]{1,0:T(8,128)(2,1)S(1)}, u32[]{:S(2)}, u32[]{:S(2)}) %collective-permute-start.17) | collective-permute-done | bytes 147488 | tf_op jit(solution)/shard_map/ppermute | solution.py:589
  55.6 0.7 %copy-done.2 = bf16[64,1152]{1,0:T(8,128)(2,1)} copy-done((bf16[64,1152]{1,0:T(8,128)(2,1)}, bf16[64,1152]{1,0:T(8,128)(2,1)S(1)}, u32[]{:S(2)}) %copy-start.2) | copy-done | bytes 147480
  56.3 4.0 %all-to-all-done.1.refs_10_ = bf16[16,72,240]{2,1,0:T(8,128)(2,1)S(1)} async-done(((bf16[16,72,240]{2,1,0:T(8,128)(2,1)}), bf16[16,72,240]{2,1,0:T(8,128)(2,1)S(1)}, u32[]{:S(2)}, u32[]{:S(2)}) %all-to-all-start.1) | async-done | bytes 552992 | tf_op jit(solution)/shard_map/all_to_all | solution.py:707
  60.3 0.9 %copy-done.3 = bf16[64,1152]{1,0:T(8,128)(2,1)S(1)} copy-done((bf16[64,1152]{1,0:T(8,128)(2,1)S(1)}, bf16[64,1152]{1,0:T(8,128)(2,1)}, u32[]{:S(2)}) %copy-start.3) | copy-done | bytes 147480
  61.2 2.5 %shard_map.164 = (f32[8,240]{1,0:T(8,128)S(1)}, f32[8,240]{1,0:T(8,128)S(1)}) custom-call(bf16[144,1152]{1,0:T(8,128)(2,1)S(1)} %shard_map.162.refs_0_, bf16[144,1152]{1,0:T(8,128)(2,1)S(1)} %collective-permute-done.9.refs_1_, bf16[144,1152]{1,0:T(8,128)(2,1)S(1)} %collective-permute-done.10.refs_2_, bf16[80,1152]{1,0:T(8,128)(2,1)S(1)} %collective-permute-done.11.refs_3_, ...), custom_call_target="tpu_custom_call" | custom-call | flops 1000000 | bytes 8000000 | tf_op jit(solution)/shard_map/pallas_call | solution.py:743
  63.7 1.2 %collective-permute-done.18.partner = f32[8,240]{1,0:T(8,128)S(1)} collective-permute-done((f32[8,240]{1,0:T(8,128)S(1)}, f32[8,240]{1,0:T(8,128)S(1)}, u32[]{:S(2)}, u32[]{:S(2)}) %collective-permute-start.18) | collective-permute-done | bytes 7712 | tf_op jit(solution)/shard_map/ppermute | solution.py:589
  64.9 0.7 %shard_map.165 = (f32[4,8,48]{2,1,0:T(8,128)}, f32[4,8,48]{2,1,0:T(8,128)}) custom-call(f32[8,240]{1,0:T(8,128)S(1)} %get-tuple-element.72.mine, f32[8,240]{1,0:T(8,128)S(1)} %collective-permute-done.18.partner, f32[8,240]{1,0:T(8,128)S(1)} %copy-done.13, f32[8,240]{1,0:T(8,128)S(1)} %copy-done.15, f32[8,48]{1,0:T(8,128)S(1)} %copy-done.18, ...), custom_call_target="tpu_custom_call" | custom-call | flops 1000000 | bytes 1000000 | tf_op jit(solution)/shard_map/pallas_call | solution.py:752
  (71 shorter events, 4.6 us)
Async XLA Ops:
  0.6 32.9 %copy-start.22 = (f32[72]{0:T(128)S(1)}, f32[72]{0:T(128)}, u32[]{:S(2)}) copy-start(f32[72]{0:T(128)} %param.23) | copy-start | bytes 868
  0.6 32.9 %copy-start.23 = (f32[72]{0:T(128)S(1)}, f32[72]{0:T(128)}, u32[]{:S(2)}) copy-start(f32[72]{0:T(128)} %param.24) | copy-start | bytes 868
  3.6 16.2 %collective-permute-start = (bf16[144,504]{1,0:T(8,128)(2,1)}, bf16[144,504]{1,0:T(8,128)(2,1)S(1)}, u32[]{:S(2)}, u32[]{:S(2)}) collective-permute-start(bf16[144,504]{1,0:T(8,128)(2,1)} %get-tuple-element.40), channel_id=1, source_target_pairs={{0,4},{4,0},{8,12},{12,8},{1,5},{5,1},{9,13},{13,9},{2,6},{6,2},{1... | collective-permute-start | bytes 435464 | tf_op jit(solution)/shard_map/ppermute | solution.py:589
  6.6 13.8 %collective-permute-start.1 = (bf16[144,504]{1,0:T(8,128)(2,1)}, bf16[144,504]{1,0:T(8,128)(2,1)S(1)}, u32[]{:S(2)}, u32[]{:S(2)}) collective-permute-start(bf16[144,504]{1,0:T(8,128)(2,1)} %get-tuple-element.47), channel_id=1, source_target_pairs={{0,8},{4,12},{8,0},{12,4},{1,9},{5,13},{9,1},{13,5},{2,10},{6,14},... | collective-permute-start | bytes 435464 | tf_op jit(solution)/shard_map/ppermute | solution.py:589
  9.2 17.7 %all-to-all-start = ((bf16[16,32,96]{2,1,0:T(8,128)(2,1)}), bf16[16,32,96]{2,1,0:T(8,128)(2,1)S(1)}, u32[]{:S(2)}, u32[]{:S(2)}) async-start(bf16[16,32,96]{2,1,0:T(8,128)(2,1)} %get-tuple-element.50), calls=%async_computation | async-start | bytes 262144 | tf_op jit(solution)/shard_map/all_to_all | solution.py:666
  13.0 13.8 %collective-permute-start.2 = (bf16[144,504]{1,0:T(8,128)(2,1)}, bf16[144,504]{1,0:T(8,128)(2,1)S(1)}, u32[]{:S(2)}, u32[]{:S(2)}) collective-permute-start(bf16[144,504]{1,0:T(8,128)(2,1)} %get-tuple-element.48), channel_id=1, source_target_pairs={{0,12},{4,8},{8,4},{12,0},{1,13},{5,9},{9,5},{13,1},{2,14},{6,10},... | collective-permute-start | bytes 435464 | tf_op jit(solution)/shard_map/ppermute | solution.py:589
  16.8 10.1 %collective-permute-start.4 = (bf16[144,504]{1,0:T(8,128)(2,1)}, bf16[144,504]{1,0:T(8,128)(2,1)S(1)}, u32[]{:S(2)}, u32[]{:S(2)}) collective-permute-start(bf16[144,504]{1,0:T(8,128)(2,1)} %get-tuple-element.41.own_source), channel_id=1, source_target_pairs={{0,1},{1,0},{2,3},{3,2},{4,5},{5,4},{6,7},{7,6},{8,9},{9,8},{10,11... | collective-permute-start | bytes 435464 | tf_op jit(solution)/shard_map/ppermute | solution.py:589
  19.8 7.1 %collective-permute-start.5 = (bf16[144,504]{1,0:T(8,128)(2,1)S(1)}, bf16[144,504]{1,0:T(8,128)(2,1)S(1)}, u32[]{:S(2)}, u32[]{:S(2)}) collective-permute-start(bf16[144,504]{1,0:T(8,128)(2,1)S(1)} %collective-permute-done.refs_1_), channel_id=1, source_target_pairs={{0,1},{1,0},{2,3},{3,2},{4,5},{5,4},{6,7},{7,6},{8,9},{9,8},{10,11... | collective-permute-start | bytes 435464 | tf_op jit(solution)/shard_map/ppermute | solution.py:589
  20.4 6.5 %collective-permute-start.6 = (bf16[144,504]{1,0:T(8,128)(2,1)S(1)}, bf16[144,504]{1,0:T(8,128)(2,1)S(1)}, u32[]{:S(2)}, u32[]{:S(2)}) collective-permute-start(bf16[144,504]{1,0:T(8,128)(2,1)S(1)} %collective-permute-done.1.refs_2_), channel_id=1, source_target_pairs={{0,1},{1,0},{2,3},{3,2},{4,5},{5,4},{6,7},{7,6},{8,9},{9,8},{10,11... | collective-permute-start | bytes 435464 | tf_op jit(solution)/shard_map/ppermute | solution.py:589
  20.5 5.8 %collective-permute-start.3 = (f32[24,48]{1,0:T(8,128)}, f32[24,48]{1,0:T(8,128)S(1)}, u32[]{:S(2)}, u32[]{:S(2)}) collective-permute-start(f32[24,48]{1,0:T(8,128)} %get-tuple-element.49), channel_id=1, source_target_pairs={{4,0},{8,4},{12,8},{5,1},{9,5},{13,9},{6,2},{10,6},{14,10},{7,3},{... | collective-permute-start | bytes 13832 | tf_op jit(solution)/shard_map/ppermute | solution.py:669
  27.1 12.7 %collective-permute-start.9 = (bf16[144,1152]{1,0:T(8,128)(2,1)S(1)}, bf16[144,1152]{1,0:T(8,128)(2,1)S(1)}, u32[]{:S(2)}, u32[]{:S(2)}) collective-permute-start(bf16[144,1152]{1,0:T(8,128)(2,1)S(1)} %shard_map.162.refs_0_), channel_id=1, source_target_pairs={{0,2},{2,0},{1,3},{3,1},{4,6},{6,4},{5,7},{7,5},{8,10},{10,8},{9,1... | collective-permute-start | bytes 995336 | tf_op jit(solution)/shard_map/ppermute | solution.py:589
  28.6 11.1 %collective-permute-start.10 = (bf16[144,1152]{1,0:T(8,128)(2,1)S(1)}, bf16[144,1152]{1,0:T(8,128)(2,1)S(1)}, u32[]{:S(2)}, u32[]{:S(2)}) collective-permute-start(bf16[144,1152]{1,0:T(8,128)(2,1)S(1)} %shard_map.162.refs_0_), channel_id=1, source_target_pairs={{0,16},{16,0},{1,17},{17,1},{2,18},{18,2},{3,19},{19,3},{4,20},{20... | collective-permute-start | bytes 995336 | tf_op jit(solution)/shard_map/ppermute | solution.py:589
  30.1 3.4 %collective-permute-start.7 = (bf16[144,504]{1,0:T(8,128)(2,1)S(1)}, bf16[144,504]{1,0:T(8,128)(2,1)S(1)}, u32[]{:S(2)}, u32[]{:S(2)}) collective-permute-start(bf16[144,504]{1,0:T(8,128)(2,1)S(1)} %collective-permute-done.2.refs_3_), channel_id=1, source_target_pairs={{0,1},{1,0},{2,3},{3,2},{4,5},{5,4},{6,7},{7,6},{8,9},{9,8},{10,11... | collective-permute-start | bytes 435464 | tf_op jit(solution)/shard_map/ppermute | solution.py:589
  30.1 1.6 %collective-permute-start.8 = (bf16[16,32,96]{2,1,0:T(8,128)(2,1)S(1)}, bf16[16,32,96]{2,1,0:T(8,128)(2,1)S(1)}, u32[]{:S(2)}, u32[]{:S(2)}) collective-permute-start(bf16[16,32,96]{2,1,0:T(8,128)(2,1)S(1)} %all-to-all-done.mine), channel_id=1, source_target_pairs={{0,1},{1,0},{2,3},{3,2},{4,5},{5,4},{6,7},{7,6},{8,9},{9,8},{10,11... | collective-permute-start | bytes 294920 | tf_op jit(solution)/shard_map/ppermute | solution.py:589
  33.6 13.8 %copy-start.24 = (f32[1152]{0:T(1024)S(1)}, f32[1152]{0:T(1024)}, u32[]{:S(2)}) copy-start(f32[1152]{0:T(1024)} %param.26) | copy-start | bytes 13828
  33.6 14.5 %copy-start.1 = (f32[16,3,1152]{2,0,1:T(8,128)S(1)}, f32[16,3,1152]{2,0,1:T(8,128)}, u32[]{:S(2)}) copy-start(f32[16,3,1152]{2,0,1:T(8,128)} %param.20) | copy-start | bytes 663556
  33.6 14.4 %copy-start.6 = (bf16[16,1152]{1,0:T(8,128)(2,1)S(1)}, bf16[16,1152]{1,0:T(8,128)(2,1)}, u32[]{:S(2)}) copy-start(bf16[16,1152]{1,0:T(8,128)(2,1)} %refs_4_.1) | copy-start | bytes 110596
  33.6 14.4 %copy-start.7 = (bf16[1152,16]{0,1:T(8,128)(2,1)S(1)}, bf16[1152,16]{0,1:T(8,128)(2,1)}, u32[]{:S(2)}) copy-start(bf16[1152,16]{0,1:T(8,128)(2,1)} %param.27) | copy-start | bytes 110596
  33.6 14.4 %copy-start.8 = (f32[24,192]{1,0:T(8,128)S(1)}, f32[24,192]{1,0:T(8,128)}, u32[]{:S(2)}) copy-start(f32[24,192]{1,0:T(8,128)} %get-tuple-element.65.refs_0_) | copy-start | bytes 55300
  33.6 14.4 %copy-start.9 = (f32[1,1152]{1,0:T(1,128)S(1)}, f32[1,1152]{1,0:T(1,128)}, u32[]{:S(2)}) copy-start(f32[1,1152]{1,0:T(1,128)} %refs_2_.1) | copy-start | bytes 13828
  39.8 20.5 %all-to-all-start.1 = ((bf16[16,72,240]{2,1,0:T(8,128)(2,1)}), bf16[16,72,240]{2,1,0:T(8,128)(2,1)S(1)}, u32[]{:S(2)}, u32[]{:S(2)}) async-start(bf16[16,72,240]{2,1,0:T(8,128)(2,1)} %shard_map.161), calls=%async_computation.1 | async-start | bytes 1179648 | tf_op jit(solution)/shard_map/all_to_all | solution.py:707
  43.4 10.6 %collective-permute-start.11 = (bf16[80,1152]{1,0:T(8,128)(2,1)S(1)}, bf16[80,1152]{1,0:T(8,128)(2,1)S(1)}, u32[]{:S(2)}, u32[]{:S(2)}) collective-permute-start(bf16[80,1152]{1,0:T(8,128)(2,1)S(1)} %slice.6), channel_id=1, source_target_pairs={{0,16},{16,0},{1,17},{17,1},{2,18},{18,2},{3,19},{19,3},{4,20},{20... | collective-permute-start | bytes 552968 | tf_op jit(solution)/shard_map/ppermute | solution.py:589
  45.3 8.7 %collective-permute-start.12 = (bf16[64,1152]{1,0:T(8,128)(2,1)S(1)}, bf16[64,1152]{1,0:T(8,128)(2,1)S(1)}, u32[]{:S(2)}, u32[]{:S(2)}) collective-permute-start(bf16[64,1152]{1,0:T(8,128)(2,1)S(1)} %slice.7), channel_id=1, source_target_pairs={{0,2},{2,0},{1,3},{3,1},{4,6},{6,4},{5,7},{7,5},{8,10},{10,8},{9,1... | collective-permute-start | bytes 442376 | tf_op jit(solution)/shard_map/ppermute | solution.py:589
  46.8 7.6 %collective-permute-start.13 = (bf16[144,1152]{1,0:T(8,128)(2,1)S(1)}, bf16[144,1152]{1,0:T(8,128)(2,1)S(1)}, u32[]{:S(2)}, u32[]{:S(2)}) collective-permute-start(bf16[144,1152]{1,0:T(8,128)(2,1)S(1)} %shard_map.162.refs_0_), channel_id=1, source_target_pairs={{0,1},{1,0},{2,3},{3,2},{4,5},{5,4},{6,7},{7,6},{8,9},{9,8},{10,11... | collective-permute-start | bytes 995336 | tf_op jit(solution)/shard_map/ppermute | solution.py:589
  46.8 7.6 %collective-permute-start.14 = (bf16[144,1152]{1,0:T(8,128)(2,1)S(1)}, bf16[144,1152]{1,0:T(8,128)(2,1)S(1)}, u32[]{:S(2)}, u32[]{:S(2)}) collective-permute-start(bf16[144,1152]{1,0:T(8,128)(2,1)S(1)} %collective-permute-done.9.refs_1_), channel_id=1, source_target_pairs={{0,1},{1,0},{2,3},{3,2},{4,5},{5,4},{6,7},{7,6},{8,9},{9,8},{10,11... | collective-permute-start | bytes 995336 | tf_op jit(solution)/shard_map/ppermute | solution.py:589
  47.4 7.1 %collective-permute-start.15 = (bf16[144,1152]{1,0:T(8,128)(2,1)S(1)}, bf16[144,1152]{1,0:T(8,128)(2,1)S(1)}, u32[]{:S(2)}, u32[]{:S(2)}) collective-permute-start(bf16[144,1152]{1,0:T(8,128)(2,1)S(1)} %collective-permute-done.10.refs_2_), channel_id=1, source_target_pairs={{0,1},{1,0},{2,3},{3,2},{4,5},{5,4},{6,7},{7,6},{8,9},{9,8},{10,11... | collective-permute-start | bytes 995336 | tf_op jit(solution)/shard_map/ppermute | solution.py:589
  54.0 2.3 %collective-permute-start.16 = (bf16[80,1152]{1,0:T(8,128)(2,1)S(1)}, bf16[80,1152]{1,0:T(8,128)(2,1)S(1)}, u32[]{:S(2)}, u32[]{:S(2)}) collective-permute-start(bf16[80,1152]{1,0:T(8,128)(2,1)S(1)} %collective-permute-done.11.refs_3_), channel_id=1, source_target_pairs={{0,1},{1,0},{2,3},{3,2},{4,5},{5,4},{6,7},{7,6},{8,9},{9,8},{10,11... | collective-permute-start | bytes 552968 | tf_op jit(solution)/shard_map/ppermute | solution.py:589
  54.0 1.6 %collective-permute-start.17 = (bf16[64,1152]{1,0:T(8,128)(2,1)S(1)}, bf16[64,1152]{1,0:T(8,128)(2,1)S(1)}, u32[]{:S(2)}, u32[]{:S(2)}) collective-permute-start(bf16[64,1152]{1,0:T(8,128)(2,1)S(1)} %collective-permute-done.12.refs_4_), channel_id=1, source_target_pairs={{0,1},{1,0},{2,3},{3,2},{4,5},{5,4},{6,7},{7,6},{8,9},{9,8},{10,11... | collective-permute-start | bytes 442376 | tf_op jit(solution)/shard_map/ppermute | solution.py:589
  61.2 3.7 %copy-start.15 = (f32[8,240]{1,0:T(8,128)S(1)}, f32[8,240]{1,0:T(8,128)}, u32[]{:S(2)}) copy-start(f32[8,240]{1,0:T(8,128)} %copy-done.14) | copy-start | bytes 23044
  61.2 3.7 %copy-start.18 = (f32[8,48]{1,0:T(8,128)S(1)}, f32[8,48]{1,0:T(8,128)}, u32[]{:S(2)}) copy-start(f32[8,48]{1,0:T(8,128)} %copy-done.17) | copy-start | bytes 4612
  61.2 3.7 %copy-start.20 = (f32[8,128]{1,0:T(8,128)S(1)}, f32[8,128]{1,0:T(8,128)}, u32[]{:S(2)}) copy-start(f32[8,128]{1,0:T(8,128)} %copy-done.19) | copy-start | bytes 12292
  63.7 1.2 %collective-permute-start.18 = (f32[8,240]{1,0:T(8,128)S(1)}, f32[8,240]{1,0:T(8,128)S(1)}, u32[]{:S(2)}, u32[]{:S(2)}) collective-permute-start(f32[8,240]{1,0:T(8,128)S(1)} %get-tuple-element.73), channel_id=1, source_target_pairs={{0,1},{1,0},{2,3},{3,2},{4,5},{5,4},{6,7},{7,6},{8,9},{9,8},{10,11... | collective-permute-start | bytes 23048 | tf_op jit(solution)/shard_map/ppermute | solution.py:589
  (14 other events, 12.9 us)
